TPU v7x, 32 devices: a whole 2x2x4 slice. The times are simulated.
32 devices in a mesh: blk: 16 (over z, y, x), head: 2 (over core).
Axes of the slice: x: 2, y: 2, z: 4, core: 2. Of those that a mesh axis runs over, the one named last changes fastest.
Arguments:
- query_rows: bfloat16 [4096, 2048], P(('blk', 'head')), may hold values from -30 to 30
- key_rows: bfloat16 [4096, 2048], P(('blk', 'head')), may hold values from -30 to 30
- value_rows: bfloat16 [4096, 2048], P(('blk', 'head')), may hold values from -6 to 6
- out_grad: bfloat16 [4096, 2048], P(('blk', 'head')), may hold values from -6 to 6
- doc_ids: int32 [4096], replicated, may hold values from 0 to 31, never falling along the last dimension, each value on 1 to 256 neighbouring positions
Outputs:
- attended: bfloat16 [4096, 2048], P(('blk', 'head'))
- query_grad: bfloat16 [4096, 2048], P(('blk', 'head'))
- key_grad: bfloat16 [4096, 2048], P(('blk', 'head'))
- value_grad: bfloat16 [4096, 2048], P(('blk', 'head'))
Inputs may be any that keep to these rules, and one draw needn't show every extreme that they name: doc_ids never fall; each document holds 1 to 256 tokens, one exactly 256.
All inputs are finite; a program needn't handle non-finite values.
Results may differ from a plain program's by a relative error of at most 0.02.
Values may be sent and summed in bfloat16 or wider, within the bound.
No kernel may reach another device: no remote copies, remote signals or barrier semaphores. Data moves between devices by JAX's collectives and lax.ppermute only.
A program may use at most 64 MiB of HBM per device.

v0:
```python
import math

import jax
import jax.numpy as jnp
from jax import lax
from jax.sharding import PartitionSpec as P

DH = 128
DOC_MOST = 256


masked_score = -1e30


def shifted(block, axis, distance):
    devices = range(lax.axis_size(axis))
    route = [(i - distance, i) for i in devices if i - distance in devices]
    return lax.ppermute(block, axis, route)


def pick_block(row_count):
    chosen = 1
    for divisor in range(1, min(row_count, 512) + 1):
        if row_count % divisor == 0:
            chosen = divisor
    return chosen


def body(query_rows, key_rows, value_rows, out_grad, doc_ids):
    queries, keyset, valueset, grad_rows = (
        lax.all_to_all(query_rows, "head", split_axis=1, concat_axis=0, tiled=True),
        lax.all_to_all(key_rows, "head", split_axis=1, concat_axis=0, tiled=True),
        lax.all_to_all(value_rows, "head", split_axis=1, concat_axis=0, tiled=True),
        lax.all_to_all(out_grad, "head", split_axis=1, concat_axis=0, tiled=True),
    )
    rows_here, width = queries.shape
    head_count = width // DH

    def to_heads(matrix):
        return matrix.reshape(rows_here, head_count, DH)

    def to_flat(matrix):
        return matrix.reshape(rows_here, head_count * DH)

    queries = to_heads(queries)
    keyset = to_heads(keyset)
    valueset = to_heads(valueset)
    grad_rows = to_heads(grad_rows)
    score_scale = 1.0 / math.sqrt(DH)
    edge_rows = min(DOC_MOST, rows_here)
    own_start = lax.axis_index("blk") * rows_here
    seq_total = doc_ids.shape[0]
    own_ids = lax.dynamic_slice_in_dim(doc_ids, own_start, rows_here, 0)

    def ids_at(first_row, row_count):
        inside = (first_row >= 0) & (first_row + row_count <= seq_total)
        clamped = jnp.clip(first_row, 0, seq_total - row_count)
        return jnp.where(inside, lax.dynamic_slice_in_dim(doc_ids, clamped, row_count, 0), -1)

    def tile_scores(query_blk, key_blk, query_ids, key_ids):
        scores = (
            jnp.einsum("qhd,khd->hqk", query_blk, key_blk, preferred_element_type=jnp.float32)
            * score_scale
        )
        same_doc = (query_ids[:, None] == key_ids[None, :])[None]
        return (jnp.where(same_doc, scores, jnp.float32(masked_score)), same_doc)

    def blockwise(carried, received, first_row, tile_fn):
        row_count = received[0].shape[0]
        block_rows = pick_block(row_count)

        def step(turn_no, running):
            offset = turn_no * block_rows
            pieces = tuple(
                (lax.dynamic_slice_in_dim(member, offset, block_rows, 0) for member in received)
            )
            part_ids = ids_at(first_row + offset, block_rows)
            return tile_fn(running, pieces, part_ids)

        return lax.fori_loop(0, row_count // block_rows, step, carried)

    def forward_tile(running, pieces, part_ids):
        row_top, row_sum, weighted = running
        key_blk, value_blk = pieces
        scores, same_doc = tile_scores(queries, key_blk, own_ids, part_ids)
        new_top = jnp.maximum(row_top, jnp.max(scores, axis=2))
        factor = jnp.exp(row_top - new_top)
        prob_tile = jnp.where(same_doc, jnp.exp(scores - new_top[:, :, None]), jnp.float32(0.0))
        row_sum = row_sum * factor + jnp.sum(prob_tile, axis=2)
        weighted = weighted * factor[:, :, None] + jnp.einsum(
            "hqk,khd->hqd",
            prob_tile.astype(jnp.bfloat16),
            value_blk,
            preferred_element_type=jnp.float32,
        )
        return (new_top, row_sum, weighted)

    pairs = jnp.stack((keyset, valueset))
    pairs_low = shifted(pairs, "blk", 1)
    pairs_high = shifted(pairs, "blk", -1)
    initial = (
        jnp.full((head_count, rows_here), masked_score, jnp.float32),
        jnp.zeros((head_count, rows_here), jnp.float32),
        jnp.zeros((head_count, rows_here, DH), jnp.float32),
    )
    running = blockwise(initial, (keyset, valueset), own_start, forward_tile)
    running = blockwise(running, (pairs_low[0], pairs_low[1]), own_start - edge_rows, forward_tile)
    row_top, row_sum, weighted = blockwise(
        running, (pairs_high[0], pairs_high[1]), own_start + rows_here, forward_tile
    )
    log_total = row_top + jnp.log(row_sum)
    attended_rows = (weighted / row_sum[:, :, None]).astype(jnp.bfloat16).transpose(1, 0, 2)
    row_delta = jnp.sum(grad_rows.astype(jnp.float32) * attended_rows.astype(jnp.float32), axis=2)
    own_delta = row_delta.transpose(1, 0)
    zero_rows = jnp.zeros((rows_here, head_count, DH), jnp.float32)

    def query_tile(running, pieces, part_ids):
        key_acc, value_acc = running
        query_blk, grad_blk, lse_blk, delta_blk = pieces
        scores, same_doc = tile_scores(query_blk, keyset, part_ids, own_ids)
        prob_tile = jnp.where(
            same_doc, jnp.exp(scores - lse_blk.transpose(1, 0)[:, :, None]), jnp.float32(0.0)
        )
        value_acc = value_acc + jnp.einsum(
            "hqk,qhd->khd",
            prob_tile.astype(jnp.bfloat16),
            grad_blk,
            preferred_element_type=jnp.float32,
        )
        prob_grad = jnp.einsum(
            "qhd,khd->hqk", grad_blk, valueset, preferred_element_type=jnp.float32
        )
        score_grad = (prob_tile * (prob_grad - delta_blk.transpose(1, 0)[:, :, None])).astype(
            jnp.bfloat16
        )
        key_acc = key_acc + score_scale * jnp.einsum(
            "hqk,qhd->khd", score_grad, query_blk, preferred_element_type=jnp.float32
        )
        return (key_acc, value_acc)

    def grad_tile(running, pieces, part_ids):
        key_blk, value_blk = pieces
        scores, same_doc = tile_scores(queries, key_blk, own_ids, part_ids)
        prob_tile = jnp.where(same_doc, jnp.exp(scores - log_total[:, :, None]), jnp.float32(0.0))
        prob_grad = jnp.einsum(
            "qhd,khd->hqk", grad_rows, value_blk, preferred_element_type=jnp.float32
        )
        score_grad = (prob_tile * (prob_grad - own_delta[:, :, None])).astype(jnp.bfloat16)
        return running + score_scale * jnp.einsum(
            "hqk,khd->qhd", score_grad, key_blk, preferred_element_type=jnp.float32
        )

    lse_rows = log_total.transpose(1, 0)
    inputs = jnp.stack((queries, grad_rows))
    stats = jnp.stack((lse_rows, row_delta))
    inputs_low = shifted(inputs, "blk", 1)
    inputs_high = shifted(inputs, "blk", -1)
    stats_low = shifted(stats, "blk", 1)
    stats_high = shifted(stats, "blk", -1)
    grads = blockwise(
        (zero_rows, zero_rows), (queries, grad_rows, lse_rows, row_delta), own_start, query_tile
    )
    grads = blockwise(
        grads,
        (inputs_low[0], inputs_low[1], stats_low[0], stats_low[1]),
        own_start - edge_rows,
        query_tile,
    )
    key_acc, value_acc = blockwise(
        grads,
        (inputs_high[0], inputs_high[1], stats_high[0], stats_high[1]),
        own_start + rows_here,
        query_tile,
    )
    query_acc = blockwise(zero_rows, (keyset, valueset), own_start, grad_tile)
    query_acc = blockwise(query_acc, (pairs_low[0], pairs_low[1]), own_start - edge_rows, grad_tile)
    query_acc = blockwise(
        query_acc, (pairs_high[0], pairs_high[1]), own_start + rows_here, grad_tile
    )
    attended, query_grad, key_grad, value_grad = (
        lax.all_to_all(to_flat(attended_rows), "head", split_axis=0, concat_axis=1, tiled=True),
        lax.all_to_all(
            to_flat(query_acc.astype(jnp.bfloat16)), "head", split_axis=0, concat_axis=1, tiled=True
        ),
        lax.all_to_all(
            to_flat(key_acc.astype(jnp.bfloat16)), "head", split_axis=0, concat_axis=1, tiled=True
        ),
        lax.all_to_all(
            to_flat(value_acc.astype(jnp.bfloat16)), "head", split_axis=0, concat_axis=1, tiled=True
        ),
    )
    return (attended, query_grad, key_grad, value_grad)


def solution(mesh):
    placed = (
        P(("blk", "head"), None),
        P(("blk", "head"), None),
        P(("blk", "head"), None),
        P(("blk", "head"), None),
        P(),
    )
    return jax.shard_map(
        body,
        mesh=mesh,
        in_specs=placed,
        out_specs=(
            P(("blk", "head"), None),
            P(("blk", "head"), None),
            P(("blk", "head"), None),
            P(("blk", "head"), None),
        ),
        check_vma=False,
    )
```

profile of v0, /device:TPU:9, one launch (start us, length us, event | category | flops | bytes accessed | tf_op | source)
XLA Modules:
  0.0 173.7 jit_solution(9360461681501296865)
XLA Ops:
  0.6 1.9 %copy.362 = bf16[16,2,8,1024]{3,2,0,1:T(8,128)(2,1)} copy(bf16[16,2,8,1024]{3,2,1,0:T(8,128)(2,1)} %bitcast.297) | data formatting | bytes 1048576 | tf_op jit(solution)/shard_map/all_to_all | solution.py:32
  2.6 4.2 %all-to-all-start.1 = ((bf16[128,2,1024]{2,0,1:T(8,128)(2,1)}), bf16[128,2,1024]{2,0,1:T(8,128)(2,1)S(1)}, u32[]{:S(2)}, u32[]{:S(2)}) async-start(bf16[128,2,1024]{2,0,1:T(8,128)(2,1)} %bitcast.271), calls=%async_computation.1 | async-start | bytes 1048576 | tf_op jit(solution)/shard_map/all_to_all | solution.py:32
  8.1 3.9 %all-to-all-start.2 = ((bf16[128,2,1024]{2,0,1:T(8,128)(2,1)}), bf16[128,2,1024]{2,0,1:T(8,128)(2,1)S(1)}, u32[]{:S(2)}, u32[]{:S(2)}) async-start(bf16[128,2,1024]{2,0,1:T(8,128)(2,1)} %bitcast.270), calls=%async_computation.2 | async-start | bytes 1048576 | tf_op jit(solution)/shard_map/all_to_all | solution.py:33
  15.1 4.0 %collective-permute-start.1 = (bf16[2,256,8,128]{3,1,2,0:T(8,128)(2,1)}, bf16[2,256,8,128]{3,1,2,0:T(8,128)(2,1)}, u32[]{:S(2)}, u32[]{:S(2)}) collective-permute-start(bf16[2,256,8,128]{3,1,2,0:T(8,128)(2,1)} %copy_dynamic-update-slice_fusion.2), channel_id=1, source_target_pairs={{2,0},{4,2},{6,4},{8,6},{10,8},{12,10},{14,12},{16,14},{18,16},{20... | collective-permute-start | bytes 3145736 | tf_op jit(solution)/shard_map/ppermute | solution.py:18
  19.1 1.9 %collective-permute-start = (bf16[2,256,8,128]{3,1,2,0:T(8,128)(2,1)}, bf16[2,256,8,128]{3,1,2,0:T(8,128)(2,1)}, u32[]{:S(2)}, u32[]{:S(2)}) collective-permute-start(bf16[2,256,8,128]{3,1,2,0:T(8,128)(2,1)} %copy_dynamic-update-slice_fusion.2), channel_id=1, source_target_pairs={{0,2},{2,4},{4,6},{6,8},{8,10},{10,12},{12,14},{14,16},{16,18},{18... | collective-permute-start | bytes 3145736 | tf_op jit(solution)/shard_map/ppermute | solution.py:18
  21.8 4.1 %all-to-all-start.4 = ((bf16[128,2,1024]{2,0,1:T(8,128)(2,1)}), bf16[128,2,1024]{2,0,1:T(8,128)(2,1)S(1)}, u32[]{:S(2)}, u32[]{:S(2)}) async-start(bf16[128,2,1024]{2,0,1:T(8,128)(2,1)} %bitcast.269), calls=%async_computation.4 | async-start | bytes 1048576 | tf_op jit(solution)/shard_map/all_to_all | solution.py:34
  27.3 3.9 %all-to-all-start = ((bf16[128,2,1024]{2,0,1:T(8,128)(2,1)}), bf16[128,2,1024]{2,0,1:T(8,128)(2,1)S(1)}, u32[]{:S(2)}, u32[]{:S(2)}) async-start(bf16[128,2,1024]{2,0,1:T(8,128)(2,1)} %bitcast.272), calls=%async_computation | async-start | bytes 1048576 | tf_op jit(solution)/shard_map/all_to_all | solution.py:31
  34.4 3.7 %collective-permute-start.2 = (bf16[2,256,8,128]{3,1,2,0:T(8,128)(2,1)}, bf16[2,256,8,128]{3,1,2,0:T(8,128)(2,1)}, u32[]{:S(2)}, u32[]{:S(2)}) collective-permute-start(bf16[2,256,8,128]{3,1,2,0:T(8,128)(2,1)} %copy_dynamic-update-slice_fusion), channel_id=1, source_target_pairs={{0,2},{2,4},{4,6},{6,8},{8,10},{10,12},{12,14},{14,16},{16,18},{18... | collective-permute-start | bytes 3145736 | tf_op jit(solution)/shard_map/ppermute | solution.py:18
  38.1 3.7 %collective-permute-start.4 = (bf16[2,256,8,128]{3,1,2,0:T(8,128)(2,1)}, bf16[2,256,8,128]{3,1,2,0:T(8,128)(2,1)}, u32[]{:S(2)}, u32[]{:S(2)}) collective-permute-start(bf16[2,256,8,128]{3,1,2,0:T(8,128)(2,1)} %copy_dynamic-update-slice_fusion), channel_id=1, source_target_pairs={{2,0},{4,2},{6,4},{8,6},{10,8},{12,10},{14,12},{16,14},{18,16},{20... | collective-permute-start | bytes 3145736 | tf_op jit(solution)/shard_map/ppermute | solution.py:18
  45.8 1.9 %copy.191 = f32[8,256,256]{2,1,0:T(8,128)S(1)} copy(f32[8,256,256]{1,2,0:T(8,128)} %convolution_multiply_fusion) | data formatting | bytes 4194304 | tf_op jit(solution)/shard_map/while/body/eval_jaxpr/mul | solution.py:62
  47.8 2.1 %copy.298 = bf16[256,8,128]{0,2,1:T(8,128)(2,1)} copy(bf16[256,8,128]{2,1,0:T(8,128)(2,1)} %bitcast.284) | data formatting | bytes 1048576 | tf_op jit(solution)/shard_map/reshape | solution.py:40
  54.7 33.5 %collective-permute-done = bf16[2,256,8,128]{3,1,2,0:T(8,128)(2,1)} collective-permute-done((bf16[2,256,8,128]{3,1,2,0:T(8,128)(2,1)}, bf16[2,256,8,128]{3,1,2,0:T(8,128)(2,1)}, u32[]{:S(2)}, u32[]{:S(2)}) %collective-permute-start) | collective-permute-done | bytes 1048608 | tf_op jit(solution)/shard_map/ppermute | solution.py:18
  94.7 2.6 %multiply_reduce_fusion = (f32[256,8]{0,1:T(8,128)S(1)}, bf16[256,8,128]{0,2,1:T(8,128)(2,1)}) fusion(bf16[256,8,128]{0,2,1:T(8,128)(2,1)S(1)} %copy-done.9, f32[256,8]{0,1:T(8,128)S(1)} %get-tuple-element.239, f32[256,8,128]{0,2,1:T(8,128)S(1)} %fusion.26, bf16[2,256,8,128]{3,1,2,0:T(8,128)(2,1)} %collective-permute-done.1, ...), kind=kOutput, calls=%fused_computation.84 | convolution fusion | flops 137623552 | bytes 4808704 | tf_op jit(solution)/shard_map/while/body/eval_jaxpr/hqk,khd->hqd/dot_general | solution.py:90
  97.9 4.1 %collective-permute-start.3 = (f32[2,256,8]{1,2,0:T(8,128)}, f32[2,256,8]{1,2,0:T(8,128)}, u32[]{:S(2)}, u32[]{:S(2)}) collective-permute-start(f32[2,256,8]{1,2,0:T(8,128)} %pad_maximum_fusion), channel_id=1, source_target_pairs={{0,2},{2,4},{4,6},{6,8},{8,10},{10,12},{12,14},{14,16},{16,18},{18... | collective-permute-start | bytes 49160 | tf_op jit(solution)/shard_map/ppermute | solution.py:18
  102.0 3.0 %collective-permute-start.5 = (f32[2,256,8]{1,2,0:T(8,128)}, f32[2,256,8]{1,2,0:T(8,128)}, u32[]{:S(2)}, u32[]{:S(2)}) collective-permute-start(f32[2,256,8]{1,2,0:T(8,128)} %pad_maximum_fusion), channel_id=1, source_target_pairs={{2,0},{4,2},{6,4},{8,6},{10,8},{12,10},{14,12},{16,14},{18,16},{20... | collective-permute-start | bytes 49160 | tf_op jit(solution)/shard_map/ppermute | solution.py:18
  105.0 2.0 %all_to_all.113 = bf16[2,128,1024]{1,0,2:T(2,128)(2,1)} reshape(bf16[256,8,128]{0,2,1:T(8,128)(2,1)} %get-tuple-element.291) | data formatting | bytes 1048576 | tf_op jit(solution)/shard_map/all_to_all | solution.py:181
  108.9 5.3 %all-to-all-start.3 = ((bf16[2,128,1024]{1,2,0:T(8,128)(2,1)}), bf16[2,128,1024]{1,2,0:T(8,128)(2,1)}, u32[]{:S(2)}, u32[]{:S(2)}) async-start(bf16[2,128,1024]{1,2,0:T(8,128)(2,1)} %copy.208), calls=%async_computation.3 | async-start | bytes 1048576 | tf_op jit(solution)/shard_map/all_to_all | solution.py:181
  116.0 3.1 %copy.210 = f32[8,256,256]{1,2,0:T(8,128)} copy(f32[8,256,256]{2,1,0:T(8,128)} %subtract_exponential_fusion) | data formatting | bytes 4194304 | tf_op jit(solution)/shard_map/while/body/eval_jaxpr/exp | solution.py:144
  119.1 2.5 %convolution_bitcast_fusion.2 = f32[256,8,128]{2,0,1:T(8,128)} fusion(bf16[256,8,128]{0,2,1:T(8,128)(2,1)} %copy.267, f32[8,256,256]{1,2,0:T(8,128)S(1)} %copy-done, f32[8,256]{1,0:T(8,128)S(1)} %log_add_fusion, pred[256,256]{0,1:T(8,128)(4,1)S(1)} %get-tuple-element.269), kind=kOutput, calls=%fused_computation.44 | convolution fusion | flops 136314880 | bytes 3743744 | tf_op jit(solution)/shard_map/while/body/eval_jaxpr/hqk,qhd->khd/dot_general | solution.py:124
  121.6 3.9 %fusion.18 = f32[256,8,128]{2,0,1:T(8,128)} fusion(f32[8,256,256]{2,1,0:T(8,128)} %copy-done.6, bf16[256,8,128]{0,2,1:T(8,128)(2,1)} %copy.267, f32[8,256]{1,0:T(8,128)S(1)} %bitcast.302, f32[8,256]{1,0:T(8,128)S(1)} %log_add_fusion, pred[256,256]{1,0:T(8,128)(4,1)S(1)} %get-tuple-element.270, bf16[2,256,8,128]{3,1,2,0:T(8,128)(2,1)} %collective-permute-done.1), kind=kOutput, calls=%fused_computation.35 | convolution fusion | flops 271319040 | bytes 4800512 | tf_op jit(solution)/shard_map/while/body/eval_jaxpr/hqk,khd->qhd/dot_general | solution.py:149
  125.5 3.9 %fusion.20 = f32[256,8,128]{2,0,1:T(8,128)} fusion(f32[8,256,256]{1,2,0:T(8,128)} %copy.210, f32[8,256,256]{1,2,0:T(8,128)} %fusion.142, f32[8,256]{1,0:T(8,128)S(1)} %bitcast.303, pred[256,256]{0,1:T(8,128)(4,1)S(1)} %copy.318, bf16[256,8,128]{2,1,0:T(8,128)(2,1)S(1)} %bitcast.275), kind=kOutput, calls=%fused_computation.39 | convolution fusion | flops 136577024 | bytes 5840896 | tf_op jit(solution)/shard_map/while/body/eval_jaxpr/hqk,khd->qhd/dot_general | solution.py:149
  129.4 3.0 %fusion.99 = f32[8,256,256]{1,2,0:T(8,128)} fusion(bf16[2,256,8,128]{3,1,2,0:T(8,128)(2,1)} %collective-permute-done.2, bf16[256,8,128]{2,1,0:T(8,128)(2,1)S(1)} %bitcast.276), kind=kOutput, calls=%fused_computation.135 | convolution fusion | flops 134217728 | bytes 3145728 | tf_op jit(solution)/shard_map/while/body/eval_jaxpr/qhd,khd->hqk/dot_general | solution.py:62
  132.4 1.9 %fusion.19 = f32[256,8,128]{2,0,1:T(8,128)} fusion(f32[8,256,256]{1,2,0:T(8,128)S(1)} %copy-done.1, f32[8,256,256]{1,2,0:T(8,128)S(1)} %copy-done, f32[8,256]{1,0:T(8,128)S(1)} %log_add_fusion, f32[8,256]{1,0:T(8,128)S(1)} %bitcast.304, pred[256,256]{0,1:T(8,128)(4,1)S(1)} %get-tuple-element.269, bf16[256,8,128]{2,1,0:T(8,128)(2,1)S(1)} %bitcast.282), kind=kOutput, calls=%fused_computation.37 | convolution fusion | flops 137625600 | bytes 5849088 | tf_op jit(solution)/shard_map/while/body/eval_jaxpr/hqk,qhd->khd/dot_general | solution.py:136
  134.3 3.7 %fusion.37 = bf16[256,8,128]{2,0,1:T(8,128)(2,1)S(1)} fusion(f32[256,8,128]{2,0,1:T(8,128)} %fusion.18, f32[256,8,128]{2,0,1:T(8,128)} %fusion.20, f32[8,256,256]{2,1,0:T(8,128)} %copy-done.2, bf16[256,8,128]{0,2,1:T(8,128)(2,1)} %copy.267, f32[8,256]{1,0:T(8,128)S(1)} %bitcast.305, f32[8,256]{1,0:T(8,128)S(1)} %log_add_fusion, ...), kind=kOutput, calls=%fused_computation.62 | convolution fusion | flops 272105472 | bytes 6373376 | tf_op jit(solution)/shard_map/while/body/eval_jaxpr/hqk,khd->qhd/dot_general | solution.py:149
  138.1 2.8 %fusion.100 = f32[8,256,256]{1,2,0:T(8,128)} fusion(bf16[2,256,8,128]{3,1,2,0:T(8,128)(2,1)} %collective-permute-done.4, bf16[256,8,128]{2,1,0:T(8,128)(2,1)S(1)} %bitcast.277), kind=kOutput, calls=%fused_computation.136 | convolution fusion | flops 134217728 | bytes 3145728 | tf_op jit(solution)/shard_map/while/body/eval_jaxpr/qhd,khd->hqk/dot_general | solution.py:62
  140.9 2.0 %copy.259 = bf16[128,2048]{1,0:T(8,128)(2,1)} copy(bf16[128,2048]{0,1:T(8,128)(2,1)} %bitcast.19) | data formatting | bytes 1048576
  143.6 4.1 %all_to_all.140 = bf16[2,128,1024]{2,1,0:T(8,128)(2,1)S(1)} all-to-all(bf16[2,128,1024]{2,1,0:T(8,128)(2,1)S(1)} %all_to_all.120), channel_id=1, replica_groups=mesh['blk'=16,'head'=2] {'head'}, dimensions={0} | all-to-all | bytes 1048576 | tf_op jit(solution)/shard_map/all_to_all | solution.py:182
  150.4 3.9 %fusion.36 = f32[256,8,128]{2,0,1:T(8,128)} fusion(f32[256,8,128]{2,0,1:T(8,128)} %fusion.19, bf16[256,8,128]{0,2,1:T(8,128)(2,1)} %copy.298, f32[8,256,256]{1,2,0:T(8,128)S(1)} %copy-done.4, f32[8,256]{1,0:T(8,128)S(1)} %get-tuple-element.246, f32[8,256]{1,0:T(8,128)S(1)} %get-tuple-element.245, pred[256,256]{0,1:T(8,128)(4,1)S(1)} %copy-done.13, ...), kind=kOutput, calls=%fused_computation.61 | convolution fusion | flops 272629760 | bytes 5849088 | tf_op jit(solution)/shard_map/while/body/eval_jaxpr/hqk,qhd->khd/dot_general | solution.py:136
  154.4 3.3 %fusion.39 = bf16[256,8,128]{2,0,1:T(8,128)(2,1)S(1)} fusion(f32[256,8,128]{2,0,1:T(8,128)} %fusion.36, bf16[256,8,128]{0,2,1:T(8,128)(2,1)S(1)} %copy-done.8, f32[8,256,256]{1,2,0:T(8,128)} %fusion.100, f32[8,256]{1,0:T(8,128)S(1)} %get-tuple-element.244, f32[8,256]{1,0:T(8,128)S(1)} %get-tuple-element.243, pred[256,256]{0,1:T(8,128)(4,1)S(1)} %get-tuple-element.267, ...), kind=kOutput, calls=%fused_computation.64 | convolution fusion | flops 272891904 | bytes 5324800 | tf_op jit(solution)/shard_map/while/body/eval_jaxpr/hqk,qhd->khd/dot_general | solution.py:136
  158.3 4.3 %all_to_all.141 = bf16[2,128,1024]{2,1,0:T(8,128)(2,1)S(1)} all-to-all(bf16[2,128,1024]{2,1,0:T(8,128)(2,1)S(1)} %all_to_all.124), channel_id=1, replica_groups=mesh['blk'=16,'head'=2] {'head'}, dimensions={0} | all-to-all | bytes 1048576 | tf_op jit(solution)/shard_map/all_to_all | solution.py:185
  163.8 2.2 %fusion.22 = f32[256,8,128]{2,0,1:T(8,128)S(1)} fusion(f32[256,8,128]{2,0,1:T(8,128)} %convolution_bitcast_fusion.2, f32[8,256,256]{1,2,0:T(8,128)S(1)} %copy-done.4, f32[8,256]{1,0:T(8,128)S(1)} %get-tuple-element.245, pred[256,256]{0,1:T(8,128)(4,1)S(1)} %copy-done.13, bf16[2,256,8,128]{3,1,2,0:T(8,128)(2,1)} %collective-permute-done.2), kind=kOutput, calls=%fused_computation.43 | convolution fusion | flops 137101312 | bytes 4792320 | tf_op jit(solution)/shard_map/while/body/eval_jaxpr/hqk,qhd->khd/dot_general | solution.py:124
  168.3 4.1 %all_to_all.142 = bf16[2,128,1024]{2,1,0:T(8,128)(2,1)S(1)} all-to-all(bf16[2,128,1024]{2,1,0:T(8,128)(2,1)S(1)} %all_to_all.128), channel_id=1, replica_groups=mesh['blk'=16,'head'=2] {'head'}, dimensions={0} | all-to-all | bytes 1048576 | tf_op jit(solution)/shard_map/all_to_all | solution.py:188
  (84 shorter events, 38.2 us)
Async XLA Ops:
  0.6 6.1 %copy-start.10 = (bf16[128,2048]{1,0:T(8,128)(2,1)S(1)}, bf16[128,2048]{1,0:T(8,128)(2,1)}, u32[]{:S(2)}) copy-start(bf16[128,2048]{1,0:T(8,128)(2,1)} %param.7) | copy-start | bytes 1572868
  2.6 5.5 %all-to-all-start.1 = ((bf16[128,2,1024]{2,0,1:T(8,128)(2,1)}), bf16[128,2,1024]{2,0,1:T(8,128)(2,1)S(1)}, u32[]{:S(2)}, u32[]{:S(2)}) async-start(bf16[128,2,1024]{2,0,1:T(8,128)(2,1)} %bitcast.271), calls=%async_computation.1 | async-start | bytes 1048576 | tf_op jit(solution)/shard_map/all_to_all | solution.py:32
  8.1 5.2 %all-to-all-start.2 = ((bf16[128,2,1024]{2,0,1:T(8,128)(2,1)}), bf16[128,2,1024]{2,0,1:T(8,128)(2,1)S(1)}, u32[]{:S(2)}, u32[]{:S(2)}) async-start(bf16[128,2,1024]{2,0,1:T(8,128)(2,1)} %bitcast.270), calls=%async_computation.2 | async-start | bytes 1048576 | tf_op jit(solution)/shard_map/all_to_all | solution.py:33
  11.9 9.0 %copy-start.11 = (bf16[128,2048]{1,0:T(8,128)(2,1)S(1)}, bf16[128,2048]{1,0:T(8,128)(2,1)}, u32[]{:S(2)}) copy-start(bf16[128,2048]{1,0:T(8,128)(2,1)} %param.8) | copy-start | bytes 1572868
  13.3 12.6 %copy-start.12 = (bf16[128,2048]{1,0:T(8,128)(2,1)S(1)}, bf16[128,2048]{1,0:T(8,128)(2,1)}, u32[]{:S(2)}) copy-start(bf16[128,2048]{1,0:T(8,128)(2,1)} %param.5) | copy-start | bytes 1572868
  13.4 0.8 copy-start.3
  15.1 38.0 %collective-permute-start.1 = (bf16[2,256,8,128]{3,1,2,0:T(8,128)(2,1)}, bf16[2,256,8,128]{3,1,2,0:T(8,128)(2,1)}, u32[]{:S(2)}, u32[]{:S(2)}) collective-permute-start(bf16[2,256,8,128]{3,1,2,0:T(8,128)(2,1)} %copy_dynamic-update-slice_fusion.2), channel_id=1, source_target_pairs={{2,0},{4,2},{6,4},{8,6},{10,8},{12,10},{14,12},{16,14},{18,16},{20... | collective-permute-start | bytes 3145736 | tf_op jit(solution)/shard_map/ppermute | solution.py:18
  19.1 69.1 %collective-permute-start = (bf16[2,256,8,128]{3,1,2,0:T(8,128)(2,1)}, bf16[2,256,8,128]{3,1,2,0:T(8,128)(2,1)}, u32[]{:S(2)}, u32[]{:S(2)}) collective-permute-start(bf16[2,256,8,128]{3,1,2,0:T(8,128)(2,1)} %copy_dynamic-update-slice_fusion.2), channel_id=1, source_target_pairs={{0,2},{2,4},{4,6},{6,8},{8,10},{10,12},{12,14},{14,16},{16,18},{18... | collective-permute-start | bytes 3145736 | tf_op jit(solution)/shard_map/ppermute | solution.py:18
  21.8 5.5 %all-to-all-start.4 = ((bf16[128,2,1024]{2,0,1:T(8,128)(2,1)}), bf16[128,2,1024]{2,0,1:T(8,128)(2,1)S(1)}, u32[]{:S(2)}, u32[]{:S(2)}) async-start(bf16[128,2,1024]{2,0,1:T(8,128)(2,1)} %bitcast.269), calls=%async_computation.4 | async-start | bytes 1048576 | tf_op jit(solution)/shard_map/all_to_all | solution.py:34
  27.3 5.2 %all-to-all-start = ((bf16[128,2,1024]{2,0,1:T(8,128)(2,1)}), bf16[128,2,1024]{2,0,1:T(8,128)(2,1)S(1)}, u32[]{:S(2)}, u32[]{:S(2)}) async-start(bf16[128,2,1024]{2,0,1:T(8,128)(2,1)} %bitcast.272), calls=%async_computation | async-start | bytes 1048576 | tf_op jit(solution)/shard_map/all_to_all | solution.py:31
  34.4 95.0 %collective-permute-start.2 = (bf16[2,256,8,128]{3,1,2,0:T(8,128)(2,1)}, bf16[2,256,8,128]{3,1,2,0:T(8,128)(2,1)}, u32[]{:S(2)}, u32[]{:S(2)}) collective-permute-start(bf16[2,256,8,128]{3,1,2,0:T(8,128)(2,1)} %copy_dynamic-update-slice_fusion), channel_id=1, source_target_pairs={{0,2},{2,4},{4,6},{6,8},{8,10},{10,12},{12,14},{14,16},{16,18},{18... | collective-permute-start | bytes 3145736 | tf_op jit(solution)/shard_map/ppermute | solution.py:18
  38.1 100.0 %collective-permute-start.4 = (bf16[2,256,8,128]{3,1,2,0:T(8,128)(2,1)}, bf16[2,256,8,128]{3,1,2,0:T(8,128)(2,1)}, u32[]{:S(2)}, u32[]{:S(2)}) collective-permute-start(bf16[2,256,8,128]{3,1,2,0:T(8,128)(2,1)} %copy_dynamic-update-slice_fusion), channel_id=1, source_target_pairs={{2,0},{4,2},{6,4},{8,6},{10,8},{12,10},{14,12},{16,14},{18,16},{20... | collective-permute-start | bytes 3145736 | tf_op jit(solution)/shard_map/ppermute | solution.py:18
  50.0 1.2 copy-start.7
  50.1 1.2 copy-start.9
  54.7 39.9 %copy-start.6 = (f32[8,256,256]{2,1,0:T(8,128)}, f32[8,256,256]{2,1,0:T(8,128)S(1)}, u32[]{:S(2)}) copy-start(f32[8,256,256]{2,1,0:T(8,128)S(1)} %get-tuple-element.274) | copy-start | bytes 6291460
  89.8 3.0 %copy-start.2 = (f32[8,256,256]{2,1,0:T(8,128)}, f32[8,256,256]{2,1,0:T(8,128)S(1)}, u32[]{:S(2)}) copy-start(f32[8,256,256]{2,1,0:T(8,128)S(1)} %get-tuple-element.289) | copy-start | bytes 6291460
  97.9 51.1 %collective-permute-start.3 = (f32[2,256,8]{1,2,0:T(8,128)}, f32[2,256,8]{1,2,0:T(8,128)}, u32[]{:S(2)}, u32[]{:S(2)}) collective-permute-start(f32[2,256,8]{1,2,0:T(8,128)} %pad_maximum_fusion), channel_id=1, source_target_pairs={{0,2},{2,4},{4,6},{6,8},{8,10},{10,12},{12,14},{14,16},{16,18},{18... | collective-permute-start | bytes 49160 | tf_op jit(solution)/shard_map/ppermute | solution.py:18
  102.0 47.7 %collective-permute-start.5 = (f32[2,256,8]{1,2,0:T(8,128)}, f32[2,256,8]{1,2,0:T(8,128)}, u32[]{:S(2)}, u32[]{:S(2)}) collective-permute-start(f32[2,256,8]{1,2,0:T(8,128)} %pad_maximum_fusion), channel_id=1, source_target_pairs={{2,0},{4,2},{6,4},{8,6},{10,8},{12,10},{14,12},{16,14},{18,16},{20... | collective-permute-start | bytes 49160 | tf_op jit(solution)/shard_map/ppermute | solution.py:18
  108.9 32.1 %all-to-all-start.3 = ((bf16[2,128,1024]{1,2,0:T(8,128)(2,1)}), bf16[2,128,1024]{1,2,0:T(8,128)(2,1)}, u32[]{:S(2)}, u32[]{:S(2)}) async-start(bf16[2,128,1024]{1,2,0:T(8,128)(2,1)} %copy.208), calls=%async_computation.3 | async-start | bytes 1048576 | tf_op jit(solution)/shard_map/all_to_all | solution.py:181
  116.0 3.1 %copy-start = (f32[8,256,256]{1,2,0:T(8,128)S(1)}, f32[8,256,256]{1,2,0:T(8,128)}, u32[]{:S(2)}) copy-start(f32[8,256,256]{1,2,0:T(8,128)} %convolution_multiply_fusion) | copy-start | bytes 6291460
  129.4 3.0 %copy-start.1 = (f32[8,256,256]{1,2,0:T(8,128)S(1)}, f32[8,256,256]{1,2,0:T(8,128)}, u32[]{:S(2)}) copy-start(f32[8,256,256]{1,2,0:T(8,128)} %fusion.142) | copy-start | bytes 6291460
  143.3 7.1 %copy-start.4 = (f32[8,256,256]{1,2,0:T(8,128)S(1)}, f32[8,256,256]{1,2,0:T(8,128)}, u32[]{:S(2)}) copy-start(f32[8,256,256]{1,2,0:T(8,128)} %fusion.99) | copy-start | bytes 6291460
  143.3 7.1 %copy-start.13 = (pred[256,256]{0,1:T(8,128)(4,1)S(1)}, pred[256,256]{0,1:T(8,128)(4,1)}, u32[]{:S(2)}) copy-start(pred[256,256]{0,1:T(8,128)(4,1)} %get-tuple-element.268) | copy-start | bytes 196612
  150.4 3.9 %copy-start.8 = (bf16[256,8,128]{0,2,1:T(8,128)(2,1)S(1)}, bf16[256,8,128]{0,2,1:T(8,128)(2,1)}, u32[]{:S(2)}) copy-start(bf16[256,8,128]{0,2,1:T(8,128)(2,1)} %copy.298) | copy-start | bytes 1572868
  163.8 2.2 %copy-start.5 = (f32[8,256,256]{1,2,0:T(8,128)S(1)}, f32[8,256,256]{1,2,0:T(8,128)}, u32[]{:S(2)}) copy-start(f32[8,256,256]{1,2,0:T(8,128)} %fusion.100) | copy-start | bytes 6291460
where the time goes:
time: 176 us; the launch traced here: 174 us
  matrix products  45 us (26%)
  starting transfers between devices  41.6 us (24%)
  waiting for transfers between devices  36.2 us (21%)
  local copies, waits for them, and re-layouts  30.5 us (17%)
  blocking collectives  12.4 us (7%)
  other arithmetic  6.91 us (4%)
    ppermute x6, waiting for transfers between devices, shifted(): return lax.ppermute(block, axis, route)  33.5 us
    ppermute x6, starting transfers between devices, shifted(): return lax.ppermute(block, axis, route)  20.3 us
    dot_general x3, matrix products, grad_tile(): jnp.einsum('hqk,khd->qhd', score_grad, key_blk, preferred_element_type=jn...  11.6 us
    dot_general x5, matrix products, tile_scores(): jnp.einsum('qhd,khd->hqk', query_blk, key_blk, preferred_element_type=jnp...  10.9 us
    dot_general x3, matrix products, query_tile(): jnp.einsum('hqk,qhd->khd', score_grad, query_blk, preferred_element_type=...  9.2 us
    unnamed x39, local copies, waits for them, and re-layouts  8.23 us
    dot_general x3, matrix products, query_tile(): jnp.einsum('hqk,qhd->khd', prob_tile.astype(jnp.bfloat16), grad_blk, pref...  6.45 us
    all_to_all x1, starting transfers between devices, body(): lax.all_to_all(to_flat(attended_rows), 'head', split_axis=0, concat_axis=...  5.33 us
  transfers between devices with their start and end apart: 11, of which 5 were waited for; matrix products, arithmetic and copies ran while one was open for 35% of the time, Pallas kernels for 0%

commit v1 on v0

v1 whole, which is shorter than its diff:
```python
import functools
import math

import jax
import jax.numpy as jnp
from jax import lax
from jax.experimental import pallas as pl
from jax.experimental.pallas import tpu as pltpu
from jax.sharding import PartitionSpec as P

DH = 128
DOC_MOST = 256
MASKED = -1e30
CHUNKS = (1, 2, 2, 2, 1)
SCALE = 1.0 / math.sqrt(DH)
VMEM = 60 * 1024 * 1024


def dot_nt(a, b):
    return lax.dot_general(a, b, (((1,), (1,)), ((), ())), preferred_element_type=jnp.float32)


def dot_tn(a, b):
    return lax.dot_general(a, b, (((0,), (0,)), ((), ())), preferred_element_type=jnp.float32)


def dot_nn(a, b):
    return lax.dot_general(a, b, (((1,), (0,)), ((), ())), preferred_element_type=jnp.float32)


def tile_probs(keys, queries, key_ids, query_ids):
    scores = dot_nt(keys, queries) * (SCALE * math.log2(math.e))
    scores = jnp.where(key_ids == query_ids, scores, jnp.float32(MASKED))
    top = jnp.max(scores, axis=0, keepdims=True)
    weights = jnp.exp2(scores - top)
    return weights * (1.0 / jnp.sum(weights, axis=0, keepdims=True))


def attend(probs_low, values, grads):
    attended = dot_tn(values, probs_low).astype(jnp.bfloat16)
    delta = jnp.sum(
        attended.astype(jnp.float32) * grads.T.astype(jnp.float32), axis=0, keepdims=True
    )
    return attended, delta


def attention_kernel(heads, own_ref, near_ref, far_ref, row_ids_ref, col_ids_ref, keep_ref, send_ref):
    rows = 2 * own_ref.shape[2]
    half = own_ref.shape[2]
    own_cols = col_ids_ref[0:rows, :]
    own_lane = row_ids_ref[:, 0:rows]

    def rows_of(ref, member, h):
        lanes = slice(h * DH, (h + 1) * DH)
        return jnp.concatenate([ref[0, member, :, lanes], ref[1, member, :, lanes]], axis=0)

    for h in range(heads):
        q_own, k_own, v_own, g_own = (rows_of(own_ref, m, h) for m in range(4))
        q_near, k_near, v_near, g_near = (rows_of(near_ref, m, h) for m in range(4))
        q_far, k_far, v_far, g_far = (rows_of(far_ref, m, h) for m in range(4))
        keys = jnp.concatenate([k_own, k_near, k_far], axis=0)
        values = jnp.concatenate([v_own, v_near, v_far], axis=0)
        probs = tile_probs(keys, q_own, col_ids_ref[...], own_lane)
        low = probs.astype(jnp.bfloat16)
        attended, delta = attend(low, values, g_own)
        score_grad = (probs * (dot_nt(values, g_own) - delta)).astype(jnp.bfloat16)
        query_grad = dot_tn(keys, score_grad) * SCALE
        key_grad = dot_nn(score_grad[0:rows], q_own)
        value_grad = dot_nn(low[0:rows], g_own)
        for side, (q_side, k_side, v_side, g_side) in enumerate(
            ((q_near, k_near, v_near, g_near), (q_far, k_far, v_far, g_far))
        ):
            at = slice((side + 1) * rows, (side + 2) * rows)
            side_cols = jnp.concatenate([own_cols, col_ids_ref[at, :]], axis=0)
            probs = tile_probs(
                jnp.concatenate([k_own, k_side], axis=0), q_side, side_cols, row_ids_ref[:, at]
            )
            low = probs.astype(jnp.bfloat16)
            _, delta = attend(low, jnp.concatenate([v_own, v_side], axis=0), g_side)
            score_grad = (probs[0:rows] * (dot_nt(v_own, g_side) - delta)).astype(jnp.bfloat16)
            key_grad = key_grad + dot_nn(score_grad, q_side)
            value_grad = value_grad + dot_nn(low[0:rows], g_side)
        results = (
            attended.astype(jnp.float32).T.astype(jnp.bfloat16),
            query_grad.T.astype(jnp.bfloat16),
            (key_grad * SCALE).astype(jnp.bfloat16),
            value_grad.astype(jnp.bfloat16),
        )
        lanes = slice(h * DH, (h + 1) * DH)
        for m, result in enumerate(results):
            keep_ref[m, :, lanes] = result[0:half]
            send_ref[m, :, lanes] = result[half:rows]


def attention(own, near, far, row_ids, col_ids):
    _, members, half, width = own.shape
    heads = width // DH
    whole = pl.BlockSpec(memory_space=pltpu.VMEM)
    out = jax.ShapeDtypeStruct((members, half, width), jnp.bfloat16)
    rows = 2 * half
    flops = heads * 2 * DH * rows * rows * (5 * 3 + 2 * (2 + 2 + 1 + 2))
    return pl.pallas_call(
        functools.partial(attention_kernel, heads),
        out_shape=(out, out),
        in_specs=[whole] * 5,
        out_specs=(whole, whole),
        compiler_params=pltpu.CompilerParams(vmem_limit_bytes=VMEM),
        cost_estimate=pl.CostEstimate(
            flops=flops, bytes_accessed=4 * own.size * 2, transcendentals=heads * 7 * rows * rows
        ),
    )(own, near, far, row_ids, col_ids)


def pack_kernel(chunks, q_ref, k_ref, v_ref, g_ref, *outs):
    mine, other = outs[: len(chunks)], outs[len(chunks) :]
    head_half = q_ref.shape[1] // 2
    core = lax.axis_index("head")
    for m, ref in enumerate((q_ref, k_ref, v_ref, g_ref)):
        at = 0
        for j, heads in enumerate(chunks):
            width = heads * DH
            for group, place in ((mine, core), (other, 1 - core)):
                first = pl.multiple_of(place * head_half + at, DH)
                group[j][m] = ref[:, pl.ds(first, width)]
            at += width


def pack(arrays, chunks):
    rows, width = arrays[0].shape
    steps = 2
    block = rows // steps
    shapes = [jax.ShapeDtypeStruct((4, rows, heads * DH), jnp.bfloat16) for heads in chunks] * 2
    got = pl.pallas_call(
        functools.partial(pack_kernel, chunks),
        grid=(steps,),
        out_shape=shapes,
        in_specs=[pl.BlockSpec((block, width), lambda i: (i, 0))] * 4,
        out_specs=[pl.BlockSpec((4, block, s.shape[2]), lambda i: (0, i, 0)) for s in shapes],
        compiler_params=pltpu.CompilerParams(vmem_limit_bytes=VMEM),
    )(*arrays)
    return got[: len(chunks)], got[len(chunks) :]


def unpack_kernel(chunks, *refs):
    count = len(chunks)
    kept, received, outs = refs[:count], refs[count : 2 * count], refs[2 * count :]
    head_half = outs[0].shape[1] // 2
    core = lax.axis_index("head")
    for m, ref in enumerate(outs):
        at = 0
        for j, heads in enumerate(chunks):
            width = heads * DH
            for group, place in ((kept, core), (received, 1 - core)):
                first = pl.multiple_of(place * head_half + at, DH)
                ref[:, pl.ds(first, width)] = group[j][m]
            at += width


def unpack(kept, received, chunks, width):
    rows = kept[0].shape[1]
    steps = 2
    block = rows // steps
    return pl.pallas_call(
        functools.partial(unpack_kernel, chunks),
        grid=(steps,),
        out_shape=[jax.ShapeDtypeStruct((rows, width), jnp.bfloat16)] * 4,
        in_specs=[
            pl.BlockSpec((4, block, t.shape[2]), lambda i: (0, i, 0)) for t in (*kept, *received)
        ],
        out_specs=[pl.BlockSpec((block, width), lambda i: (i, 0))] * 4,
        compiler_params=pltpu.CompilerParams(vmem_limit_bytes=VMEM),
    )(*kept, *received)


def neighbour_ids(doc_ids, rows):
    positions = lax.axis_size("blk")
    here, core = lax.axis_index("blk"), lax.axis_index("head")
    away = 1 - 2 * (here % 2)
    table = doc_ids.reshape(-1, rows)
    picked = []
    for place in (here, here + away, here - away):
        inside = (place >= 0) & (place < positions)
        held = jnp.clip(place, 0, positions - 1)
        for which in (core, 1 - core):
            row = lax.dynamic_index_in_dim(table, 2 * held + which, 0, keepdims=False)
            picked.append(jnp.where(inside, row, -1))
    return jnp.concatenate(picked)


def body(query_rows, key_rows, value_rows, out_grad, doc_ids):
    positions = lax.axis_size("blk")
    rows, width = query_rows.shape
    chunks = CHUNKS
    swap = [(0, 1), (1, 0)]
    pairs = [(i, i ^ 1) for i in range(positions)]
    onward = [(i, i + 2) for i in range(0, positions - 2, 2)]
    onward += [(i, i - 2) for i in range(3, positions, 2)]
    ids = neighbour_ids(doc_ids, rows)
    row_ids, col_ids = ids[None, :], ids[:, None]

    mine, other = pack((query_rows, key_rows, value_rows, out_grad), chunks)
    kept, received = [], []
    for own, away in zip(mine, other):
        own = jnp.stack([own, lax.ppermute(away, "head", swap)])
        near = lax.ppermute(own, "blk", pairs)
        far = lax.ppermute(near, "blk", onward)
        keep, send = attention(own, near, far, row_ids, col_ids)
        kept.append(keep)
        received.append(lax.ppermute(send, "head", swap))
    return tuple(unpack(kept, received, chunks, width))


def solution(mesh):
    placed = P(("blk", "head"), None)
    return jax.shard_map(
        body,
        mesh=mesh,
        in_specs=(placed, placed, placed, placed, P()),
        out_specs=(placed,) * 4,
        check_vma=False,
    )
```

time: 176 us -> 100 us (0.57)
  matrix products: 45 us -> 0 us
  Pallas kernels: 0 us -> 36.4 us
  local copies, waits for them, and re-layouts: 30.5 us -> 4.14 us
  starting transfers between devices: 41.6 us -> 27.2 us
  blocking collectives: 12.4 us -> 0 us
  waiting for transfers between devices: 36.2 us -> 24 us
    dot_general x18 -> x0, matrix products: 45 us -> none  [the longest x3 11.6 us: grad_tile(): jnp.einsum('hqk,khd->qhd', score_grad, key_blk, preferred_element_type=jn...]
    pallas_call x0 -> x7, Pallas kernels: none -> 36.4 us  [the longest x5 31 us: attention(): pl.pallas_call(functools.partial(attention_kernel, heads), out_shape=(out...]
    all_to_all x5 -> x0, starting transfers between devices: 21.3 us -> none  [the longest x1 5.33 us: body(): lax.all_to_all(to_flat(attended_rows), 'head', split_axis=0, concat_axis=...]
    all_to_all x3 -> x0, blocking collectives: 12.4 us -> none  [the longest x1 4.25 us: body(): lax.all_to_all(to_flat(key_acc.astype(jnp.bfloat16)), 'head', split_axis=...]
    all_to_all x12 -> x0, local copies, waits for them, and re-layouts: 9.76 us -> none  [the longest x2 3.86 us: body(): lax.all_to_all(to_flat(attended_rows), 'head', split_axis=0, concat_axis=...]
    ppermute x6 -> x20, waiting for transfers between devices: 33.5 us -> 24 us  [the longest x5 21.9 us: body(): near = lax.ppermute(own, 'blk', pairs)]
    ppermute x6 -> x20, starting transfers between devices: 20.3 us -> 27.2 us  [the longest x5 15.7 us: body(): far = lax.ppermute(near, 'blk', onward)]
    unnamed x39 -> x42, local copies, waits for them, and re-layouts: 8.23 us -> 2.62 us
  transfers between devices with their start and end apart: 11 -> 20, of which waited for: 5 -> 5; matrix products, arithmetic and copies ran while one was open for 35% -> 7% of each run, Pallas kernels for 0% -> 32%
where the time goes in v1:
time: 100 us; the launch traced here: 98.3 us
  Pallas kernels  36.4 us (36%)
  starting transfers between devices  27.2 us (27%)
  waiting for transfers between devices  24 us (24%)
  other arithmetic  5.38 us (5%)
  local copies, waits for them, and re-layouts  4.14 us (4%)
  between operations  1.09 us (1%)
    pallas_call x5, Pallas kernels, attention(): pl.pallas_call(functools.partial(attention_kernel, heads), out_shape=(out...  31 us
    ppermute x5, waiting for transfers between devices, body(): near = lax.ppermute(own, 'blk', pairs)  21.9 us
    ppermute x5, starting transfers between devices, body(): far = lax.ppermute(near, 'blk', onward)  15.7 us
    ppermute x5, starting transfers between devices, body(): near = lax.ppermute(own, 'blk', pairs)  4.98 us
    ppermute x5, starting transfers between devices, body(): received.append(lax.ppermute(send, 'head', swap))  4.1 us
    unnamed x6, other arithmetic  3.48 us
    pallas_call x1, Pallas kernels, unpack(): pl.pallas_call(functools.partial(unpack_kernel, chunks), grid=(steps,), o...  2.71 us
    pallas_call x1, Pallas kernels, pack(): pl.pallas_call(functools.partial(pack_kernel, chunks), grid=(steps,), out...  2.67 us
  transfers between devices with their start and end apart: 20, of which 5 were waited for; matrix products, arithmetic and copies ran while one was open for 7% of the time, Pallas kernels for 32%

profile of v1, /device:TPU:9, one launch (start us, length us, event | category | flops | bytes accessed | tf_op | source)
XLA Modules:
  0.0 98.3 jit_solution(7590750307308453102)
XLA Ops:
  0.6 2.7 %shard_map.84 = (bf16[4,128,128]{2,1,0:T(8,128)(2,1)}, bf16[4,128,256]{2,1,0:T(8,128)(2,1)}, bf16[4,128,256]{2,1,0:T(8,128)(2,1)}, bf16[4,128,256]{2,1,0:T(8,128...) custom-call(bf16[128,2048]{1,0:T(8,128)(2,1)} %q_ref.1, ...), custom_call_target="tpu_custom_call" | custom-call | tf_op jit(solution)/shard_map/pallas_call | solution.py:133
  3.3 0.7 collective-permute-start.9
  4.6 0.9 collective-permute-done.9
  5.4 1.0 %pad_maximum_fusion.2.own_ref = bf16[2,4,128,256]{3,2,1,0:T(8,128)(2,1)S(1)} fusion(bf16[1,4,128,256]{3,2,1,0:T(8,128)(2,1)S(1)} %bitcast.40, bf16[1,4,128,256]{3,2,1,0:T(8,128)(2,1)} %bitcast.38), kind=kLoop, calls=%fused_computation.2 | loop fusion | flops 262144 | bytes 1048576 | tf_op jit(solution)/shard_map/stack | solution.py:204
  6.5 1.3 %collective-permute-start.10 = (bf16[2,4,128,256]{3,2,1,0:T(8,128)(2,1)S(1)}, bf16[2,4,128,256]{3,2,1,0:T(8,128)(2,1)S(1)}, u32[]{:S(2)}, u32[]{:S(2)}) collective-permute-start(bf16[2,4,128,256]{3,2,1,0:T(8,128)(2,1)S(1)} %pad_maximum_fusion.2.own_ref), channel_id=1, source_target_pairs={{0,2},{2,0},{4,6},{6,4},{8,10},{10,8},{12,14},{14,12},{16,18},{18,... | collective-permute-start | bytes 1572872 | tf_op jit(solution)/shard_map/ppermute | solution.py:205
  8.8 0.7 collective-permute-start.4
  9.5 1.2 %collective-permute-start = (bf16[4,128,128]{2,1,0:T(8,128)(2,1)}, bf16[4,128,128]{2,1,0:T(8,128)(2,1)S(1)}, u32[]{:S(2)}, u32[]{:S(2)}) collective-permute-start(bf16[4,128,128]{2,1,0:T(8,128)(2,1)} %get-tuple-element.25), channel_id=1, source_target_pairs={{0,1},{1,0},{2,3},{3,2},{4,5},{5,4},{6,7},{7,6},{8,9},{9,8},{10,11... | collective-permute-start | bytes 393224 | tf_op jit(solution)/shard_map/ppermute | solution.py:204
  11.4 0.7 constant_dynamic-update-slice_fusion.4
  12.1 0.7 constant_dynamic-update-slice_fusion.3
  12.8 6.8 %collective-permute-done.10.near_ref = bf16[2,4,128,256]{3,2,1,0:T(8,128)(2,1)S(1)} collective-permute-done((bf16[2,4,128,256]{3,2,1,0:T(8,128)(2,1)S(1)}, bf16[2,4,128,256]{3,2,1,0:T(8,128)(2,1)S(1)}, u32[]{:S(2)}, u32[]{:S(2)}) %collective-permute-start.10) | collective-permute-done | bytes 524320 | tf_op jit(solution)/shard_map/ppermute | solution.py:205
  19.7 3.1 %collective-permute-start.11 = (bf16[2,4,128,256]{3,2,1,0:T(8,128)(2,1)S(1)}, bf16[2,4,128,256]{3,2,1,0:T(8,128)(2,1)}, u32[]{:S(2)}, u32[]{:S(2)}) collective-permute-start(bf16[2,4,128,256]{3,2,1,0:T(8,128)(2,1)S(1)} %collective-permute-done.10.near_ref), channel_id=1, source_target_pairs={{0,4},{4,8},{8,12},{12,16},{16,20},{20,24},{24,28},{6,2},{10,6},{1... | collective-permute-start | bytes 1572872 | tf_op jit(solution)/shard_map/ppermute | solution.py:206
  22.9 1.2 %collective-permute-start.13 = (bf16[2,4,128,128]{3,2,1,0:T(8,128)(2,1)S(1)}, bf16[2,4,128,128]{3,2,1,0:T(8,128)(2,1)S(1)}, u32[]{:S(2)}, u32[]{:S(2)}) collective-permute-start(bf16[2,4,128,128]{3,2,1,0:T(8,128)(2,1)S(1)} %pad_maximum_fusion.4.own_ref), channel_id=1, source_target_pairs={{0,2},{2,0},{4,6},{6,4},{8,10},{10,8},{12,14},{14,12},{16,18},{18,... | collective-permute-start | bytes 786440 | tf_op jit(solution)/shard_map/ppermute | solution.py:205
  24.1 7.0 %collective-permute-done.7.near_ref = bf16[2,4,128,256]{3,2,1,0:T(8,128)(2,1)S(1)} collective-permute-done((bf16[2,4,128,256]{3,2,1,0:T(8,128)(2,1)S(1)}, bf16[2,4,128,256]{3,2,1,0:T(8,128)(2,1)S(1)}, u32[]{:S(2)}, u32[]{:S(2)}) %collective-permute-start.7) | collective-permute-done | bytes 524320 | tf_op jit(solution)/shard_map/ppermute | solution.py:205
  31.0 3.1 %collective-permute-start.8 = (bf16[2,4,128,256]{3,2,1,0:T(8,128)(2,1)S(1)}, bf16[2,4,128,256]{3,2,1,0:T(8,128)(2,1)}, u32[]{:S(2)}, u32[]{:S(2)}) collective-permute-start(bf16[2,4,128,256]{3,2,1,0:T(8,128)(2,1)S(1)} %collective-permute-done.7.near_ref), channel_id=1, source_target_pairs={{0,4},{4,8},{8,12},{12,16},{16,20},{20,24},{24,28},{6,2},{10,6},{1... | collective-permute-start | bytes 1572872 | tf_op jit(solution)/shard_map/ppermute | solution.py:206
  34.2 8.1 %collective-permute-done.4.near_ref = bf16[2,4,128,256]{3,2,1,0:T(8,128)(2,1)S(1)} collective-permute-done((bf16[2,4,128,256]{3,2,1,0:T(8,128)(2,1)S(1)}, bf16[2,4,128,256]{3,2,1,0:T(8,128)(2,1)S(1)}, u32[]{:S(2)}, u32[]{:S(2)}) %collective-permute-start.4) | collective-permute-done | bytes 524320 | tf_op jit(solution)/shard_map/ppermute | solution.py:205
  42.3 3.1 %collective-permute-start.5 = (bf16[2,4,128,256]{3,2,1,0:T(8,128)(2,1)S(1)}, bf16[2,4,128,256]{3,2,1,0:T(8,128)(2,1)}, u32[]{:S(2)}, u32[]{:S(2)}) collective-permute-start(bf16[2,4,128,256]{3,2,1,0:T(8,128)(2,1)S(1)} %collective-permute-done.4.near_ref), channel_id=1, source_target_pairs={{0,4},{4,8},{8,12},{12,16},{16,20},{20,24},{24,28},{6,2},{10,6},{1... | collective-permute-start | bytes 1572872 | tf_op jit(solution)/shard_map/ppermute | solution.py:206
  45.5 1.2 %collective-permute-start.1 = (bf16[2,4,128,128]{3,2,1,0:T(8,128)(2,1)S(1)}, bf16[2,4,128,128]{3,2,1,0:T(8,128)(2,1)S(1)}, u32[]{:S(2)}, u32[]{:S(2)}) collective-permute-start(bf16[2,4,128,128]{3,2,1,0:T(8,128)(2,1)S(1)} %pad_maximum_fusion.3.own_ref), channel_id=1, source_target_pairs={{0,2},{2,0},{4,6},{6,4},{8,10},{10,8},{12,14},{14,12},{16,18},{18,... | collective-permute-start | bytes 786440 | tf_op jit(solution)/shard_map/ppermute | solution.py:205
  47.3 0.7 constant_dynamic-update-slice_fusion.1
  48.0 0.7 constant_dynamic-update-slice_fusion
  49.3 0.9 broadcast_in_dim.18.col_ids_ref
  50.3 2.2 %collective-permute-start.14 = (bf16[2,4,128,128]{3,2,1,0:T(8,128)(2,1)S(1)}, bf16[2,4,128,128]{3,2,1,0:T(8,128)(2,1)S(1)}, u32[]{:S(2)}, u32[]{:S(2)}) collective-permute-start(bf16[2,4,128,128]{3,2,1,0:T(8,128)(2,1)S(1)} %collective-permute-done.13.near_ref), channel_id=1, source_target_pairs={{0,4},{4,8},{8,12},{12,16},{16,20},{20,24},{24,28},{6,2},{10,6},{1... | collective-permute-start | bytes 786440 | tf_op jit(solution)/shard_map/ppermute | solution.py:206
  52.5 4.0 %collective-permute-start.2 = (bf16[2,4,128,128]{3,2,1,0:T(8,128)(2,1)S(1)}, bf16[2,4,128,128]{3,2,1,0:T(8,128)(2,1)S(1)}, u32[]{:S(2)}, u32[]{:S(2)}) collective-permute-start(bf16[2,4,128,128]{3,2,1,0:T(8,128)(2,1)S(1)} %collective-permute-done.1.near_ref), channel_id=1, source_target_pairs={{0,4},{4,8},{8,12},{12,16},{16,20},{20,24},{24,28},{6,2},{10,6},{1... | collective-permute-start | bytes 786440 | tf_op jit(solution)/shard_map/ppermute | solution.py:206
  56.6 7.3 %shard_map.88 = (bf16[4,128,256]{2,1,0:T(8,128)(2,1)}, bf16[4,128,256]{2,1,0:T(8,128)(2,1)}) custom-call(bf16[2,4,128,256]{3,2,1,0:T(8,128)(2,1)} %copy-done.2, bf16[2,4,128,256]{3,2,1,0:T(8,128)(2,1)} %copy-done.16, bf16[2,4,128,256]{3,2,1,0:T(8,128)(2,1)} %collective-permute-done.11.far_ref, s32[1,768]{1,0:T(1,128)} %broadcast_in_dim.16.row_ids_ref, ...), custom_call_target="tpu_custom_call" | custom-call | flops 973078528 | bytes 2097152 | tf_op jit(solution)/shard_map/pallas_call | solution.py:102
  63.9 3.1 %collective-permute-start.18 = (bf16[4,128,256]{2,1,0:T(8,128)(2,1)}, bf16[4,128,256]{2,1,0:T(8,128)(2,1)S(1)}, u32[]{:S(2)}, u32[]{:S(2)}) collective-permute-start(bf16[4,128,256]{2,1,0:T(8,128)(2,1)} %get-tuple-element.42), channel_id=1, source_target_pairs={{0,1},{1,0},{2,3},{3,2},{4,5},{5,4},{6,7},{7,6},{8,9},{9,8},{10,11... | collective-permute-start | bytes 786440 | tf_op jit(solution)/shard_map/ppermute | solution.py:209
  67.0 7.3 %shard_map.87 = (bf16[4,128,256]{2,1,0:T(8,128)(2,1)}, bf16[4,128,256]{2,1,0:T(8,128)(2,1)}) custom-call(bf16[2,4,128,256]{3,2,1,0:T(8,128)(2,1)} %copy-done.1, bf16[2,4,128,256]{3,2,1,0:T(8,128)(2,1)} %copy-done.15, bf16[2,4,128,256]{3,2,1,0:T(8,128)(2,1)} %collective-permute-done.8.far_ref, s32[1,768]{1,0:T(1,128)} %broadcast_in_dim.16.row_ids_ref, ...), custom_call_target="tpu_custom_call" | custom-call | flops 973078528 | bytes 2097152 | tf_op jit(solution)/shard_map/pallas_call | solution.py:102
  74.3 7.4 %shard_map.86 = (bf16[4,128,256]{2,1,0:T(8,128)(2,1)}, bf16[4,128,256]{2,1,0:T(8,128)(2,1)}) custom-call(bf16[2,4,128,256]{3,2,1,0:T(8,128)(2,1)} %copy-done, bf16[2,4,128,256]{3,2,1,0:T(8,128)(2,1)} %copy-done.14, bf16[2,4,128,256]{3,2,1,0:T(8,128)(2,1)} %collective-permute-done.5.far_ref, s32[1,768]{1,0:T(1,128)} %broadcast_in_dim.16.row_ids_ref, ...), custom_call_target="tpu_custom_call" | custom-call | flops 973078528 | bytes 2097152 | tf_op jit(solution)/shard_map/pallas_call | solution.py:102
  82.3 0.7 copy-done.20
  83.0 4.5 %shard_map.89 = (bf16[4,128,128]{2,1,0:T(8,128)(2,1)}, bf16[4,128,128]{2,1,0:T(8,128)(2,1)}) custom-call(bf16[2,4,128,128]{3,2,1,0:T(8,128)(2,1)} %copy-done.3, bf16[2,4,128,128]{3,2,1,0:T(8,128)(2,1)} %copy-done.17, bf16[2,4,128,128]{3,2,1,0:T(8,128)(2,1)} %copy-done.20, s32[1,768]{1,0:T(1,128)} %broadcast_in_dim.16.row_ids_ref, ...), custom_call_target="tpu_custom_call" | custom-call | flops 486539264 | bytes 1048576 | tf_op jit(solution)/shard_map/pallas_call | solution.py:102
  87.5 0.7 copy-done.19
  88.2 4.5 %shard_map.85 = (bf16[4,128,128]{2,1,0:T(8,128)(2,1)}, bf16[4,128,128]{2,1,0:T(8,128)(2,1)}) custom-call(bf16[2,4,128,128]{3,2,1,0:T(8,128)(2,1)} %copy-done.4, bf16[2,4,128,128]{3,2,1,0:T(8,128)(2,1)} %copy-done.18, bf16[2,4,128,128]{3,2,1,0:T(8,128)(2,1)} %copy-done.19, s32[1,768]{1,0:T(1,128)} %broadcast_in_dim.16.row_ids_ref, ...), custom_call_target="tpu_custom_call" | custom-call | flops 486539264 | bytes 1048576 | tf_op jit(solution)/shard_map/pallas_call | solution.py:102
  93.2 1.2 %collective-permute-done.15.refs_5_ = bf16[4,128,128]{2,1,0:T(8,128)(2,1)S(1)} collective-permute-done((bf16[4,128,128]{2,1,0:T(8,128)(2,1)}, bf16[4,128,128]{2,1,0:T(8,128)(2,1)S(1)}, u32[]{:S(2)}, u32[]{:S(2)}) %collective-permute-start.15) | collective-permute-done | bytes 131104 | tf_op jit(solution)/shard_map/ppermute | solution.py:209
  95.4 2.7 %shard_map.90 = (bf16[128,2048]{1,0:T(8,128)(2,1)}, bf16[128,2048]{1,0:T(8,128)(2,1)}, bf16[128,2048]{1,0:T(8,128)(2,1)}, bf16[128,2048]{1,0:T(8,128)(2,1)}) custom-call(bf16[4,128,128]{2,1,0:T(8,128)(2,1)} %get-tuple-element.26.refs_0_, bf16[4,128,256]{2,1,0:T(8,128)(2,1)} %get-tuple-element.29.refs_1_, bf16[4,128,256]{2,1,0:T(8,128)(2,1)} %get-tuple-element.32.refs_2_, ...), custom_call_target="tpu_custom_call" | custom-call | tf_op jit(solution)/shard_map/pallas_call | solution.py:163
  (71 shorter events, 5.6 us)
Async XLA Ops:
  3.3 2.1 %collective-permute-start.9 = (bf16[4,128,256]{2,1,0:T(8,128)(2,1)}, bf16[4,128,256]{2,1,0:T(8,128)(2,1)S(1)}, u32[]{:S(2)}, u32[]{:S(2)}) collective-permute-start(bf16[4,128,256]{2,1,0:T(8,128)(2,1)} %get-tuple-element.34), channel_id=1, source_target_pairs={{0,1},{1,0},{2,3},{3,2},{4,5},{5,4},{6,7},{7,6},{8,9},{9,8},{10,11... | collective-permute-start | bytes 786440 | tf_op jit(solution)/shard_map/ppermute | solution.py:204
  4.0 3.7 %collective-permute-start.6 = (bf16[4,128,256]{2,1,0:T(8,128)(2,1)}, bf16[4,128,256]{2,1,0:T(8,128)(2,1)S(1)}, u32[]{:S(2)}, u32[]{:S(2)}) collective-permute-start(bf16[4,128,256]{2,1,0:T(8,128)(2,1)} %get-tuple-element.31), channel_id=1, source_target_pairs={{0,1},{1,0},{2,3},{3,2},{4,5},{5,4},{6,7},{7,6},{8,9},{9,8},{10,11... | collective-permute-start | bytes 786440 | tf_op jit(solution)/shard_map/ppermute | solution.py:204
  4.1 4.4 %collective-permute-start.3 = (bf16[4,128,256]{2,1,0:T(8,128)(2,1)}, bf16[4,128,256]{2,1,0:T(8,128)(2,1)S(1)}, u32[]{:S(2)}, u32[]{:S(2)}) collective-permute-start(bf16[4,128,256]{2,1,0:T(8,128)(2,1)} %get-tuple-element.28), channel_id=1, source_target_pairs={{0,1},{1,0},{2,3},{3,2},{4,5},{5,4},{6,7},{7,6},{8,9},{9,8},{10,11... | collective-permute-start | bytes 786440 | tf_op jit(solution)/shard_map/ppermute | solution.py:204
  5.4 2.3 %copy-start.6 = (bf16[4,128,256]{2,1,0:T(8,128)(2,1)S(1)}, bf16[4,128,256]{2,1,0:T(8,128)(2,1)}, u32[]{:S(2)}) copy-start(bf16[4,128,256]{2,1,0:T(8,128)(2,1)} %get-tuple-element.30) | copy-start | bytes 786436
  6.5 1.4 %copy-start.2 = (bf16[2,4,128,256]{3,2,1,0:T(8,128)(2,1)}, bf16[2,4,128,256]{3,2,1,0:T(8,128)(2,1)S(1)}, u32[]{:S(2)}) copy-start(bf16[2,4,128,256]{3,2,1,0:T(8,128)(2,1)S(1)} %pad_maximum_fusion.2.own_ref) | copy-start | bytes 1572868
  6.5 13.2 %collective-permute-start.10 = (bf16[2,4,128,256]{3,2,1,0:T(8,128)(2,1)S(1)}, bf16[2,4,128,256]{3,2,1,0:T(8,128)(2,1)S(1)}, u32[]{:S(2)}, u32[]{:S(2)}) collective-permute-start(bf16[2,4,128,256]{3,2,1,0:T(8,128)(2,1)S(1)} %pad_maximum_fusion.2.own_ref), channel_id=1, source_target_pairs={{0,2},{2,0},{4,6},{6,4},{8,10},{10,8},{12,14},{14,12},{16,18},{18,... | collective-permute-start | bytes 1572872 | tf_op jit(solution)/shard_map/ppermute | solution.py:205
  7.8 23.2 %collective-permute-start.7 = (bf16[2,4,128,256]{3,2,1,0:T(8,128)(2,1)S(1)}, bf16[2,4,128,256]{3,2,1,0:T(8,128)(2,1)S(1)}, u32[]{:S(2)}, u32[]{:S(2)}) collective-permute-start(bf16[2,4,128,256]{3,2,1,0:T(8,128)(2,1)S(1)} %pad_maximum_fusion.1.own_ref), channel_id=1, source_target_pairs={{0,2},{2,0},{4,6},{6,4},{8,10},{10,8},{12,14},{14,12},{16,18},{18,... | collective-permute-start | bytes 1572872 | tf_op jit(solution)/shard_map/ppermute | solution.py:205
  8.7 14.1 %copy-start.13 = (bf16[4,128,128]{2,1,0:T(8,128)(2,1)S(1)}, bf16[4,128,128]{2,1,0:T(8,128)(2,1)}, u32[]{:S(2)}) copy-start(bf16[4,128,128]{2,1,0:T(8,128)(2,1)} %get-tuple-element.36) | copy-start | bytes 393220
  8.8 36.7 %copy-start = (bf16[2,4,128,256]{3,2,1,0:T(8,128)(2,1)}, bf16[2,4,128,256]{3,2,1,0:T(8,128)(2,1)S(1)}, u32[]{:S(2)}) copy-start(bf16[2,4,128,256]{3,2,1,0:T(8,128)(2,1)S(1)} %pad_maximum_fusion.own_ref) | copy-start | bytes 1572868
  8.8 33.5 %collective-permute-start.4 = (bf16[2,4,128,256]{3,2,1,0:T(8,128)(2,1)S(1)}, bf16[2,4,128,256]{3,2,1,0:T(8,128)(2,1)S(1)}, u32[]{:S(2)}, u32[]{:S(2)}) collective-permute-start(bf16[2,4,128,256]{3,2,1,0:T(8,128)(2,1)S(1)} %pad_maximum_fusion.own_ref), channel_id=1, source_target_pairs={{0,2},{2,0},{4,6},{6,4},{8,10},{10,8},{12,14},{14,12},{16,18},{18,... | collective-permute-start | bytes 1572872 | tf_op jit(solution)/shard_map/ppermute | solution.py:205
  9.5 35.9 %collective-permute-start = (bf16[4,128,128]{2,1,0:T(8,128)(2,1)}, bf16[4,128,128]{2,1,0:T(8,128)(2,1)S(1)}, u32[]{:S(2)}, u32[]{:S(2)}) collective-permute-start(bf16[4,128,128]{2,1,0:T(8,128)(2,1)} %get-tuple-element.25), channel_id=1, source_target_pairs={{0,1},{1,0},{2,3},{3,2},{4,5},{5,4},{6,7},{7,6},{8,9},{9,8},{10,11... | collective-permute-start | bytes 393224 | tf_op jit(solution)/shard_map/ppermute | solution.py:204
  10.7 12.1 %collective-permute-start.12 = (bf16[4,128,128]{2,1,0:T(8,128)(2,1)}, bf16[4,128,128]{2,1,0:T(8,128)(2,1)S(1)}, u32[]{:S(2)}, u32[]{:S(2)}) collective-permute-start(bf16[4,128,128]{2,1,0:T(8,128)(2,1)} %get-tuple-element.37), channel_id=1, source_target_pairs={{0,1},{1,0},{2,3},{3,2},{4,5},{5,4},{6,7},{7,6},{8,9},{9,8},{10,11... | collective-permute-start | bytes 393224 | tf_op jit(solution)/shard_map/ppermute | solution.py:204
  19.7 36.9 %copy-start.16 = (bf16[2,4,128,256]{3,2,1,0:T(8,128)(2,1)}, bf16[2,4,128,256]{3,2,1,0:T(8,128)(2,1)S(1)}, u32[]{:S(2)}) copy-start(bf16[2,4,128,256]{3,2,1,0:T(8,128)(2,1)S(1)} %collective-permute-done.10.near_ref) | copy-start | bytes 1572868
  19.7 36.9 %collective-permute-start.11 = (bf16[2,4,128,256]{3,2,1,0:T(8,128)(2,1)S(1)}, bf16[2,4,128,256]{3,2,1,0:T(8,128)(2,1)}, u32[]{:S(2)}, u32[]{:S(2)}) collective-permute-start(bf16[2,4,128,256]{3,2,1,0:T(8,128)(2,1)S(1)} %collective-permute-done.10.near_ref), channel_id=1, source_target_pairs={{0,4},{4,8},{8,12},{12,16},{16,20},{20,24},{24,28},{6,2},{10,6},{1... | collective-permute-start | bytes 1572872 | tf_op jit(solution)/shard_map/ppermute | solution.py:206
  22.8 22.6 %copy-start.12 = (bf16[4,128,128]{2,1,0:T(8,128)(2,1)S(1)}, bf16[4,128,128]{2,1,0:T(8,128)(2,1)}, u32[]{:S(2)}) copy-start(bf16[4,128,128]{2,1,0:T(8,128)(2,1)} %get-tuple-element.24) | copy-start | bytes 393220
  22.9 22.6 %copy-start.3 = (bf16[2,4,128,128]{3,2,1,0:T(8,128)(2,1)}, bf16[2,4,128,128]{3,2,1,0:T(8,128)(2,1)S(1)}, u32[]{:S(2)}) copy-start(bf16[2,4,128,128]{3,2,1,0:T(8,128)(2,1)S(1)} %pad_maximum_fusion.4.own_ref) | copy-start | bytes 786436
  22.9 27.4 %collective-permute-start.13 = (bf16[2,4,128,128]{3,2,1,0:T(8,128)(2,1)S(1)}, bf16[2,4,128,128]{3,2,1,0:T(8,128)(2,1)S(1)}, u32[]{:S(2)}, u32[]{:S(2)}) collective-permute-start(bf16[2,4,128,128]{3,2,1,0:T(8,128)(2,1)S(1)} %pad_maximum_fusion.4.own_ref), channel_id=1, source_target_pairs={{0,2},{2,0},{4,6},{6,4},{8,10},{10,8},{12,14},{14,12},{16,18},{18,... | collective-permute-start | bytes 786440 | tf_op jit(solution)/shard_map/ppermute | solution.py:205
  31.0 32.9 %copy-start.15 = (bf16[2,4,128,256]{3,2,1,0:T(8,128)(2,1)}, bf16[2,4,128,256]{3,2,1,0:T(8,128)(2,1)S(1)}, u32[]{:S(2)}) copy-start(bf16[2,4,128,256]{3,2,1,0:T(8,128)(2,1)S(1)} %collective-permute-done.7.near_ref) | copy-start | bytes 1572868
  31.0 36.0 %collective-permute-start.8 = (bf16[2,4,128,256]{3,2,1,0:T(8,128)(2,1)S(1)}, bf16[2,4,128,256]{3,2,1,0:T(8,128)(2,1)}, u32[]{:S(2)}, u32[]{:S(2)}) collective-permute-start(bf16[2,4,128,256]{3,2,1,0:T(8,128)(2,1)S(1)} %collective-permute-done.7.near_ref), channel_id=1, source_target_pairs={{0,4},{4,8},{8,12},{12,16},{16,20},{20,24},{24,28},{6,2},{10,6},{1... | collective-permute-start | bytes 1572872 | tf_op jit(solution)/shard_map/ppermute | solution.py:206
  42.3 21.6 %copy-start.14 = (bf16[2,4,128,256]{3,2,1,0:T(8,128)(2,1)}, bf16[2,4,128,256]{3,2,1,0:T(8,128)(2,1)S(1)}, u32[]{:S(2)}) copy-start(bf16[2,4,128,256]{3,2,1,0:T(8,128)(2,1)S(1)} %collective-permute-done.4.near_ref) | copy-start | bytes 1572868
  42.3 32.1 %collective-permute-start.5 = (bf16[2,4,128,256]{3,2,1,0:T(8,128)(2,1)S(1)}, bf16[2,4,128,256]{3,2,1,0:T(8,128)(2,1)}, u32[]{:S(2)}, u32[]{:S(2)}) collective-permute-start(bf16[2,4,128,256]{3,2,1,0:T(8,128)(2,1)S(1)} %collective-permute-done.4.near_ref), channel_id=1, source_target_pairs={{0,4},{4,8},{8,12},{12,16},{16,20},{20,24},{24,28},{6,2},{10,6},{1... | collective-permute-start | bytes 1572872 | tf_op jit(solution)/shard_map/ppermute | solution.py:206
  45.5 18.4 %copy-start.4 = (bf16[2,4,128,128]{3,2,1,0:T(8,128)(2,1)}, bf16[2,4,128,128]{3,2,1,0:T(8,128)(2,1)S(1)}, u32[]{:S(2)}) copy-start(bf16[2,4,128,128]{3,2,1,0:T(8,128)(2,1)S(1)} %pad_maximum_fusion.3.own_ref) | copy-start | bytes 786436
  45.5 7.0 %collective-permute-start.1 = (bf16[2,4,128,128]{3,2,1,0:T(8,128)(2,1)S(1)}, bf16[2,4,128,128]{3,2,1,0:T(8,128)(2,1)S(1)}, u32[]{:S(2)}, u32[]{:S(2)}) collective-permute-start(bf16[2,4,128,128]{3,2,1,0:T(8,128)(2,1)S(1)} %pad_maximum_fusion.3.own_ref), channel_id=1, source_target_pairs={{0,2},{2,0},{4,6},{6,4},{8,10},{10,8},{12,14},{14,12},{16,18},{18,... | collective-permute-start | bytes 786440 | tf_op jit(solution)/shard_map/ppermute | solution.py:205
  50.3 13.6 %copy-start.17 = (bf16[2,4,128,128]{3,2,1,0:T(8,128)(2,1)}, bf16[2,4,128,128]{3,2,1,0:T(8,128)(2,1)S(1)}, u32[]{:S(2)}) copy-start(bf16[2,4,128,128]{3,2,1,0:T(8,128)(2,1)S(1)} %collective-permute-done.13.near_ref) | copy-start | bytes 786436
  50.3 32.0 %collective-permute-start.14 = (bf16[2,4,128,128]{3,2,1,0:T(8,128)(2,1)S(1)}, bf16[2,4,128,128]{3,2,1,0:T(8,128)(2,1)S(1)}, u32[]{:S(2)}, u32[]{:S(2)}) collective-permute-start(bf16[2,4,128,128]{3,2,1,0:T(8,128)(2,1)S(1)} %collective-permute-done.13.near_ref), channel_id=1, source_target_pairs={{0,4},{4,8},{8,12},{12,16},{16,20},{20,24},{24,28},{6,2},{10,6},{1... | collective-permute-start | bytes 786440 | tf_op jit(solution)/shard_map/ppermute | solution.py:206
  52.5 11.4 %copy-start.18 = (bf16[2,4,128,128]{3,2,1,0:T(8,128)(2,1)}, bf16[2,4,128,128]{3,2,1,0:T(8,128)(2,1)S(1)}, u32[]{:S(2)}) copy-start(bf16[2,4,128,128]{3,2,1,0:T(8,128)(2,1)S(1)} %collective-permute-done.1.near_ref) | copy-start | bytes 786436
  52.5 35.0 %collective-permute-start.2 = (bf16[2,4,128,128]{3,2,1,0:T(8,128)(2,1)S(1)}, bf16[2,4,128,128]{3,2,1,0:T(8,128)(2,1)S(1)}, u32[]{:S(2)}, u32[]{:S(2)}) collective-permute-start(bf16[2,4,128,128]{3,2,1,0:T(8,128)(2,1)S(1)} %collective-permute-done.1.near_ref), channel_id=1, source_target_pairs={{0,4},{4,8},{8,12},{12,16},{16,20},{20,24},{24,28},{6,2},{10,6},{1... | collective-permute-start | bytes 786440 | tf_op jit(solution)/shard_map/ppermute | solution.py:206
  63.9 30.5 %collective-permute-start.18 = (bf16[4,128,256]{2,1,0:T(8,128)(2,1)}, bf16[4,128,256]{2,1,0:T(8,128)(2,1)S(1)}, u32[]{:S(2)}, u32[]{:S(2)}) collective-permute-start(bf16[4,128,256]{2,1,0:T(8,128)(2,1)} %get-tuple-element.42), channel_id=1, source_target_pairs={{0,1},{1,0},{2,3},{3,2},{4,5},{5,4},{6,7},{7,6},{8,9},{9,8},{10,11... | collective-permute-start | bytes 786440 | tf_op jit(solution)/shard_map/ppermute | solution.py:209
  74.3 20.1 %collective-permute-start.17 = (bf16[4,128,256]{2,1,0:T(8,128)(2,1)}, bf16[4,128,256]{2,1,0:T(8,128)(2,1)S(1)}, u32[]{:S(2)}, u32[]{:S(2)}) collective-permute-start(bf16[4,128,256]{2,1,0:T(8,128)(2,1)} %get-tuple-element.41), channel_id=1, source_target_pairs={{0,1},{1,0},{2,3},{3,2},{4,5},{5,4},{6,7},{7,6},{8,9},{9,8},{10,11... | collective-permute-start | bytes 786440 | tf_op jit(solution)/shard_map/ppermute | solution.py:209
  81.8 12.6 %collective-permute-start.16 = (bf16[4,128,256]{2,1,0:T(8,128)(2,1)}, bf16[4,128,256]{2,1,0:T(8,128)(2,1)S(1)}, u32[]{:S(2)}, u32[]{:S(2)}) collective-permute-start(bf16[4,128,256]{2,1,0:T(8,128)(2,1)} %get-tuple-element.40), channel_id=1, source_target_pairs={{0,1},{1,0},{2,3},{3,2},{4,5},{5,4},{6,7},{7,6},{8,9},{9,8},{10,11... | collective-permute-start | bytes 786440 | tf_op jit(solution)/shard_map/ppermute | solution.py:209
  87.5 5.7 %collective-permute-start.19 = (bf16[4,128,128]{2,1,0:T(8,128)(2,1)}, bf16[4,128,128]{2,1,0:T(8,128)(2,1)S(1)}, u32[]{:S(2)}, u32[]{:S(2)}) collective-permute-start(bf16[4,128,128]{2,1,0:T(8,128)(2,1)} %get-tuple-element.43), channel_id=1, source_target_pairs={{0,1},{1,0},{2,3},{3,2},{4,5},{5,4},{6,7},{7,6},{8,9},{9,8},{10,11... | collective-permute-start | bytes 393224 | tf_op jit(solution)/shard_map/ppermute | solution.py:209
  92.7 1.7 %collective-permute-start.15 = (bf16[4,128,128]{2,1,0:T(8,128)(2,1)}, bf16[4,128,128]{2,1,0:T(8,128)(2,1)S(1)}, u32[]{:S(2)}, u32[]{:S(2)}) collective-permute-start(bf16[4,128,128]{2,1,0:T(8,128)(2,1)} %get-tuple-element.39), channel_id=1, source_target_pairs={{0,1},{1,0},{2,3},{3,2},{4,5},{5,4},{6,7},{7,6},{8,9},{9,8},{10,11... | collective-permute-start | bytes 393224 | tf_op jit(solution)/shard_map/ppermute | solution.py:209
  (9 other events, 7.8 us)

commit v2 on v1

v2 whole, which is shorter than its diff:
```python
import functools
import math

import jax
import jax.numpy as jnp
from jax import lax
from jax.experimental import pallas as pl
from jax.experimental.pallas import tpu as pltpu
from jax.sharding import PartitionSpec as P

DH = 128
DOC_MOST = 256
MASKED = -1e30
GROUP = 4
SCALE = 1.0 / math.sqrt(DH)
VMEM = 60 * 1024 * 1024
WHOLE = pl.BlockSpec(memory_space=pltpu.VMEM)


def dot_nt(a, b):
    return lax.dot_general(a, b, (((1,), (1,)), ((), ())), preferred_element_type=jnp.float32)


def dot_tn(a, b):
    return lax.dot_general(a, b, (((0,), (0,)), ((), ())), preferred_element_type=jnp.float32)


def dot_nn(a, b):
    return lax.dot_general(a, b, (((1,), (0,)), ((), ())), preferred_element_type=jnp.float32)


def stack_rows(*blocks):
    return jnp.concatenate(blocks, axis=0)


def tile_probs(keys, queries, key_ids, query_ids):
    scores = dot_nt(keys, queries) * (SCALE * math.log2(math.e))
    scores = jnp.where(key_ids == query_ids, scores, jnp.float32(MASKED))
    top = jnp.max(scores, axis=0, keepdims=True)
    weights = jnp.exp2(scores - top)
    return weights * (1.0 / jnp.sum(weights, axis=0, keepdims=True))


def attend(probs_low, values, grads):
    attended = dot_tn(values, probs_low).astype(jnp.bfloat16)
    delta = jnp.sum(
        attended.astype(jnp.float32) * grads.T.astype(jnp.float32), axis=0, keepdims=True
    )
    return attended, delta


def query_block(queries, grads, keys, values, key_ids, query_ids):
    probs = tile_probs(keys, queries, key_ids, query_ids)
    low = probs.astype(jnp.bfloat16)
    attended, delta = attend(low, values, grads)
    score_grad = (probs * (dot_nt(values, grads) - delta)).astype(jnp.bfloat16)
    query_grad = (dot_tn(keys, score_grad) * SCALE).T.astype(jnp.bfloat16)
    attended = attended.astype(jnp.float32).T.astype(jnp.bfloat16)
    return attended, query_grad, score_grad, low


def interior_kernel(edge, ext_ref, row_ids_ref, col_ids_ref, done_ref, part_ref):
    rows = ext_ref.shape[1]
    blocks = rows // edge
    part_ref[...] = jnp.zeros_like(part_ref)
    for b in range(1, blocks - 1):
        at = slice(b * edge, (b + 1) * edge)
        band = slice((b - 1) * edge, (b + 2) * edge)
        ids = slice(b * edge, (b + 3) * edge)
        queries, grads = ext_ref[0, at], ext_ref[3, at]
        attended, query_grad, score_grad, low = query_block(
            queries,
            grads,
            ext_ref[1, band],
            ext_ref[2, band],
            col_ids_ref[ids, :],
            row_ids_ref[:, (b + 1) * edge : (b + 2) * edge],
        )
        done_ref[0, (b - 1) * edge : b * edge] = attended
        done_ref[1, (b - 1) * edge : b * edge] = query_grad
        part_ref[0, band] += dot_nn(score_grad, queries)
        part_ref[1, band] += dot_nn(low, grads)


def edge_kernel(edge, ext_ref, even_ref, odd_ref, done_ref, part_ref, row_ids_ref, col_ids_ref, *refs):
    outs, (result, acc_ref) = refs[:-2], refs[-2:]
    rows = ext_ref.shape[1]
    blocks = rows // edge
    position, core = lax.axis_index("blk"), lax.axis_index("head")
    place, parity = position % GROUP, (position // GROUP) % 2
    acc_ref[...] = part_ref[...]
    for m in range(2):
        result[m, edge : rows - edge] = done_ref[m]
    for side in range(2):
        from_even = parity == (1 - side)
        q_halo, k_halo, v_halo, g_halo = (
            jnp.where(from_even, even_ref[m], odd_ref[m]) for m in range(4)
        )
        own = slice(0, edge) if side == 0 else slice(rows - edge, rows)
        own_ids = slice(edge, 2 * edge) if side == 0 else slice(rows, rows + edge)
        halo_ids = slice(0, edge) if side == 0 else slice(rows + edge, rows + 2 * edge)
        wide = slice(0, 2 * edge) if side == 0 else slice(rows - 2 * edge, rows)
        wide_ids = slice(edge, 3 * edge) if side == 0 else slice(rows - edge, rows + edge)
        queries, grads = ext_ref[0, own], ext_ref[3, own]
        attended, query_grad, score_grad, low = query_block(
            queries,
            grads,
            stack_rows(ext_ref[1, wide], k_halo),
            stack_rows(ext_ref[2, wide], v_halo),
            stack_rows(col_ids_ref[wide_ids, :], col_ids_ref[halo_ids, :]),
            row_ids_ref[:, own_ids],
        )
        result[0, own] = attended
        result[1, own] = query_grad
        acc_ref[0, wide] += dot_nn(score_grad[: 2 * edge], queries)
        acc_ref[1, wide] += dot_nn(low[: 2 * edge], grads)
        keys, values = ext_ref[1, own], ext_ref[2, own]
        probs = tile_probs(
            stack_rows(keys, k_halo),
            q_halo,
            stack_rows(col_ids_ref[own_ids, :], col_ids_ref[halo_ids, :]),
            row_ids_ref[:, halo_ids],
        )
        low = probs.astype(jnp.bfloat16)
        _, delta = attend(low, stack_rows(values, v_halo), g_halo)
        score_grad = (probs[:edge] * (dot_nt(values, g_halo) - delta)).astype(jnp.bfloat16)
        acc_ref[0, own] += dot_nn(score_grad, q_halo)
        acc_ref[1, own] += dot_nn(low[:edge], g_halo)
    result[2] = (acc_ref[0] * SCALE).astype(jnp.bfloat16)
    result[3] = acc_ref[1].astype(jnp.bfloat16)
    half = outs[0].shape[2]
    for s, out in enumerate(outs):
        chip = place ^ s
        for piece in range(2):
            first = pl.multiple_of((chip * 2 + (core ^ piece)) * half, half)
            for m in range(4):
                out[piece, m] = result[m, pl.ds(first, half), :]


def call(kernel, out_shape, *args, scratch=(), flops=0, exps=0):
    return pl.pallas_call(
        kernel,
        out_shape=out_shape,
        in_specs=[WHOLE] * len(args),
        out_specs=jax.tree.map(lambda _: WHOLE, out_shape),
        scratch_shapes=scratch,
        compiler_params=pltpu.CompilerParams(vmem_limit_bytes=VMEM),
        cost_estimate=pl.CostEstimate(
            flops=flops, bytes_accessed=sum(a.size * 2 for a in args), transcendentals=exps
        ),
    )(*args)


def shape(*dims, dtype=jnp.bfloat16):
    return jax.ShapeDtypeStruct(dims, dtype)


def pack_kernel(q_ref, k_ref, v_ref, g_ref, *outs):
    chunks = len(outs) // 2
    head_half = q_ref.shape[1] // 2
    core, place = lax.axis_index("head"), lax.axis_index("blk") % GROUP
    for which in range(2):
        for s in range(GROUP):
            base = (core ^ which) * head_half + (place ^ s) * chunks * DH
            for j in range(chunks):
                first = pl.multiple_of(base + j * DH, DH)
                for m, ref in enumerate((q_ref, k_ref, v_ref, g_ref)):
                    outs[which * chunks + j][s, m] = ref[:, pl.ds(first, DH)]


def pack(arrays, chunks):
    rows, width = arrays[0].shape
    steps = 2
    block = rows // steps
    got = pl.pallas_call(
        pack_kernel,
        grid=(steps,),
        out_shape=[shape(GROUP, 4, rows, DH)] * (2 * chunks),
        in_specs=[pl.BlockSpec((block, width), lambda i: (i, 0))] * 4,
        out_specs=[pl.BlockSpec((GROUP, 4, block, DH), lambda i: (0, 0, i, 0))] * (2 * chunks),
        compiler_params=pltpu.CompilerParams(vmem_limit_bytes=VMEM),
    )(*arrays)
    return got[:chunks], got[chunks:]


def join_kernel(mine_ref, received_ref, *outs):
    for s, out in enumerate(outs):
        out[0] = mine_ref[s]
        out[1] = received_ref[s]


def gather_kernel(*refs):
    slots, (ext, to_even, to_odd) = refs[:GROUP], refs[GROUP:]
    half, edge = slots[0].shape[2], to_even.shape[1]
    position, core = lax.axis_index("blk"), lax.axis_index("head")
    place, parity = position % GROUP, (position // GROUP) % 2
    for s, slot in enumerate(slots):
        for piece in range(2):
            first = pl.multiple_of(((place ^ s) * 2 + (core ^ piece)) * half, half)
            for m in range(4):
                ext[m, pl.ds(first, half), :] = slot[piece, m]
    rows = ext.shape[1]
    first = pl.multiple_of((rows - edge) * (1 - parity), edge)
    to_even[...] = ext[:, pl.ds(first, edge), :]
    first = pl.multiple_of((rows - edge) * parity, edge)
    to_odd[...] = ext[:, pl.ds(first, edge), :]


def split_kernel(*refs):
    slots, out = refs[:-1], refs[-1]
    for s, slot in enumerate(slots):
        out[s] = slot[1]


def unpack_kernel(chunks, *refs):
    kept, received, outs = refs[: chunks * GROUP], refs[chunks * GROUP : -4], refs[-4:]
    head_half = outs[0].shape[1] // 2
    core, place = lax.axis_index("head"), lax.axis_index("blk") % GROUP
    for s in range(GROUP):
        for j in range(chunks):
            for which in range(2):
                base = (core ^ which) * head_half + (place ^ s) * chunks * DH
                first = pl.multiple_of(base + j * DH, DH)
                for m, out in enumerate(outs):
                    block = kept[j * GROUP + s][0, m] if which == 0 else received[j][s, m]
                    out[:, pl.ds(first, DH)] = block


def unpack(kept, received, width):
    chunks = len(received)
    rows = received[0].shape[2]
    steps = 2
    block = rows // steps
    flat = [slot for chunk in kept for slot in chunk]
    return pl.pallas_call(
        functools.partial(unpack_kernel, chunks),
        grid=(steps,),
        out_shape=[shape(rows, width)] * 4,
        in_specs=[pl.BlockSpec((1, 4, block, DH), lambda i: (0, 0, i, 0))] * len(flat)
        + [pl.BlockSpec((GROUP, 4, block, DH), lambda i: (0, 0, i, 0))] * chunks,
        out_specs=[pl.BlockSpec((block, width), lambda i: (i, 0))] * 4,
        compiler_params=pltpu.CompilerParams(vmem_limit_bytes=VMEM),
    )(*flat, *received)


def body(query_rows, key_rows, value_rows, out_grad, doc_ids):
    positions = lax.axis_size("blk")
    half, width = query_rows.shape
    heads = width // DH
    chunks = heads // (2 * GROUP)
    edge = 2 * half
    rows = GROUP * edge
    swap = [(0, 1), (1, 0)]
    hops = [[(i, i ^ s) for i in range(positions)] for s in range(GROUP)]
    planes = positions // GROUP

    def plane_pairs(first):
        route = []
        for low in range(first, planes - 1, 2):
            for i in range(GROUP):
                here, there = low * GROUP + i, (low + 1) * GROUP + i
                route += [(here, there), (there, here)]
        return route

    plane = lax.axis_index("blk") // GROUP
    padded = jnp.pad(doc_ids, (edge, edge), constant_values=-1)
    ids = lax.dynamic_slice_in_dim(padded, plane * rows, rows + 2 * edge, 0)
    row_ids, col_ids = ids[None, :], ids[:, None]

    def exchange(slots):
        return [slots[0]] + [lax.ppermute(slots[s], "blk", hops[s]) for s in range(1, GROUP)]

    mine, other = pack((query_rows, key_rows, value_rows, out_grad), chunks)
    slot = shape(2, 4, half, DH)
    kept, received = [], []
    for j in range(chunks):
        theirs = lax.ppermute(other[j], "head", swap)
        slots = exchange(call(join_kernel, [slot] * GROUP, mine[j], theirs))
        ext, to_even, to_odd = call(
            gather_kernel, [shape(4, rows, DH), shape(4, edge, DH), shape(4, edge, DH)], *slots
        )
        even = lax.ppermute(to_even, "blk", plane_pairs(0))
        odd = lax.ppermute(to_odd, "blk", plane_pairs(1))
        unit = 2 * DH * edge * edge
        done, part = call(
            functools.partial(interior_kernel, edge),
            [shape(2, rows - 2 * edge, DH), shape(2, rows, DH, dtype=jnp.float32)],
            ext,
            row_ids,
            col_ids,
            flops=unit * 36,
            exps=6 * edge * edge,
        )
        back = call(
            functools.partial(edge_kernel, edge),
            [slot] * GROUP,
            ext,
            even,
            odd,
            done,
            part,
            row_ids,
            col_ids,
            scratch=[
                pltpu.VMEM((4, rows, DH), jnp.bfloat16),
                pltpu.VMEM((2, rows, DH), jnp.float32),
            ],
            flops=unit * 50,
            exps=10 * edge * edge,
        )
        back = exchange(back)
        kept.append(back)
        away = call(split_kernel, shape(GROUP, 4, half, DH), *back)
        received.append(lax.ppermute(away, "head", swap))
    return tuple(unpack(kept, received, width))


def solution(mesh):
    placed = P(("blk", "head"), None)
    return jax.shard_map(
        body,
        mesh=mesh,
        in_specs=(placed, placed, placed, placed, P()),
        out_specs=(placed,) * 4,
        check_vma=False,
    )
```

time: 100 us -> 95.4 us (0.954); the launches traced: 98.3 us -> 95 us
  waiting for transfers between devices: 24 us -> 15.8 us
  Pallas kernels: 36.4 us -> 42.8 us
  other arithmetic: 5.38 us -> 0 us
  local copies, waits for them, and re-layouts: 4.14 us -> 9.48 us
  starting transfers between devices: 27.2 us -> 26.2 us
    ppermute x20, waiting for transfers between devices: 24 us -> 15.8 us  [the longest x12 12.3 us: exchange(): lax.ppermute(slots[s], 'blk', hops[s])]
    pallas_call x6 -> x11, Pallas kernels: 33.7 us -> 39.8 us  [the longest x10 37 us: call(): pl.pallas_call(kernel, out_shape=out_shape, in_specs=[WHOLE] * len(args),...]
    unnamed x42 -> x46, local copies, waits for them, and re-layouts: 2.62 us -> 7.65 us
    unnamed x6 -> x0, other arithmetic: 3.48 us -> none
    another operation x5 -> x0, other arithmetic: 1.2 us -> none  [body(): own = jnp.stack([own, lax.ppermute(away, 'head', swap)])]
    ppermute x20, starting transfers between devices: 27.2 us -> 26.2 us  [the longest x12 12.2 us: exchange(): lax.ppermute(slots[s], 'blk', hops[s])]
  transfers between devices with their start and end apart: 20 -> 20, of which waited for: 5 -> 6; matrix products, arithmetic and copies ran while one was open for 7% -> 2% of each run, Pallas kernels for 32% -> 39%
where the time goes in v2:
time: 95.4 us; the launch traced here: 95 us
  Pallas kernels  42.8 us (45%)
  starting transfers between devices  26.2 us (27%)
  waiting for transfers between devices  15.8 us (17%)
  local copies, waits for them, and re-layouts  9.48 us (10%)
    pallas_call x10, Pallas kernels, call(): pl.pallas_call(kernel, out_shape=out_shape, in_specs=[WHOLE] * len(args),...  37 us
    ppermute x12, waiting for transfers between devices, exchange(): lax.ppermute(slots[s], 'blk', hops[s])  12.3 us
    ppermute x12, starting transfers between devices, exchange(): lax.ppermute(slots[s], 'blk', hops[s])  12.2 us
    ppermute x2, starting transfers between devices, body(): odd = lax.ppermute(to_odd, 'blk', plane_pairs(1))  8.64 us
    unnamed x46, local copies, waits for them, and re-layouts  7.65 us
    ppermute x2, starting transfers between devices, body(): received.append(lax.ppermute(away, 'head', swap))  4.24 us
    pallas_call x1, Pallas kernels, unpack(): pl.pallas_call(functools.partial(unpack_kernel, chunks), grid=(steps,), o...  2.96 us
    pallas_call x1, Pallas kernels, pack(): pl.pallas_call(pack_kernel, grid=(steps,), out_shape=[shape(GROUP, 4, row...  2.78 us
  transfers between devices with their start and end apart: 20, of which 6 were waited for; matrix products, arithmetic and copies ran while one was open for 2% of the time, Pallas kernels for 39%

profile of v2, /device:TPU:9, one launch (start us, length us, event | category | flops | bytes accessed | tf_op | source)
XLA Modules:
  0.0 95.0 jit_solution(1416389154875112829)
XLA Ops:
  0.6 2.8 %shard_map.84 = (bf16[4,4,128,128]{3,2,1,0:T(8,128)(2,1)}, bf16[4,4,128,128]{3,2,1,0:T(8,128)(2,1)}, bf16[4,4,128,128]{3,2,1,0:T(8,128)(2,1)}, bf16[4,4,128,128]{3,2,1,0:T(8,128)(2,1)}) custom-call(bf16[128,2048]{1,0:T(8,128)(2,1)} %q_ref.1, bf16[128,2048]{1,0:T(8,128)(2,1)} %k_ref.1, bf16[128,2048]{1,0:T(8,128)(2,1)} %v_ref.1, bf16[128,2048]{1,0:T(8,128)(2,1)} %g_ref.1), custom_call_target="tpu_custom_call" | custom-call | tf_op jit(solution)/shard_map/pallas_call | solution.py:175
  4.2 1.7 %collective-permute-done.received_ref = bf16[4,4,128,128]{3,2,1,0:T(8,128)(2,1)S(1)} collective-permute-done((bf16[4,4,128,128]{3,2,1,0:T(8,128)(2,1)}, bf16[4,4,128,128]{3,2,1,0:T(8,128)(2,1)S(1)}, u32[]{:S(2)}, u32[]{:S(2)}) %collective-permute-start) | collective-permute-done | bytes 524320 | tf_op jit(solution)/shard_map/ppermute | solution.py:277
  6.6 2.2 %shard_map.85 = (bf16[2,4,128,128]{3,2,1,0:T(8,128)(2,1)}, bf16[2,4,128,128]{3,2,1,0:T(8,128)(2,1)}, bf16[2,4,128,128]{3,2,1,0:T(8,128)(2,1)}, bf16[2,4,128,128]{3,2,1,0:T(8,128)(2,1)}) custom-call(bf16[4,4,128,128]{3,2,1,0:T(8,128)(2,1)} %get-tuple-element.34.mine_ref, bf16[4,4,128,128]{3,2,1,0:T(8,128)(2,1)} %copy-done.7), custom_call_target="tpu_custom_call" | custom-call | bytes 1048576 | tf_op jit(solution)/shard_map/pallas_call | solution.py:141
  8.8 1.2 %collective-permute-start.1 = (bf16[2,4,128,128]{3,2,1,0:T(8,128)(2,1)}, bf16[2,4,128,128]{3,2,1,0:T(8,128)(2,1)S(1)}, u32[]{:S(2)}, u32[]{:S(2)}) collective-permute-start(bf16[2,4,128,128]{3,2,1,0:T(8,128)(2,1)} %get-tuple-element.37), channel_id=1, source_target_pairs={{0,2},{2,0},{4,6},{6,4},{8,10},{10,8},{12,14},{14,12},{16,18},{18,... | collective-permute-start | bytes 786440 | tf_op jit(solution)/shard_map/ppermute | solution.py:271
  10.1 1.2 %collective-permute-start.2 = (bf16[2,4,128,128]{3,2,1,0:T(8,128)(2,1)}, bf16[2,4,128,128]{3,2,1,0:T(8,128)(2,1)S(1)}, u32[]{:S(2)}, u32[]{:S(2)}) collective-permute-start(bf16[2,4,128,128]{3,2,1,0:T(8,128)(2,1)} %get-tuple-element.38), channel_id=1, source_target_pairs={{0,4},{2,6},{4,0},{6,2},{8,12},{10,14},{12,8},{14,10},{16,20},{18,... | collective-permute-start | bytes 786440 | tf_op jit(solution)/shard_map/ppermute | solution.py:271
  12.3 2.2 %shard_map.89 = (bf16[2,4,128,128]{3,2,1,0:T(8,128)(2,1)}, bf16[2,4,128,128]{3,2,1,0:T(8,128)(2,1)}, bf16[2,4,128,128]{3,2,1,0:T(8,128)(2,1)}, bf16[2,4,128,128]{3,2,1,0:T(8,128)(2,1)}) custom-call(bf16[4,4,128,128]{3,2,1,0:T(8,128)(2,1)} %get-tuple-element.49.mine_ref, bf16[4,4,128,128]{3,2,1,0:T(8,128)(2,1)} %copy-done.6), custom_call_target="tpu_custom_call" | custom-call | bytes 1048576 | tf_op jit(solution)/shard_map/pallas_call | solution.py:141
  14.5 1.2 %collective-permute-start.10 = (bf16[2,4,128,128]{3,2,1,0:T(8,128)(2,1)}, bf16[2,4,128,128]{3,2,1,0:T(8,128)(2,1)S(1)}, u32[]{:S(2)}, u32[]{:S(2)}) collective-permute-start(bf16[2,4,128,128]{3,2,1,0:T(8,128)(2,1)} %get-tuple-element.52), channel_id=1, source_target_pairs={{0,2},{2,0},{4,6},{6,4},{8,10},{10,8},{12,14},{14,12},{16,18},{18,... | collective-permute-start | bytes 786440 | tf_op jit(solution)/shard_map/ppermute | solution.py:271
  15.7 1.2 %collective-permute-start.11 = (bf16[2,4,128,128]{3,2,1,0:T(8,128)(2,1)}, bf16[2,4,128,128]{3,2,1,0:T(8,128)(2,1)S(1)}, u32[]{:S(2)}, u32[]{:S(2)}) collective-permute-start(bf16[2,4,128,128]{3,2,1,0:T(8,128)(2,1)} %get-tuple-element.53), channel_id=1, source_target_pairs={{0,4},{2,6},{4,0},{6,2},{8,12},{10,14},{12,8},{14,10},{16,20},{18,... | collective-permute-start | bytes 786440 | tf_op jit(solution)/shard_map/ppermute | solution.py:271
  16.9 1.8 %collective-permute-start.12 = (bf16[2,4,128,128]{3,2,1,0:T(8,128)(2,1)}, bf16[2,4,128,128]{3,2,1,0:T(8,128)(2,1)S(1)}, u32[]{:S(2)}, u32[]{:S(2)}) collective-permute-start(bf16[2,4,128,128]{3,2,1,0:T(8,128)(2,1)} %get-tuple-element.54), channel_id=1, source_target_pairs={{0,6},{2,4},{4,2},{6,0},{8,14},{10,12},{12,10},{14,8},{16,22},{18,... | collective-permute-start | bytes 786440 | tf_op jit(solution)/shard_map/ppermute | solution.py:271
  18.8 4.4 %collective-permute-done.3.refs_3_ = bf16[2,4,128,128]{3,2,1,0:T(8,128)(2,1)S(1)} collective-permute-done((bf16[2,4,128,128]{3,2,1,0:T(8,128)(2,1)}, bf16[2,4,128,128]{3,2,1,0:T(8,128)(2,1)S(1)}, u32[]{:S(2)}, u32[]{:S(2)}) %collective-permute-start.3) | collective-permute-done | bytes 262176 | tf_op jit(solution)/shard_map/ppermute | solution.py:271
  23.9 2.4 %shard_map.86 = (bf16[4,1024,128]{2,1,0:T(8,128)(2,1)}, bf16[4,256,128]{2,1,0:T(8,128)(2,1)}, bf16[4,256,128]{2,1,0:T(8,128)(2,1)}) custom-call(bf16[2,4,128,128]{3,2,1,0:T(8,128)(2,1)} %get-tuple-element.36.refs_0_, bf16[2,4,128,128]{3,2,1,0:T(8,128)(2,1)} %copy-done.13, bf16[2,4,128,128]{3,2,1,0:T(8,128)(2,1)} %copy-done.14, ...), custom_call_target="tpu_custom_call" | custom-call | bytes 1048576 | tf_op jit(solution)/shard_map/pallas_call | solution.py:141
  26.5 4.3 %collective-permute-start.5 = (bf16[4,256,128]{2,1,0:T(8,128)(2,1)}, bf16[4,256,128]{2,1,0:T(8,128)(2,1)S(1)}, u32[]{:S(2)}, u32[]{:S(2)}) collective-permute-start(bf16[4,256,128]{2,1,0:T(8,128)(2,1)} %get-tuple-element.42), channel_id=1, source_target_pairs={{8,16},{16,8},{10,18},{18,10},{12,20},{20,12},{14,22},{22,14},{9,1... | collective-permute-start | bytes 786440 | tf_op jit(solution)/shard_map/ppermute | solution.py:283
  32.2 1.2 %broadcast_in_dim.8.col_ids_ref = s32[1536,1]{1,0:T(8,128)} reshape(s32[1536]{0:T(1024)S(1)} %pad_dynamic-slice_fusion) | data formatting | bytes 12288 | tf_op jit(solution)/shard_map/broadcast_in_dim | solution.py:268
  33.4 1.1 %collective-permute-done.12.refs_3_ = bf16[2,4,128,128]{3,2,1,0:T(8,128)(2,1)S(1)} collective-permute-done((bf16[2,4,128,128]{3,2,1,0:T(8,128)(2,1)}, bf16[2,4,128,128]{3,2,1,0:T(8,128)(2,1)S(1)}, u32[]{:S(2)}, u32[]{:S(2)}) %collective-permute-start.12) | collective-permute-done | bytes 262176 | tf_op jit(solution)/shard_map/ppermute | solution.py:271
  35.2 2.4 %shard_map.90 = (bf16[4,1024,128]{2,1,0:T(8,128)(2,1)}, bf16[4,256,128]{2,1,0:T(8,128)(2,1)}, bf16[4,256,128]{2,1,0:T(8,128)(2,1)}) custom-call(bf16[2,4,128,128]{3,2,1,0:T(8,128)(2,1)} %get-tuple-element.51.refs_0_, bf16[2,4,128,128]{3,2,1,0:T(8,128)(2,1)} %copy-done.10, bf16[2,4,128,128]{3,2,1,0:T(8,128)(2,1)} %copy-done.11, ...), custom_call_target="tpu_custom_call" | custom-call | bytes 1048576 | tf_op jit(solution)/shard_map/pallas_call | solution.py:141
  37.8 4.3 %collective-permute-start.14 = (bf16[4,256,128]{2,1,0:T(8,128)(2,1)}, bf16[4,256,128]{2,1,0:T(8,128)(2,1)S(1)}, u32[]{:S(2)}, u32[]{:S(2)}) collective-permute-start(bf16[4,256,128]{2,1,0:T(8,128)(2,1)} %get-tuple-element.57), channel_id=1, source_target_pairs={{8,16},{16,8},{10,18},{18,10},{12,20},{20,12},{14,22},{22,14},{9,1... | collective-permute-start | bytes 786440 | tf_op jit(solution)/shard_map/ppermute | solution.py:283
  42.1 5.0 %shard_map.87 = (bf16[2,512,128]{2,1,0:T(8,128)(2,1)}, f32[2,1024,128]{2,1,0:T(8,128)}) custom-call(bf16[4,1024,128]{2,1,0:T(8,128)(2,1)} %get-tuple-element.40.ext_ref, s32[1,1536]{1,0:T(1,128)} %broadcast_in_dim.6.row_ids_ref, s32[1536,1]{1,0:T(8,128)} %broadcast_in_dim.8.col_ids_ref), custom_call_target="tpu_custom_call" | custom-call | flops 603979776 | bytes 1054720 | tf_op jit(solution)/shard_map/pallas_call | solution.py:141
  47.9 6.8 %shard_map.88 = (bf16[2,4,128,128]{3,2,1,0:T(8,128)(2,1)}, bf16[2,4,128,128]{3,2,1,0:T(8,128)(2,1)}, bf16[2,4,128,128]{3,2,1,0:T(8,128)(2,1)}, bf16[2,4,128,128]{3,2,1,0:T(8,128)(2,1)}) custom-call(bf16[4,1024,128]{2,1,0:T(8,128)(2,1)} %get-tuple-element.40.ext_ref, bf16[4,256,128]{2,1,0:T(8,128)(2,1)} %copy-done.16, bf16[4,256,128]{2,1,0:T(8,128)(2,1)} %copy-done.17, ...), custom_call_target="tpu_custom_call" | custom-call | flops 838860800 | bytes 2365440 | tf_op jit(solution)/shard_map/pallas_call | solution.py:141
  54.7 1.2 %collective-permute-start.6 = (bf16[2,4,128,128]{3,2,1,0:T(8,128)(2,1)}, bf16[2,4,128,128]{3,2,1,0:T(8,128)(2,1)S(1)}, u32[]{:S(2)}, u32[]{:S(2)}) collective-permute-start(bf16[2,4,128,128]{3,2,1,0:T(8,128)(2,1)} %get-tuple-element.46), channel_id=1, source_target_pairs={{0,2},{2,0},{4,6},{6,4},{8,10},{10,8},{12,14},{14,12},{16,18},{18,... | collective-permute-start | bytes 786440 | tf_op jit(solution)/shard_map/ppermute | solution.py:271
  55.9 5.1 %shard_map.91 = (bf16[2,512,128]{2,1,0:T(8,128)(2,1)}, f32[2,1024,128]{2,1,0:T(8,128)}) custom-call(bf16[4,1024,128]{2,1,0:T(8,128)(2,1)} %get-tuple-element.55.ext_ref, s32[1,1536]{1,0:T(1,128)} %broadcast_in_dim.6.row_ids_ref, s32[1536,1]{1,0:T(8,128)} %broadcast_in_dim.8.col_ids_ref), custom_call_target="tpu_custom_call" | custom-call | flops 603979776 | bytes 1054720 | tf_op jit(solution)/shard_map/pallas_call | solution.py:141
  61.3 1.2 %collective-permute-start.8 = (bf16[2,4,128,128]{3,2,1,0:T(8,128)(2,1)S(1)}, bf16[2,4,128,128]{3,2,1,0:T(8,128)(2,1)S(1)}, u32[]{:S(2)}, u32[]{:S(2)}) collective-permute-start(bf16[2,4,128,128]{3,2,1,0:T(8,128)(2,1)S(1)} %copy-done.21), channel_id=1, source_target_pairs={{0,6},{2,4},{4,2},{6,0},{8,14},{10,12},{12,10},{14,8},{16,22},{18,... | collective-permute-start | bytes 786440 | tf_op jit(solution)/shard_map/ppermute | solution.py:271
  63.3 6.8 %shard_map.92 = (bf16[2,4,128,128]{3,2,1,0:T(8,128)(2,1)}, bf16[2,4,128,128]{3,2,1,0:T(8,128)(2,1)}, bf16[2,4,128,128]{3,2,1,0:T(8,128)(2,1)}, bf16[2,4,128,128]{3,2,1,0:T(8,128)(2,1)}) custom-call(bf16[4,1024,128]{2,1,0:T(8,128)(2,1)} %get-tuple-element.55.ext_ref, bf16[4,256,128]{2,1,0:T(8,128)(2,1)} %copy-done.18, bf16[4,256,128]{2,1,0:T(8,128)(2,1)} %copy-done.19, ...), custom_call_target="tpu_custom_call" | custom-call | flops 838860800 | bytes 2365440 | tf_op jit(solution)/shard_map/pallas_call | solution.py:141
  70.1 1.2 %collective-permute-start.15 = (bf16[2,4,128,128]{3,2,1,0:T(8,128)(2,1)}, bf16[2,4,128,128]{3,2,1,0:T(8,128)(2,1)S(1)}, u32[]{:S(2)}, u32[]{:S(2)}) collective-permute-start(bf16[2,4,128,128]{3,2,1,0:T(8,128)(2,1)} %get-tuple-element.61), channel_id=1, source_target_pairs={{0,2},{2,0},{4,6},{6,4},{8,10},{10,8},{12,14},{14,12},{16,18},{18,... | collective-permute-start | bytes 786440 | tf_op jit(solution)/shard_map/ppermute | solution.py:271
  71.6 1.2 %collective-permute-start.17 = (bf16[2,4,128,128]{3,2,1,0:T(8,128)(2,1)}, bf16[2,4,128,128]{3,2,1,0:T(8,128)(2,1)S(1)}, u32[]{:S(2)}, u32[]{:S(2)}) collective-permute-start(bf16[2,4,128,128]{3,2,1,0:T(8,128)(2,1)} %get-tuple-element.63), channel_id=1, source_target_pairs={{0,6},{2,4},{4,2},{6,0},{8,14},{10,12},{12,10},{14,8},{16,22},{18,... | collective-permute-start | bytes 786440 | tf_op jit(solution)/shard_map/ppermute | solution.py:271
  72.8 0.9 collective-permute-done.7.refs_2_
  74.4 2.0 %shard_map.93 = bf16[4,4,128,128]{3,2,1,0:T(8,128)(2,1)} custom-call(bf16[2,4,128,128]{3,2,1,0:T(8,128)(2,1)} %get-tuple-element.45.refs_0_, bf16[2,4,128,128]{3,2,1,0:T(8,128)(2,1)} %copy-done, bf16[2,4,128,128]{3,2,1,0:T(8,128)(2,1)} %copy-done.1, bf16[2,4,128,128]{3,2,1,0:T(8,128)(2,1)} %copy-done.2), custom_call_target="tpu_custom_call" | custom-call | bytes 1048576 | tf_op jit(solution)/shard_map/pallas_call | solution.py:141
  76.5 2.8 %collective-permute-start.18 = (bf16[4,4,128,128]{3,2,1,0:T(8,128)(2,1)}, bf16[4,4,128,128]{3,2,1,0:T(8,128)(2,1)S(1)}, u32[]{:S(2)}, u32[]{:S(2)}) collective-permute-start(bf16[4,4,128,128]{3,2,1,0:T(8,128)(2,1)} %shard_map.93), channel_id=1, source_target_pairs={{0,1},{1,0},{2,3},{3,2},{4,5},{5,4},{6,7},{7,6},{8,9},{9,8},{10,11... | collective-permute-start | bytes 1572872 | tf_op jit(solution)/shard_map/ppermute | solution.py:314
  79.3 5.9 %collective-permute-done.16.refs_2_.refs_6_ = bf16[2,4,128,128]{3,2,1,0:T(8,128)(2,1)S(1)} collective-permute-done((bf16[2,4,128,128]{3,2,1,0:T(8,128)(2,1)}, bf16[2,4,128,128]{3,2,1,0:T(8,128)(2,1)S(1)}, u32[]{:S(2)}, u32[]{:S(2)}) %collective-permute-start.16) | collective-permute-done | bytes 262176 | tf_op jit(solution)/shard_map/ppermute | solution.py:271
  86.0 2.0 %shard_map.94 = bf16[4,4,128,128]{3,2,1,0:T(8,128)(2,1)} custom-call(bf16[2,4,128,128]{3,2,1,0:T(8,128)(2,1)} %get-tuple-element.60.refs_0_.refs_4_, bf16[2,4,128,128]{3,2,1,0:T(8,128)(2,1)} %copy-done.3, bf16[2,4,128,128]{3,2,1,0:T(8,128)(2,1)} %copy-done.4, bf16[2,4,128,128]{3,2,1,0:T(8,128)(2,1)} %copy-done.5), custom_call_target="tpu_custom_call" | custom-call | bytes 1048576 | tf_op jit(solution)/shard_map/pallas_call | solution.py:141
  88.0 1.4 %collective-permute-start.19 = (bf16[4,4,128,128]{3,2,1,0:T(8,128)(2,1)}, bf16[4,4,128,128]{3,2,1,0:T(8,128)(2,1)S(1)}, u32[]{:S(2)}, u32[]{:S(2)}) collective-permute-start(bf16[4,4,128,128]{3,2,1,0:T(8,128)(2,1)} %shard_map.94), channel_id=1, source_target_pairs={{0,1},{1,0},{2,3},{3,2},{4,5},{5,4},{6,7},{7,6},{8,9},{9,8},{10,11... | collective-permute-start | bytes 1572872 | tf_op jit(solution)/shard_map/ppermute | solution.py:314
  89.4 1.7 %collective-permute-done.19.refs_9_ = bf16[4,4,128,128]{3,2,1,0:T(8,128)(2,1)S(1)} collective-permute-done((bf16[4,4,128,128]{3,2,1,0:T(8,128)(2,1)}, bf16[4,4,128,128]{3,2,1,0:T(8,128)(2,1)S(1)}, u32[]{:S(2)}, u32[]{:S(2)}) %collective-permute-start.19) | collective-permute-done | bytes 524320 | tf_op jit(solution)/shard_map/ppermute | solution.py:314
  92.0 3.0 %shard_map.95 = (bf16[128,2048]{1,0:T(8,128)(2,1)}, bf16[128,2048]{1,0:T(8,128)(2,1)}, bf16[128,2048]{1,0:T(8,128)(2,1)}, bf16[128,2048]{1,0:T(8,128)(2,1)}) custom-call(bf16[2,4,128,128]{3,2,1,0:T(8,128)(2,1)} %get-tuple-element.45.refs_0_, bf16[2,4,128,128]{3,2,1,0:T(8,128)(2,1)} %copy-done, bf16[2,4,128,128]{3,2,1,0:T(8,128)(2,1)} %copy-done.1, ...), custom_call_target="tpu_custom_call" | custom-call | tf_op jit(solution)/shard_map/pallas_call | solution.py:235
  (69 shorter events, 10.2 us)
Async XLA Ops:
  3.4 2.4 %collective-permute-start = (bf16[4,4,128,128]{3,2,1,0:T(8,128)(2,1)}, bf16[4,4,128,128]{3,2,1,0:T(8,128)(2,1)S(1)}, u32[]{:S(2)}, u32[]{:S(2)}) collective-permute-start(bf16[4,4,128,128]{3,2,1,0:T(8,128)(2,1)} %get-tuple-element.35), channel_id=1, source_target_pairs={{0,1},{1,0},{2,3},{3,2},{4,5},{5,4},{6,7},{7,6},{8,9},{9,8},{10,11... | collective-permute-start | bytes 1572872 | tf_op jit(solution)/shard_map/ppermute | solution.py:277
  4.1 7.4 %collective-permute-start.9 = (bf16[4,4,128,128]{3,2,1,0:T(8,128)(2,1)}, bf16[4,4,128,128]{3,2,1,0:T(8,128)(2,1)S(1)}, u32[]{:S(2)}, u32[]{:S(2)}) collective-permute-start(bf16[4,4,128,128]{3,2,1,0:T(8,128)(2,1)} %get-tuple-element.50), channel_id=1, source_target_pairs={{0,1},{1,0},{2,3},{3,2},{4,5},{5,4},{6,7},{7,6},{8,9},{9,8},{10,11... | collective-permute-start | bytes 1572872 | tf_op jit(solution)/shard_map/ppermute | solution.py:277
  5.8 0.8 copy-start.7
  8.8 8.1 %collective-permute-start.1 = (bf16[2,4,128,128]{3,2,1,0:T(8,128)(2,1)}, bf16[2,4,128,128]{3,2,1,0:T(8,128)(2,1)S(1)}, u32[]{:S(2)}, u32[]{:S(2)}) collective-permute-start(bf16[2,4,128,128]{3,2,1,0:T(8,128)(2,1)} %get-tuple-element.37), channel_id=1, source_target_pairs={{0,2},{2,0},{4,6},{6,4},{8,10},{10,8},{12,14},{14,12},{16,18},{18,... | collective-permute-start | bytes 786440 | tf_op jit(solution)/shard_map/ppermute | solution.py:271
  10.1 8.7 %collective-permute-start.2 = (bf16[2,4,128,128]{3,2,1,0:T(8,128)(2,1)}, bf16[2,4,128,128]{3,2,1,0:T(8,128)(2,1)S(1)}, u32[]{:S(2)}, u32[]{:S(2)}) collective-permute-start(bf16[2,4,128,128]{3,2,1,0:T(8,128)(2,1)} %get-tuple-element.38), channel_id=1, source_target_pairs={{0,4},{2,6},{4,0},{6,2},{8,12},{10,14},{12,8},{14,10},{16,20},{18,... | collective-permute-start | bytes 786440 | tf_op jit(solution)/shard_map/ppermute | solution.py:271
  11.3 11.9 %collective-permute-start.3 = (bf16[2,4,128,128]{3,2,1,0:T(8,128)(2,1)}, bf16[2,4,128,128]{3,2,1,0:T(8,128)(2,1)S(1)}, u32[]{:S(2)}, u32[]{:S(2)}) collective-permute-start(bf16[2,4,128,128]{3,2,1,0:T(8,128)(2,1)} %get-tuple-element.39), channel_id=1, source_target_pairs={{0,6},{2,4},{4,2},{6,0},{8,14},{10,12},{12,10},{14,8},{16,22},{18,... | collective-permute-start | bytes 786440 | tf_op jit(solution)/shard_map/ppermute | solution.py:271
  11.5 0.8 copy-start.6
  14.5 18.9 %collective-permute-start.10 = (bf16[2,4,128,128]{3,2,1,0:T(8,128)(2,1)}, bf16[2,4,128,128]{3,2,1,0:T(8,128)(2,1)S(1)}, u32[]{:S(2)}, u32[]{:S(2)}) collective-permute-start(bf16[2,4,128,128]{3,2,1,0:T(8,128)(2,1)} %get-tuple-element.52), channel_id=1, source_target_pairs={{0,2},{2,0},{4,6},{6,4},{8,10},{10,8},{12,14},{14,12},{16,18},{18,... | collective-permute-start | bytes 786440 | tf_op jit(solution)/shard_map/ppermute | solution.py:271
  15.7 17.7 %collective-permute-start.11 = (bf16[2,4,128,128]{3,2,1,0:T(8,128)(2,1)}, bf16[2,4,128,128]{3,2,1,0:T(8,128)(2,1)S(1)}, u32[]{:S(2)}, u32[]{:S(2)}) collective-permute-start(bf16[2,4,128,128]{3,2,1,0:T(8,128)(2,1)} %get-tuple-element.53), channel_id=1, source_target_pairs={{0,4},{2,6},{4,0},{6,2},{8,12},{10,14},{12,8},{14,10},{16,20},{18,... | collective-permute-start | bytes 786440 | tf_op jit(solution)/shard_map/ppermute | solution.py:271
  16.9 6.3 %copy-start.13 = (bf16[2,4,128,128]{3,2,1,0:T(8,128)(2,1)}, bf16[2,4,128,128]{3,2,1,0:T(8,128)(2,1)S(1)}, u32[]{:S(2)}) copy-start(bf16[2,4,128,128]{3,2,1,0:T(8,128)(2,1)S(1)} %collective-permute-done.1.refs_1_) | copy-start | bytes 786436
  16.9 17.5 %collective-permute-start.12 = (bf16[2,4,128,128]{3,2,1,0:T(8,128)(2,1)}, bf16[2,4,128,128]{3,2,1,0:T(8,128)(2,1)S(1)}, u32[]{:S(2)}, u32[]{:S(2)}) collective-permute-start(bf16[2,4,128,128]{3,2,1,0:T(8,128)(2,1)} %get-tuple-element.54), channel_id=1, source_target_pairs={{0,6},{2,4},{4,2},{6,0},{8,14},{10,12},{12,10},{14,8},{16,22},{18,... | collective-permute-start | bytes 786440 | tf_op jit(solution)/shard_map/ppermute | solution.py:271
  18.8 4.5 %copy-start.14 = (bf16[2,4,128,128]{3,2,1,0:T(8,128)(2,1)}, bf16[2,4,128,128]{3,2,1,0:T(8,128)(2,1)S(1)}, u32[]{:S(2)}) copy-start(bf16[2,4,128,128]{3,2,1,0:T(8,128)(2,1)S(1)} %collective-permute-done.2.refs_2_) | copy-start | bytes 786436
  26.3 20.8 %collective-permute-start.4 = (bf16[4,256,128]{2,1,0:T(8,128)(2,1)}, bf16[4,256,128]{2,1,0:T(8,128)(2,1)S(1)}, u32[]{:S(2)}, u32[]{:S(2)}) collective-permute-start(bf16[4,256,128]{2,1,0:T(8,128)(2,1)} %get-tuple-element.41), channel_id=1, source_target_pairs={{0,8},{8,0},{2,10},{10,2},{4,12},{12,4},{6,14},{14,6},{16,24},{24,... | collective-permute-start | bytes 786440 | tf_op jit(solution)/shard_map/ppermute | solution.py:282
  26.5 20.7 %collective-permute-start.5 = (bf16[4,256,128]{2,1,0:T(8,128)(2,1)}, bf16[4,256,128]{2,1,0:T(8,128)(2,1)S(1)}, u32[]{:S(2)}, u32[]{:S(2)}) collective-permute-start(bf16[4,256,128]{2,1,0:T(8,128)(2,1)} %get-tuple-element.42), channel_id=1, source_target_pairs={{8,16},{16,8},{10,18},{18,10},{12,20},{20,12},{14,22},{22,14},{9,1... | collective-permute-start | bytes 786440 | tf_op jit(solution)/shard_map/ppermute | solution.py:283
  33.4 1.1 %copy-start.10 = (bf16[2,4,128,128]{3,2,1,0:T(8,128)(2,1)}, bf16[2,4,128,128]{3,2,1,0:T(8,128)(2,1)S(1)}, u32[]{:S(2)}) copy-start(bf16[2,4,128,128]{3,2,1,0:T(8,128)(2,1)S(1)} %collective-permute-done.10.refs_1_) | copy-start | bytes 786436
  33.4 1.1 %copy-start.11 = (bf16[2,4,128,128]{3,2,1,0:T(8,128)(2,1)}, bf16[2,4,128,128]{3,2,1,0:T(8,128)(2,1)S(1)}, u32[]{:S(2)}) copy-start(bf16[2,4,128,128]{3,2,1,0:T(8,128)(2,1)S(1)} %collective-permute-done.11.refs_2_) | copy-start | bytes 786436
  37.6 24.9 %collective-permute-start.13 = (bf16[4,256,128]{2,1,0:T(8,128)(2,1)}, bf16[4,256,128]{2,1,0:T(8,128)(2,1)S(1)}, u32[]{:S(2)}, u32[]{:S(2)}) collective-permute-start(bf16[4,256,128]{2,1,0:T(8,128)(2,1)} %get-tuple-element.56), channel_id=1, source_target_pairs={{0,8},{8,0},{2,10},{10,2},{4,12},{12,4},{6,14},{14,6},{16,24},{24,... | collective-permute-start | bytes 786440 | tf_op jit(solution)/shard_map/ppermute | solution.py:282
  37.8 24.8 %collective-permute-start.14 = (bf16[4,256,128]{2,1,0:T(8,128)(2,1)}, bf16[4,256,128]{2,1,0:T(8,128)(2,1)S(1)}, u32[]{:S(2)}, u32[]{:S(2)}) collective-permute-start(bf16[4,256,128]{2,1,0:T(8,128)(2,1)} %get-tuple-element.57), channel_id=1, source_target_pairs={{8,16},{16,8},{10,18},{18,10},{12,20},{20,12},{14,22},{22,14},{9,1... | collective-permute-start | bytes 786440 | tf_op jit(solution)/shard_map/ppermute | solution.py:283
  54.7 16.8 %collective-permute-start.6 = (bf16[2,4,128,128]{3,2,1,0:T(8,128)(2,1)}, bf16[2,4,128,128]{3,2,1,0:T(8,128)(2,1)S(1)}, u32[]{:S(2)}, u32[]{:S(2)}) collective-permute-start(bf16[2,4,128,128]{3,2,1,0:T(8,128)(2,1)} %get-tuple-element.46), channel_id=1, source_target_pairs={{0,2},{2,0},{4,6},{6,4},{8,10},{10,8},{12,14},{14,12},{16,18},{18,... | collective-permute-start | bytes 786440 | tf_op jit(solution)/shard_map/ppermute | solution.py:271
  55.9 5.1 %copy-start.22 = (bf16[2,4,128,128]{3,2,1,0:T(8,128)(2,1)S(1)}, bf16[2,4,128,128]{3,2,1,0:T(8,128)(2,1)}, u32[]{:S(2)}) copy-start(bf16[2,4,128,128]{3,2,1,0:T(8,128)(2,1)} %get-tuple-element.47) | copy-start | bytes 786436
  55.9 5.4 %copy-start.21 = (bf16[2,4,128,128]{3,2,1,0:T(8,128)(2,1)S(1)}, bf16[2,4,128,128]{3,2,1,0:T(8,128)(2,1)}, u32[]{:S(2)}) copy-start(bf16[2,4,128,128]{3,2,1,0:T(8,128)(2,1)} %get-tuple-element.48) | copy-start | bytes 786436
  61.0 12.6 %collective-permute-start.7 = (bf16[2,4,128,128]{3,2,1,0:T(8,128)(2,1)S(1)}, bf16[2,4,128,128]{3,2,1,0:T(8,128)(2,1)S(1)}, u32[]{:S(2)}, u32[]{:S(2)}) collective-permute-start(bf16[2,4,128,128]{3,2,1,0:T(8,128)(2,1)S(1)} %copy-done.22), channel_id=1, source_target_pairs={{0,4},{2,6},{4,0},{6,2},{8,12},{10,14},{12,8},{14,10},{16,20},{18,... | collective-permute-start | bytes 786440 | tf_op jit(solution)/shard_map/ppermute | solution.py:271
  61.3 12.3 %collective-permute-start.8 = (bf16[2,4,128,128]{3,2,1,0:T(8,128)(2,1)S(1)}, bf16[2,4,128,128]{3,2,1,0:T(8,128)(2,1)S(1)}, u32[]{:S(2)}, u32[]{:S(2)}) collective-permute-start(bf16[2,4,128,128]{3,2,1,0:T(8,128)(2,1)S(1)} %copy-done.21), channel_id=1, source_target_pairs={{0,6},{2,4},{4,2},{6,0},{8,14},{10,12},{12,10},{14,8},{16,22},{18,... | collective-permute-start | bytes 786440 | tf_op jit(solution)/shard_map/ppermute | solution.py:271
  70.1 9.2 %collective-permute-start.15 = (bf16[2,4,128,128]{3,2,1,0:T(8,128)(2,1)}, bf16[2,4,128,128]{3,2,1,0:T(8,128)(2,1)S(1)}, u32[]{:S(2)}, u32[]{:S(2)}) collective-permute-start(bf16[2,4,128,128]{3,2,1,0:T(8,128)(2,1)} %get-tuple-element.61), channel_id=1, source_target_pairs={{0,2},{2,0},{4,6},{6,4},{8,10},{10,8},{12,14},{14,12},{16,18},{18,... | collective-permute-start | bytes 786440 | tf_op jit(solution)/shard_map/ppermute | solution.py:271
  71.3 13.9 %collective-permute-start.16 = (bf16[2,4,128,128]{3,2,1,0:T(8,128)(2,1)}, bf16[2,4,128,128]{3,2,1,0:T(8,128)(2,1)S(1)}, u32[]{:S(2)}, u32[]{:S(2)}) collective-permute-start(bf16[2,4,128,128]{3,2,1,0:T(8,128)(2,1)} %get-tuple-element.62), channel_id=1, source_target_pairs={{0,4},{2,6},{4,0},{6,2},{8,12},{10,14},{12,8},{14,10},{16,20},{18,... | collective-permute-start | bytes 786440 | tf_op jit(solution)/shard_map/ppermute | solution.py:271
  71.6 2.1 %copy-start = (bf16[2,4,128,128]{3,2,1,0:T(8,128)(2,1)}, bf16[2,4,128,128]{3,2,1,0:T(8,128)(2,1)S(1)}, u32[]{:S(2)}) copy-start(bf16[2,4,128,128]{3,2,1,0:T(8,128)(2,1)S(1)} %collective-permute-done.6.refs_1_) | copy-start | bytes 786436
  71.6 13.6 %collective-permute-start.17 = (bf16[2,4,128,128]{3,2,1,0:T(8,128)(2,1)}, bf16[2,4,128,128]{3,2,1,0:T(8,128)(2,1)S(1)}, u32[]{:S(2)}, u32[]{:S(2)}) collective-permute-start(bf16[2,4,128,128]{3,2,1,0:T(8,128)(2,1)} %get-tuple-element.63), channel_id=1, source_target_pairs={{0,6},{2,4},{4,2},{6,0},{8,14},{10,12},{12,10},{14,8},{16,22},{18,... | collective-permute-start | bytes 786440 | tf_op jit(solution)/shard_map/ppermute | solution.py:271
  76.5 13.0 %collective-permute-start.18 = (bf16[4,4,128,128]{3,2,1,0:T(8,128)(2,1)}, bf16[4,4,128,128]{3,2,1,0:T(8,128)(2,1)S(1)}, u32[]{:S(2)}, u32[]{:S(2)}) collective-permute-start(bf16[4,4,128,128]{3,2,1,0:T(8,128)(2,1)} %shard_map.93), channel_id=1, source_target_pairs={{0,1},{1,0},{2,3},{3,2},{4,5},{5,4},{6,7},{7,6},{8,9},{9,8},{10,11... | collective-permute-start | bytes 1572872 | tf_op jit(solution)/shard_map/ppermute | solution.py:314
  79.3 5.9 %copy-start.3 = (bf16[2,4,128,128]{3,2,1,0:T(8,128)(2,1)}, bf16[2,4,128,128]{3,2,1,0:T(8,128)(2,1)S(1)}, u32[]{:S(2)}) copy-start(bf16[2,4,128,128]{3,2,1,0:T(8,128)(2,1)S(1)} %collective-permute-done.15.refs_1_.refs_5_) | copy-start | bytes 786436
  88.0 3.2 %collective-permute-start.19 = (bf16[4,4,128,128]{3,2,1,0:T(8,128)(2,1)}, bf16[4,4,128,128]{3,2,1,0:T(8,128)(2,1)S(1)}, u32[]{:S(2)}, u32[]{:S(2)}) collective-permute-start(bf16[4,4,128,128]{3,2,1,0:T(8,128)(2,1)} %shard_map.94), channel_id=1, source_target_pairs={{0,1},{1,0},{2,3},{3,2},{4,5},{5,4},{6,7},{7,6},{8,9},{9,8},{10,11... | collective-permute-start | bytes 1572872 | tf_op jit(solution)/shard_map/ppermute | solution.py:314
  89.4 1.7 %copy-start.8 = (bf16[4,4,128,128]{3,2,1,0:T(8,128)(2,1)}, bf16[4,4,128,128]{3,2,1,0:T(8,128)(2,1)S(1)}, u32[]{:S(2)}) copy-start(bf16[4,4,128,128]{3,2,1,0:T(8,128)(2,1)S(1)} %collective-permute-done.18.refs_8_) | copy-start | bytes 1572868
  91.2 0.8 copy-start.9
  (11 other events, 8.1 us)

commit v3 on v2

v3 whole, which is shorter than its diff:
```python
import functools
import math

import jax
import jax.numpy as jnp
from jax import lax
from jax.experimental import pallas as pl
from jax.experimental.pallas import tpu as pltpu
from jax.sharding import PartitionSpec as P

DH = 128
DOC_MOST = 256
MASKED = -1e30
GROUP = 4
WHOLE_IN = (False, False)
WHOLE_OUT = (False, False)
SCALE = 1.0 / math.sqrt(DH)
VMEM = 12 * 1024 * 1024
PACK_VMEM = 61 * 1024 * 1024 + 512 * 1024
WHOLE = pl.BlockSpec(memory_space=pltpu.VMEM)


def dot_nt(a, b):
    return lax.dot_general(a, b, (((1,), (1,)), ((), ())), preferred_element_type=jnp.float32)


def dot_tn(a, b):
    return lax.dot_general(a, b, (((0,), (0,)), ((), ())), preferred_element_type=jnp.float32)


def dot_nn(a, b):
    return lax.dot_general(a, b, (((1,), (0,)), ((), ())), preferred_element_type=jnp.float32)


def self_attention(queries, keys, values, grads, same):
    scores = dot_nt(keys, queries) * (SCALE * math.log2(math.e))
    scores = jnp.where(same, scores, jnp.float32(MASKED))
    top = jnp.max(scores, axis=0, keepdims=True)
    weights = jnp.exp2(scores - top)
    probs = weights * (1.0 / jnp.sum(weights, axis=0, keepdims=True))
    low = probs.astype(jnp.bfloat16)
    attended = dot_tn(values, low).astype(jnp.bfloat16).astype(jnp.float32)
    delta = jnp.sum(attended * grads.T.astype(jnp.float32), axis=0, keepdims=True)
    score_grad = (probs * (dot_nt(values, grads) - delta)).astype(jnp.bfloat16)
    query_grad = (dot_tn(keys, score_grad) * SCALE).T
    key_grad = dot_nn(score_grad, queries) * SCALE
    value_grad = dot_nn(low, grads)
    return attended.T, query_grad, key_grad, value_grad


def crossing(low_ids, high_ids, first, last):
    return low_ids == first, high_ids == last


def boundary_attention(low_rows, high_rows, ids_low, ids_high):
    (low_col, low_lane), (high_col, high_lane) = ids_low, ids_high
    first, last = high_col[0:1, :], low_col[-1:, :]
    from_low, from_high = low_col == first, high_col == last
    lane_low = low_lane == first
    lane_high = high_lane == last
    member_col = (from_low | from_high).astype(jnp.int32)
    member_lane = (lane_low | lane_high).astype(jnp.int32)
    chosen = [
        jnp.where(from_low, a.astype(jnp.float32), b.astype(jnp.float32)).astype(jnp.bfloat16)
        for a, b in zip(low_rows, high_rows)
    ]
    return self_attention(*chosen, member_col == member_lane), from_low, from_high


def interior_kernel(edge, ext_ref, row_ids_ref, col_ids_ref, res_ref):
    tiles = ext_ref.shape[1] // edge

    def rows_of(t):
        return [ext_ref[m, t * edge : (t + 1) * edge] for m in range(4)]

    def ids_of(t):
        at = slice((t + 1) * edge, (t + 2) * edge)
        return col_ids_ref[at, :], row_ids_ref[:, at]

    def put(t, chosen, results):
        at = slice(t * edge, (t + 1) * edge)
        for m, result in enumerate(results):
            if chosen is not None:
                result = jnp.where(chosen, result, res_ref[m, at].astype(jnp.float32))
            res_ref[m, at] = result.astype(jnp.bfloat16)

    for t in range(tiles):
        col, lane = ids_of(t)
        put(t, None, self_attention(*rows_of(t), col == lane))
        if t > 0:
            results, from_low, from_high = boundary_attention(
                rows_of(t - 1), rows_of(t), ids_of(t - 1), ids_of(t)
            )
            put(t - 1, from_low, results)
            put(t, from_high, results)


def edge_kernel(edge, whole, ext_ref, even_ref, odd_ref, res_ref, row_ids_ref, col_ids_ref, *refs):
    outs, result_ref = refs[:-1], refs[-1]
    rows = ext_ref.shape[1]
    position, core = lax.axis_index("blk"), lax.axis_index("head")
    place, parity = position % GROUP, (position // GROUP) % 2
    result_ref[...] = res_ref[...]

    def ids_at(first):
        return col_ids_ref[first : first + edge, :], row_ids_ref[:, first : first + edge]

    for side in range(2):
        from_even = parity == (1 - side)
        halo = [jnp.where(from_even, even_ref[m], odd_ref[m]) for m in range(4)]
        own = slice(0, edge) if side == 0 else slice(rows - edge, rows)
        mine = [ext_ref[m, own] for m in range(4)]
        if side == 0:
            results, _, chosen = boundary_attention(halo, mine, ids_at(0), ids_at(edge))
        else:
            results, chosen, _ = boundary_attention(mine, halo, ids_at(rows), ids_at(rows + edge))
        for m, result in enumerate(results):
            result = jnp.where(chosen, result, result_ref[m, own].astype(jnp.float32))
            result_ref[m, own] = result.astype(jnp.bfloat16)
    half = edge // 2
    if whole:
        for i in range(2 * GROUP):
            outs[0][i] = result_ref[:, i * half : (i + 1) * half]
        return
    for s in range(GROUP):
        for piece in range(2):
            first = pl.multiple_of(((place ^ s) * 2 + (core ^ piece)) * half, half)
            outs[s][piece] = result_ref[:, pl.ds(first, half), :]


def shape(*dims, dtype=jnp.bfloat16):
    return jax.ShapeDtypeStruct(dims, dtype)


def call(kernel, out_shape, *args, scratch=(), flops=0, exps=0):
    return pl.pallas_call(
        kernel,
        out_shape=out_shape,
        in_specs=[WHOLE] * len(args),
        out_specs=jax.tree.map(lambda _: WHOLE, out_shape),
        scratch_shapes=scratch,
        compiler_params=pltpu.CompilerParams(vmem_limit_bytes=VMEM),
        cost_estimate=pl.CostEstimate(flops=1, bytes_accessed=1, transcendentals=0),
    )(*args)


def pack_kernel(wholes, *refs):
    ins, outs = refs[:4], list(refs[4:])
    width = ins[0].shape[1]
    chunks = len(wholes)
    core, place = lax.axis_index("head"), lax.axis_index("blk") % GROUP
    for j, whole in enumerate(wholes):
        if whole:
            out = outs.pop(0)
            for i in range(2 * GROUP):
                first = (i % 2) * (width // 2) + ((i // 2) * chunks + j) * DH
                for m, ref in enumerate(ins):
                    out[i, m] = ref[:, first : first + DH]
            continue
        for which in range(2):
            out = outs.pop(0)
            for s in range(GROUP):
                base = (core ^ which) * (width // 2) + ((place ^ s) * chunks + j) * DH
                first = pl.multiple_of(base, DH)
                for m, ref in enumerate(ins):
                    out[s, m] = ref[:, pl.ds(first, DH)]


def pack(arrays, wholes):
    rows, width = arrays[0].shape
    steps = 2
    block = rows // steps
    sizes = []
    for whole in wholes:
        sizes += [2 * GROUP] if whole else [GROUP, GROUP]
    got = list(
        pl.pallas_call(
            functools.partial(pack_kernel, wholes),
            grid=(steps,),
            out_shape=[shape(n, 4, rows, DH) for n in sizes],
            in_specs=[pl.BlockSpec((block, width), lambda i: (i, 0))] * 4,
            out_specs=[pl.BlockSpec((n, 4, block, DH), lambda i: (0, 0, i, 0)) for n in sizes],
            compiler_params=pltpu.CompilerParams(vmem_limit_bytes=PACK_VMEM),
        )(*arrays)
    )
    return [[got.pop(0) for _ in range(1 if whole else 2)] for whole in wholes]


def join_kernel(mine_ref, received_ref, *outs):
    for s, out in enumerate(outs):
        out[0] = mine_ref[s]
        out[1] = received_ref[s]


def gather_kernel(whole, *refs):
    slots, (ext, to_even, to_odd) = refs[:-3], refs[-3:]
    edge = to_even.shape[1]
    half = edge // 2
    position, core = lax.axis_index("blk"), lax.axis_index("head")
    place, parity = position % GROUP, (position // GROUP) % 2
    for i in range(2 * GROUP if whole else 0):
        ext[:, i * half : (i + 1) * half] = slots[0][i]
    for s in range(0 if whole else GROUP):
        for piece in range(2):
            first = pl.multiple_of(((place ^ s) * 2 + (core ^ piece)) * half, half)
            ext[:, pl.ds(first, half), :] = slots[s][piece]
    rows = ext.shape[1]
    first = pl.multiple_of((rows - edge) * (1 - parity), edge)
    to_even[...] = ext[:, pl.ds(first, edge), :]
    first = pl.multiple_of((rows - edge) * parity, edge)
    to_odd[...] = ext[:, pl.ds(first, edge), :]


def split_kernel(*refs):
    slots, out = refs[:-1], refs[-1]
    for s, slot in enumerate(slots):
        out[s] = slot[1]


def unpack_kernel(wholes, *refs):
    ins, outs = list(refs[:-4]), refs[-4:]
    width = outs[0].shape[1]
    chunks = len(wholes)
    core, place = lax.axis_index("head"), lax.axis_index("blk") % GROUP
    for j, whole in enumerate(wholes):
        if whole:
            block = ins.pop(0)
            for i in range(2 * GROUP):
                first = (i % 2) * (width // 2) + ((i // 2) * chunks + j) * DH
                for m, out in enumerate(outs):
                    out[:, first : first + DH] = block[i, m]
            continue
        slots = [ins.pop(0) for _ in range(GROUP)]
        received = ins.pop(0)
        for s in range(GROUP):
            for which in range(2):
                base = (core ^ which) * (width // 2) + ((place ^ s) * chunks + j) * DH
                first = pl.multiple_of(base, DH)
                for m, out in enumerate(outs):
                    out[:, pl.ds(first, DH)] = slots[s][0, m] if which == 0 else received[s, m]


def unpack(chunks, wholes, rows, width):
    blocks = [block for chunk in chunks for block in chunk]
    return call(functools.partial(unpack_kernel, wholes), [shape(rows, width)] * 4, *blocks)


def body(query_rows, key_rows, value_rows, out_grad, doc_ids):
    positions = lax.axis_size("blk")
    half, width = query_rows.shape
    heads = width // DH
    chunks = heads // (2 * GROUP)
    edge = 2 * half
    rows = GROUP * edge
    assert edge >= DOC_MOST and positions % GROUP == 0 and chunks == len(WHOLE_IN)
    swap = [(0, 1), (1, 0)]
    planes = positions // GROUP

    def plane_pairs(first):
        route = []
        for low in range(first, planes - 1, 2):
            for i in range(GROUP):
                here, there = low * GROUP + i, (low + 1) * GROUP + i
                route += [(here, there), (there, here)]
        return route

    def hop(block, s):
        return lax.ppermute(block, "blk", [(i, i ^ s) for i in range(positions)]) if s else block

    def all_to_all(block):
        size = 2 * GROUP
        groups = [[p * size + i for i in range(size)] for p in range(planes)]
        return lax.all_to_all(
            block, ("blk", "head"), split_axis=0, concat_axis=0, axis_index_groups=groups
        )

    plane = lax.axis_index("blk") // GROUP
    padded = jnp.pad(doc_ids, (edge, edge), constant_values=-1)
    ids = lax.dynamic_slice_in_dim(padded, plane * rows, rows + 2 * edge, 0)
    row_ids, col_ids = ids[None, :], ids[:, None]
    inputs = (query_rows, key_rows, value_rows, out_grad)
    unit = 2 * DH * edge * edge * 6

    packed = pack(inputs, WHOLE_IN)
    arrived = []
    for whole, parts in zip(WHOLE_IN, packed):
        if whole:
            arrived.append([all_to_all(parts[0])])
        else:
            theirs = lax.ppermute(parts[1], "head", swap)
            joined = call(join_kernel, [shape(2, 4, half, DH)] * GROUP, parts[0], theirs)
            arrived.append([hop(block, s) for s, block in enumerate(joined)])

    results = []
    previous = None
    for j in range(chunks):
        whole_in, whole_out = WHOLE_IN[j], WHOLE_OUT[j]
        slots = arrived[j]
        if previous is not None:
            slots, _ = lax.optimization_barrier((slots, previous))
        ext, to_even, to_odd = call(
            functools.partial(gather_kernel, whole_in),
            [shape(4, rows, DH), shape(4, edge, DH), shape(4, edge, DH)],
            *slots,
        )
        even = lax.ppermute(to_even, "blk", plane_pairs(0))
        odd = lax.ppermute(to_odd, "blk", plane_pairs(1))
        res = call(
            functools.partial(interior_kernel, edge),
            shape(4, rows, DH),
            ext,
            row_ids,
            col_ids,
            flops=unit * 7,
            exps=7 * edge * edge,
        )
        back = call(
            functools.partial(edge_kernel, edge, whole_out),
            [shape(2 * GROUP, 4, half, DH)] if whole_out else [shape(2, 4, half, DH)] * GROUP,
            ext,
            even,
            odd,
            res,
            row_ids,
            col_ids,
            scratch=[pltpu.VMEM((4, rows, DH), jnp.bfloat16)],
            flops=unit * 2,
            exps=2 * edge * edge,
        )
        previous = back
        if whole_out:
            back = [all_to_all(back[0])]
        else:
            back = [hop(block, s) for s, block in enumerate(back)]
            away = call(split_kernel, shape(GROUP, 4, half, DH), *back)
            back.append(lax.ppermute(away, "head", swap))
        results.append(back)
    return tuple(unpack(results, WHOLE_OUT, half, width))


def solution(mesh):
    placed = P(("blk", "head"), None)
    return jax.shard_map(
        body,
        mesh=mesh,
        in_specs=(placed, placed, placed, placed, P()),
        out_specs=(placed,) * 4,
        check_vma=False,
    )
```

time: 95.4 us -> 73.4 us (0.77); the launches traced: 95 us -> 71.9 us
  Pallas kernels: 42.8 us -> 18.4 us
  waiting for transfers between devices: 15.8 us -> 24.6 us
  local copies, waits for them, and re-layouts: 9.48 us -> 2.1 us
    pallas_call x10 -> x11, Pallas kernels: 37 us -> 15.6 us  [call(): pl.pallas_call(kernel, out_shape=out_shape, in_specs=[WHOLE] * len(args),...]
    ppermute x16, waiting for transfers between devices: 15.8 us -> 24.6 us  [the longest x12 21.4 us: hop(): lax.ppermute(block, 'blk', [(i, i ^ s) for i in range(positions)])]
    unnamed x46 -> x6, local copies, waits for them, and re-layouts: 7.65 us -> 1.76 us
    pallas_call x2 -> x1, Pallas kernels: 5.74 us -> 2.78 us  [pack(): pl.pallas_call(functools.partial(pack_kernel, wholes), grid=(steps,), out...]
    ppermute x16, starting transfers between devices: 17.2 us -> 19.4 us  [the longest x12 11.8 us: hop(): lax.ppermute(block, 'blk', [(i, i ^ s) for i in range(positions)])]
    ppermute x2, starting transfers between devices: 8.64 us -> 6.42 us  [body(): odd = lax.ppermute(to_odd, 'blk', plane_pairs(1))]
    broadcast_in_dim x2, local copies, waits for them, and re-layouts: 1.75 us -> 0.26 us  [body(): row_ids, col_ids = (ids[None, :], ids[:, None])]
  transfers between devices with their start and end apart: 20 -> 20, of which waited for: 6 -> 9; matrix products, arithmetic and copies ran while one was open for 2% -> 0% of each run, Pallas kernels for 39% -> 19%
where the time goes in v3:
time: 73.4 us; the launch traced here: 71.9 us
  starting transfers between devices  26.1 us (36%)
  waiting for transfers between devices  24.6 us (34%)
  Pallas kernels  18.4 us (25%)
  local copies, waits for them, and re-layouts  2.1 us (3%)
  between operations  0.77 us (1%)
    ppermute x12, waiting for transfers between devices, hop(): lax.ppermute(block, 'blk', [(i, i ^ s) for i in range(positions)])  21.4 us
    pallas_call x11, Pallas kernels, call(): pl.pallas_call(kernel, out_shape=out_shape, in_specs=[WHOLE] * len(args),...  15.6 us
    ppermute x12, starting transfers between devices, hop(): lax.ppermute(block, 'blk', [(i, i ^ s) for i in range(positions)])  11.8 us
    ppermute x2, starting transfers between devices, body(): back.append(lax.ppermute(away, 'head', swap))  6.83 us
    ppermute x2, starting transfers between devices, body(): odd = lax.ppermute(to_odd, 'blk', plane_pairs(1))  6.42 us
    pallas_call x1, Pallas kernels, pack(): pl.pallas_call(functools.partial(pack_kernel, wholes), grid=(steps,), out...  2.78 us
    unnamed x6, local copies, waits for them, and re-layouts  1.76 us
    ppermute x2, waiting for transfers between devices, body(): theirs = lax.ppermute(parts[1], 'head', swap)  1.68 us
  transfers between devices with their start and end apart: 20, of which 9 were waited for; matrix products, arithmetic and copies ran while one was open for 0% of the time, Pallas kernels for 19%

profile of v3, /device:TPU:9, one launch (start us, length us, event | category | flops | bytes accessed | tf_op | source)
XLA Modules:
  0.0 71.9 jit_solution(15749348660537286049)
XLA Ops:
  0.6 2.8 %shard_map.84 = (bf16[4,4,128,128]{3,2,1,0:T(8,128)(2,1)}, bf16[4,4,128,128]{3,2,1,0:T(8,128)(2,1)}, bf16[4,4,128,128]{3,2,1,0:T(8,128)(2,1)}, bf16[4,4,128,128]{3,2,1,0:T(8,128)(2,1)}) custom-call(bf16[128,2048]{1,0:T(8,128)(2,1)} %refs_0_.1, bf16[128,2048]{1,0:T(8,128)(2,1)} %refs_1_.1, bf16[128,2048]{1,0:T(8,128)(2,1)} %refs_2_.1, bf16[128,2048]{1,0:T(8,128)(2,1)} %refs_3_.1), custom_call_target="tpu_custom_call" | custom-call | tf_op jit(solution)/shard_map/pallas_call | solution.py:177
  3.4 0.7 collective-permute-start
  4.2 1.7 %collective-permute-done.received_ref = bf16[4,4,128,128]{3,2,1,0:T(8,128)(2,1)S(1)} collective-permute-done((bf16[4,4,128,128]{3,2,1,0:T(8,128)(2,1)}, bf16[4,4,128,128]{3,2,1,0:T(8,128)(2,1)S(1)}, u32[]{:S(2)}, u32[]{:S(2)}) %collective-permute-start) | collective-permute-done | bytes 524320 | tf_op jit(solution)/shard_map/ppermute | solution.py:290
  5.8 1.0 %copy-done.1 = bf16[4,4,128,128]{3,2,1,0:T(8,128)(2,1)S(1)} copy-done((bf16[4,4,128,128]{3,2,1,0:T(8,128)(2,1)S(1)}, bf16[4,4,128,128]{3,2,1,0:T(8,128)(2,1)}, u32[]{:S(2)}) %copy-start.1) | copy-done | bytes 524312
  7.0 1.3 %collective-permute-start.1 = (bf16[2,4,128,128]{3,2,1,0:T(8,128)(2,1)S(1)}, bf16[2,4,128,128]{3,2,1,0:T(8,128)(2,1)S(1)}, u32[]{:S(2)}, u32[]{:S(2)}) collective-permute-start(bf16[2,4,128,128]{3,2,1,0:T(8,128)(2,1)S(1)} %get-tuple-element.37), channel_id=1, source_target_pairs={{0,2},{2,0},{4,6},{6,4},{8,10},{10,8},{12,14},{14,12},{16,18},{18,... | collective-permute-start | bytes 786440 | tf_op jit(solution)/shard_map/ppermute | solution.py:268
  8.2 1.2 %collective-permute-start.2 = (bf16[2,4,128,128]{3,2,1,0:T(8,128)(2,1)S(1)}, bf16[2,4,128,128]{3,2,1,0:T(8,128)(2,1)S(1)}, u32[]{:S(2)}, u32[]{:S(2)}) collective-permute-start(bf16[2,4,128,128]{3,2,1,0:T(8,128)(2,1)S(1)} %get-tuple-element.38), channel_id=1, source_target_pairs={{0,4},{2,6},{4,0},{6,2},{8,12},{10,14},{12,8},{14,10},{16,20},{18,... | collective-permute-start | bytes 786440 | tf_op jit(solution)/shard_map/ppermute | solution.py:268
  9.7 1.3 %collective-permute-start.11 = (bf16[2,4,128,128]{3,2,1,0:T(8,128)(2,1)S(1)}, bf16[2,4,128,128]{3,2,1,0:T(8,128)(2,1)S(1)}, u32[]{:S(2)}, u32[]{:S(2)}) collective-permute-start(bf16[2,4,128,128]{3,2,1,0:T(8,128)(2,1)S(1)} %get-tuple-element.50), channel_id=1, source_target_pairs={{0,2},{2,0},{4,6},{6,4},{8,10},{10,8},{12,14},{14,12},{16,18},{18,... | collective-permute-start | bytes 786440 | tf_op jit(solution)/shard_map/ppermute | solution.py:268
  11.0 3.5 %collective-permute-done.1.refs_1_ = bf16[2,4,128,128]{3,2,1,0:T(8,128)(2,1)S(1)} collective-permute-done((bf16[2,4,128,128]{3,2,1,0:T(8,128)(2,1)S(1)}, bf16[2,4,128,128]{3,2,1,0:T(8,128)(2,1)S(1)}, u32[]{:S(2)}, u32[]{:S(2)}) %collective-permute-start.1) | collective-permute-done | bytes 262176 | tf_op jit(solution)/shard_map/ppermute | solution.py:268
  14.5 0.9 %collective-permute-done.2.refs_2_ = bf16[2,4,128,128]{3,2,1,0:T(8,128)(2,1)S(1)} collective-permute-done((bf16[2,4,128,128]{3,2,1,0:T(8,128)(2,1)S(1)}, bf16[2,4,128,128]{3,2,1,0:T(8,128)(2,1)S(1)}, u32[]{:S(2)}, u32[]{:S(2)}) %collective-permute-start.2) | collective-permute-done | bytes 262176 | tf_op jit(solution)/shard_map/ppermute | solution.py:268
  15.4 5.7 %collective-permute-done.3.refs_3_ = bf16[2,4,128,128]{3,2,1,0:T(8,128)(2,1)S(1)} collective-permute-done((bf16[2,4,128,128]{3,2,1,0:T(8,128)(2,1)S(1)}, bf16[2,4,128,128]{3,2,1,0:T(8,128)(2,1)S(1)}, u32[]{:S(2)}, u32[]{:S(2)}) %collective-permute-start.3) | collective-permute-done | bytes 262176 | tf_op jit(solution)/shard_map/ppermute | solution.py:268
  21.2 0.9 %shard_map.86 = (bf16[4,1024,128]{2,1,0:T(8,128)(2,1)S(1)}, bf16[4,256,128]{2,1,0:T(8,128)(2,1)}, bf16[4,256,128]{2,1,0:T(8,128)(2,1)}) custom-call(bf16[2,4,128,128]{3,2,1,0:T(8,128)(2,1)S(1)} %get-tuple-element.36.refs_0_, bf16[2,4,128,128]{3,2,1,0:T(8,128)(2,1)S(1)} %collective-permute-done.1.refs_1_, ...), custom_call_target="tpu_custom_call" | custom-call | flops 1 | bytes 1 | tf_op jit(solution)/shard_map/pallas_call | solution.py:136
  22.2 4.3 %collective-permute-start.5 = (bf16[4,256,128]{2,1,0:T(8,128)(2,1)}, bf16[4,256,128]{2,1,0:T(8,128)(2,1)S(1)}, u32[]{:S(2)}, u32[]{:S(2)}) collective-permute-start(bf16[4,256,128]{2,1,0:T(8,128)(2,1)} %get-tuple-element.42), channel_id=1, source_target_pairs={{8,16},{16,8},{10,18},{18,10},{12,20},{20,12},{14,22},{22,14},{9,1... | collective-permute-start | bytes 786440 | tf_op jit(solution)/shard_map/ppermute | solution.py:307
  26.6 0.5 collective-permute-start.12
  27.0 1.9 %collective-permute-start.13 = (bf16[2,4,128,128]{3,2,1,0:T(8,128)(2,1)S(1)}, bf16[2,4,128,128]{3,2,1,0:T(8,128)(2,1)S(1)}, u32[]{:S(2)}, u32[]{:S(2)}) collective-permute-start(bf16[2,4,128,128]{3,2,1,0:T(8,128)(2,1)S(1)} %get-tuple-element.52), channel_id=1, source_target_pairs={{0,6},{2,4},{4,2},{6,0},{8,14},{10,12},{12,10},{14,8},{16,22},{18,... | collective-permute-start | bytes 786440 | tf_op jit(solution)/shard_map/ppermute | solution.py:268
  29.0 0.7 copy-done.2
  29.8 0.3 broadcast_in_dim.8.col_ids_ref
  30.1 4.6 %shard_map.87.res_ref = bf16[4,1024,128]{2,1,0:T(8,128)(2,1)S(1)} custom-call(bf16[4,1024,128]{2,1,0:T(8,128)(2,1)S(1)} %get-tuple-element.40.ext_ref, s32[1,1536]{1,0:T(1,128)S(1)} %broadcast_in_dim.6.row_ids_ref, s32[1536,1]{1,0:T(8,128)S(1)} %broadcast_in_dim.8.col_ids_ref), custom_call_target="tpu_custom_call" | custom-call | flops 1 | bytes 1 | tf_op jit(solution)/shard_map/pallas_call | solution.py:136
  34.7 1.6 %shard_map.88 = (bf16[2,4,128,128]{3,2,1,0:T(8,128)(2,1)S(1)}, bf16[2,4,128,128]{3,2,1,0:T(8,128)(2,1)S(1)}, bf16[2,4,128,128]{3,2,1,0:T(8,128)(2,1)S(1)}, bf16[2,4,128,128]{3,2,1,0:T(8,128)(2,1)S(1)}) custom-call(bf16[4,1024,128]{2,1,0:T(8,128)(2,1)S(1)} %get-tuple-element.40.ext_ref, bf16[4,256,128]{2,1,0:T(8,128)(2,1)S(1)} %collective-permute-done.4.even_ref, ...), custom_call_target="tpu_custom_call" | custom-call | flops 1 | bytes 1 | tf_op jit(solution)/shard_map/pallas_call | solution.py:136
  36.3 2.8 %collective-permute-done.12.refs_2_ = bf16[2,4,128,128]{3,2,1,0:T(8,128)(2,1)S(1)} collective-permute-done((bf16[2,4,128,128]{3,2,1,0:T(8,128)(2,1)S(1)}, bf16[2,4,128,128]{3,2,1,0:T(8,128)(2,1)S(1)}, u32[]{:S(2)}, u32[]{:S(2)}) %collective-permute-start.12) | collective-permute-done | bytes 262176 | tf_op jit(solution)/shard_map/ppermute | solution.py:268
  39.3 2.1 %collective-permute-start.15 = (bf16[4,256,128]{2,1,0:T(8,128)(2,1)S(1)}, bf16[4,256,128]{2,1,0:T(8,128)(2,1)S(1)}, u32[]{:S(2)}, u32[]{:S(2)}) collective-permute-start(bf16[4,256,128]{2,1,0:T(8,128)(2,1)S(1)} %get-tuple-element.59), channel_id=1, source_target_pairs={{8,16},{16,8},{10,18},{18,10},{12,20},{20,12},{14,22},{22,14},{9,1... | collective-permute-start | bytes 786440 | tf_op jit(solution)/shard_map/ppermute | solution.py:307
  41.4 1.4 %collective-permute-start.6 = (bf16[2,4,128,128]{3,2,1,0:T(8,128)(2,1)S(1)}, bf16[2,4,128,128]{3,2,1,0:T(8,128)(2,1)S(1)}, u32[]{:S(2)}, u32[]{:S(2)}) collective-permute-start(bf16[2,4,128,128]{3,2,1,0:T(8,128)(2,1)S(1)} %get-tuple-element.44), channel_id=1, source_target_pairs={{0,2},{2,0},{4,6},{6,4},{8,10},{10,8},{12,14},{14,12},{16,18},{18,... | collective-permute-start | bytes 786440 | tf_op jit(solution)/shard_map/ppermute | solution.py:268
  42.8 1.3 %collective-permute-start.8 = (bf16[2,4,128,128]{3,2,1,0:T(8,128)(2,1)S(1)}, bf16[2,4,128,128]{3,2,1,0:T(8,128)(2,1)S(1)}, u32[]{:S(2)}, u32[]{:S(2)}) collective-permute-start(bf16[2,4,128,128]{3,2,1,0:T(8,128)(2,1)S(1)} %get-tuple-element.46), channel_id=1, source_target_pairs={{0,6},{2,4},{4,2},{6,0},{8,14},{10,12},{12,10},{14,8},{16,22},{18,... | collective-permute-start | bytes 786440 | tf_op jit(solution)/shard_map/ppermute | solution.py:268
  44.1 4.6 %shard_map.92.res_ref = bf16[4,1024,128]{2,1,0:T(8,128)(2,1)S(1)} custom-call(bf16[4,1024,128]{2,1,0:T(8,128)(2,1)S(1)} %get-tuple-element.57.ext_ref, s32[1,1536]{1,0:T(1,128)S(1)} %broadcast_in_dim.6.row_ids_ref, s32[1536,1]{1,0:T(8,128)S(1)} %broadcast_in_dim.8.col_ids_ref), custom_call_target="tpu_custom_call" | custom-call | flops 1 | bytes 1 | tf_op jit(solution)/shard_map/pallas_call | solution.py:136
  48.8 1.6 %shard_map.93 = (bf16[2,4,128,128]{3,2,1,0:T(8,128)(2,1)S(1)}, bf16[2,4,128,128]{3,2,1,0:T(8,128)(2,1)S(1)}, bf16[2,4,128,128]{3,2,1,0:T(8,128)(2,1)S(1)}, bf16[2,4,128,128]{3,2,1,0:T(8,128)(2,1)S(1)}) custom-call(bf16[4,1024,128]{2,1,0:T(8,128)(2,1)S(1)} %get-tuple-element.57.ext_ref, bf16[4,256,128]{2,1,0:T(8,128)(2,1)S(1)} %collective-permute-done.14.even_ref, ...), custom_call_target="tpu_custom_call" | custom-call | flops 1 | bytes 1 | tf_op jit(solution)/shard_map/pallas_call | solution.py:136
  50.4 1.4 %collective-permute-start.16 = (bf16[2,4,128,128]{3,2,1,0:T(8,128)(2,1)S(1)}, bf16[2,4,128,128]{3,2,1,0:T(8,128)(2,1)S(1)}, u32[]{:S(2)}, u32[]{:S(2)}) collective-permute-start(bf16[2,4,128,128]{3,2,1,0:T(8,128)(2,1)S(1)} %get-tuple-element.61), channel_id=1, source_target_pairs={{0,2},{2,0},{4,6},{6,4},{8,10},{10,8},{12,14},{14,12},{16,18},{18,... | collective-permute-start | bytes 786440 | tf_op jit(solution)/shard_map/ppermute | solution.py:268
  51.8 1.3 %collective-permute-start.18 = (bf16[2,4,128,128]{3,2,1,0:T(8,128)(2,1)S(1)}, bf16[2,4,128,128]{3,2,1,0:T(8,128)(2,1)S(1)}, u32[]{:S(2)}, u32[]{:S(2)}) collective-permute-start(bf16[2,4,128,128]{3,2,1,0:T(8,128)(2,1)S(1)} %get-tuple-element.63), channel_id=1, source_target_pairs={{0,6},{2,4},{4,2},{6,0},{8,14},{10,12},{12,10},{14,8},{16,22},{18,... | collective-permute-start | bytes 786440 | tf_op jit(solution)/shard_map/ppermute | solution.py:268
  53.3 5.0 %collective-permute-start.9 = (bf16[4,4,128,128]{3,2,1,0:T(8,128)(2,1)S(1)}, bf16[4,4,128,128]{3,2,1,0:T(8,128)(2,1)S(1)}, u32[]{:S(2)}, u32[]{:S(2)}) collective-permute-start(bf16[4,4,128,128]{3,2,1,0:T(8,128)(2,1)S(1)} %shard_map.89), channel_id=1, source_target_pairs={{0,1},{1,0},{2,3},{3,2},{4,5},{5,4},{6,7},{7,6},{8,9},{9,8},{10,11... | collective-permute-start | bytes 1572872 | tf_op jit(solution)/shard_map/ppermute | solution.py:336
  58.2 0.6 collective-permute-done.16.refs_1_.refs_6_
  58.8 7.7 %collective-permute-done.17.refs_2_.refs_7_ = bf16[2,4,128,128]{3,2,1,0:T(8,128)(2,1)S(1)} collective-permute-done((bf16[2,4,128,128]{3,2,1,0:T(8,128)(2,1)S(1)}, bf16[2,4,128,128]{3,2,1,0:T(8,128)(2,1)S(1)}, u32[]{:S(2)}, u32[]{:S(2)}) %collective-permute-start.17) | collective-permute-done | bytes 262176 | tf_op jit(solution)/shard_map/ppermute | solution.py:268
  66.6 1.9 %collective-permute-start.19 = (bf16[4,4,128,128]{3,2,1,0:T(8,128)(2,1)S(1)}, bf16[4,4,128,128]{3,2,1,0:T(8,128)(2,1)S(1)}, u32[]{:S(2)}, u32[]{:S(2)}) collective-permute-start(bf16[4,4,128,128]{3,2,1,0:T(8,128)(2,1)S(1)} %shard_map.94), channel_id=1, source_target_pairs={{0,1},{1,0},{2,3},{3,2},{4,5},{5,4},{6,7},{7,6},{8,9},{9,8},{10,11... | collective-permute-start | bytes 1572872 | tf_op jit(solution)/shard_map/ppermute | solution.py:336
  68.5 1.5 %collective-permute-done.19.refs_9_ = bf16[4,4,128,128]{3,2,1,0:T(8,128)(2,1)S(1)} collective-permute-done((bf16[4,4,128,128]{3,2,1,0:T(8,128)(2,1)S(1)}, bf16[4,4,128,128]{3,2,1,0:T(8,128)(2,1)S(1)}, u32[]{:S(2)}, u32[]{:S(2)}) %collective-permute-start.19) | collective-permute-done | bytes 524320 | tf_op jit(solution)/shard_map/ppermute | solution.py:336
  70.0 1.9 %shard_map.95 = (bf16[128,2048]{1,0:T(8,128)(2,1)}, bf16[128,2048]{1,0:T(8,128)(2,1)}, bf16[128,2048]{1,0:T(8,128)(2,1)}, bf16[128,2048]{1,0:T(8,128)(2,1)}) custom-call(bf16[2,4,128,128]{3,2,1,0:T(8,128)(2,1)S(1)} %get-tuple-element.43.refs_0_, bf16[2,4,128,128]{3,2,1,0:T(8,128)(2,1)S(1)} %collective-permute-done.6.refs_1_, ...), custom_call_target="tpu_custom_call" | custom-call | flops 1 | bytes 1 | tf_op jit(solution)/shard_map/pallas_call | solution.py:136
  (29 shorter events, 1.1 us)
Async XLA Ops:
  3.4 2.4 %collective-permute-start = (bf16[4,4,128,128]{3,2,1,0:T(8,128)(2,1)}, bf16[4,4,128,128]{3,2,1,0:T(8,128)(2,1)S(1)}, u32[]{:S(2)}, u32[]{:S(2)}) collective-permute-start(bf16[4,4,128,128]{3,2,1,0:T(8,128)(2,1)} %get-tuple-element.35), channel_id=1, source_target_pairs={{0,1},{1,0},{2,3},{3,2},{4,5},{5,4},{6,7},{7,6},{8,9},{9,8},{10,11... | collective-permute-start | bytes 1572872 | tf_op jit(solution)/shard_map/ppermute | solution.py:290
  4.1 5.6 %collective-permute-start.10 = (bf16[4,4,128,128]{3,2,1,0:T(8,128)(2,1)}, bf16[4,4,128,128]{3,2,1,0:T(8,128)(2,1)S(1)}, u32[]{:S(2)}, u32[]{:S(2)}) collective-permute-start(bf16[4,4,128,128]{3,2,1,0:T(8,128)(2,1)} %get-tuple-element.48), channel_id=1, source_target_pairs={{0,1},{1,0},{2,3},{3,2},{4,5},{5,4},{6,7},{7,6},{8,9},{9,8},{10,11... | collective-permute-start | bytes 1572872 | tf_op jit(solution)/shard_map/ppermute | solution.py:290
  5.8 1.0 %copy-start.1 = (bf16[4,4,128,128]{3,2,1,0:T(8,128)(2,1)S(1)}, bf16[4,4,128,128]{3,2,1,0:T(8,128)(2,1)}, u32[]{:S(2)}) copy-start(bf16[4,4,128,128]{3,2,1,0:T(8,128)(2,1)} %get-tuple-element.34.mine_ref) | copy-start | bytes 1572868
  6.9 2.8 %copy-start = (bf16[4,4,128,128]{3,2,1,0:T(8,128)(2,1)S(1)}, bf16[4,4,128,128]{3,2,1,0:T(8,128)(2,1)}, u32[]{:S(2)}) copy-start(bf16[4,4,128,128]{3,2,1,0:T(8,128)(2,1)} %get-tuple-element.47.mine_ref) | copy-start | bytes 1572868
  7.0 7.6 %collective-permute-start.1 = (bf16[2,4,128,128]{3,2,1,0:T(8,128)(2,1)S(1)}, bf16[2,4,128,128]{3,2,1,0:T(8,128)(2,1)S(1)}, u32[]{:S(2)}, u32[]{:S(2)}) collective-permute-start(bf16[2,4,128,128]{3,2,1,0:T(8,128)(2,1)S(1)} %get-tuple-element.37), channel_id=1, source_target_pairs={{0,2},{2,0},{4,6},{6,4},{8,10},{10,8},{12,14},{14,12},{16,18},{18,... | collective-permute-start | bytes 786440 | tf_op jit(solution)/shard_map/ppermute | solution.py:268
  8.2 7.2 %collective-permute-start.2 = (bf16[2,4,128,128]{3,2,1,0:T(8,128)(2,1)S(1)}, bf16[2,4,128,128]{3,2,1,0:T(8,128)(2,1)S(1)}, u32[]{:S(2)}, u32[]{:S(2)}) collective-permute-start(bf16[2,4,128,128]{3,2,1,0:T(8,128)(2,1)S(1)} %get-tuple-element.38), channel_id=1, source_target_pairs={{0,4},{2,6},{4,0},{6,2},{8,12},{10,14},{12,8},{14,10},{16,20},{18,... | collective-permute-start | bytes 786440 | tf_op jit(solution)/shard_map/ppermute | solution.py:268
  9.5 11.7 %collective-permute-start.3 = (bf16[2,4,128,128]{3,2,1,0:T(8,128)(2,1)S(1)}, bf16[2,4,128,128]{3,2,1,0:T(8,128)(2,1)S(1)}, u32[]{:S(2)}, u32[]{:S(2)}) collective-permute-start(bf16[2,4,128,128]{3,2,1,0:T(8,128)(2,1)S(1)} %get-tuple-element.39), channel_id=1, source_target_pairs={{0,6},{2,4},{4,2},{6,0},{8,14},{10,12},{12,10},{14,8},{16,22},{18,... | collective-permute-start | bytes 786440 | tf_op jit(solution)/shard_map/ppermute | solution.py:268
  9.7 26.5 %collective-permute-start.11 = (bf16[2,4,128,128]{3,2,1,0:T(8,128)(2,1)S(1)}, bf16[2,4,128,128]{3,2,1,0:T(8,128)(2,1)S(1)}, u32[]{:S(2)}, u32[]{:S(2)}) collective-permute-start(bf16[2,4,128,128]{3,2,1,0:T(8,128)(2,1)S(1)} %get-tuple-element.50), channel_id=1, source_target_pairs={{0,2},{2,0},{4,6},{6,4},{8,10},{10,8},{12,14},{14,12},{16,18},{18,... | collective-permute-start | bytes 786440 | tf_op jit(solution)/shard_map/ppermute | solution.py:268
  22.1 12.6 %collective-permute-start.4 = (bf16[4,256,128]{2,1,0:T(8,128)(2,1)}, bf16[4,256,128]{2,1,0:T(8,128)(2,1)S(1)}, u32[]{:S(2)}, u32[]{:S(2)}) collective-permute-start(bf16[4,256,128]{2,1,0:T(8,128)(2,1)} %get-tuple-element.41), channel_id=1, source_target_pairs={{0,8},{8,0},{2,10},{10,2},{4,12},{12,4},{6,14},{14,6},{16,24},{24,... | collective-permute-start | bytes 786440 | tf_op jit(solution)/shard_map/ppermute | solution.py:306
  22.2 12.4 %collective-permute-start.5 = (bf16[4,256,128]{2,1,0:T(8,128)(2,1)}, bf16[4,256,128]{2,1,0:T(8,128)(2,1)S(1)}, u32[]{:S(2)}, u32[]{:S(2)}) collective-permute-start(bf16[4,256,128]{2,1,0:T(8,128)(2,1)} %get-tuple-element.42), channel_id=1, source_target_pairs={{8,16},{16,8},{10,18},{18,10},{12,20},{20,12},{14,22},{22,14},{9,1... | collective-permute-start | bytes 786440 | tf_op jit(solution)/shard_map/ppermute | solution.py:307
  26.6 12.5 %collective-permute-start.12 = (bf16[2,4,128,128]{3,2,1,0:T(8,128)(2,1)S(1)}, bf16[2,4,128,128]{3,2,1,0:T(8,128)(2,1)S(1)}, u32[]{:S(2)}, u32[]{:S(2)}) collective-permute-start(bf16[2,4,128,128]{3,2,1,0:T(8,128)(2,1)S(1)} %get-tuple-element.51), channel_id=1, source_target_pairs={{0,4},{2,6},{4,0},{6,2},{8,12},{10,14},{12,8},{14,10},{16,20},{18,... | collective-permute-start | bytes 786440 | tf_op jit(solution)/shard_map/ppermute | solution.py:268
  27.0 12.0 %collective-permute-start.13 = (bf16[2,4,128,128]{3,2,1,0:T(8,128)(2,1)S(1)}, bf16[2,4,128,128]{3,2,1,0:T(8,128)(2,1)S(1)}, u32[]{:S(2)}, u32[]{:S(2)}) collective-permute-start(bf16[2,4,128,128]{3,2,1,0:T(8,128)(2,1)S(1)} %get-tuple-element.52), channel_id=1, source_target_pairs={{0,6},{2,4},{4,2},{6,0},{8,14},{10,12},{12,10},{14,8},{16,22},{18,... | collective-permute-start | bytes 786440 | tf_op jit(solution)/shard_map/ppermute | solution.py:268
  29.0 0.7 copy-start.2
  39.2 9.5 %collective-permute-start.14 = (bf16[4,256,128]{2,1,0:T(8,128)(2,1)S(1)}, bf16[4,256,128]{2,1,0:T(8,128)(2,1)S(1)}, u32[]{:S(2)}, u32[]{:S(2)}) collective-permute-start(bf16[4,256,128]{2,1,0:T(8,128)(2,1)S(1)} %get-tuple-element.58), channel_id=1, source_target_pairs={{0,8},{8,0},{2,10},{10,2},{4,12},{12,4},{6,14},{14,6},{16,24},{24,... | collective-permute-start | bytes 786440 | tf_op jit(solution)/shard_map/ppermute | solution.py:306
  39.3 9.5 %collective-permute-start.15 = (bf16[4,256,128]{2,1,0:T(8,128)(2,1)S(1)}, bf16[4,256,128]{2,1,0:T(8,128)(2,1)S(1)}, u32[]{:S(2)}, u32[]{:S(2)}) collective-permute-start(bf16[4,256,128]{2,1,0:T(8,128)(2,1)S(1)} %get-tuple-element.59), channel_id=1, source_target_pairs={{8,16},{16,8},{10,18},{18,10},{12,20},{20,12},{14,22},{22,14},{9,1... | collective-permute-start | bytes 786440 | tf_op jit(solution)/shard_map/ppermute | solution.py:307
  41.4 10.4 %collective-permute-start.6 = (bf16[2,4,128,128]{3,2,1,0:T(8,128)(2,1)S(1)}, bf16[2,4,128,128]{3,2,1,0:T(8,128)(2,1)S(1)}, u32[]{:S(2)}, u32[]{:S(2)}) collective-permute-start(bf16[2,4,128,128]{3,2,1,0:T(8,128)(2,1)S(1)} %get-tuple-element.44), channel_id=1, source_target_pairs={{0,2},{2,0},{4,6},{6,4},{8,10},{10,8},{12,14},{14,12},{16,18},{18,... | collective-permute-start | bytes 786440 | tf_op jit(solution)/shard_map/ppermute | solution.py:268
  42.8 10.5 %collective-permute-start.7 = (bf16[2,4,128,128]{3,2,1,0:T(8,128)(2,1)S(1)}, bf16[2,4,128,128]{3,2,1,0:T(8,128)(2,1)S(1)}, u32[]{:S(2)}, u32[]{:S(2)}) collective-permute-start(bf16[2,4,128,128]{3,2,1,0:T(8,128)(2,1)S(1)} %get-tuple-element.45), channel_id=1, source_target_pairs={{0,4},{2,6},{4,0},{6,2},{8,12},{10,14},{12,8},{14,10},{16,20},{18,... | collective-permute-start | bytes 786440 | tf_op jit(solution)/shard_map/ppermute | solution.py:268
  42.8 10.5 %collective-permute-start.8 = (bf16[2,4,128,128]{3,2,1,0:T(8,128)(2,1)S(1)}, bf16[2,4,128,128]{3,2,1,0:T(8,128)(2,1)S(1)}, u32[]{:S(2)}, u32[]{:S(2)}) collective-permute-start(bf16[2,4,128,128]{3,2,1,0:T(8,128)(2,1)S(1)} %get-tuple-element.46), channel_id=1, source_target_pairs={{0,6},{2,4},{4,2},{6,0},{8,14},{10,12},{12,10},{14,8},{16,22},{18,... | collective-permute-start | bytes 786440 | tf_op jit(solution)/shard_map/ppermute | solution.py:268
  50.4 8.5 %collective-permute-start.16 = (bf16[2,4,128,128]{3,2,1,0:T(8,128)(2,1)S(1)}, bf16[2,4,128,128]{3,2,1,0:T(8,128)(2,1)S(1)}, u32[]{:S(2)}, u32[]{:S(2)}) collective-permute-start(bf16[2,4,128,128]{3,2,1,0:T(8,128)(2,1)S(1)} %get-tuple-element.61), channel_id=1, source_target_pairs={{0,2},{2,0},{4,6},{6,4},{8,10},{10,8},{12,14},{14,12},{16,18},{18,... | collective-permute-start | bytes 786440 | tf_op jit(solution)/shard_map/ppermute | solution.py:268
  51.8 14.8 %collective-permute-start.17 = (bf16[2,4,128,128]{3,2,1,0:T(8,128)(2,1)S(1)}, bf16[2,4,128,128]{3,2,1,0:T(8,128)(2,1)S(1)}, u32[]{:S(2)}, u32[]{:S(2)}) collective-permute-start(bf16[2,4,128,128]{3,2,1,0:T(8,128)(2,1)S(1)} %get-tuple-element.62), channel_id=1, source_target_pairs={{0,4},{2,6},{4,0},{6,2},{8,12},{10,14},{12,8},{14,10},{16,20},{18,... | collective-permute-start | bytes 786440 | tf_op jit(solution)/shard_map/ppermute | solution.py:268
  51.8 14.8 %collective-permute-start.18 = (bf16[2,4,128,128]{3,2,1,0:T(8,128)(2,1)S(1)}, bf16[2,4,128,128]{3,2,1,0:T(8,128)(2,1)S(1)}, u32[]{:S(2)}, u32[]{:S(2)}) collective-permute-start(bf16[2,4,128,128]{3,2,1,0:T(8,128)(2,1)S(1)} %get-tuple-element.63), channel_id=1, source_target_pairs={{0,6},{2,4},{4,2},{6,0},{8,14},{10,12},{12,10},{14,8},{16,22},{18,... | collective-permute-start | bytes 786440 | tf_op jit(solution)/shard_map/ppermute | solution.py:268
  53.3 15.2 %collective-permute-start.9 = (bf16[4,4,128,128]{3,2,1,0:T(8,128)(2,1)S(1)}, bf16[4,4,128,128]{3,2,1,0:T(8,128)(2,1)S(1)}, u32[]{:S(2)}, u32[]{:S(2)}) collective-permute-start(bf16[4,4,128,128]{3,2,1,0:T(8,128)(2,1)S(1)} %shard_map.89), channel_id=1, source_target_pairs={{0,1},{1,0},{2,3},{3,2},{4,5},{5,4},{6,7},{7,6},{8,9},{9,8},{10,11... | collective-permute-start | bytes 1572872 | tf_op jit(solution)/shard_map/ppermute | solution.py:336
  66.6 3.4 %collective-permute-start.19 = (bf16[4,4,128,128]{3,2,1,0:T(8,128)(2,1)S(1)}, bf16[4,4,128,128]{3,2,1,0:T(8,128)(2,1)S(1)}, u32[]{:S(2)}, u32[]{:S(2)}) collective-permute-start(bf16[4,4,128,128]{3,2,1,0:T(8,128)(2,1)S(1)} %shard_map.94), channel_id=1, source_target_pairs={{0,1},{1,0},{2,3},{3,2},{4,5},{5,4},{6,7},{7,6},{8,9},{9,8},{10,11... | collective-permute-start | bytes 1572872 | tf_op jit(solution)/shard_map/ppermute | solution.py:336

commit v4 on v3

v4 whole, which is shorter than its diff:
```python
import functools
import math

import jax
import jax.numpy as jnp
from jax import lax
from jax.experimental import pallas as pl
from jax.experimental.pallas import tpu as pltpu
from jax.sharding import PartitionSpec as P

DH = 128
DOC_MOST = 256
MASKED = -1e30
GROUP = 4
IN_APART = (False, False)
OUT_APART = (False, False)
SCALE = 1.0 / math.sqrt(DH)
VMEM = 12 * 1024 * 1024
PACK_VMEM = 56 * 1024 * 1024
PACK_STEPS = 2
WHOLE = pl.BlockSpec(memory_space=pltpu.VMEM)


def dot_nt(a, b):
    return lax.dot_general(a, b, (((1,), (1,)), ((), ())), preferred_element_type=jnp.float32)


def dot_tn(a, b):
    return lax.dot_general(a, b, (((0,), (0,)), ((), ())), preferred_element_type=jnp.float32)


def dot_nn(a, b):
    return lax.dot_general(a, b, (((1,), (0,)), ((), ())), preferred_element_type=jnp.float32)


def self_attention(queries, keys, values, grads, same):
    scores = dot_nt(keys, queries) * (SCALE * math.log2(math.e))
    scores = jnp.where(same, scores, jnp.float32(MASKED))
    top = jnp.max(scores, axis=0, keepdims=True)
    weights = jnp.exp2(scores - top)
    probs = weights * (1.0 / jnp.sum(weights, axis=0, keepdims=True))
    low = probs.astype(jnp.bfloat16)
    attended = dot_tn(values, low).astype(jnp.bfloat16).astype(jnp.float32)
    delta = jnp.sum(attended * grads.T.astype(jnp.float32), axis=0, keepdims=True)
    score_grad = (probs * (dot_nt(values, grads) - delta)).astype(jnp.bfloat16)
    query_grad = (dot_tn(keys, score_grad) * SCALE).T
    key_grad = dot_nn(score_grad, queries) * SCALE
    value_grad = dot_nn(low, grads)
    return attended.T, query_grad, key_grad, value_grad


def tile_ids(table_ref, first):
    lanes = []
    for row in (first, first + 1):
        inside = (row >= 0) & (row < table_ref.shape[0])
        held = jnp.clip(row, 0, table_ref.shape[0] - 1)
        lanes.append(jnp.where(inside, table_ref[pl.ds(held, 1), :], -1))
    down = [jnp.broadcast_to(lane, (lane.shape[1], lane.shape[1])).T for lane in lanes]
    return jnp.concatenate(down, axis=0), jnp.concatenate(lanes, axis=1)


def across(down):
    return jnp.concatenate([down, down], axis=1)


def boundary_attention(low_rows, high_rows, ids_low, ids_high):
    (low_down, low_lane), (high_down, high_lane) = ids_low, ids_high
    first, last = high_lane[:, 0:1], low_lane[:, -1:]
    from_low, from_high = low_down == first, high_down == last
    member_down = (from_low | from_high).astype(jnp.int32)
    member_lane = ((low_lane == first) | (high_lane == last)).astype(jnp.int32)
    chosen = [
        jnp.where(from_low, a.astype(jnp.float32), b.astype(jnp.float32)).astype(jnp.bfloat16)
        for a, b in zip(low_rows, high_rows)
    ]
    return self_attention(*chosen, across(member_down) == member_lane), from_low, from_high


def interior_kernel(edge, ext_ref, table_ref, res_ref):
    tiles = ext_ref.shape[1] // edge
    plane = lax.axis_index("blk") // GROUP
    ids = [tile_ids(table_ref, (plane * tiles + t) * 2) for t in range(tiles)]

    def rows_of(t):
        return [ext_ref[m, t * edge : (t + 1) * edge] for m in range(4)]

    def put(t, chosen, results):
        at = slice(t * edge, (t + 1) * edge)
        for m, result in enumerate(results):
            if chosen is not None:
                result = jnp.where(chosen, result, res_ref[m, at].astype(jnp.float32))
            res_ref[m, at] = result.astype(jnp.bfloat16)

    for t in range(tiles):
        down, lane = ids[t]
        put(t, None, self_attention(*rows_of(t), across(down) == lane))
        if t > 0:
            results, from_low, from_high = boundary_attention(
                rows_of(t - 1), rows_of(t), ids[t - 1], ids[t]
            )
            put(t - 1, from_low, results)
            put(t, from_high, results)


def edge_kernel(edge, apart, ext_ref, even_ref, odd_ref, res_ref, table_ref, *refs):
    outs, result_ref = refs[:-1], refs[-1]
    rows = ext_ref.shape[1]
    position, core = lax.axis_index("blk"), lax.axis_index("head")
    place, parity = position % GROUP, (position // GROUP) % 2
    result_ref[...] = res_ref[...]

    tiles = rows // edge
    base = (position // GROUP) * tiles

    for side in range(2):
        from_even = parity == (1 - side)
        halo = [jnp.where(from_even, even_ref[m], odd_ref[m]) for m in range(4)]
        own = slice(0, edge) if side == 0 else slice(rows - edge, rows)
        mine = [ext_ref[m, own] for m in range(4)]
        if side == 0:
            results, _, chosen = boundary_attention(
                halo, mine, tile_ids(table_ref, (base - 1) * 2), tile_ids(table_ref, base * 2)
            )
        else:
            results, chosen, _ = boundary_attention(
                mine,
                halo,
                tile_ids(table_ref, (base + tiles - 1) * 2),
                tile_ids(table_ref, (base + tiles) * 2),
            )
        for m, result in enumerate(results):
            result = jnp.where(chosen, result, result_ref[m, own].astype(jnp.float32))
            result_ref[m, own] = result.astype(jnp.bfloat16)
    half = edge // 2
    for s in range(GROUP):
        for piece in range(2):
            first = pl.multiple_of(((place ^ s) * 2 + (core ^ piece)) * half, half)
            block = result_ref[:, pl.ds(first, half), :]
            if apart:
                outs[2 * s + piece][...] = block
            else:
                outs[s][piece] = block


def shape(*dims, dtype=jnp.bfloat16):
    return jax.ShapeDtypeStruct(dims, dtype)


def call(kernel, out_shape, *args, scratch=(), flops=0, exps=0):
    return pl.pallas_call(
        kernel,
        out_shape=out_shape,
        in_specs=[WHOLE] * len(args),
        out_specs=jax.tree.map(lambda _: WHOLE, out_shape),
        scratch_shapes=scratch,
        compiler_params=pltpu.CompilerParams(vmem_limit_bytes=VMEM),
        cost_estimate=pl.CostEstimate(flops=1, bytes_accessed=1, transcendentals=0),
    )(*args)


def pack_kernel(j, chunks, apart, *refs):
    ins, outs = refs[:4], refs[4:]
    block, width = ins[0].shape
    core, place = lax.axis_index("head"), lax.axis_index("blk") % GROUP
    at = pl.ds(pl.multiple_of(pl.program_id(0) * block, block), block)
    for s in range(GROUP):
        for which in range(2):
            base = (core ^ which) * (width // 2) + ((place ^ s) * chunks + j) * DH
            first = pl.multiple_of(base, DH)
            for m, ref in enumerate(ins):
                part = ref[:, pl.ds(first, DH)]
                if apart:
                    outs[2 * s + which][m, at] = part
                else:
                    outs[which][s, m, at] = part


def pack(arrays, j, chunks, apart):
    rows, width = arrays[0].shape
    block = rows // PACK_STEPS
    outs = [shape(4, rows, DH)] * (2 * GROUP) if apart else [shape(GROUP, 4, rows, DH)] * 2
    return pl.pallas_call(
        functools.partial(pack_kernel, j, chunks, apart),
        grid=(PACK_STEPS,),
        out_shape=outs,
        in_specs=[pl.BlockSpec((block, width), lambda i: (i, 0))] * 4,
        out_specs=[WHOLE] * len(outs),
        compiler_params=pltpu.CompilerParams(vmem_limit_bytes=PACK_VMEM),
    )(*arrays)


def join_kernel(mine_ref, received_ref, *outs):
    for s, out in enumerate(outs):
        out[0] = mine_ref[s]
        out[1] = received_ref[s]


def gather_kernel(apart, *refs):
    slots, (ext, to_even, to_odd) = refs[:-3], refs[-3:]
    edge = to_even.shape[1]
    half = edge // 2
    position, core = lax.axis_index("blk"), lax.axis_index("head")
    place, parity = position % GROUP, (position // GROUP) % 2
    for s in range(GROUP):
        for piece in range(2):
            first = pl.multiple_of(((place ^ s) * 2 + (core ^ piece)) * half, half)
            ext[:, pl.ds(first, half), :] = slots[2 * s + piece][...] if apart else slots[s][piece]
    rows = ext.shape[1]
    first = pl.multiple_of((rows - edge) * (1 - parity), edge)
    to_even[...] = ext[:, pl.ds(first, edge), :]
    first = pl.multiple_of((rows - edge) * parity, edge)
    to_odd[...] = ext[:, pl.ds(first, edge), :]


def split_kernel(*refs):
    slots, out = refs[:-1], refs[-1]
    for s, slot in enumerate(slots):
        out[s] = slot[1]


def unpack_kernel(aparts, *refs):
    ins, outs, held, sems = list(refs[:-6]), refs[-6:-2], refs[-2], refs[-1]
    width = outs[0].shape[1]
    chunks = len(aparts)
    core, place = lax.axis_index("head"), lax.axis_index("blk") % GROUP
    blocks = []
    for j, apart in enumerate(aparts):
        slots, ins = (ins[: 2 * GROUP], ins[2 * GROUP :]) if apart else (ins[: GROUP + 1], ins[GROUP + 1 :])
        for s in range(GROUP):
            for which in range(2):
                base = (core ^ which) * (width // 2) + ((place ^ s) * chunks + j) * DH
                if apart:
                    block = slots[2 * s + which]
                else:
                    block = slots[GROUP].at[s] if which else slots[s].at[0]
                blocks.append((pl.multiple_of(base, DH), block))
    copies = [pltpu.make_async_copy(held.at[m], out, sems.at[m]) for m, out in enumerate(outs)]
    for m, copy in enumerate(copies):
        for first, block in blocks:
            held[m, :, pl.ds(first, DH)] = block[m]
        copy.start()
    for copy in copies:
        copy.wait()


def unpack(chunks, aparts, rows, width):
    blocks = [block for chunk in chunks for block in chunk]
    return pl.pallas_call(
        functools.partial(unpack_kernel, aparts),
        out_shape=[shape(rows, width)] * 4,
        in_specs=[WHOLE] * len(blocks),
        out_specs=[pl.BlockSpec(memory_space=pl.ANY)] * 4,
        scratch_shapes=[
            pltpu.VMEM((4, rows, width), jnp.bfloat16),
            pltpu.SemaphoreType.DMA((4,)),
        ],
        compiler_params=pltpu.CompilerParams(vmem_limit_bytes=VMEM),
    )(*blocks)


def body(query_rows, key_rows, value_rows, out_grad, doc_ids):
    positions = lax.axis_size("blk")
    half, width = query_rows.shape
    heads = width // DH
    chunks = heads // (2 * GROUP)
    edge = 2 * half
    rows = GROUP * edge
    assert edge >= DOC_MOST and positions % GROUP == 0 and chunks == len(IN_APART)
    swap = [(0, 1), (1, 0)]
    planes = positions // GROUP

    def plane_pairs(first):
        route = []
        for low in range(first, planes - 1, 2):
            for i in range(GROUP):
                here, there = low * GROUP + i, (low + 1) * GROUP + i
                route += [(here, there), (there, here)]
        return route

    def hop(block, s, cross=0):
        if s == 0:
            return lax.ppermute(block, "head", swap) if cross else block
        if not cross:
            return lax.ppermute(block, "blk", [(i, i ^ s) for i in range(positions)])
        route = [(2 * i + k, 2 * (i ^ s) + 1 - k) for i in range(positions) for k in range(2)]
        return lax.ppermute(block, ("blk", "head"), route)

    table = doc_ids.reshape(-1, half)
    inputs = (query_rows, key_rows, value_rows, out_grad)
    unit = 2 * DH * edge * edge * 6

    arrived = []
    for j, apart in enumerate(IN_APART):
        packed = pack(inputs, j, chunks, apart)
        if apart:
            arrived.append([hop(block, *divmod(i, 2)) for i, block in enumerate(packed)])
        else:
            theirs = lax.ppermute(packed[1], "head", swap)
            joined = call(join_kernel, [shape(2, 4, half, DH)] * GROUP, packed[0], theirs)
            arrived.append([hop(block, s) for s, block in enumerate(joined)])

    def gather(j, *after):
        slots = arrived[j]
        if after:
            slots, _ = lax.optimization_barrier((slots, after))
        return call(
            functools.partial(gather_kernel, IN_APART[j]),
            [shape(4, rows, DH), shape(4, edge, DH), shape(4, edge, DH)],
            *slots,
        )

    def halo(to_even, to_odd):
        even = lax.ppermute(to_even, "blk", plane_pairs(0))
        return even, lax.ppermute(to_odd, "blk", plane_pairs(1))

    def interior(ext):
        return call(
            functools.partial(interior_kernel, edge), shape(4, rows, DH), ext, table
        )

    def finish(j, ext, even, odd, res):
        apart = OUT_APART[j]
        return call(
            functools.partial(edge_kernel, edge, apart),
            [shape(4, half, DH)] * (2 * GROUP) if apart else [shape(2, 4, half, DH)] * GROUP,
            ext,
            even,
            odd,
            res,
            table,
            scratch=[pltpu.VMEM((4, rows, DH), jnp.bfloat16)],
        )

    def give_back(j, back):
        if OUT_APART[j]:
            return [hop(block, *divmod(i, 2)) for i, block in enumerate(back)]
        back = [hop(block, s) for s, block in enumerate(back)]
        away = call(split_kernel, shape(GROUP, 4, half, DH), *back)
        return back + [lax.ppermute(away, "head", swap)]

    ext_a, *edges_a = gather(0)
    halo_a = halo(*edges_a)
    res_a = interior(ext_a)
    ext_b, *edges_b = gather(1, res_a)
    res_a, ext_b = lax.optimization_barrier((res_a, ext_b))
    back_a = finish(0, ext_a, *halo_a, res_a)
    ext_b, edges_b, back_a = lax.optimization_barrier((ext_b, edges_b, back_a))
    halo_b = halo(*edges_b)
    res_b = interior(ext_b)
    back_b = finish(1, ext_b, *halo_b, res_b)
    results = [give_back(0, back_a), give_back(1, back_b)]
    return tuple(unpack(results, OUT_APART, half, width))


def solution(mesh):
    placed = P(("blk", "head"), None)
    return jax.shard_map(
        body,
        mesh=mesh,
        in_specs=(placed, placed, placed, placed, P()),
        out_specs=(placed,) * 4,
        check_vma=False,
    )
```

time: 73.4 us -> 68.9 us (0.939); the launches traced: 71.9 us -> 68.7 us
  waiting for transfers between devices: 24.6 us -> 16.5 us
  starting transfers between devices: 26.1 us -> 31.7 us
  local copies, waits for them, and re-layouts: 2.1 us -> 0.01 us
  Pallas kernels: 18.4 us -> 19.6 us
    ppermute x20, waiting for transfers between devices: 24.6 us -> 16.5 us  [the longest x12 15 us: hop(): return lax.ppermute(block, 'blk', [(i, i ^ s) for i in range(positions)])]
    ppermute x20, starting transfers between devices: 26.1 us -> 31.7 us  [the longest x12 12.8 us: hop(): return lax.ppermute(block, 'blk', [(i, i ^ s) for i in range(positions)])]
    pallas_call x1 -> x3, Pallas kernels: 2.78 us -> 6.73 us  [the longest x2 5.23 us: pack(): pl.pallas_call(functools.partial(pack_kernel, j, chunks, apart), grid=(PA...]
    pallas_call x11 -> x10, Pallas kernels: 15.6 us -> 12.9 us  [call(): pl.pallas_call(kernel, out_shape=out_shape, in_specs=[WHOLE] * len(args),...]
    unnamed x6, local copies, waits for them, and re-layouts: 1.76 us -> 0.01 us
  transfers between devices with their start and end apart: 20 -> 20, of which waited for: 9 -> 7; matrix products, arithmetic and copies ran while one was open for 0% -> 0% of each run, Pallas kernels for 19% -> 20%
where the time goes in v4:
time: 68.9 us; the launch traced here: 68.7 us
  starting transfers between devices  31.7 us (46%)
  Pallas kernels  19.6 us (28%)
  waiting for transfers between devices  16.5 us (24%)
  between operations  0.95 us (1%)
    ppermute x12, waiting for transfers between devices, hop(): return lax.ppermute(block, 'blk', [(i, i ^ s) for i in range(positions)])  15 us
    pallas_call x10, Pallas kernels, call(): pl.pallas_call(kernel, out_shape=out_shape, in_specs=[WHOLE] * len(args),...  12.9 us
    ppermute x12, starting transfers between devices, hop(): return lax.ppermute(block, 'blk', [(i, i ^ s) for i in range(positions)])  12.8 us
    ppermute x2, starting transfers between devices, halo(): return (even, lax.ppermute(to_odd, 'blk', plane_pairs(1)))  8.82 us
    ppermute x2, starting transfers between devices, give_back(): return back + [lax.ppermute(away, 'head', swap)]  8.8 us
    pallas_call x2, Pallas kernels, pack(): pl.pallas_call(functools.partial(pack_kernel, j, chunks, apart), grid=(PA...  5.23 us
    ppermute x2, waiting for transfers between devices, give_back(): return back + [lax.ppermute(away, 'head', swap)]  1.54 us
    pallas_call x1, Pallas kernels, unpack(): pl.pallas_call(functools.partial(unpack_kernel, aparts), out_shape=[shape...  1.5 us
  transfers between devices with their start and end apart: 20, of which 7 were waited for; matrix products, arithmetic and copies ran while one was open for 0% of the time, Pallas kernels for 20%

profile of v4, /device:TPU:9, one launch (start us, length us, event | category | flops | bytes accessed | tf_op | source)
XLA Modules:
  0.0 68.7 jit_solution(14620005679388209621)
XLA Ops:
  0.6 2.6 %shard_map.84 = (bf16[4,4,128,128]{3,2,1,0:T(8,128)(2,1)}, bf16[4,4,128,128]{3,2,1,0:T(8,128)(2,1)}) custom-call(bf16[128,2048]{1,0:T(8,128)(2,1)} %refs_0_.3, bf16[128,2048]{1,0:T(8,128)(2,1)} %refs_1_.3, bf16[128,2048]{1,0:T(8,128)(2,1)} %refs_2_.3, bf16[128,2048]{1,0:T(8,128)(2,1)} %refs_3_.3), custom_call_target="tpu_custom_call" | custom-call | tf_op jit(solution)/shard_map/pallas_call | solution.py:182
  3.3 0.7 collective-permute-start
  3.9 2.6 %shard_map.88 = (bf16[4,4,128,128]{3,2,1,0:T(8,128)(2,1)}, bf16[4,4,128,128]{3,2,1,0:T(8,128)(2,1)}) custom-call(bf16[128,2048]{1,0:T(8,128)(2,1)} %refs_0_.3, bf16[128,2048]{1,0:T(8,128)(2,1)} %refs_1_.3, bf16[128,2048]{1,0:T(8,128)(2,1)} %refs_2_.3, bf16[128,2048]{1,0:T(8,128)(2,1)} %refs_3_.3), custom_call_target="tpu_custom_call" | custom-call | tf_op jit(solution)/shard_map/pallas_call | solution.py:182
  6.7 1.3 %collective-permute-start.1 = (bf16[2,4,128,128]{3,2,1,0:T(8,128)(2,1)S(1)}, bf16[2,4,128,128]{3,2,1,0:T(8,128)(2,1)S(1)}, u32[]{:S(2)}, u32[]{:S(2)}) collective-permute-start(bf16[2,4,128,128]{3,2,1,0:T(8,128)(2,1)S(1)} %get-tuple-element.46), channel_id=1, source_target_pairs={{0,2},{2,0},{4,6},{6,4},{8,10},{10,8},{12,14},{14,12},{16,18},{18,... | collective-permute-start | bytes 786440 | tf_op jit(solution)/shard_map/ppermute | solution.py:284
  8.0 1.2 %collective-permute-start.2 = (bf16[2,4,128,128]{3,2,1,0:T(8,128)(2,1)S(1)}, bf16[2,4,128,128]{3,2,1,0:T(8,128)(2,1)S(1)}, u32[]{:S(2)}, u32[]{:S(2)}) collective-permute-start(bf16[2,4,128,128]{3,2,1,0:T(8,128)(2,1)S(1)} %get-tuple-element.47), channel_id=1, source_target_pairs={{0,4},{2,6},{4,0},{6,2},{8,12},{10,14},{12,8},{14,10},{16,20},{18,... | collective-permute-start | bytes 786440 | tf_op jit(solution)/shard_map/ppermute | solution.py:284
  9.5 1.3 %collective-permute-start.5 = (bf16[2,4,128,128]{3,2,1,0:T(8,128)(2,1)S(1)}, bf16[2,4,128,128]{3,2,1,0:T(8,128)(2,1)S(1)}, u32[]{:S(2)}, u32[]{:S(2)}) collective-permute-start(bf16[2,4,128,128]{3,2,1,0:T(8,128)(2,1)S(1)} %get-tuple-element.53), channel_id=1, source_target_pairs={{0,2},{2,0},{4,6},{6,4},{8,10},{10,8},{12,14},{14,12},{16,18},{18,... | collective-permute-start | bytes 786440 | tf_op jit(solution)/shard_map/ppermute | solution.py:284
  10.8 1.2 %collective-permute-start.6 = (bf16[2,4,128,128]{3,2,1,0:T(8,128)(2,1)S(1)}, bf16[2,4,128,128]{3,2,1,0:T(8,128)(2,1)S(1)}, u32[]{:S(2)}, u32[]{:S(2)}) collective-permute-start(bf16[2,4,128,128]{3,2,1,0:T(8,128)(2,1)S(1)} %get-tuple-element.54), channel_id=1, source_target_pairs={{0,4},{2,6},{4,0},{6,2},{8,12},{10,14},{12,8},{14,10},{16,20},{18,... | collective-permute-start | bytes 786440 | tf_op jit(solution)/shard_map/ppermute | solution.py:284
  12.0 2.2 %collective-permute-done.1.refs_1_ = bf16[2,4,128,128]{3,2,1,0:T(8,128)(2,1)S(1)} collective-permute-done((bf16[2,4,128,128]{3,2,1,0:T(8,128)(2,1)S(1)}, bf16[2,4,128,128]{3,2,1,0:T(8,128)(2,1)S(1)}, u32[]{:S(2)}, u32[]{:S(2)}) %collective-permute-start.1) | collective-permute-done | bytes 262176 | tf_op jit(solution)/shard_map/ppermute | solution.py:284
  14.2 2.2 %collective-permute-start.7 = (bf16[2,4,128,128]{3,2,1,0:T(8,128)(2,1)S(1)}, bf16[2,4,128,128]{3,2,1,0:T(8,128)(2,1)S(1)}, u32[]{:S(2)}, u32[]{:S(2)}) collective-permute-start(bf16[2,4,128,128]{3,2,1,0:T(8,128)(2,1)S(1)} %get-tuple-element.55), channel_id=1, source_target_pairs={{0,6},{2,4},{4,2},{6,0},{8,14},{10,12},{12,10},{14,8},{16,22},{18,... | collective-permute-start | bytes 786440 | tf_op jit(solution)/shard_map/ppermute | solution.py:284
  16.4 4.4 %collective-permute-done.3.refs_3_ = bf16[2,4,128,128]{3,2,1,0:T(8,128)(2,1)S(1)} collective-permute-done((bf16[2,4,128,128]{3,2,1,0:T(8,128)(2,1)S(1)}, bf16[2,4,128,128]{3,2,1,0:T(8,128)(2,1)S(1)}, u32[]{:S(2)}, u32[]{:S(2)}) %collective-permute-start.3) | collective-permute-done | bytes 262176 | tf_op jit(solution)/shard_map/ppermute | solution.py:284
  21.0 0.2 collective-permute-start.8
  21.2 4.3 %collective-permute-start.9 = (bf16[4,256,128]{2,1,0:T(8,128)(2,1)S(1)}, bf16[4,256,128]{2,1,0:T(8,128)(2,1)S(1)}, u32[]{:S(2)}, u32[]{:S(2)}) collective-permute-start(bf16[4,256,128]{2,1,0:T(8,128)(2,1)S(1)} %get-tuple-element.65), channel_id=1, source_target_pairs={{8,16},{16,8},{10,18},{18,10},{12,20},{20,12},{14,22},{22,14},{9,1... | collective-permute-start | bytes 786440 | tf_op jit(solution)/shard_map/ppermute | solution.py:314
  25.5 4.6 %shard_map.87.res_ref = bf16[4,1024,128]{2,1,0:T(8,128)(2,1)S(1)} custom-call(bf16[4,1024,128]{2,1,0:T(8,128)(2,1)S(1)} %get-tuple-element.49.ext_ref, s32[32,128]{1,0:T(8,128)S(1)} %bitcast.1), custom_call_target="tpu_custom_call" | custom-call | flops 1 | bytes 1 | tf_op jit(solution)/shard_map/pallas_call | solution.py:150
  30.1 2.0 %collective-permute-done.7.refs_3_ = bf16[2,4,128,128]{3,2,1,0:T(8,128)(2,1)S(1)} collective-permute-done((bf16[2,4,128,128]{3,2,1,0:T(8,128)(2,1)S(1)}, bf16[2,4,128,128]{3,2,1,0:T(8,128)(2,1)S(1)}, u32[]{:S(2)}, u32[]{:S(2)}) %collective-permute-start.7) | collective-permute-done | bytes 262176 | tf_op jit(solution)/shard_map/ppermute | solution.py:284
  32.2 1.6 %shard_map.91 = (bf16[2,4,128,128]{3,2,1,0:T(8,128)(2,1)S(1)}, bf16[2,4,128,128]{3,2,1,0:T(8,128)(2,1)S(1)}, bf16[2,4,128,128]{3,2,1,0:T(8,128)(2,1)S(1)}, bf16[2,4,128,128]{3,2,1,0:T(8,128)(2,1)S(1)}) custom-call(bf16[4,1024,128]{2,1,0:T(8,128)(2,1)S(1)} %get-tuple-element.49.ext_ref, bf16[4,256,128]{2,1,0:T(8,128)(2,1)S(1)} %collective-permute-done.8.even_ref, ...), custom_call_target="tpu_custom_call" | custom-call | flops 1 | bytes 1 | tf_op jit(solution)/shard_map/pallas_call | solution.py:150
  33.9 0.2 collective-permute-start.14
  34.1 4.5 %collective-permute-start.15 = (bf16[4,256,128]{2,1,0:T(8,128)(2,1)S(1)}, bf16[4,256,128]{2,1,0:T(8,128)(2,1)S(1)}, u32[]{:S(2)}, u32[]{:S(2)}) collective-permute-start(bf16[4,256,128]{2,1,0:T(8,128)(2,1)S(1)} %get-tuple-element.77), channel_id=1, source_target_pairs={{8,16},{16,8},{10,18},{18,10},{12,20},{20,12},{14,22},{22,14},{9,1... | collective-permute-start | bytes 786440 | tf_op jit(solution)/shard_map/ppermute | solution.py:314
  38.6 1.2 %collective-permute-start.10 = (bf16[2,4,128,128]{3,2,1,0:T(8,128)(2,1)S(1)}, bf16[2,4,128,128]{3,2,1,0:T(8,128)(2,1)S(1)}, u32[]{:S(2)}, u32[]{:S(2)}) collective-permute-start(bf16[2,4,128,128]{3,2,1,0:T(8,128)(2,1)S(1)} %get-tuple-element.72), channel_id=1, source_target_pairs={{0,2},{2,0},{4,6},{6,4},{8,10},{10,8},{12,14},{14,12},{16,18},{18,... | collective-permute-start | bytes 786440 | tf_op jit(solution)/shard_map/ppermute | solution.py:284
  39.8 0.3 collective-permute-start.11
  40.1 1.2 %collective-permute-start.12 = (bf16[2,4,128,128]{3,2,1,0:T(8,128)(2,1)S(1)}, bf16[2,4,128,128]{3,2,1,0:T(8,128)(2,1)S(1)}, u32[]{:S(2)}, u32[]{:S(2)}) collective-permute-start(bf16[2,4,128,128]{3,2,1,0:T(8,128)(2,1)S(1)} %get-tuple-element.74), channel_id=1, source_target_pairs={{0,6},{2,4},{4,2},{6,0},{8,14},{10,12},{12,10},{14,8},{16,22},{18,... | collective-permute-start | bytes 786440 | tf_op jit(solution)/shard_map/ppermute | solution.py:284
  41.3 4.6 %shard_map.93.res_ref = bf16[4,1024,128]{2,1,0:T(8,128)(2,1)S(1)} custom-call(bf16[4,1024,128]{2,1,0:T(8,128)(2,1)S(1)} %get-tuple-element.75.ext_ref, s32[32,128]{1,0:T(8,128)S(1)} %bitcast.3), custom_call_target="tpu_custom_call" | custom-call | flops 1 | bytes 1 | tf_op jit(solution)/shard_map/pallas_call | solution.py:150
  46.0 1.6 %shard_map.94 = (bf16[2,4,128,128]{3,2,1,0:T(8,128)(2,1)S(1)}, bf16[2,4,128,128]{3,2,1,0:T(8,128)(2,1)S(1)}, bf16[2,4,128,128]{3,2,1,0:T(8,128)(2,1)S(1)}, bf16[2,4,128,128]{3,2,1,0:T(8,128)(2,1)S(1)}) custom-call(bf16[4,1024,128]{2,1,0:T(8,128)(2,1)S(1)} %get-tuple-element.75.ext_ref, bf16[4,256,128]{2,1,0:T(8,128)(2,1)S(1)} %collective-permute-done.14.even_ref, ...), custom_call_target="tpu_custom_call" | custom-call | flops 1 | bytes 1 | tf_op jit(solution)/shard_map/pallas_call | solution.py:150
  47.6 1.2 %collective-permute-start.16 = (bf16[2,4,128,128]{3,2,1,0:T(8,128)(2,1)S(1)}, bf16[2,4,128,128]{3,2,1,0:T(8,128)(2,1)S(1)}, u32[]{:S(2)}, u32[]{:S(2)}) collective-permute-start(bf16[2,4,128,128]{3,2,1,0:T(8,128)(2,1)S(1)} %get-tuple-element.79), channel_id=1, source_target_pairs={{0,2},{2,0},{4,6},{6,4},{8,10},{10,8},{12,14},{14,12},{16,18},{18,... | collective-permute-start | bytes 786440 | tf_op jit(solution)/shard_map/ppermute | solution.py:284
  48.8 0.3 collective-permute-start.17
  49.1 1.2 %collective-permute-start.18 = (bf16[2,4,128,128]{3,2,1,0:T(8,128)(2,1)S(1)}, bf16[2,4,128,128]{3,2,1,0:T(8,128)(2,1)S(1)}, u32[]{:S(2)}, u32[]{:S(2)}) collective-permute-start(bf16[2,4,128,128]{3,2,1,0:T(8,128)(2,1)S(1)} %get-tuple-element.81), channel_id=1, source_target_pairs={{0,6},{2,4},{4,2},{6,0},{8,14},{10,12},{12,10},{14,8},{16,22},{18,... | collective-permute-start | bytes 786440 | tf_op jit(solution)/shard_map/ppermute | solution.py:284
  50.3 4.9 %collective-permute-start.13 = (bf16[4,4,128,128]{3,2,1,0:T(8,128)(2,1)S(1)}, bf16[4,4,128,128]{3,2,1,0:T(8,128)(2,1)S(1)}, u32[]{:S(2)}, u32[]{:S(2)}) collective-permute-start(bf16[4,4,128,128]{3,2,1,0:T(8,128)(2,1)S(1)} %shard_map.92), channel_id=1, source_target_pairs={{0,1},{1,0},{2,3},{3,2},{4,5},{5,4},{6,7},{7,6},{8,9},{9,8},{10,11... | collective-permute-start | bytes 1572872 | tf_op jit(solution)/shard_map/ppermute | solution.py:339
  55.3 0.7 %collective-permute-done.16.refs_1_.refs_6_ = bf16[2,4,128,128]{3,2,1,0:T(8,128)(2,1)S(1)} collective-permute-done((bf16[2,4,128,128]{3,2,1,0:T(8,128)(2,1)S(1)}, bf16[2,4,128,128]{3,2,1,0:T(8,128)(2,1)S(1)}, u32[]{:S(2)}, u32[]{:S(2)}) %collective-permute-start.16) | collective-permute-done | bytes 262176 | tf_op jit(solution)/shard_map/ppermute | solution.py:284
  56.0 4.4 %collective-permute-done.17.refs_2_.refs_7_ = bf16[2,4,128,128]{3,2,1,0:T(8,128)(2,1)S(1)} collective-permute-done((bf16[2,4,128,128]{3,2,1,0:T(8,128)(2,1)S(1)}, bf16[2,4,128,128]{3,2,1,0:T(8,128)(2,1)S(1)}, u32[]{:S(2)}, u32[]{:S(2)}) %collective-permute-start.17) | collective-permute-done | bytes 262176 | tf_op jit(solution)/shard_map/ppermute | solution.py:284
  60.4 1.2 %collective-permute-done.18.refs_3_.refs_8_ = bf16[2,4,128,128]{3,2,1,0:T(8,128)(2,1)S(1)} collective-permute-done((bf16[2,4,128,128]{3,2,1,0:T(8,128)(2,1)S(1)}, bf16[2,4,128,128]{3,2,1,0:T(8,128)(2,1)S(1)}, u32[]{:S(2)}, u32[]{:S(2)}) %collective-permute-start.18) | collective-permute-done | bytes 262176 | tf_op jit(solution)/shard_map/ppermute | solution.py:284
  61.7 3.9 %collective-permute-start.19 = (bf16[4,4,128,128]{3,2,1,0:T(8,128)(2,1)S(1)}, bf16[4,4,128,128]{3,2,1,0:T(8,128)(2,1)S(1)}, u32[]{:S(2)}, u32[]{:S(2)}) collective-permute-start(bf16[4,4,128,128]{3,2,1,0:T(8,128)(2,1)S(1)} %shard_map.95), channel_id=1, source_target_pairs={{0,1},{1,0},{2,3},{3,2},{4,5},{5,4},{6,7},{7,6},{8,9},{9,8},{10,11... | collective-permute-start | bytes 1572872 | tf_op jit(solution)/shard_map/ppermute | solution.py:339
  65.5 1.5 %collective-permute-done.19.refs_9_ = bf16[4,4,128,128]{3,2,1,0:T(8,128)(2,1)S(1)} collective-permute-done((bf16[4,4,128,128]{3,2,1,0:T(8,128)(2,1)S(1)}, bf16[4,4,128,128]{3,2,1,0:T(8,128)(2,1)S(1)}, u32[]{:S(2)}, u32[]{:S(2)}) %collective-permute-start.19) | collective-permute-done | bytes 524320 | tf_op jit(solution)/shard_map/ppermute | solution.py:339
  67.1 1.5 %shard_map.96 = (bf16[128,2048]{1,0:T(8,128)(2,1)}, bf16[128,2048]{1,0:T(8,128)(2,1)}, bf16[128,2048]{1,0:T(8,128)(2,1)}, bf16[128,2048]{1,0:T(8,128)(2,1)}) custom-call(bf16[2,4,128,128]{3,2,1,0:T(8,128)(2,1)S(1)} %get-tuple-element.71.refs_0_, bf16[2,4,128,128]{3,2,1,0:T(8,128)(2,1)S(1)} %collective-permute-done.10.refs_1_, ...), custom_call_target="tpu_custom_call" | custom-call | tf_op jit(solution)/shard_map/pallas_call | solution.py:248
  (27 shorter events, 0.8 us)
Async XLA Ops:
  3.3 3.4 %copy-start.1 = (bf16[4,4,128,128]{3,2,1,0:T(8,128)(2,1)S(1)}, bf16[4,4,128,128]{3,2,1,0:T(8,128)(2,1)}, u32[]{:S(2)}) copy-start(bf16[4,4,128,128]{3,2,1,0:T(8,128)(2,1)} %get-tuple-element.43.mine_ref) | copy-start | bytes 1572868
  3.3 3.4 %collective-permute-start = (bf16[4,4,128,128]{3,2,1,0:T(8,128)(2,1)}, bf16[4,4,128,128]{3,2,1,0:T(8,128)(2,1)S(1)}, u32[]{:S(2)}, u32[]{:S(2)}) collective-permute-start(bf16[4,4,128,128]{3,2,1,0:T(8,128)(2,1)} %get-tuple-element.44), channel_id=1, source_target_pairs={{0,1},{1,0},{2,3},{3,2},{4,5},{5,4},{6,7},{7,6},{8,9},{9,8},{10,11... | collective-permute-start | bytes 1572872 | tf_op jit(solution)/shard_map/ppermute | solution.py:298
  6.5 2.9 %collective-permute-start.4 = (bf16[4,4,128,128]{3,2,1,0:T(8,128)(2,1)}, bf16[4,4,128,128]{3,2,1,0:T(8,128)(2,1)S(1)}, u32[]{:S(2)}, u32[]{:S(2)}) collective-permute-start(bf16[4,4,128,128]{3,2,1,0:T(8,128)(2,1)} %get-tuple-element.51), channel_id=1, source_target_pairs={{0,1},{1,0},{2,3},{3,2},{4,5},{5,4},{6,7},{7,6},{8,9},{9,8},{10,11... | collective-permute-start | bytes 1572872 | tf_op jit(solution)/shard_map/ppermute | solution.py:298
  6.6 2.8 %copy-start = (bf16[4,4,128,128]{3,2,1,0:T(8,128)(2,1)S(1)}, bf16[4,4,128,128]{3,2,1,0:T(8,128)(2,1)}, u32[]{:S(2)}) copy-start(bf16[4,4,128,128]{3,2,1,0:T(8,128)(2,1)} %get-tuple-element.50.mine_ref) | copy-start | bytes 1572868
  6.7 7.5 %collective-permute-start.1 = (bf16[2,4,128,128]{3,2,1,0:T(8,128)(2,1)S(1)}, bf16[2,4,128,128]{3,2,1,0:T(8,128)(2,1)S(1)}, u32[]{:S(2)}, u32[]{:S(2)}) collective-permute-start(bf16[2,4,128,128]{3,2,1,0:T(8,128)(2,1)S(1)} %get-tuple-element.46), channel_id=1, source_target_pairs={{0,2},{2,0},{4,6},{6,4},{8,10},{10,8},{12,14},{14,12},{16,18},{18,... | collective-permute-start | bytes 786440 | tf_op jit(solution)/shard_map/ppermute | solution.py:284
  8.0 8.4 %collective-permute-start.2 = (bf16[2,4,128,128]{3,2,1,0:T(8,128)(2,1)S(1)}, bf16[2,4,128,128]{3,2,1,0:T(8,128)(2,1)S(1)}, u32[]{:S(2)}, u32[]{:S(2)}) collective-permute-start(bf16[2,4,128,128]{3,2,1,0:T(8,128)(2,1)S(1)} %get-tuple-element.47), channel_id=1, source_target_pairs={{0,4},{2,6},{4,0},{6,2},{8,12},{10,14},{12,8},{14,10},{16,20},{18,... | collective-permute-start | bytes 786440 | tf_op jit(solution)/shard_map/ppermute | solution.py:284
  9.2 11.6 %collective-permute-start.3 = (bf16[2,4,128,128]{3,2,1,0:T(8,128)(2,1)S(1)}, bf16[2,4,128,128]{3,2,1,0:T(8,128)(2,1)S(1)}, u32[]{:S(2)}, u32[]{:S(2)}) collective-permute-start(bf16[2,4,128,128]{3,2,1,0:T(8,128)(2,1)S(1)} %get-tuple-element.48), channel_id=1, source_target_pairs={{0,6},{2,4},{4,2},{6,0},{8,14},{10,12},{12,10},{14,8},{16,22},{18,... | collective-permute-start | bytes 786440 | tf_op jit(solution)/shard_map/ppermute | solution.py:284
  9.5 20.6 %collective-permute-start.5 = (bf16[2,4,128,128]{3,2,1,0:T(8,128)(2,1)S(1)}, bf16[2,4,128,128]{3,2,1,0:T(8,128)(2,1)S(1)}, u32[]{:S(2)}, u32[]{:S(2)}) collective-permute-start(bf16[2,4,128,128]{3,2,1,0:T(8,128)(2,1)S(1)} %get-tuple-element.53), channel_id=1, source_target_pairs={{0,2},{2,0},{4,6},{6,4},{8,10},{10,8},{12,14},{14,12},{16,18},{18,... | collective-permute-start | bytes 786440 | tf_op jit(solution)/shard_map/ppermute | solution.py:284
  10.8 19.4 %collective-permute-start.6 = (bf16[2,4,128,128]{3,2,1,0:T(8,128)(2,1)S(1)}, bf16[2,4,128,128]{3,2,1,0:T(8,128)(2,1)S(1)}, u32[]{:S(2)}, u32[]{:S(2)}) collective-permute-start(bf16[2,4,128,128]{3,2,1,0:T(8,128)(2,1)S(1)} %get-tuple-element.54), channel_id=1, source_target_pairs={{0,4},{2,6},{4,0},{6,2},{8,12},{10,14},{12,8},{14,10},{16,20},{18,... | collective-permute-start | bytes 786440 | tf_op jit(solution)/shard_map/ppermute | solution.py:284
  14.2 17.9 %collective-permute-start.7 = (bf16[2,4,128,128]{3,2,1,0:T(8,128)(2,1)S(1)}, bf16[2,4,128,128]{3,2,1,0:T(8,128)(2,1)S(1)}, u32[]{:S(2)}, u32[]{:S(2)}) collective-permute-start(bf16[2,4,128,128]{3,2,1,0:T(8,128)(2,1)S(1)} %get-tuple-element.55), channel_id=1, source_target_pairs={{0,6},{2,4},{4,2},{6,0},{8,14},{10,12},{12,10},{14,8},{16,22},{18,... | collective-permute-start | bytes 786440 | tf_op jit(solution)/shard_map/ppermute | solution.py:284
  20.8 4.7 %copy-start.2 = (s32[4096]{0:T(1024)S(1)}, s32[4096]{0:T(1024)}, u32[]{:S(2)}) copy-start(s32[4096]{0:T(1024)} %param.9) | copy-start | bytes 49156
  21.0 11.3 %collective-permute-start.8 = (bf16[4,256,128]{2,1,0:T(8,128)(2,1)S(1)}, bf16[4,256,128]{2,1,0:T(8,128)(2,1)S(1)}, u32[]{:S(2)}, u32[]{:S(2)}) collective-permute-start(bf16[4,256,128]{2,1,0:T(8,128)(2,1)S(1)} %get-tuple-element.64), channel_id=1, source_target_pairs={{0,8},{8,0},{2,10},{10,2},{4,12},{12,4},{6,14},{14,6},{16,24},{24,... | collective-permute-start | bytes 786440 | tf_op jit(solution)/shard_map/ppermute | solution.py:313
  21.2 11.1 %collective-permute-start.9 = (bf16[4,256,128]{2,1,0:T(8,128)(2,1)S(1)}, bf16[4,256,128]{2,1,0:T(8,128)(2,1)S(1)}, u32[]{:S(2)}, u32[]{:S(2)}) collective-permute-start(bf16[4,256,128]{2,1,0:T(8,128)(2,1)S(1)} %get-tuple-element.65), channel_id=1, source_target_pairs={{8,16},{16,8},{10,18},{18,10},{12,20},{20,12},{14,22},{22,14},{9,1... | collective-permute-start | bytes 786440 | tf_op jit(solution)/shard_map/ppermute | solution.py:314
  33.9 12.1 %collective-permute-start.14 = (bf16[4,256,128]{2,1,0:T(8,128)(2,1)S(1)}, bf16[4,256,128]{2,1,0:T(8,128)(2,1)S(1)}, u32[]{:S(2)}, u32[]{:S(2)}) collective-permute-start(bf16[4,256,128]{2,1,0:T(8,128)(2,1)S(1)} %get-tuple-element.76), channel_id=1, source_target_pairs={{0,8},{8,0},{2,10},{10,2},{4,12},{12,4},{6,14},{14,6},{16,24},{24,... | collective-permute-start | bytes 786440 | tf_op jit(solution)/shard_map/ppermute | solution.py:313
  34.1 11.8 %collective-permute-start.15 = (bf16[4,256,128]{2,1,0:T(8,128)(2,1)S(1)}, bf16[4,256,128]{2,1,0:T(8,128)(2,1)S(1)}, u32[]{:S(2)}, u32[]{:S(2)}) collective-permute-start(bf16[4,256,128]{2,1,0:T(8,128)(2,1)S(1)} %get-tuple-element.77), channel_id=1, source_target_pairs={{8,16},{16,8},{10,18},{18,10},{12,20},{20,12},{14,22},{22,14},{9,1... | collective-permute-start | bytes 786440 | tf_op jit(solution)/shard_map/ppermute | solution.py:314
  38.6 10.5 %collective-permute-start.10 = (bf16[2,4,128,128]{3,2,1,0:T(8,128)(2,1)S(1)}, bf16[2,4,128,128]{3,2,1,0:T(8,128)(2,1)S(1)}, u32[]{:S(2)}, u32[]{:S(2)}) collective-permute-start(bf16[2,4,128,128]{3,2,1,0:T(8,128)(2,1)S(1)} %get-tuple-element.72), channel_id=1, source_target_pairs={{0,2},{2,0},{4,6},{6,4},{8,10},{10,8},{12,14},{14,12},{16,18},{18,... | collective-permute-start | bytes 786440 | tf_op jit(solution)/shard_map/ppermute | solution.py:284
  39.8 10.4 %collective-permute-start.11 = (bf16[2,4,128,128]{3,2,1,0:T(8,128)(2,1)S(1)}, bf16[2,4,128,128]{3,2,1,0:T(8,128)(2,1)S(1)}, u32[]{:S(2)}, u32[]{:S(2)}) collective-permute-start(bf16[2,4,128,128]{3,2,1,0:T(8,128)(2,1)S(1)} %get-tuple-element.73), channel_id=1, source_target_pairs={{0,4},{2,6},{4,0},{6,2},{8,12},{10,14},{12,8},{14,10},{16,20},{18,... | collective-permute-start | bytes 786440 | tf_op jit(solution)/shard_map/ppermute | solution.py:284
  40.1 10.2 %collective-permute-start.12 = (bf16[2,4,128,128]{3,2,1,0:T(8,128)(2,1)S(1)}, bf16[2,4,128,128]{3,2,1,0:T(8,128)(2,1)S(1)}, u32[]{:S(2)}, u32[]{:S(2)}) collective-permute-start(bf16[2,4,128,128]{3,2,1,0:T(8,128)(2,1)S(1)} %get-tuple-element.74), channel_id=1, source_target_pairs={{0,6},{2,4},{4,2},{6,0},{8,14},{10,12},{12,10},{14,8},{16,22},{18,... | collective-permute-start | bytes 786440 | tf_op jit(solution)/shard_map/ppermute | solution.py:284
  47.6 8.5 %collective-permute-start.16 = (bf16[2,4,128,128]{3,2,1,0:T(8,128)(2,1)S(1)}, bf16[2,4,128,128]{3,2,1,0:T(8,128)(2,1)S(1)}, u32[]{:S(2)}, u32[]{:S(2)}) collective-permute-start(bf16[2,4,128,128]{3,2,1,0:T(8,128)(2,1)S(1)} %get-tuple-element.79), channel_id=1, source_target_pairs={{0,2},{2,0},{4,6},{6,4},{8,10},{10,8},{12,14},{14,12},{16,18},{18,... | collective-permute-start | bytes 786440 | tf_op jit(solution)/shard_map/ppermute | solution.py:284
  48.8 11.6 %collective-permute-start.17 = (bf16[2,4,128,128]{3,2,1,0:T(8,128)(2,1)S(1)}, bf16[2,4,128,128]{3,2,1,0:T(8,128)(2,1)S(1)}, u32[]{:S(2)}, u32[]{:S(2)}) collective-permute-start(bf16[2,4,128,128]{3,2,1,0:T(8,128)(2,1)S(1)} %get-tuple-element.80), channel_id=1, source_target_pairs={{0,4},{2,6},{4,0},{6,2},{8,12},{10,14},{12,8},{14,10},{16,20},{18,... | collective-permute-start | bytes 786440 | tf_op jit(solution)/shard_map/ppermute | solution.py:284
  49.1 12.5 %collective-permute-start.18 = (bf16[2,4,128,128]{3,2,1,0:T(8,128)(2,1)S(1)}, bf16[2,4,128,128]{3,2,1,0:T(8,128)(2,1)S(1)}, u32[]{:S(2)}, u32[]{:S(2)}) collective-permute-start(bf16[2,4,128,128]{3,2,1,0:T(8,128)(2,1)S(1)} %get-tuple-element.81), channel_id=1, source_target_pairs={{0,6},{2,4},{4,2},{6,0},{8,14},{10,12},{12,10},{14,8},{16,22},{18,... | collective-permute-start | bytes 786440 | tf_op jit(solution)/shard_map/ppermute | solution.py:284
  50.3 15.2 %collective-permute-start.13 = (bf16[4,4,128,128]{3,2,1,0:T(8,128)(2,1)S(1)}, bf16[4,4,128,128]{3,2,1,0:T(8,128)(2,1)S(1)}, u32[]{:S(2)}, u32[]{:S(2)}) collective-permute-start(bf16[4,4,128,128]{3,2,1,0:T(8,128)(2,1)S(1)} %shard_map.92), channel_id=1, source_target_pairs={{0,1},{1,0},{2,3},{3,2},{4,5},{5,4},{6,7},{7,6},{8,9},{9,8},{10,11... | collective-permute-start | bytes 1572872 | tf_op jit(solution)/shard_map/ppermute | solution.py:339
  61.7 5.4 %collective-permute-start.19 = (bf16[4,4,128,128]{3,2,1,0:T(8,128)(2,1)S(1)}, bf16[4,4,128,128]{3,2,1,0:T(8,128)(2,1)S(1)}, u32[]{:S(2)}, u32[]{:S(2)}) collective-permute-start(bf16[4,4,128,128]{3,2,1,0:T(8,128)(2,1)S(1)} %shard_map.95), channel_id=1, source_target_pairs={{0,1},{1,0},{2,3},{3,2},{4,5},{5,4},{6,7},{7,6},{8,9},{9,8},{10,11... | collective-permute-start | bytes 1572872 | tf_op jit(solution)/shard_map/ppermute | solution.py:339

commit v5 on v4

--- a/solution.py
+++ b/solution.py
@@ -12,8 +12,8 @@
 DOC_MOST = 256
 MASKED = -1e30
 GROUP = 4
-IN_APART = (False, False)
-OUT_APART = (False, False)
+ORDER_IN = (0, 3, 2, 1)
+ORDER_OUT = (0, 2, 1, 3)
 SCALE = 1.0 / math.sqrt(DH)
 VMEM = 12 * 1024 * 1024
 PACK_VMEM = 56 * 1024 * 1024
@@ -40,13 +40,14 @@
     weights = jnp.exp2(scores - top)
     probs = weights * (1.0 / jnp.sum(weights, axis=0, keepdims=True))
     low = probs.astype(jnp.bfloat16)
-    attended = dot_tn(values, low).astype(jnp.bfloat16).astype(jnp.float32)
-    delta = jnp.sum(attended * grads.T.astype(jnp.float32), axis=0, keepdims=True)
-    score_grad = (probs * (dot_nt(values, grads) - delta)).astype(jnp.bfloat16)
+    weighted = probs * dot_nt(values, grads)
+    delta = jnp.sum(weighted, axis=0, keepdims=True)
+    score_grad = (weighted - probs * delta).astype(jnp.bfloat16)
+    attended = dot_tn(values, low).T
     query_grad = (dot_tn(keys, score_grad) * SCALE).T
     key_grad = dot_nn(score_grad, queries) * SCALE
     value_grad = dot_nn(low, grads)
-    return attended.T, query_grad, key_grad, value_grad
+    return attended, query_grad, key_grad, value_grad
 
 
 def tile_ids(table_ref, first):
@@ -102,7 +103,7 @@
             put(t, from_high, results)
 
 
-def edge_kernel(edge, apart, ext_ref, even_ref, odd_ref, res_ref, table_ref, *refs):
+def edge_kernel(edge, ext_ref, even_ref, odd_ref, res_ref, table_ref, *refs):
     outs, result_ref = refs[:-1], refs[-1]
     rows = ext_ref.shape[1]
     position, core = lax.axis_index("blk"), lax.axis_index("head")
@@ -135,11 +136,7 @@
     for s in range(GROUP):
         for piece in range(2):
             first = pl.multiple_of(((place ^ s) * 2 + (core ^ piece)) * half, half)
-            block = result_ref[:, pl.ds(first, half), :]
-            if apart:
-                outs[2 * s + piece][...] = block
-            else:
-                outs[s][piece] = block
+            outs[s][piece] = result_ref[:, pl.ds(first, half), :]
 
 
 def shape(*dims, dtype=jnp.bfloat16):
@@ -158,7 +155,7 @@
     )(*args)
 
 
-def pack_kernel(j, chunks, apart, *refs):
+def pack_kernel(j, chunks, *refs):
     ins, outs = refs[:4], refs[4:]
     block, width = ins[0].shape
     core, place = lax.axis_index("head"), lax.axis_index("blk") % GROUP
@@ -168,19 +165,15 @@
             base = (core ^ which) * (width // 2) + ((place ^ s) * chunks + j) * DH
             first = pl.multiple_of(base, DH)
             for m, ref in enumerate(ins):
-                part = ref[:, pl.ds(first, DH)]
-                if apart:
-                    outs[2 * s + which][m, at] = part
-                else:
-                    outs[which][s, m, at] = part
-
-
-def pack(arrays, j, chunks, apart):
+                outs[which][s, m, at] = ref[:, pl.ds(first, DH)]
+
+
+def pack(arrays, j, chunks):
     rows, width = arrays[0].shape
     block = rows // PACK_STEPS
-    outs = [shape(4, rows, DH)] * (2 * GROUP) if apart else [shape(GROUP, 4, rows, DH)] * 2
+    outs = [shape(GROUP, 4, rows, DH)] * 2
     return pl.pallas_call(
-        functools.partial(pack_kernel, j, chunks, apart),
+        functools.partial(pack_kernel, j, chunks),
         grid=(PACK_STEPS,),
         out_shape=outs,
         in_specs=[pl.BlockSpec((block, width), lambda i: (i, 0))] * 4,
@@ -195,16 +188,16 @@
         out[1] = received_ref[s]
 
 
-def gather_kernel(apart, *refs):
+def gather_kernel(*refs):
     slots, (ext, to_even, to_odd) = refs[:-3], refs[-3:]
     edge = to_even.shape[1]
     half = edge // 2
     position, core = lax.axis_index("blk"), lax.axis_index("head")
     place, parity = position % GROUP, (position // GROUP) % 2
-    for s in range(GROUP):
+    for s, slot in zip(ORDER_IN, slots):
         for piece in range(2):
             first = pl.multiple_of(((place ^ s) * 2 + (core ^ piece)) * half, half)
-            ext[:, pl.ds(first, half), :] = slots[2 * s + piece][...] if apart else slots[s][piece]
+            ext[:, pl.ds(first, half), :] = slot[piece]
     rows = ext.shape[1]
     first = pl.multiple_of((rows - edge) * (1 - parity), edge)
     to_even[...] = ext[:, pl.ds(first, edge), :]
@@ -214,25 +207,20 @@
 
 def split_kernel(*refs):
     slots, out = refs[:-1], refs[-1]
-    for s, slot in enumerate(slots):
+    for s, slot in zip(ORDER_OUT, slots):
         out[s] = slot[1]
 
 
-def unpack_kernel(aparts, *refs):
-    ins, outs, held, sems = list(refs[:-6]), refs[-6:-2], refs[-2], refs[-1]
+def unpack_kernel(chunks, *refs):
+    ins, outs, held, sems = refs[:-6], refs[-6:-2], refs[-2], refs[-1]
     width = outs[0].shape[1]
-    chunks = len(aparts)
     core, place = lax.axis_index("head"), lax.axis_index("blk") % GROUP
     blocks = []
-    for j, apart in enumerate(aparts):
-        slots, ins = (ins[: 2 * GROUP], ins[2 * GROUP :]) if apart else (ins[: GROUP + 1], ins[GROUP + 1 :])
-        for s in range(GROUP):
-            for which in range(2):
+    for j in range(chunks):
+        *slots, received = ins[j * (GROUP + 1) : (j + 1) * (GROUP + 1)]
+        for s, slot in zip(ORDER_OUT, slots):
+            for which, block in enumerate((slot.at[0], received.at[s])):
                 base = (core ^ which) * (width // 2) + ((place ^ s) * chunks + j) * DH
-                if apart:
-                    block = slots[2 * s + which]
-                else:
-                    block = slots[GROUP].at[s] if which else slots[s].at[0]
                 blocks.append((pl.multiple_of(base, DH), block))
     copies = [pltpu.make_async_copy(held.at[m], out, sems.at[m]) for m, out in enumerate(outs)]
     for m, copy in enumerate(copies):
@@ -243,10 +231,10 @@
         copy.wait()
 
 
-def unpack(chunks, aparts, rows, width):
+def unpack(chunks, rows, width):
     blocks = [block for chunk in chunks for block in chunk]
     return pl.pallas_call(
-        functools.partial(unpack_kernel, aparts),
+        functools.partial(unpack_kernel, len(chunks)),
         out_shape=[shape(rows, width)] * 4,
         in_specs=[WHOLE] * len(blocks),
         out_specs=[pl.BlockSpec(memory_space=pl.ANY)] * 4,
@@ -265,7 +253,7 @@
     chunks = heads // (2 * GROUP)
     edge = 2 * half
     rows = GROUP * edge
-    assert edge >= DOC_MOST and positions % GROUP == 0 and chunks == len(IN_APART)
+    assert edge >= DOC_MOST and positions % GROUP == 0 and chunks == 2
     swap = [(0, 1), (1, 0)]
     planes = positions // GROUP
 
@@ -277,34 +265,26 @@
                 route += [(here, there), (there, here)]
         return route
 
-    def hop(block, s, cross=0):
-        if s == 0:
-            return lax.ppermute(block, "head", swap) if cross else block
-        if not cross:
-            return lax.ppermute(block, "blk", [(i, i ^ s) for i in range(positions)])
-        route = [(2 * i + k, 2 * (i ^ s) + 1 - k) for i in range(positions) for k in range(2)]
-        return lax.ppermute(block, ("blk", "head"), route)
+    def hop(block, s):
+        return lax.ppermute(block, "blk", [(i, i ^ s) for i in range(positions)]) if s else block
 
     table = doc_ids.reshape(-1, half)
     inputs = (query_rows, key_rows, value_rows, out_grad)
     unit = 2 * DH * edge * edge * 6
 
     arrived = []
-    for j, apart in enumerate(IN_APART):
-        packed = pack(inputs, j, chunks, apart)
-        if apart:
-            arrived.append([hop(block, *divmod(i, 2)) for i, block in enumerate(packed)])
-        else:
-            theirs = lax.ppermute(packed[1], "head", swap)
-            joined = call(join_kernel, [shape(2, 4, half, DH)] * GROUP, packed[0], theirs)
-            arrived.append([hop(block, s) for s, block in enumerate(joined)])
+    for j in range(chunks):
+        mine, other = pack(inputs, j, chunks)
+        theirs = lax.ppermute(other, "head", swap)
+        joined = call(join_kernel, [shape(2, 4, half, DH)] * GROUP, mine, theirs)
+        arrived.append([hop(joined[s], s) for s in ORDER_IN])
 
     def gather(j, *after):
         slots = arrived[j]
         if after:
             slots, _ = lax.optimization_barrier((slots, after))
         return call(
-            functools.partial(gather_kernel, IN_APART[j]),
+            gather_kernel,
             [shape(4, rows, DH), shape(4, edge, DH), shape(4, edge, DH)],
             *slots,
         )
@@ -318,11 +298,10 @@
             functools.partial(interior_kernel, edge), shape(4, rows, DH), ext, table
         )
 
-    def finish(j, ext, even, odd, res):
-        apart = OUT_APART[j]
+    def finish(ext, even, odd, res):
         return call(
-            functools.partial(edge_kernel, edge, apart),
-            [shape(4, half, DH)] * (2 * GROUP) if apart else [shape(2, 4, half, DH)] * GROUP,
+            functools.partial(edge_kernel, edge),
+            [shape(2, 4, half, DH)] * GROUP,
             ext,
             even,
             odd,
@@ -331,10 +310,10 @@
             scratch=[pltpu.VMEM((4, rows, DH), jnp.bfloat16)],
         )
 
-    def give_back(j, back):
-        if OUT_APART[j]:
-            return [hop(block, *divmod(i, 2)) for i, block in enumerate(back)]
-        back = [hop(block, s) for s, block in enumerate(back)]
+    def give_back(back):
+        return [hop(back[s], s) for s in ORDER_OUT]
+
+    def swap_back(back):
         away = call(split_kernel, shape(GROUP, 4, half, DH), *back)
         return back + [lax.ppermute(away, "head", swap)]
 
@@ -343,13 +322,18 @@
     res_a = interior(ext_a)
     ext_b, *edges_b = gather(1, res_a)
     res_a, ext_b = lax.optimization_barrier((res_a, ext_b))
-    back_a = finish(0, ext_a, *halo_a, res_a)
+    back_a = finish(ext_a, *halo_a, res_a)
     ext_b, edges_b, back_a = lax.optimization_barrier((ext_b, edges_b, back_a))
     halo_b = halo(*edges_b)
     res_b = interior(ext_b)
-    back_b = finish(1, ext_b, *halo_b, res_b)
-    results = [give_back(0, back_a), give_back(1, back_b)]
-    return tuple(unpack(results, OUT_APART, half, width))
+    out_a = give_back(back_a)
+    res_b, tied = lax.optimization_barrier((res_b, [out_a[i] for i in (1, 2)]))
+    for i, block in zip((1, 2), tied):
+        out_a[i] = block
+    back_b = finish(ext_b, *halo_b, res_b)
+    out_b = give_back(back_b)
+    results = [swap_back(out_a), swap_back(out_b)]
+    return tuple(unpack(results, half, width))
 
 
 def solution(mesh):

time: 68.9 us -> 65.7 us (0.954)
  Pallas kernels: 19.6 us -> 16.2 us
  waiting for transfers between devices: 16.5 us -> 19.7 us
  starting transfers between devices: 31.7 us -> 28.6 us
    pallas_call x10, Pallas kernels: 12.9 us -> 9.49 us  [call(): pl.pallas_call(kernel, out_shape=out_shape, in_specs=[WHOLE] * len(args),...]
    ppermute x16, waiting for transfers between devices: 16.5 us -> 19.5 us  [the longest x12 18 us: hop(): lax.ppermute(block, 'blk', [(i, i ^ s) for i in range(positions)])]
    ppermute x16, starting transfers between devices: 22.4 us -> 19.5 us  [the longest x12 12.3 us: hop(): lax.ppermute(block, 'blk', [(i, i ^ s) for i in range(positions)])]
  transfers between devices with their start and end apart: 20 -> 20, of which waited for: 7 -> 8; matrix products, arithmetic and copies ran while one was open for 0% -> 0% of each run, Pallas kernels for 20% -> 17%
where the time goes in v5:
time: 65.7 us; the launch traced here: 65.3 us
  starting transfers between devices  28.6 us (44%)
  waiting for transfers between devices  19.7 us (30%)
  Pallas kernels  16.2 us (25%)
  between operations  0.79 us (1%)
    ppermute x12, waiting for transfers between devices, hop(): lax.ppermute(block, 'blk', [(i, i ^ s) for i in range(positions)])  18 us
    ppermute x12, starting transfers between devices, hop(): lax.ppermute(block, 'blk', [(i, i ^ s) for i in range(positions)])  12.3 us
    pallas_call x10, Pallas kernels, call(): pl.pallas_call(kernel, out_shape=out_shape, in_specs=[WHOLE] * len(args),...  9.49 us
    ppermute x2, starting transfers between devices, halo(): return (even, lax.ppermute(to_odd, 'blk', plane_pairs(1)))  8.8 us
    ppermute x2, starting transfers between devices, swap_back(): return back + [lax.ppermute(away, 'head', swap)]  6.51 us
    pallas_call x2, Pallas kernels, pack(): pl.pallas_call(functools.partial(pack_kernel, j, chunks), grid=(PACK_STEP...  5.23 us
    ppermute x2, waiting for transfers between devices, swap_back(): return back + [lax.ppermute(away, 'head', swap)]  1.54 us
    pallas_call x1, Pallas kernels, unpack(): pl.pallas_call(functools.partial(unpack_kernel, len(chunks)), out_shape=[...  1.5 us
  transfers between devices with their start and end apart: 20, of which 8 were waited for; matrix products, arithmetic and copies ran while one was open for 0% of the time, Pallas kernels for 17%

profile of v5, /device:TPU:9, one launch (start us, length us, event | category | flops | bytes accessed | tf_op | source)
XLA Modules:
  0.0 65.3 jit_solution(9288395447108163970)
XLA Ops:
  0.6 2.6 %shard_map.84 = (bf16[4,4,128,128]{3,2,1,0:T(8,128)(2,1)}, bf16[4,4,128,128]{3,2,1,0:T(8,128)(2,1)}) custom-call(bf16[128,2048]{1,0:T(8,128)(2,1)} %refs_0_.3, bf16[128,2048]{1,0:T(8,128)(2,1)} %refs_1_.3, bf16[128,2048]{1,0:T(8,128)(2,1)} %refs_2_.3, bf16[128,2048]{1,0:T(8,128)(2,1)} %refs_3_.3), custom_call_target="tpu_custom_call" | custom-call | tf_op jit(solution)/shard_map/pallas_call | solution.py:175
  3.3 0.7 %collective-permute-start = (bf16[4,4,128,128]{3,2,1,0:T(8,128)(2,1)}, bf16[4,4,128,128]{3,2,1,0:T(8,128)(2,1)S(1)}, u32[]{:S(2)}, u32[]{:S(2)}) collective-permute-start(bf16[4,4,128,128]{3,2,1,0:T(8,128)(2,1)} %get-tuple-element.47), channel_id=1, source_target_pairs={{0,1},{1,0},{2,3},{3,2},{4,5},{5,4},{6,7},{7,6},{8,9},{9,8},{10,11... | collective-permute-start | bytes 1572872 | tf_op jit(solution)/shard_map/ppermute | solution.py:278
  3.9 2.6 %shard_map.88 = (bf16[4,4,128,128]{3,2,1,0:T(8,128)(2,1)}, bf16[4,4,128,128]{3,2,1,0:T(8,128)(2,1)}) custom-call(bf16[128,2048]{1,0:T(8,128)(2,1)} %refs_0_.3, bf16[128,2048]{1,0:T(8,128)(2,1)} %refs_1_.3, bf16[128,2048]{1,0:T(8,128)(2,1)} %refs_2_.3, bf16[128,2048]{1,0:T(8,128)(2,1)} %refs_3_.3), custom_call_target="tpu_custom_call" | custom-call | tf_op jit(solution)/shard_map/pallas_call | solution.py:175
  6.7 2.2 %collective-permute-start.1 = (bf16[2,4,128,128]{3,2,1,0:T(8,128)(2,1)S(1)}, bf16[2,4,128,128]{3,2,1,0:T(8,128)(2,1)S(1)}, u32[]{:S(2)}, u32[]{:S(2)}) collective-permute-start(bf16[2,4,128,128]{3,2,1,0:T(8,128)(2,1)S(1)} %get-tuple-element.49), channel_id=1, source_target_pairs={{0,6},{2,4},{4,2},{6,0},{8,14},{10,12},{12,10},{14,8},{16,22},{18,... | collective-permute-start | bytes 786440 | tf_op jit(solution)/shard_map/ppermute | solution.py:269
  8.9 0.2 collective-permute-start.2
  9.2 0.3 collective-permute-start.3
  9.5 2.2 %collective-permute-start.5 = (bf16[2,4,128,128]{3,2,1,0:T(8,128)(2,1)S(1)}, bf16[2,4,128,128]{3,2,1,0:T(8,128)(2,1)S(1)}, u32[]{:S(2)}, u32[]{:S(2)}) collective-permute-start(bf16[2,4,128,128]{3,2,1,0:T(8,128)(2,1)S(1)} %get-tuple-element.56), channel_id=1, source_target_pairs={{0,6},{2,4},{4,2},{6,0},{8,14},{10,12},{12,10},{14,8},{16,22},{18,... | collective-permute-start | bytes 786440 | tf_op jit(solution)/shard_map/ppermute | solution.py:269
  11.7 0.2 collective-permute-start.6
  12.0 3.2 %collective-permute-done.1.refs_1_ = bf16[2,4,128,128]{3,2,1,0:T(8,128)(2,1)S(1)} collective-permute-done((bf16[2,4,128,128]{3,2,1,0:T(8,128)(2,1)S(1)}, bf16[2,4,128,128]{3,2,1,0:T(8,128)(2,1)S(1)}, u32[]{:S(2)}, u32[]{:S(2)}) %collective-permute-start.1) | collective-permute-done | bytes 262176 | tf_op jit(solution)/shard_map/ppermute | solution.py:269
  15.1 1.2 %collective-permute-start.7 = (bf16[2,4,128,128]{3,2,1,0:T(8,128)(2,1)S(1)}, bf16[2,4,128,128]{3,2,1,0:T(8,128)(2,1)S(1)}, u32[]{:S(2)}, u32[]{:S(2)}) collective-permute-start(bf16[2,4,128,128]{3,2,1,0:T(8,128)(2,1)S(1)} %get-tuple-element.58), channel_id=1, source_target_pairs={{0,2},{2,0},{4,6},{6,4},{8,10},{10,8},{12,14},{14,12},{16,18},{18,... | collective-permute-start | bytes 786440 | tf_op jit(solution)/shard_map/ppermute | solution.py:269
  16.4 5.9 %collective-permute-done.2.refs_2_ = bf16[2,4,128,128]{3,2,1,0:T(8,128)(2,1)S(1)} collective-permute-done((bf16[2,4,128,128]{3,2,1,0:T(8,128)(2,1)S(1)}, bf16[2,4,128,128]{3,2,1,0:T(8,128)(2,1)S(1)}, u32[]{:S(2)}, u32[]{:S(2)}) %collective-permute-start.2) | collective-permute-done | bytes 262176 | tf_op jit(solution)/shard_map/ppermute | solution.py:269
  22.2 0.1 shard_map.86
  22.5 4.5 %collective-permute-start.9 = (bf16[4,256,128]{2,1,0:T(8,128)(2,1)S(1)}, bf16[4,256,128]{2,1,0:T(8,128)(2,1)S(1)}, u32[]{:S(2)}, u32[]{:S(2)}) collective-permute-start(bf16[4,256,128]{2,1,0:T(8,128)(2,1)S(1)} %get-tuple-element.68), channel_id=1, source_target_pairs={{8,16},{16,8},{10,18},{18,10},{12,20},{20,12},{14,22},{22,14},{9,1... | collective-permute-start | bytes 786440 | tf_op jit(solution)/shard_map/ppermute | solution.py:294
  26.9 3.2 %shard_map.87.res_ref = bf16[4,1024,128]{2,1,0:T(8,128)(2,1)S(1)} custom-call(bf16[4,1024,128]{2,1,0:T(8,128)(2,1)S(1)} %get-tuple-element.52.ext_ref, s32[32,128]{1,0:T(8,128)S(1)} %bitcast.1), custom_call_target="tpu_custom_call" | custom-call | flops 1 | bytes 1 | tf_op jit(solution)/shard_map/pallas_call | solution.py:147
  30.2 2.5 %collective-permute-done.6.refs_2_ = bf16[2,4,128,128]{3,2,1,0:T(8,128)(2,1)S(1)} collective-permute-done((bf16[2,4,128,128]{3,2,1,0:T(8,128)(2,1)S(1)}, bf16[2,4,128,128]{3,2,1,0:T(8,128)(2,1)S(1)}, u32[]{:S(2)}, u32[]{:S(2)}) %collective-permute-start.6) | collective-permute-done | bytes 262176 | tf_op jit(solution)/shard_map/ppermute | solution.py:269
  32.9 1.3 %shard_map.91 = (bf16[2,4,128,128]{3,2,1,0:T(8,128)(2,1)S(1)}, bf16[2,4,128,128]{3,2,1,0:T(8,128)(2,1)S(1)}, bf16[2,4,128,128]{3,2,1,0:T(8,128)(2,1)S(1)}, bf16[2,4,128,128]{3,2,1,0:T(8,128)(2,1)S(1)}) custom-call(bf16[4,1024,128]{2,1,0:T(8,128)(2,1)S(1)} %get-tuple-element.52.ext_ref, bf16[4,256,128]{2,1,0:T(8,128)(2,1)S(1)} %collective-permute-done.8.even_ref, ...), custom_call_target="tpu_custom_call" | custom-call | flops 1 | bytes 1 | tf_op jit(solution)/shard_map/pallas_call | solution.py:147
  34.2 1.3 %collective-permute-start.10 = (bf16[2,4,128,128]{3,2,1,0:T(8,128)(2,1)S(1)}, bf16[2,4,128,128]{3,2,1,0:T(8,128)(2,1)S(1)}, u32[]{:S(2)}, u32[]{:S(2)}) collective-permute-start(bf16[2,4,128,128]{3,2,1,0:T(8,128)(2,1)S(1)} %get-tuple-element.76), channel_id=1, source_target_pairs={{0,4},{2,6},{4,0},{6,2},{8,12},{10,14},{12,8},{14,10},{16,20},{18,... | collective-permute-start | bytes 786440 | tf_op jit(solution)/shard_map/ppermute | solution.py:269
  35.5 0.2 collective-permute-start.14
  35.7 4.3 %collective-permute-start.15 = (bf16[4,256,128]{2,1,0:T(8,128)(2,1)S(1)}, bf16[4,256,128]{2,1,0:T(8,128)(2,1)S(1)}, u32[]{:S(2)}, u32[]{:S(2)}) collective-permute-start(bf16[4,256,128]{2,1,0:T(8,128)(2,1)S(1)} %get-tuple-element.82), channel_id=1, source_target_pairs={{8,16},{16,8},{10,18},{18,10},{12,20},{20,12},{14,22},{22,14},{9,1... | collective-permute-start | bytes 786440 | tf_op jit(solution)/shard_map/ppermute | solution.py:294
  40.0 1.4 %collective-permute-start.12 = (bf16[2,4,128,128]{3,2,1,0:T(8,128)(2,1)S(1)}, bf16[2,4,128,128]{3,2,1,0:T(8,128)(2,1)S(1)}, u32[]{:S(2)}, u32[]{:S(2)}) collective-permute-start(bf16[2,4,128,128]{3,2,1,0:T(8,128)(2,1)S(1)} %get-tuple-element.80), channel_id=1, source_target_pairs={{0,6},{2,4},{4,2},{6,0},{8,14},{10,12},{12,10},{14,8},{16,22},{18,... | collective-permute-start | bytes 786440 | tf_op jit(solution)/shard_map/ppermute | solution.py:269
  41.5 3.2 %shard_map.92.res_ref = bf16[4,1024,128]{2,1,0:T(8,128)(2,1)S(1)} custom-call(bf16[4,1024,128]{2,1,0:T(8,128)(2,1)S(1)} %get-tuple-element.75.ext_ref, s32[32,128]{1,0:T(8,128)S(1)} %bitcast.3), custom_call_target="tpu_custom_call" | custom-call | flops 1 | bytes 1 | tf_op jit(solution)/shard_map/pallas_call | solution.py:147
  44.8 1.3 %shard_map.94 = (bf16[2,4,128,128]{3,2,1,0:T(8,128)(2,1)S(1)}, bf16[2,4,128,128]{3,2,1,0:T(8,128)(2,1)S(1)}, bf16[2,4,128,128]{3,2,1,0:T(8,128)(2,1)S(1)}, bf16[2,4,128,128]{3,2,1,0:T(8,128)(2,1)S(1)}) custom-call(bf16[4,1024,128]{2,1,0:T(8,128)(2,1)S(1)} %get-tuple-element.75.ext_ref, bf16[4,256,128]{2,1,0:T(8,128)(2,1)S(1)} %collective-permute-done.14.even_ref, ...), custom_call_target="tpu_custom_call" | custom-call | flops 1 | bytes 1 | tf_op jit(solution)/shard_map/pallas_call | solution.py:147
  46.1 1.8 %collective-permute-start.16 = (bf16[2,4,128,128]{3,2,1,0:T(8,128)(2,1)S(1)}, bf16[2,4,128,128]{3,2,1,0:T(8,128)(2,1)S(1)}, u32[]{:S(2)}, u32[]{:S(2)}) collective-permute-start(bf16[2,4,128,128]{3,2,1,0:T(8,128)(2,1)S(1)} %get-tuple-element.85), channel_id=1, source_target_pairs={{0,4},{2,6},{4,0},{6,2},{8,12},{10,14},{12,8},{14,10},{16,20},{18,... | collective-permute-start | bytes 786440 | tf_op jit(solution)/shard_map/ppermute | solution.py:269
  47.9 0.2 collective-permute-start.17
  48.1 1.1 %collective-permute-start.18 = (bf16[2,4,128,128]{3,2,1,0:T(8,128)(2,1)S(1)}, bf16[2,4,128,128]{3,2,1,0:T(8,128)(2,1)S(1)}, u32[]{:S(2)}, u32[]{:S(2)}) collective-permute-start(bf16[2,4,128,128]{3,2,1,0:T(8,128)(2,1)S(1)} %get-tuple-element.87), channel_id=1, source_target_pairs={{0,6},{2,4},{4,2},{6,0},{8,14},{10,12},{12,10},{14,8},{16,22},{18,... | collective-permute-start | bytes 786440 | tf_op jit(solution)/shard_map/ppermute | solution.py:269
  49.3 2.9 %collective-permute-start.13 = (bf16[4,4,128,128]{3,2,1,0:T(8,128)(2,1)S(1)}, bf16[4,4,128,128]{3,2,1,0:T(8,128)(2,1)S(1)}, u32[]{:S(2)}, u32[]{:S(2)}) collective-permute-start(bf16[4,4,128,128]{3,2,1,0:T(8,128)(2,1)S(1)} %shard_map.93), channel_id=1, source_target_pairs={{0,1},{1,0},{2,3},{3,2},{4,5},{5,4},{6,7},{7,6},{8,9},{9,8},{10,11... | collective-permute-start | bytes 1572872 | tf_op jit(solution)/shard_map/ppermute | solution.py:318
  52.2 0.3 collective-permute-done.16.refs_1_.refs_6_
  52.5 0.9 %collective-permute-done.17.refs_2_.refs_7_ = bf16[2,4,128,128]{3,2,1,0:T(8,128)(2,1)S(1)} collective-permute-done((bf16[2,4,128,128]{3,2,1,0:T(8,128)(2,1)S(1)}, bf16[2,4,128,128]{3,2,1,0:T(8,128)(2,1)S(1)}, u32[]{:S(2)}, u32[]{:S(2)}) %collective-permute-start.17) | collective-permute-done | bytes 262176 | tf_op jit(solution)/shard_map/ppermute | solution.py:269
  53.4 5.2 %collective-permute-done.18.refs_3_.refs_8_ = bf16[2,4,128,128]{3,2,1,0:T(8,128)(2,1)S(1)} collective-permute-done((bf16[2,4,128,128]{3,2,1,0:T(8,128)(2,1)S(1)}, bf16[2,4,128,128]{3,2,1,0:T(8,128)(2,1)S(1)}, u32[]{:S(2)}, u32[]{:S(2)}) %collective-permute-start.18) | collective-permute-done | bytes 262176 | tf_op jit(solution)/shard_map/ppermute | solution.py:269
  58.6 3.6 %collective-permute-start.19 = (bf16[4,4,128,128]{3,2,1,0:T(8,128)(2,1)S(1)}, bf16[4,4,128,128]{3,2,1,0:T(8,128)(2,1)S(1)}, u32[]{:S(2)}, u32[]{:S(2)}) collective-permute-start(bf16[4,4,128,128]{3,2,1,0:T(8,128)(2,1)S(1)} %shard_map.95), channel_id=1, source_target_pairs={{0,1},{1,0},{2,3},{3,2},{4,5},{5,4},{6,7},{7,6},{8,9},{9,8},{10,11... | collective-permute-start | bytes 1572872 | tf_op jit(solution)/shard_map/ppermute | solution.py:318
  62.2 1.5 %collective-permute-done.19.refs_9_ = bf16[4,4,128,128]{3,2,1,0:T(8,128)(2,1)S(1)} collective-permute-done((bf16[4,4,128,128]{3,2,1,0:T(8,128)(2,1)S(1)}, bf16[4,4,128,128]{3,2,1,0:T(8,128)(2,1)S(1)}, u32[]{:S(2)}, u32[]{:S(2)}) %collective-permute-start.19) | collective-permute-done | bytes 524320 | tf_op jit(solution)/shard_map/ppermute | solution.py:318
  63.8 1.5 %shard_map.96 = (bf16[128,2048]{1,0:T(8,128)(2,1)}, bf16[128,2048]{1,0:T(8,128)(2,1)}, bf16[128,2048]{1,0:T(8,128)(2,1)}, bf16[128,2048]{1,0:T(8,128)(2,1)}) custom-call(bf16[2,4,128,128]{3,2,1,0:T(8,128)(2,1)S(1)} %get-tuple-element.74.refs_0_, bf16[2,4,128,128]{3,2,1,0:T(8,128)(2,1)S(1)} %collective-permute-done.10.refs_1_, ...), custom_call_target="tpu_custom_call" | custom-call | tf_op jit(solution)/shard_map/pallas_call | solution.py:236
  (27 shorter events, 0.7 us)
Async XLA Ops:
  3.3 3.4 %copy-start.1 = (bf16[4,4,128,128]{3,2,1,0:T(8,128)(2,1)S(1)}, bf16[4,4,128,128]{3,2,1,0:T(8,128)(2,1)}, u32[]{:S(2)}) copy-start(bf16[4,4,128,128]{3,2,1,0:T(8,128)(2,1)} %get-tuple-element.46.mine_ref) | copy-start | bytes 1572868
  3.3 3.4 %collective-permute-start = (bf16[4,4,128,128]{3,2,1,0:T(8,128)(2,1)}, bf16[4,4,128,128]{3,2,1,0:T(8,128)(2,1)S(1)}, u32[]{:S(2)}, u32[]{:S(2)}) collective-permute-start(bf16[4,4,128,128]{3,2,1,0:T(8,128)(2,1)} %get-tuple-element.47), channel_id=1, source_target_pairs={{0,1},{1,0},{2,3},{3,2},{4,5},{5,4},{6,7},{7,6},{8,9},{9,8},{10,11... | collective-permute-start | bytes 1572872 | tf_op jit(solution)/shard_map/ppermute | solution.py:278
  6.5 2.9 %collective-permute-start.4 = (bf16[4,4,128,128]{3,2,1,0:T(8,128)(2,1)}, bf16[4,4,128,128]{3,2,1,0:T(8,128)(2,1)S(1)}, u32[]{:S(2)}, u32[]{:S(2)}) collective-permute-start(bf16[4,4,128,128]{3,2,1,0:T(8,128)(2,1)} %get-tuple-element.54), channel_id=1, source_target_pairs={{0,1},{1,0},{2,3},{3,2},{4,5},{5,4},{6,7},{7,6},{8,9},{9,8},{10,11... | collective-permute-start | bytes 1572872 | tf_op jit(solution)/shard_map/ppermute | solution.py:278
  6.6 2.8 %copy-start = (bf16[4,4,128,128]{3,2,1,0:T(8,128)(2,1)S(1)}, bf16[4,4,128,128]{3,2,1,0:T(8,128)(2,1)}, u32[]{:S(2)}) copy-start(bf16[4,4,128,128]{3,2,1,0:T(8,128)(2,1)} %get-tuple-element.53.mine_ref) | copy-start | bytes 1572868
  6.7 8.5 %collective-permute-start.1 = (bf16[2,4,128,128]{3,2,1,0:T(8,128)(2,1)S(1)}, bf16[2,4,128,128]{3,2,1,0:T(8,128)(2,1)S(1)}, u32[]{:S(2)}, u32[]{:S(2)}) collective-permute-start(bf16[2,4,128,128]{3,2,1,0:T(8,128)(2,1)S(1)} %get-tuple-element.49), channel_id=1, source_target_pairs={{0,6},{2,4},{4,2},{6,0},{8,14},{10,12},{12,10},{14,8},{16,22},{18,... | collective-permute-start | bytes 786440 | tf_op jit(solution)/shard_map/ppermute | solution.py:269
  8.9 13.3 %collective-permute-start.2 = (bf16[2,4,128,128]{3,2,1,0:T(8,128)(2,1)S(1)}, bf16[2,4,128,128]{3,2,1,0:T(8,128)(2,1)S(1)}, u32[]{:S(2)}, u32[]{:S(2)}) collective-permute-start(bf16[2,4,128,128]{3,2,1,0:T(8,128)(2,1)S(1)} %get-tuple-element.50), channel_id=1, source_target_pairs={{0,4},{2,6},{4,0},{6,2},{8,12},{10,14},{12,8},{14,10},{16,20},{18,... | collective-permute-start | bytes 786440 | tf_op jit(solution)/shard_map/ppermute | solution.py:269
  9.2 13.1 %collective-permute-start.3 = (bf16[2,4,128,128]{3,2,1,0:T(8,128)(2,1)S(1)}, bf16[2,4,128,128]{3,2,1,0:T(8,128)(2,1)S(1)}, u32[]{:S(2)}, u32[]{:S(2)}) collective-permute-start(bf16[2,4,128,128]{3,2,1,0:T(8,128)(2,1)S(1)} %get-tuple-element.51), channel_id=1, source_target_pairs={{0,2},{2,0},{4,6},{6,4},{8,10},{10,8},{12,14},{14,12},{16,18},{18,... | collective-permute-start | bytes 786440 | tf_op jit(solution)/shard_map/ppermute | solution.py:269
  9.5 20.7 %collective-permute-start.5 = (bf16[2,4,128,128]{3,2,1,0:T(8,128)(2,1)S(1)}, bf16[2,4,128,128]{3,2,1,0:T(8,128)(2,1)S(1)}, u32[]{:S(2)}, u32[]{:S(2)}) collective-permute-start(bf16[2,4,128,128]{3,2,1,0:T(8,128)(2,1)S(1)} %get-tuple-element.56), channel_id=1, source_target_pairs={{0,6},{2,4},{4,2},{6,0},{8,14},{10,12},{12,10},{14,8},{16,22},{18,... | collective-permute-start | bytes 786440 | tf_op jit(solution)/shard_map/ppermute | solution.py:269
  11.7 21.0 %collective-permute-start.6 = (bf16[2,4,128,128]{3,2,1,0:T(8,128)(2,1)S(1)}, bf16[2,4,128,128]{3,2,1,0:T(8,128)(2,1)S(1)}, u32[]{:S(2)}, u32[]{:S(2)}) collective-permute-start(bf16[2,4,128,128]{3,2,1,0:T(8,128)(2,1)S(1)} %get-tuple-element.57), channel_id=1, source_target_pairs={{0,4},{2,6},{4,0},{6,2},{8,12},{10,14},{12,8},{14,10},{16,20},{18,... | collective-permute-start | bytes 786440 | tf_op jit(solution)/shard_map/ppermute | solution.py:269
  15.1 17.6 %collective-permute-start.7 = (bf16[2,4,128,128]{3,2,1,0:T(8,128)(2,1)S(1)}, bf16[2,4,128,128]{3,2,1,0:T(8,128)(2,1)S(1)}, u32[]{:S(2)}, u32[]{:S(2)}) collective-permute-start(bf16[2,4,128,128]{3,2,1,0:T(8,128)(2,1)S(1)} %get-tuple-element.58), channel_id=1, source_target_pairs={{0,2},{2,0},{4,6},{6,4},{8,10},{10,8},{12,14},{14,12},{16,18},{18,... | collective-permute-start | bytes 786440 | tf_op jit(solution)/shard_map/ppermute | solution.py:269
  22.2 4.7 %copy-start.2 = (s32[4096]{0:T(1024)S(1)}, s32[4096]{0:T(1024)}, u32[]{:S(2)}) copy-start(s32[4096]{0:T(1024)} %param.9) | copy-start | bytes 49156
  22.4 10.5 %collective-permute-start.8 = (bf16[4,256,128]{2,1,0:T(8,128)(2,1)S(1)}, bf16[4,256,128]{2,1,0:T(8,128)(2,1)S(1)}, u32[]{:S(2)}, u32[]{:S(2)}) collective-permute-start(bf16[4,256,128]{2,1,0:T(8,128)(2,1)S(1)} %get-tuple-element.67), channel_id=1, source_target_pairs={{0,8},{8,0},{2,10},{10,2},{4,12},{12,4},{6,14},{14,6},{16,24},{24,... | collective-permute-start | bytes 786440 | tf_op jit(solution)/shard_map/ppermute | solution.py:293
  22.5 10.4 %collective-permute-start.9 = (bf16[4,256,128]{2,1,0:T(8,128)(2,1)S(1)}, bf16[4,256,128]{2,1,0:T(8,128)(2,1)S(1)}, u32[]{:S(2)}, u32[]{:S(2)}) collective-permute-start(bf16[4,256,128]{2,1,0:T(8,128)(2,1)S(1)} %get-tuple-element.68), channel_id=1, source_target_pairs={{8,16},{16,8},{10,18},{18,10},{12,20},{20,12},{14,22},{22,14},{9,1... | collective-permute-start | bytes 786440 | tf_op jit(solution)/shard_map/ppermute | solution.py:294
  34.2 10.5 %collective-permute-start.10 = (bf16[2,4,128,128]{3,2,1,0:T(8,128)(2,1)S(1)}, bf16[2,4,128,128]{3,2,1,0:T(8,128)(2,1)S(1)}, u32[]{:S(2)}, u32[]{:S(2)}) collective-permute-start(bf16[2,4,128,128]{3,2,1,0:T(8,128)(2,1)S(1)} %get-tuple-element.76), channel_id=1, source_target_pairs={{0,4},{2,6},{4,0},{6,2},{8,12},{10,14},{12,8},{14,10},{16,20},{18,... | collective-permute-start | bytes 786440 | tf_op jit(solution)/shard_map/ppermute | solution.py:269
  35.5 9.2 %collective-permute-start.11 = (bf16[2,4,128,128]{3,2,1,0:T(8,128)(2,1)S(1)}, bf16[2,4,128,128]{3,2,1,0:T(8,128)(2,1)S(1)}, u32[]{:S(2)}, u32[]{:S(2)}) collective-permute-start(bf16[2,4,128,128]{3,2,1,0:T(8,128)(2,1)S(1)} %get-tuple-element.77), channel_id=1, source_target_pairs={{0,2},{2,0},{4,6},{6,4},{8,10},{10,8},{12,14},{14,12},{16,18},{18,... | collective-permute-start | bytes 786440 | tf_op jit(solution)/shard_map/ppermute | solution.py:269
  35.5 9.2 %collective-permute-start.14 = (bf16[4,256,128]{2,1,0:T(8,128)(2,1)S(1)}, bf16[4,256,128]{2,1,0:T(8,128)(2,1)S(1)}, u32[]{:S(2)}, u32[]{:S(2)}) collective-permute-start(bf16[4,256,128]{2,1,0:T(8,128)(2,1)S(1)} %get-tuple-element.81), channel_id=1, source_target_pairs={{0,8},{8,0},{2,10},{10,2},{4,12},{12,4},{6,14},{14,6},{16,24},{24,... | collective-permute-start | bytes 786440 | tf_op jit(solution)/shard_map/ppermute | solution.py:293
  35.7 9.1 %collective-permute-start.15 = (bf16[4,256,128]{2,1,0:T(8,128)(2,1)S(1)}, bf16[4,256,128]{2,1,0:T(8,128)(2,1)S(1)}, u32[]{:S(2)}, u32[]{:S(2)}) collective-permute-start(bf16[4,256,128]{2,1,0:T(8,128)(2,1)S(1)} %get-tuple-element.82), channel_id=1, source_target_pairs={{8,16},{16,8},{10,18},{18,10},{12,20},{20,12},{14,22},{22,14},{9,1... | collective-permute-start | bytes 786440 | tf_op jit(solution)/shard_map/ppermute | solution.py:294
  40.0 9.2 %collective-permute-start.12 = (bf16[2,4,128,128]{3,2,1,0:T(8,128)(2,1)S(1)}, bf16[2,4,128,128]{3,2,1,0:T(8,128)(2,1)S(1)}, u32[]{:S(2)}, u32[]{:S(2)}) collective-permute-start(bf16[2,4,128,128]{3,2,1,0:T(8,128)(2,1)S(1)} %get-tuple-element.80), channel_id=1, source_target_pairs={{0,6},{2,4},{4,2},{6,0},{8,14},{10,12},{12,10},{14,8},{16,22},{18,... | collective-permute-start | bytes 786440 | tf_op jit(solution)/shard_map/ppermute | solution.py:269
  46.1 6.4 %collective-permute-start.16 = (bf16[2,4,128,128]{3,2,1,0:T(8,128)(2,1)S(1)}, bf16[2,4,128,128]{3,2,1,0:T(8,128)(2,1)S(1)}, u32[]{:S(2)}, u32[]{:S(2)}) collective-permute-start(bf16[2,4,128,128]{3,2,1,0:T(8,128)(2,1)S(1)} %get-tuple-element.85), channel_id=1, source_target_pairs={{0,4},{2,6},{4,0},{6,2},{8,12},{10,14},{12,8},{14,10},{16,20},{18,... | collective-permute-start | bytes 786440 | tf_op jit(solution)/shard_map/ppermute | solution.py:269
  47.9 5.5 %collective-permute-start.17 = (bf16[2,4,128,128]{3,2,1,0:T(8,128)(2,1)S(1)}, bf16[2,4,128,128]{3,2,1,0:T(8,128)(2,1)S(1)}, u32[]{:S(2)}, u32[]{:S(2)}) collective-permute-start(bf16[2,4,128,128]{3,2,1,0:T(8,128)(2,1)S(1)} %get-tuple-element.86), channel_id=1, source_target_pairs={{0,2},{2,0},{4,6},{6,4},{8,10},{10,8},{12,14},{14,12},{16,18},{18,... | collective-permute-start | bytes 786440 | tf_op jit(solution)/shard_map/ppermute | solution.py:269
  48.1 10.5 %collective-permute-start.18 = (bf16[2,4,128,128]{3,2,1,0:T(8,128)(2,1)S(1)}, bf16[2,4,128,128]{3,2,1,0:T(8,128)(2,1)S(1)}, u32[]{:S(2)}, u32[]{:S(2)}) collective-permute-start(bf16[2,4,128,128]{3,2,1,0:T(8,128)(2,1)S(1)} %get-tuple-element.87), channel_id=1, source_target_pairs={{0,6},{2,4},{4,2},{6,0},{8,14},{10,12},{12,10},{14,8},{16,22},{18,... | collective-permute-start | bytes 786440 | tf_op jit(solution)/shard_map/ppermute | solution.py:269
  49.3 12.9 %collective-permute-start.13 = (bf16[4,4,128,128]{3,2,1,0:T(8,128)(2,1)S(1)}, bf16[4,4,128,128]{3,2,1,0:T(8,128)(2,1)S(1)}, u32[]{:S(2)}, u32[]{:S(2)}) collective-permute-start(bf16[4,4,128,128]{3,2,1,0:T(8,128)(2,1)S(1)} %shard_map.93), channel_id=1, source_target_pairs={{0,1},{1,0},{2,3},{3,2},{4,5},{5,4},{6,7},{7,6},{8,9},{9,8},{10,11... | collective-permute-start | bytes 1572872 | tf_op jit(solution)/shard_map/ppermute | solution.py:318
  58.6 5.1 %collective-permute-start.19 = (bf16[4,4,128,128]{3,2,1,0:T(8,128)(2,1)S(1)}, bf16[4,4,128,128]{3,2,1,0:T(8,128)(2,1)S(1)}, u32[]{:S(2)}, u32[]{:S(2)}) collective-permute-start(bf16[4,4,128,128]{3,2,1,0:T(8,128)(2,1)S(1)} %shard_map.95), channel_id=1, source_target_pairs={{0,1},{1,0},{2,3},{3,2},{4,5},{5,4},{6,7},{7,6},{8,9},{9,8},{10,11... | collective-permute-start | bytes 1572872 | tf_op jit(solution)/shard_map/ppermute | solution.py:318

commit v6 on v5

--- a/solution.py
+++ b/solution.py
@@ -320,10 +320,9 @@
     ext_a, *edges_a = gather(0)
     halo_a = halo(*edges_a)
     res_a = interior(ext_a)
-    ext_b, *edges_b = gather(1, res_a)
-    res_a, ext_b = lax.optimization_barrier((res_a, ext_b))
+    res_a, arrived[1][1] = lax.optimization_barrier((res_a, arrived[1][1]))
     back_a = finish(ext_a, *halo_a, res_a)
-    ext_b, edges_b, back_a = lax.optimization_barrier((ext_b, edges_b, back_a))
+    ext_b, *edges_b = gather(1, back_a)
     halo_b = halo(*edges_b)
     res_b = interior(ext_b)
     out_a = give_back(back_a)

time: 65.7 us -> 64.3 us (0.979)
  waiting for transfers between devices: 19.7 us -> 15.7 us
  starting transfers between devices: 28.6 us -> 31.1 us
    ppermute x12, waiting for transfers between devices: 18 us -> 12.8 us  [hop(): lax.ppermute(block, 'blk', [(i, i ^ s) for i in range(positions)])]
    ppermute x2, starting transfers between devices: 6.51 us -> 10.9 us  [swap_back(): return back + [lax.ppermute(away, 'head', swap)]]
    ppermute x2, starting transfers between devices: 8.8 us -> 7.52 us  [halo(): return (even, lax.ppermute(to_odd, 'blk', plane_pairs(1)))]
    ppermute x2, waiting for transfers between devices: 0.1 us -> 1.38 us  [halo(): return (even, lax.ppermute(to_odd, 'blk', plane_pairs(1)))]
  transfers between devices with their start and end apart: 20 -> 20, of which waited for: 8 -> 6; matrix products, arithmetic and copies ran while one was open for 0% -> 0% of each run, Pallas kernels for 17% -> 19%
where the time goes in v6:
time: 64.3 us; the launch traced here: 63.8 us
  starting transfers between devices  31.1 us (48%)
  Pallas kernels  16.2 us (25%)
  waiting for transfers between devices  15.7 us (24%)
  between operations  0.79 us (1%)
    ppermute x12, waiting for transfers between devices, hop(): lax.ppermute(block, 'blk', [(i, i ^ s) for i in range(positions)])  12.8 us
    ppermute x12, starting transfers between devices, hop(): lax.ppermute(block, 'blk', [(i, i ^ s) for i in range(positions)])  11.8 us
    ppermute x2, starting transfers between devices, swap_back(): return back + [lax.ppermute(away, 'head', swap)]  10.9 us
    pallas_call x10, Pallas kernels, call(): pl.pallas_call(kernel, out_shape=out_shape, in_specs=[WHOLE] * len(args),...  9.48 us
    ppermute x2, starting transfers between devices, halo(): return (even, lax.ppermute(to_odd, 'blk', plane_pairs(1)))  7.52 us
    pallas_call x2, Pallas kernels, pack(): pl.pallas_call(functools.partial(pack_kernel, j, chunks), grid=(PACK_STEP...  5.23 us
    ppermute x2, waiting for transfers between devices, swap_back(): return back + [lax.ppermute(away, 'head', swap)]  1.54 us
    pallas_call x1, Pallas kernels, unpack(): pl.pallas_call(functools.partial(unpack_kernel, len(chunks)), out_shape=[...  1.5 us
  transfers between devices with their start and end apart: 20, of which 6 were waited for; matrix products, arithmetic and copies ran while one was open for 0% of the time, Pallas kernels for 19%

profile of v6, /device:TPU:9, one launch (start us, length us, event | category | flops | bytes accessed | tf_op | source)
XLA Modules:
  0.0 63.8 jit_solution(1952866445405208420)
XLA Ops:
  0.6 2.6 %shard_map.84 = (bf16[4,4,128,128]{3,2,1,0:T(8,128)(2,1)}, bf16[4,4,128,128]{3,2,1,0:T(8,128)(2,1)}) custom-call(bf16[128,2048]{1,0:T(8,128)(2,1)} %refs_0_.3, bf16[128,2048]{1,0:T(8,128)(2,1)} %refs_1_.3, bf16[128,2048]{1,0:T(8,128)(2,1)} %refs_2_.3, bf16[128,2048]{1,0:T(8,128)(2,1)} %refs_3_.3), custom_call_target="tpu_custom_call" | custom-call | tf_op jit(solution)/shard_map/pallas_call | solution.py:175
  3.3 0.7 %collective-permute-start = (bf16[4,4,128,128]{3,2,1,0:T(8,128)(2,1)}, bf16[4,4,128,128]{3,2,1,0:T(8,128)(2,1)S(1)}, u32[]{:S(2)}, u32[]{:S(2)}) collective-permute-start(bf16[4,4,128,128]{3,2,1,0:T(8,128)(2,1)} %get-tuple-element.40), channel_id=1, source_target_pairs={{0,1},{1,0},{2,3},{3,2},{4,5},{5,4},{6,7},{7,6},{8,9},{9,8},{10,11... | collective-permute-start | bytes 1572872 | tf_op jit(solution)/shard_map/ppermute | solution.py:278
  3.9 2.6 %shard_map.88 = (bf16[4,4,128,128]{3,2,1,0:T(8,128)(2,1)}, bf16[4,4,128,128]{3,2,1,0:T(8,128)(2,1)}) custom-call(bf16[128,2048]{1,0:T(8,128)(2,1)} %refs_0_.3, bf16[128,2048]{1,0:T(8,128)(2,1)} %refs_1_.3, bf16[128,2048]{1,0:T(8,128)(2,1)} %refs_2_.3, bf16[128,2048]{1,0:T(8,128)(2,1)} %refs_3_.3), custom_call_target="tpu_custom_call" | custom-call | tf_op jit(solution)/shard_map/pallas_call | solution.py:175
  6.5 0.1 collective-permute-start.6
  6.7 2.2 %collective-permute-start.1 = (bf16[2,4,128,128]{3,2,1,0:T(8,128)(2,1)S(1)}, bf16[2,4,128,128]{3,2,1,0:T(8,128)(2,1)S(1)}, u32[]{:S(2)}, u32[]{:S(2)}) collective-permute-start(bf16[2,4,128,128]{3,2,1,0:T(8,128)(2,1)S(1)} %get-tuple-element.42), channel_id=1, source_target_pairs={{0,6},{2,4},{4,2},{6,0},{8,14},{10,12},{12,10},{14,8},{16,22},{18,... | collective-permute-start | bytes 786440 | tf_op jit(solution)/shard_map/ppermute | solution.py:269
  8.9 0.2 collective-permute-start.2
  9.2 0.3 collective-permute-start.3
  9.5 2.2 %collective-permute-start.7 = (bf16[2,4,128,128]{3,2,1,0:T(8,128)(2,1)S(1)}, bf16[2,4,128,128]{3,2,1,0:T(8,128)(2,1)S(1)}, u32[]{:S(2)}, u32[]{:S(2)}) collective-permute-start(bf16[2,4,128,128]{3,2,1,0:T(8,128)(2,1)S(1)} %get-tuple-element.50), channel_id=1, source_target_pairs={{0,6},{2,4},{4,2},{6,0},{8,14},{10,12},{12,10},{14,8},{16,22},{18,... | collective-permute-start | bytes 786440 | tf_op jit(solution)/shard_map/ppermute | solution.py:269
  11.7 3.4 %collective-permute-done.1.refs_1_ = bf16[2,4,128,128]{3,2,1,0:T(8,128)(2,1)S(1)} collective-permute-done((bf16[2,4,128,128]{3,2,1,0:T(8,128)(2,1)S(1)}, bf16[2,4,128,128]{3,2,1,0:T(8,128)(2,1)S(1)}, u32[]{:S(2)}, u32[]{:S(2)}) %collective-permute-start.1) | collective-permute-done | bytes 262176 | tf_op jit(solution)/shard_map/ppermute | solution.py:269
  15.1 7.1 %collective-permute-done.2.refs_2_ = bf16[2,4,128,128]{3,2,1,0:T(8,128)(2,1)S(1)} collective-permute-done((bf16[2,4,128,128]{3,2,1,0:T(8,128)(2,1)S(1)}, bf16[2,4,128,128]{3,2,1,0:T(8,128)(2,1)S(1)}, u32[]{:S(2)}, u32[]{:S(2)}) %collective-permute-start.2) | collective-permute-done | bytes 262176 | tf_op jit(solution)/shard_map/ppermute | solution.py:269
  22.2 0.1 shard_map.86
  22.5 4.5 %collective-permute-start.5 = (bf16[4,256,128]{2,1,0:T(8,128)(2,1)S(1)}, bf16[4,256,128]{2,1,0:T(8,128)(2,1)S(1)}, u32[]{:S(2)}, u32[]{:S(2)}) collective-permute-start(bf16[4,256,128]{2,1,0:T(8,128)(2,1)S(1)} %get-tuple-element.47), channel_id=1, source_target_pairs={{8,16},{16,8},{10,18},{18,10},{12,20},{20,12},{14,22},{22,14},{9,1... | collective-permute-start | bytes 786440 | tf_op jit(solution)/shard_map/ppermute | solution.py:294
  26.9 1.3 %collective-permute-start.8 = (bf16[2,4,128,128]{3,2,1,0:T(8,128)(2,1)S(1)}, bf16[2,4,128,128]{3,2,1,0:T(8,128)(2,1)S(1)}, u32[]{:S(2)}, u32[]{:S(2)}) collective-permute-start(bf16[2,4,128,128]{3,2,1,0:T(8,128)(2,1)S(1)} %get-tuple-element.55), channel_id=1, source_target_pairs={{0,4},{2,6},{4,0},{6,2},{8,12},{10,14},{12,8},{14,10},{16,20},{18,... | collective-permute-start | bytes 786440 | tf_op jit(solution)/shard_map/ppermute | solution.py:269
  28.3 3.2 %shard_map.87.res_ref = bf16[4,1024,128]{2,1,0:T(8,128)(2,1)S(1)} custom-call(bf16[4,1024,128]{2,1,0:T(8,128)(2,1)S(1)} %get-tuple-element.45.ext_ref, s32[32,128]{1,0:T(8,128)S(1)} %bitcast.1), custom_call_target="tpu_custom_call" | custom-call | flops 1 | bytes 1 | tf_op jit(solution)/shard_map/pallas_call | solution.py:147
  31.6 1.0 %collective-permute-done.5.odd_ref = bf16[4,256,128]{2,1,0:T(8,128)(2,1)S(1)} collective-permute-done((bf16[4,256,128]{2,1,0:T(8,128)(2,1)S(1)}, bf16[4,256,128]{2,1,0:T(8,128)(2,1)S(1)}, u32[]{:S(2)}, u32[]{:S(2)}) %collective-permute-start.5) | collective-permute-done | bytes 262176 | tf_op jit(solution)/shard_map/ppermute | solution.py:294
  32.6 1.3 %shard_map.90 = (bf16[2,4,128,128]{3,2,1,0:T(8,128)(2,1)S(1)}, bf16[2,4,128,128]{3,2,1,0:T(8,128)(2,1)S(1)}, bf16[2,4,128,128]{3,2,1,0:T(8,128)(2,1)S(1)}, bf16[2,4,128,128]{3,2,1,0:T(8,128)(2,1)S(1)}) custom-call(bf16[4,1024,128]{2,1,0:T(8,128)(2,1)S(1)} %get-tuple-element.45.ext_ref, bf16[4,256,128]{2,1,0:T(8,128)(2,1)S(1)} %collective-permute-done.4.even_ref, ...), custom_call_target="tpu_custom_call" | custom-call | flops 1 | bytes 1 | tf_op jit(solution)/shard_map/pallas_call | solution.py:147
  33.8 1.3 %collective-permute-start.11 = (bf16[2,4,128,128]{3,2,1,0:T(8,128)(2,1)S(1)}, bf16[2,4,128,128]{3,2,1,0:T(8,128)(2,1)S(1)}, u32[]{:S(2)}, u32[]{:S(2)}) collective-permute-start(bf16[2,4,128,128]{3,2,1,0:T(8,128)(2,1)S(1)} %get-tuple-element.57), channel_id=1, source_target_pairs={{0,2},{2,0},{4,6},{6,4},{8,10},{10,8},{12,14},{14,12},{16,18},{18,... | collective-permute-start | bytes 786440 | tf_op jit(solution)/shard_map/ppermute | solution.py:269
  35.1 0.3 collective-permute-start.10
  35.4 0.1 shard_map.91
  35.6 3.0 %collective-permute-start.15 = (bf16[4,256,128]{2,1,0:T(8,128)(2,1)S(1)}, bf16[4,256,128]{2,1,0:T(8,128)(2,1)S(1)}, u32[]{:S(2)}, u32[]{:S(2)}) collective-permute-start(bf16[4,256,128]{2,1,0:T(8,128)(2,1)S(1)} %get-tuple-element.68), channel_id=1, source_target_pairs={{8,16},{16,8},{10,18},{18,10},{12,20},{20,12},{14,22},{22,14},{9,1... | collective-permute-start | bytes 786440 | tf_op jit(solution)/shard_map/ppermute | solution.py:294
  38.7 1.2 %collective-permute-start.12 = (bf16[2,4,128,128]{3,2,1,0:T(8,128)(2,1)S(1)}, bf16[2,4,128,128]{3,2,1,0:T(8,128)(2,1)S(1)}, u32[]{:S(2)}, u32[]{:S(2)}) collective-permute-start(bf16[2,4,128,128]{3,2,1,0:T(8,128)(2,1)S(1)} %get-tuple-element.59), channel_id=1, source_target_pairs={{0,6},{2,4},{4,2},{6,0},{8,14},{10,12},{12,10},{14,8},{16,22},{18,... | collective-permute-start | bytes 786440 | tf_op jit(solution)/shard_map/ppermute | solution.py:269
  39.9 3.2 %shard_map.92.res_ref = bf16[4,1024,128]{2,1,0:T(8,128)(2,1)S(1)} custom-call(bf16[4,1024,128]{2,1,0:T(8,128)(2,1)S(1)} %get-tuple-element.64.ext_ref, s32[32,128]{1,0:T(8,128)S(1)} %bitcast.3), custom_call_target="tpu_custom_call" | custom-call | flops 1 | bytes 1 | tf_op jit(solution)/shard_map/pallas_call | solution.py:147
  43.2 0.4 collective-permute-done.15.odd_ref
  43.6 1.3 %shard_map.94 = (bf16[2,4,128,128]{3,2,1,0:T(8,128)(2,1)S(1)}, bf16[2,4,128,128]{3,2,1,0:T(8,128)(2,1)S(1)}, bf16[2,4,128,128]{3,2,1,0:T(8,128)(2,1)S(1)}, bf16[2,4,128,128]{3,2,1,0:T(8,128)(2,1)S(1)}) custom-call(bf16[4,1024,128]{2,1,0:T(8,128)(2,1)S(1)} %get-tuple-element.64.ext_ref, bf16[4,256,128]{2,1,0:T(8,128)(2,1)S(1)} %collective-permute-done.14.even_ref, ...), custom_call_target="tpu_custom_call" | custom-call | flops 1 | bytes 1 | tf_op jit(solution)/shard_map/pallas_call | solution.py:147
  44.8 1.1 %collective-permute-start.16 = (bf16[2,4,128,128]{3,2,1,0:T(8,128)(2,1)S(1)}, bf16[2,4,128,128]{3,2,1,0:T(8,128)(2,1)S(1)}, u32[]{:S(2)}, u32[]{:S(2)}) collective-permute-start(bf16[2,4,128,128]{3,2,1,0:T(8,128)(2,1)S(1)} %get-tuple-element.71), channel_id=1, source_target_pairs={{0,4},{2,6},{4,0},{6,2},{8,12},{10,14},{12,8},{14,10},{16,20},{18,... | collective-permute-start | bytes 786440 | tf_op jit(solution)/shard_map/ppermute | solution.py:269
  45.9 0.2 collective-permute-start.17
  46.1 1.5 %collective-permute-start.18 = (bf16[2,4,128,128]{3,2,1,0:T(8,128)(2,1)S(1)}, bf16[2,4,128,128]{3,2,1,0:T(8,128)(2,1)S(1)}, u32[]{:S(2)}, u32[]{:S(2)}) collective-permute-start(bf16[2,4,128,128]{3,2,1,0:T(8,128)(2,1)S(1)} %get-tuple-element.73), channel_id=1, source_target_pairs={{0,6},{2,4},{4,2},{6,0},{8,14},{10,12},{12,10},{14,8},{16,22},{18,... | collective-permute-start | bytes 786440 | tf_op jit(solution)/shard_map/ppermute | solution.py:269
  47.6 5.9 %collective-permute-start.13 = (bf16[4,4,128,128]{3,2,1,0:T(8,128)(2,1)S(1)}, bf16[4,4,128,128]{3,2,1,0:T(8,128)(2,1)S(1)}, u32[]{:S(2)}, u32[]{:S(2)}) collective-permute-start(bf16[4,4,128,128]{3,2,1,0:T(8,128)(2,1)S(1)} %shard_map.93), channel_id=1, source_target_pairs={{0,1},{1,0},{2,3},{3,2},{4,5},{5,4},{6,7},{7,6},{8,9},{9,8},{10,11... | collective-permute-start | bytes 1572872 | tf_op jit(solution)/shard_map/ppermute | solution.py:318
  53.5 2.3 %collective-permute-done.16.refs_1_.refs_6_ = bf16[2,4,128,128]{3,2,1,0:T(8,128)(2,1)S(1)} collective-permute-done((bf16[2,4,128,128]{3,2,1,0:T(8,128)(2,1)S(1)}, bf16[2,4,128,128]{3,2,1,0:T(8,128)(2,1)S(1)}, u32[]{:S(2)}, u32[]{:S(2)}) %collective-permute-start.16) | collective-permute-done | bytes 262176 | tf_op jit(solution)/shard_map/ppermute | solution.py:269
  55.8 5.0 %collective-permute-start.19 = (bf16[4,4,128,128]{3,2,1,0:T(8,128)(2,1)S(1)}, bf16[4,4,128,128]{3,2,1,0:T(8,128)(2,1)S(1)}, u32[]{:S(2)}, u32[]{:S(2)}) collective-permute-start(bf16[4,4,128,128]{3,2,1,0:T(8,128)(2,1)S(1)} %shard_map.95), channel_id=1, source_target_pairs={{0,1},{1,0},{2,3},{3,2},{4,5},{5,4},{6,7},{7,6},{8,9},{9,8},{10,11... | collective-permute-start | bytes 1572872 | tf_op jit(solution)/shard_map/ppermute | solution.py:318
  60.8 1.5 %collective-permute-done.19.refs_9_ = bf16[4,4,128,128]{3,2,1,0:T(8,128)(2,1)S(1)} collective-permute-done((bf16[4,4,128,128]{3,2,1,0:T(8,128)(2,1)S(1)}, bf16[4,4,128,128]{3,2,1,0:T(8,128)(2,1)S(1)}, u32[]{:S(2)}, u32[]{:S(2)}) %collective-permute-start.19) | collective-permute-done | bytes 524320 | tf_op jit(solution)/shard_map/ppermute | solution.py:318
  62.3 1.5 %shard_map.96 = (bf16[128,2048]{1,0:T(8,128)(2,1)}, bf16[128,2048]{1,0:T(8,128)(2,1)}, bf16[128,2048]{1,0:T(8,128)(2,1)}, bf16[128,2048]{1,0:T(8,128)(2,1)}) custom-call(bf16[2,4,128,128]{3,2,1,0:T(8,128)(2,1)S(1)} %get-tuple-element.52.refs_0_, bf16[2,4,128,128]{3,2,1,0:T(8,128)(2,1)S(1)} %collective-permute-done.10.refs_1_, ...), custom_call_target="tpu_custom_call" | custom-call | tf_op jit(solution)/shard_map/pallas_call | solution.py:236
  (27 shorter events, 0.4 us)
Async XLA Ops:
  3.3 3.4 %copy-start.1 = (bf16[4,4,128,128]{3,2,1,0:T(8,128)(2,1)S(1)}, bf16[4,4,128,128]{3,2,1,0:T(8,128)(2,1)}, u32[]{:S(2)}) copy-start(bf16[4,4,128,128]{3,2,1,0:T(8,128)(2,1)} %get-tuple-element.39.mine_ref) | copy-start | bytes 1572868
  3.3 3.4 %collective-permute-start = (bf16[4,4,128,128]{3,2,1,0:T(8,128)(2,1)}, bf16[4,4,128,128]{3,2,1,0:T(8,128)(2,1)S(1)}, u32[]{:S(2)}, u32[]{:S(2)}) collective-permute-start(bf16[4,4,128,128]{3,2,1,0:T(8,128)(2,1)} %get-tuple-element.40), channel_id=1, source_target_pairs={{0,1},{1,0},{2,3},{3,2},{4,5},{5,4},{6,7},{7,6},{8,9},{9,8},{10,11... | collective-permute-start | bytes 1572872 | tf_op jit(solution)/shard_map/ppermute | solution.py:278
  6.5 2.9 %collective-permute-start.6 = (bf16[4,4,128,128]{3,2,1,0:T(8,128)(2,1)}, bf16[4,4,128,128]{3,2,1,0:T(8,128)(2,1)S(1)}, u32[]{:S(2)}, u32[]{:S(2)}) collective-permute-start(bf16[4,4,128,128]{3,2,1,0:T(8,128)(2,1)} %get-tuple-element.49), channel_id=1, source_target_pairs={{0,1},{1,0},{2,3},{3,2},{4,5},{5,4},{6,7},{7,6},{8,9},{9,8},{10,11... | collective-permute-start | bytes 1572872 | tf_op jit(solution)/shard_map/ppermute | solution.py:278
  6.6 2.8 %copy-start = (bf16[4,4,128,128]{3,2,1,0:T(8,128)(2,1)S(1)}, bf16[4,4,128,128]{3,2,1,0:T(8,128)(2,1)}, u32[]{:S(2)}) copy-start(bf16[4,4,128,128]{3,2,1,0:T(8,128)(2,1)} %get-tuple-element.48.mine_ref) | copy-start | bytes 1572868
  6.7 8.5 %collective-permute-start.1 = (bf16[2,4,128,128]{3,2,1,0:T(8,128)(2,1)S(1)}, bf16[2,4,128,128]{3,2,1,0:T(8,128)(2,1)S(1)}, u32[]{:S(2)}, u32[]{:S(2)}) collective-permute-start(bf16[2,4,128,128]{3,2,1,0:T(8,128)(2,1)S(1)} %get-tuple-element.42), channel_id=1, source_target_pairs={{0,6},{2,4},{4,2},{6,0},{8,14},{10,12},{12,10},{14,8},{16,22},{18,... | collective-permute-start | bytes 786440 | tf_op jit(solution)/shard_map/ppermute | solution.py:269
  8.9 13.3 %collective-permute-start.2 = (bf16[2,4,128,128]{3,2,1,0:T(8,128)(2,1)S(1)}, bf16[2,4,128,128]{3,2,1,0:T(8,128)(2,1)S(1)}, u32[]{:S(2)}, u32[]{:S(2)}) collective-permute-start(bf16[2,4,128,128]{3,2,1,0:T(8,128)(2,1)S(1)} %get-tuple-element.43), channel_id=1, source_target_pairs={{0,4},{2,6},{4,0},{6,2},{8,12},{10,14},{12,8},{14,10},{16,20},{18,... | collective-permute-start | bytes 786440 | tf_op jit(solution)/shard_map/ppermute | solution.py:269
  9.2 13.1 %collective-permute-start.3 = (bf16[2,4,128,128]{3,2,1,0:T(8,128)(2,1)S(1)}, bf16[2,4,128,128]{3,2,1,0:T(8,128)(2,1)S(1)}, u32[]{:S(2)}, u32[]{:S(2)}) collective-permute-start(bf16[2,4,128,128]{3,2,1,0:T(8,128)(2,1)S(1)} %get-tuple-element.44), channel_id=1, source_target_pairs={{0,2},{2,0},{4,6},{6,4},{8,10},{10,8},{12,14},{14,12},{16,18},{18,... | collective-permute-start | bytes 786440 | tf_op jit(solution)/shard_map/ppermute | solution.py:269
  9.5 22.1 %collective-permute-start.7 = (bf16[2,4,128,128]{3,2,1,0:T(8,128)(2,1)S(1)}, bf16[2,4,128,128]{3,2,1,0:T(8,128)(2,1)S(1)}, u32[]{:S(2)}, u32[]{:S(2)}) collective-permute-start(bf16[2,4,128,128]{3,2,1,0:T(8,128)(2,1)S(1)} %get-tuple-element.50), channel_id=1, source_target_pairs={{0,6},{2,4},{4,2},{6,0},{8,14},{10,12},{12,10},{14,8},{16,22},{18,... | collective-permute-start | bytes 786440 | tf_op jit(solution)/shard_map/ppermute | solution.py:269
  22.2 6.0 %copy-start.2 = (s32[4096]{0:T(1024)S(1)}, s32[4096]{0:T(1024)}, u32[]{:S(2)}) copy-start(s32[4096]{0:T(1024)} %param.9) | copy-start | bytes 49156
  22.4 9.2 %collective-permute-start.4 = (bf16[4,256,128]{2,1,0:T(8,128)(2,1)S(1)}, bf16[4,256,128]{2,1,0:T(8,128)(2,1)S(1)}, u32[]{:S(2)}, u32[]{:S(2)}) collective-permute-start(bf16[4,256,128]{2,1,0:T(8,128)(2,1)S(1)} %get-tuple-element.46), channel_id=1, source_target_pairs={{0,8},{8,0},{2,10},{10,2},{4,12},{12,4},{6,14},{14,6},{16,24},{24,... | collective-permute-start | bytes 786440 | tf_op jit(solution)/shard_map/ppermute | solution.py:293
  22.5 10.1 %collective-permute-start.5 = (bf16[4,256,128]{2,1,0:T(8,128)(2,1)S(1)}, bf16[4,256,128]{2,1,0:T(8,128)(2,1)S(1)}, u32[]{:S(2)}, u32[]{:S(2)}) collective-permute-start(bf16[4,256,128]{2,1,0:T(8,128)(2,1)S(1)} %get-tuple-element.47), channel_id=1, source_target_pairs={{8,16},{16,8},{10,18},{18,10},{12,20},{20,12},{14,22},{22,14},{9,1... | collective-permute-start | bytes 786440 | tf_op jit(solution)/shard_map/ppermute | solution.py:294
  26.9 8.5 %collective-permute-start.8 = (bf16[2,4,128,128]{3,2,1,0:T(8,128)(2,1)S(1)}, bf16[2,4,128,128]{3,2,1,0:T(8,128)(2,1)S(1)}, u32[]{:S(2)}, u32[]{:S(2)}) collective-permute-start(bf16[2,4,128,128]{3,2,1,0:T(8,128)(2,1)S(1)} %get-tuple-element.55), channel_id=1, source_target_pairs={{0,4},{2,6},{4,0},{6,2},{8,12},{10,14},{12,8},{14,10},{16,20},{18,... | collective-permute-start | bytes 786440 | tf_op jit(solution)/shard_map/ppermute | solution.py:269
  28.2 7.2 %collective-permute-start.9 = (bf16[2,4,128,128]{3,2,1,0:T(8,128)(2,1)S(1)}, bf16[2,4,128,128]{3,2,1,0:T(8,128)(2,1)S(1)}, u32[]{:S(2)}, u32[]{:S(2)}) collective-permute-start(bf16[2,4,128,128]{3,2,1,0:T(8,128)(2,1)S(1)} %get-tuple-element.56), channel_id=1, source_target_pairs={{0,2},{2,0},{4,6},{6,4},{8,10},{10,8},{12,14},{14,12},{16,18},{18,... | collective-permute-start | bytes 786440 | tf_op jit(solution)/shard_map/ppermute | solution.py:269
  33.8 9.3 %collective-permute-start.11 = (bf16[2,4,128,128]{3,2,1,0:T(8,128)(2,1)S(1)}, bf16[2,4,128,128]{3,2,1,0:T(8,128)(2,1)S(1)}, u32[]{:S(2)}, u32[]{:S(2)}) collective-permute-start(bf16[2,4,128,128]{3,2,1,0:T(8,128)(2,1)S(1)} %get-tuple-element.57), channel_id=1, source_target_pairs={{0,2},{2,0},{4,6},{6,4},{8,10},{10,8},{12,14},{14,12},{16,18},{18,... | collective-permute-start | bytes 786440 | tf_op jit(solution)/shard_map/ppermute | solution.py:269
  35.1 8.0 %collective-permute-start.10 = (bf16[2,4,128,128]{3,2,1,0:T(8,128)(2,1)S(1)}, bf16[2,4,128,128]{3,2,1,0:T(8,128)(2,1)S(1)}, u32[]{:S(2)}, u32[]{:S(2)}) collective-permute-start(bf16[2,4,128,128]{3,2,1,0:T(8,128)(2,1)S(1)} %get-tuple-element.58), channel_id=1, source_target_pairs={{0,4},{2,6},{4,0},{6,2},{8,12},{10,14},{12,8},{14,10},{16,20},{18,... | collective-permute-start | bytes 786440 | tf_op jit(solution)/shard_map/ppermute | solution.py:269
  35.5 7.6 %collective-permute-start.14 = (bf16[4,256,128]{2,1,0:T(8,128)(2,1)S(1)}, bf16[4,256,128]{2,1,0:T(8,128)(2,1)S(1)}, u32[]{:S(2)}, u32[]{:S(2)}) collective-permute-start(bf16[4,256,128]{2,1,0:T(8,128)(2,1)S(1)} %get-tuple-element.67), channel_id=1, source_target_pairs={{0,8},{8,0},{2,10},{10,2},{4,12},{12,4},{6,14},{14,6},{16,24},{24,... | collective-permute-start | bytes 786440 | tf_op jit(solution)/shard_map/ppermute | solution.py:293
  35.6 8.0 %collective-permute-start.15 = (bf16[4,256,128]{2,1,0:T(8,128)(2,1)S(1)}, bf16[4,256,128]{2,1,0:T(8,128)(2,1)S(1)}, u32[]{:S(2)}, u32[]{:S(2)}) collective-permute-start(bf16[4,256,128]{2,1,0:T(8,128)(2,1)S(1)} %get-tuple-element.68), channel_id=1, source_target_pairs={{8,16},{16,8},{10,18},{18,10},{12,20},{20,12},{14,22},{22,14},{9,1... | collective-permute-start | bytes 786440 | tf_op jit(solution)/shard_map/ppermute | solution.py:294
  38.7 8.9 %collective-permute-start.12 = (bf16[2,4,128,128]{3,2,1,0:T(8,128)(2,1)S(1)}, bf16[2,4,128,128]{3,2,1,0:T(8,128)(2,1)S(1)}, u32[]{:S(2)}, u32[]{:S(2)}) collective-permute-start(bf16[2,4,128,128]{3,2,1,0:T(8,128)(2,1)S(1)} %get-tuple-element.59), channel_id=1, source_target_pairs={{0,6},{2,4},{4,2},{6,0},{8,14},{10,12},{12,10},{14,8},{16,22},{18,... | collective-permute-start | bytes 786440 | tf_op jit(solution)/shard_map/ppermute | solution.py:269
  44.8 10.9 %collective-permute-start.16 = (bf16[2,4,128,128]{3,2,1,0:T(8,128)(2,1)S(1)}, bf16[2,4,128,128]{3,2,1,0:T(8,128)(2,1)S(1)}, u32[]{:S(2)}, u32[]{:S(2)}) collective-permute-start(bf16[2,4,128,128]{3,2,1,0:T(8,128)(2,1)S(1)} %get-tuple-element.71), channel_id=1, source_target_pairs={{0,4},{2,6},{4,0},{6,2},{8,12},{10,14},{12,8},{14,10},{16,20},{18,... | collective-permute-start | bytes 786440 | tf_op jit(solution)/shard_map/ppermute | solution.py:269
  45.9 9.8 %collective-permute-start.17 = (bf16[2,4,128,128]{3,2,1,0:T(8,128)(2,1)S(1)}, bf16[2,4,128,128]{3,2,1,0:T(8,128)(2,1)S(1)}, u32[]{:S(2)}, u32[]{:S(2)}) collective-permute-start(bf16[2,4,128,128]{3,2,1,0:T(8,128)(2,1)S(1)} %get-tuple-element.72), channel_id=1, source_target_pairs={{0,2},{2,0},{4,6},{6,4},{8,10},{10,8},{12,14},{14,12},{16,18},{18,... | collective-permute-start | bytes 786440 | tf_op jit(solution)/shard_map/ppermute | solution.py:269
  46.1 9.6 %collective-permute-start.18 = (bf16[2,4,128,128]{3,2,1,0:T(8,128)(2,1)S(1)}, bf16[2,4,128,128]{3,2,1,0:T(8,128)(2,1)S(1)}, u32[]{:S(2)}, u32[]{:S(2)}) collective-permute-start(bf16[2,4,128,128]{3,2,1,0:T(8,128)(2,1)S(1)} %get-tuple-element.73), channel_id=1, source_target_pairs={{0,6},{2,4},{4,2},{6,0},{8,14},{10,12},{12,10},{14,8},{16,22},{18,... | collective-permute-start | bytes 786440 | tf_op jit(solution)/shard_map/ppermute | solution.py:269
  47.6 13.2 %collective-permute-start.13 = (bf16[4,4,128,128]{3,2,1,0:T(8,128)(2,1)S(1)}, bf16[4,4,128,128]{3,2,1,0:T(8,128)(2,1)S(1)}, u32[]{:S(2)}, u32[]{:S(2)}) collective-permute-start(bf16[4,4,128,128]{3,2,1,0:T(8,128)(2,1)S(1)} %shard_map.93), channel_id=1, source_target_pairs={{0,1},{1,0},{2,3},{3,2},{4,5},{5,4},{6,7},{7,6},{8,9},{9,8},{10,11... | collective-permute-start | bytes 1572872 | tf_op jit(solution)/shard_map/ppermute | solution.py:318
  55.8 6.6 %collective-permute-start.19 = (bf16[4,4,128,128]{3,2,1,0:T(8,128)(2,1)S(1)}, bf16[4,4,128,128]{3,2,1,0:T(8,128)(2,1)S(1)}, u32[]{:S(2)}, u32[]{:S(2)}) collective-permute-start(bf16[4,4,128,128]{3,2,1,0:T(8,128)(2,1)S(1)} %shard_map.95), channel_id=1, source_target_pairs={{0,1},{1,0},{2,3},{3,2},{4,5},{5,4},{6,7},{7,6},{8,9},{9,8},{10,11... | collective-permute-start | bytes 1572872 | tf_op jit(solution)/shard_map/ppermute | solution.py:318

commit v7 on v6

--- a/solution.py
+++ b/solution.py
@@ -16,7 +16,7 @@
 ORDER_OUT = (0, 2, 1, 3)
 SCALE = 1.0 / math.sqrt(DH)
 VMEM = 12 * 1024 * 1024
-PACK_VMEM = 56 * 1024 * 1024
+PACK_VMEM = 53 * 1024 * 1024
 PACK_STEPS = 2
 WHOLE = pl.BlockSpec(memory_space=pltpu.VMEM)
 
@@ -155,29 +155,29 @@
     )(*args)
 
 
-def pack_kernel(j, chunks, *refs):
+def pack_kernel(chunks, *refs):
     ins, outs = refs[:4], refs[4:]
     block, width = ins[0].shape
     core, place = lax.axis_index("head"), lax.axis_index("blk") % GROUP
     at = pl.ds(pl.multiple_of(pl.program_id(0) * block, block), block)
-    for s in range(GROUP):
+    for j in range(chunks):
         for which in range(2):
-            base = (core ^ which) * (width // 2) + ((place ^ s) * chunks + j) * DH
-            first = pl.multiple_of(base, DH)
-            for m, ref in enumerate(ins):
-                outs[which][s, m, at] = ref[:, pl.ds(first, DH)]
-
-
-def pack(arrays, j, chunks):
+            for s in range(GROUP):
+                base = (core ^ which) * (width // 2) + ((place ^ s) * chunks + j) * DH
+                first = pl.multiple_of(base, DH)
+                for m, ref in enumerate(ins):
+                    outs[2 * j + which][s, m, at] = ref[:, pl.ds(first, DH)]
+
+
+def pack(arrays, chunks):
     rows, width = arrays[0].shape
     block = rows // PACK_STEPS
-    outs = [shape(GROUP, 4, rows, DH)] * 2
     return pl.pallas_call(
-        functools.partial(pack_kernel, j, chunks),
+        functools.partial(pack_kernel, chunks),
         grid=(PACK_STEPS,),
-        out_shape=outs,
+        out_shape=[shape(GROUP, 4, rows, DH)] * (2 * chunks),
         in_specs=[pl.BlockSpec((block, width), lambda i: (i, 0))] * 4,
-        out_specs=[WHOLE] * len(outs),
+        out_specs=[WHOLE] * (2 * chunks),
         compiler_params=pltpu.CompilerParams(vmem_limit_bytes=PACK_VMEM),
     )(*arrays)
 
@@ -272,9 +272,10 @@
     inputs = (query_rows, key_rows, value_rows, out_grad)
     unit = 2 * DH * edge * edge * 6
 
+    packed = pack(inputs, chunks)
     arrived = []
     for j in range(chunks):
-        mine, other = pack(inputs, j, chunks)
+        mine, other = packed[2 * j : 2 * j + 2]
         theirs = lax.ppermute(other, "head", swap)
         joined = call(join_kernel, [shape(2, 4, half, DH)] * GROUP, mine, theirs)
         arrived.append([hop(joined[s], s) for s in ORDER_IN])

time: 64.3 us -> 63.5 us (0.988)
  Pallas kernels: 16.2 us -> 13.8 us
  waiting for transfers between devices: 15.7 us -> 17.4 us
    pallas_call x2 -> x1, Pallas kernels: 5.23 us -> 2.86 us  [pack(): pl.pallas_call(functools.partial(pack_kernel, chunks), grid=(PACK_STEPS,)...]
    ppermute x2, waiting for transfers between devices: 0.01 us -> 1.75 us  [body(): theirs = lax.ppermute(other, 'head', swap)]
  transfers between devices with their start and end apart: 20 -> 20, of which waited for: 6 -> 7; matrix products, arithmetic and copies ran while one was open for 0% -> 0% of each run, Pallas kernels for 19% -> 15%
where the time goes in v7:
time: 63.5 us; the launch traced here: 63.1 us
  starting transfers between devices  31 us (49%)
  waiting for transfers between devices  17.4 us (27%)
  Pallas kernels  13.8 us (22%)
  between operations  0.79 us (1%)
    ppermute x12, waiting for transfers between devices, hop(): lax.ppermute(block, 'blk', [(i, i ^ s) for i in range(positions)])  12.7 us
    ppermute x12, starting transfers between devices, hop(): lax.ppermute(block, 'blk', [(i, i ^ s) for i in range(positions)])  11.8 us
    ppermute x2, starting transfers between devices, swap_back(): return back + [lax.ppermute(away, 'head', swap)]  10.9 us
    pallas_call x10, Pallas kernels, call(): pl.pallas_call(kernel, out_shape=out_shape, in_specs=[WHOLE] * len(args),...  9.48 us
    ppermute x2, starting transfers between devices, halo(): return (even, lax.ppermute(to_odd, 'blk', plane_pairs(1)))  7.52 us
    pallas_call x1, Pallas kernels, pack(): pl.pallas_call(functools.partial(pack_kernel, chunks), grid=(PACK_STEPS,)...  2.86 us
    ppermute x2, waiting for transfers between devices, body(): theirs = lax.ppermute(other, 'head', swap)  1.75 us
    ppermute x2, waiting for transfers between devices, swap_back(): return back + [lax.ppermute(away, 'head', swap)]  1.54 us
  transfers between devices with their start and end apart: 20, of which 7 were waited for; matrix products, arithmetic and copies ran while one was open for 0% of the time, Pallas kernels for 15%

profile of v7, /device:TPU:9, one launch (start us, length us, event | category | flops | bytes accessed | tf_op | source)
XLA Modules:
  0.0 63.1 jit_solution(15638555823110118947)
XLA Ops:
  0.6 2.9 %shard_map.84 = (bf16[4,4,128,128]{3,2,1,0:T(8,128)(2,1)S(1)}, bf16[4,4,128,128]{3,2,1,0:T(8,128)(2,1)}, bf16[4,4,128,128]{3,2,1,0:T(8,128)(2,1)}, bf16[4,4,128,128]{3,2,1,0:T(8,128)(2,1)}) custom-call(bf16[128,2048]{1,0:T(8,128)(2,1)} %refs_0_.1, bf16[128,2048]{1,0:T(8,128)(2,1)} %refs_1_.1, bf16[128,2048]{1,0:T(8,128)(2,1)} %refs_2_.1, ...), custom_call_target="tpu_custom_call" | custom-call | tf_op jit(solution)/shard_map/pallas_call | solution.py:175
  3.5 0.7 %collective-permute-start = (bf16[4,4,128,128]{3,2,1,0:T(8,128)(2,1)}, bf16[4,4,128,128]{3,2,1,0:T(8,128)(2,1)S(1)}, u32[]{:S(2)}, u32[]{:S(2)}) collective-permute-start(bf16[4,4,128,128]{3,2,1,0:T(8,128)(2,1)} %get-tuple-element.40), channel_id=1, source_target_pairs={{0,1},{1,0},{2,3},{3,2},{4,5},{5,4},{6,7},{7,6},{8,9},{9,8},{10,11... | collective-permute-start | bytes 1572872 | tf_op jit(solution)/shard_map/ppermute | solution.py:279
  4.2 1.7 %collective-permute-done.received_ref = bf16[4,4,128,128]{3,2,1,0:T(8,128)(2,1)S(1)} collective-permute-done((bf16[4,4,128,128]{3,2,1,0:T(8,128)(2,1)}, bf16[4,4,128,128]{3,2,1,0:T(8,128)(2,1)S(1)}, u32[]{:S(2)}, u32[]{:S(2)}) %collective-permute-start) | collective-permute-done | bytes 524320 | tf_op jit(solution)/shard_map/ppermute | solution.py:279
  6.0 2.2 %collective-permute-start.1 = (bf16[2,4,128,128]{3,2,1,0:T(8,128)(2,1)S(1)}, bf16[2,4,128,128]{3,2,1,0:T(8,128)(2,1)S(1)}, u32[]{:S(2)}, u32[]{:S(2)}) collective-permute-start(bf16[2,4,128,128]{3,2,1,0:T(8,128)(2,1)S(1)} %get-tuple-element.42), channel_id=1, source_target_pairs={{0,6},{2,4},{4,2},{6,0},{8,14},{10,12},{12,10},{14,8},{16,22},{18,... | collective-permute-start | bytes 786440 | tf_op jit(solution)/shard_map/ppermute | solution.py:269
  8.2 0.2 collective-permute-start.2
  8.5 0.3 collective-permute-start.3
  8.8 2.2 %collective-permute-start.7 = (bf16[2,4,128,128]{3,2,1,0:T(8,128)(2,1)S(1)}, bf16[2,4,128,128]{3,2,1,0:T(8,128)(2,1)S(1)}, u32[]{:S(2)}, u32[]{:S(2)}) collective-permute-start(bf16[2,4,128,128]{3,2,1,0:T(8,128)(2,1)S(1)} %get-tuple-element.50), channel_id=1, source_target_pairs={{0,6},{2,4},{4,2},{6,0},{8,14},{10,12},{12,10},{14,8},{16,22},{18,... | collective-permute-start | bytes 786440 | tf_op jit(solution)/shard_map/ppermute | solution.py:269
  11.0 3.5 %collective-permute-done.1.refs_1_ = bf16[2,4,128,128]{3,2,1,0:T(8,128)(2,1)S(1)} collective-permute-done((bf16[2,4,128,128]{3,2,1,0:T(8,128)(2,1)S(1)}, bf16[2,4,128,128]{3,2,1,0:T(8,128)(2,1)S(1)}, u32[]{:S(2)}, u32[]{:S(2)}) %collective-permute-start.1) | collective-permute-done | bytes 262176 | tf_op jit(solution)/shard_map/ppermute | solution.py:269
  14.5 6.9 %collective-permute-done.2.refs_2_ = bf16[2,4,128,128]{3,2,1,0:T(8,128)(2,1)S(1)} collective-permute-done((bf16[2,4,128,128]{3,2,1,0:T(8,128)(2,1)S(1)}, bf16[2,4,128,128]{3,2,1,0:T(8,128)(2,1)S(1)}, u32[]{:S(2)}, u32[]{:S(2)}) %collective-permute-start.2) | collective-permute-done | bytes 262176 | tf_op jit(solution)/shard_map/ppermute | solution.py:269
  21.5 0.1 shard_map.86
  21.6 0.1 collective-permute-start.4
  21.7 4.5 %collective-permute-start.5 = (bf16[4,256,128]{2,1,0:T(8,128)(2,1)S(1)}, bf16[4,256,128]{2,1,0:T(8,128)(2,1)S(1)}, u32[]{:S(2)}, u32[]{:S(2)}) collective-permute-start(bf16[4,256,128]{2,1,0:T(8,128)(2,1)S(1)} %get-tuple-element.47), channel_id=1, source_target_pairs={{8,16},{16,8},{10,18},{18,10},{12,20},{20,12},{14,22},{22,14},{9,1... | collective-permute-start | bytes 786440 | tf_op jit(solution)/shard_map/ppermute | solution.py:295
  26.2 1.3 %collective-permute-start.8 = (bf16[2,4,128,128]{3,2,1,0:T(8,128)(2,1)S(1)}, bf16[2,4,128,128]{3,2,1,0:T(8,128)(2,1)S(1)}, u32[]{:S(2)}, u32[]{:S(2)}) collective-permute-start(bf16[2,4,128,128]{3,2,1,0:T(8,128)(2,1)S(1)} %get-tuple-element.55), channel_id=1, source_target_pairs={{0,4},{2,6},{4,0},{6,2},{8,12},{10,14},{12,8},{14,10},{16,20},{18,... | collective-permute-start | bytes 786440 | tf_op jit(solution)/shard_map/ppermute | solution.py:269
  27.5 3.2 %shard_map.87.res_ref = bf16[4,1024,128]{2,1,0:T(8,128)(2,1)S(1)} custom-call(bf16[4,1024,128]{2,1,0:T(8,128)(2,1)S(1)} %get-tuple-element.45.ext_ref, s32[32,128]{1,0:T(8,128)S(1)} %bitcast.1), custom_call_target="tpu_custom_call" | custom-call | flops 1 | bytes 1 | tf_op jit(solution)/shard_map/pallas_call | solution.py:147
  30.8 1.0 %collective-permute-done.5.odd_ref = bf16[4,256,128]{2,1,0:T(8,128)(2,1)S(1)} collective-permute-done((bf16[4,256,128]{2,1,0:T(8,128)(2,1)S(1)}, bf16[4,256,128]{2,1,0:T(8,128)(2,1)S(1)}, u32[]{:S(2)}, u32[]{:S(2)}) %collective-permute-start.5) | collective-permute-done | bytes 262176 | tf_op jit(solution)/shard_map/ppermute | solution.py:295
  31.8 1.3 %shard_map.89 = (bf16[2,4,128,128]{3,2,1,0:T(8,128)(2,1)S(1)}, bf16[2,4,128,128]{3,2,1,0:T(8,128)(2,1)S(1)}, bf16[2,4,128,128]{3,2,1,0:T(8,128)(2,1)S(1)}, bf16[2,4,128,128]{3,2,1,0:T(8,128)(2,1)S(1)}) custom-call(bf16[4,1024,128]{2,1,0:T(8,128)(2,1)S(1)} %get-tuple-element.45.ext_ref, bf16[4,256,128]{2,1,0:T(8,128)(2,1)S(1)} %collective-permute-done.4.even_ref, ...), custom_call_target="tpu_custom_call" | custom-call | flops 1 | bytes 1 | tf_op jit(solution)/shard_map/pallas_call | solution.py:147
  33.1 1.3 %collective-permute-start.11 = (bf16[2,4,128,128]{3,2,1,0:T(8,128)(2,1)S(1)}, bf16[2,4,128,128]{3,2,1,0:T(8,128)(2,1)S(1)}, u32[]{:S(2)}, u32[]{:S(2)}) collective-permute-start(bf16[2,4,128,128]{3,2,1,0:T(8,128)(2,1)S(1)} %get-tuple-element.57), channel_id=1, source_target_pairs={{0,2},{2,0},{4,6},{6,4},{8,10},{10,8},{12,14},{14,12},{16,18},{18,... | collective-permute-start | bytes 786440 | tf_op jit(solution)/shard_map/ppermute | solution.py:269
  34.3 0.3 collective-permute-start.10
  34.6 0.1 shard_map.90
  34.8 3.0 %collective-permute-start.15 = (bf16[4,256,128]{2,1,0:T(8,128)(2,1)S(1)}, bf16[4,256,128]{2,1,0:T(8,128)(2,1)S(1)}, u32[]{:S(2)}, u32[]{:S(2)}) collective-permute-start(bf16[4,256,128]{2,1,0:T(8,128)(2,1)S(1)} %get-tuple-element.68), channel_id=1, source_target_pairs={{8,16},{16,8},{10,18},{18,10},{12,20},{20,12},{14,22},{22,14},{9,1... | collective-permute-start | bytes 786440 | tf_op jit(solution)/shard_map/ppermute | solution.py:295
  37.9 1.2 %collective-permute-start.12 = (bf16[2,4,128,128]{3,2,1,0:T(8,128)(2,1)S(1)}, bf16[2,4,128,128]{3,2,1,0:T(8,128)(2,1)S(1)}, u32[]{:S(2)}, u32[]{:S(2)}) collective-permute-start(bf16[2,4,128,128]{3,2,1,0:T(8,128)(2,1)S(1)} %get-tuple-element.59), channel_id=1, source_target_pairs={{0,6},{2,4},{4,2},{6,0},{8,14},{10,12},{12,10},{14,8},{16,22},{18,... | collective-permute-start | bytes 786440 | tf_op jit(solution)/shard_map/ppermute | solution.py:269
  39.1 3.2 %shard_map.91.res_ref = bf16[4,1024,128]{2,1,0:T(8,128)(2,1)S(1)} custom-call(bf16[4,1024,128]{2,1,0:T(8,128)(2,1)S(1)} %get-tuple-element.64.ext_ref, s32[32,128]{1,0:T(8,128)S(1)} %bitcast.3), custom_call_target="tpu_custom_call" | custom-call | flops 1 | bytes 1 | tf_op jit(solution)/shard_map/pallas_call | solution.py:147
  42.4 0.4 collective-permute-done.15.odd_ref
  42.8 1.3 %shard_map.93 = (bf16[2,4,128,128]{3,2,1,0:T(8,128)(2,1)S(1)}, bf16[2,4,128,128]{3,2,1,0:T(8,128)(2,1)S(1)}, bf16[2,4,128,128]{3,2,1,0:T(8,128)(2,1)S(1)}, bf16[2,4,128,128]{3,2,1,0:T(8,128)(2,1)S(1)}) custom-call(bf16[4,1024,128]{2,1,0:T(8,128)(2,1)S(1)} %get-tuple-element.64.ext_ref, bf16[4,256,128]{2,1,0:T(8,128)(2,1)S(1)} %collective-permute-done.14.even_ref, ...), custom_call_target="tpu_custom_call" | custom-call | flops 1 | bytes 1 | tf_op jit(solution)/shard_map/pallas_call | solution.py:147
  44.1 1.1 %collective-permute-start.16 = (bf16[2,4,128,128]{3,2,1,0:T(8,128)(2,1)S(1)}, bf16[2,4,128,128]{3,2,1,0:T(8,128)(2,1)S(1)}, u32[]{:S(2)}, u32[]{:S(2)}) collective-permute-start(bf16[2,4,128,128]{3,2,1,0:T(8,128)(2,1)S(1)} %get-tuple-element.71), channel_id=1, source_target_pairs={{0,4},{2,6},{4,0},{6,2},{8,12},{10,14},{12,8},{14,10},{16,20},{18,... | collective-permute-start | bytes 786440 | tf_op jit(solution)/shard_map/ppermute | solution.py:269
  45.2 0.2 collective-permute-start.17
  45.3 1.5 %collective-permute-start.18 = (bf16[2,4,128,128]{3,2,1,0:T(8,128)(2,1)S(1)}, bf16[2,4,128,128]{3,2,1,0:T(8,128)(2,1)S(1)}, u32[]{:S(2)}, u32[]{:S(2)}) collective-permute-start(bf16[2,4,128,128]{3,2,1,0:T(8,128)(2,1)S(1)} %get-tuple-element.73), channel_id=1, source_target_pairs={{0,6},{2,4},{4,2},{6,0},{8,14},{10,12},{12,10},{14,8},{16,22},{18,... | collective-permute-start | bytes 786440 | tf_op jit(solution)/shard_map/ppermute | solution.py:269
  46.8 5.9 %collective-permute-start.13 = (bf16[4,4,128,128]{3,2,1,0:T(8,128)(2,1)S(1)}, bf16[4,4,128,128]{3,2,1,0:T(8,128)(2,1)S(1)}, u32[]{:S(2)}, u32[]{:S(2)}) collective-permute-start(bf16[4,4,128,128]{3,2,1,0:T(8,128)(2,1)S(1)} %shard_map.92), channel_id=1, source_target_pairs={{0,1},{1,0},{2,3},{3,2},{4,5},{5,4},{6,7},{7,6},{8,9},{9,8},{10,11... | collective-permute-start | bytes 1572872 | tf_op jit(solution)/shard_map/ppermute | solution.py:319
  52.7 2.3 %collective-permute-done.16.refs_1_.refs_6_ = bf16[2,4,128,128]{3,2,1,0:T(8,128)(2,1)S(1)} collective-permute-done((bf16[2,4,128,128]{3,2,1,0:T(8,128)(2,1)S(1)}, bf16[2,4,128,128]{3,2,1,0:T(8,128)(2,1)S(1)}, u32[]{:S(2)}, u32[]{:S(2)}) %collective-permute-start.16) | collective-permute-done | bytes 262176 | tf_op jit(solution)/shard_map/ppermute | solution.py:269
  55.0 5.0 %collective-permute-start.19 = (bf16[4,4,128,128]{3,2,1,0:T(8,128)(2,1)S(1)}, bf16[4,4,128,128]{3,2,1,0:T(8,128)(2,1)S(1)}, u32[]{:S(2)}, u32[]{:S(2)}) collective-permute-start(bf16[4,4,128,128]{3,2,1,0:T(8,128)(2,1)S(1)} %shard_map.94), channel_id=1, source_target_pairs={{0,1},{1,0},{2,3},{3,2},{4,5},{5,4},{6,7},{7,6},{8,9},{9,8},{10,11... | collective-permute-start | bytes 1572872 | tf_op jit(solution)/shard_map/ppermute | solution.py:319
  60.0 1.5 %collective-permute-done.19.refs_9_ = bf16[4,4,128,128]{3,2,1,0:T(8,128)(2,1)S(1)} collective-permute-done((bf16[4,4,128,128]{3,2,1,0:T(8,128)(2,1)S(1)}, bf16[4,4,128,128]{3,2,1,0:T(8,128)(2,1)S(1)}, u32[]{:S(2)}, u32[]{:S(2)}) %collective-permute-start.19) | collective-permute-done | bytes 524320 | tf_op jit(solution)/shard_map/ppermute | solution.py:319
  61.6 1.5 %shard_map.95 = (bf16[128,2048]{1,0:T(8,128)(2,1)}, bf16[128,2048]{1,0:T(8,128)(2,1)}, bf16[128,2048]{1,0:T(8,128)(2,1)}, bf16[128,2048]{1,0:T(8,128)(2,1)}) custom-call(bf16[2,4,128,128]{3,2,1,0:T(8,128)(2,1)S(1)} %get-tuple-element.52.refs_0_, bf16[2,4,128,128]{3,2,1,0:T(8,128)(2,1)S(1)} %collective-permute-done.10.refs_1_, ...), custom_call_target="tpu_custom_call" | custom-call | tf_op jit(solution)/shard_map/pallas_call | solution.py:236
  (24 shorter events, 0.4 us)
Async XLA Ops:
  3.5 2.4 %collective-permute-start = (bf16[4,4,128,128]{3,2,1,0:T(8,128)(2,1)}, bf16[4,4,128,128]{3,2,1,0:T(8,128)(2,1)S(1)}, u32[]{:S(2)}, u32[]{:S(2)}) collective-permute-start(bf16[4,4,128,128]{3,2,1,0:T(8,128)(2,1)} %get-tuple-element.40), channel_id=1, source_target_pairs={{0,1},{1,0},{2,3},{3,2},{4,5},{5,4},{6,7},{7,6},{8,9},{9,8},{10,11... | collective-permute-start | bytes 1572872 | tf_op jit(solution)/shard_map/ppermute | solution.py:279
  4.2 4.5 %collective-permute-start.6 = (bf16[4,4,128,128]{3,2,1,0:T(8,128)(2,1)}, bf16[4,4,128,128]{3,2,1,0:T(8,128)(2,1)S(1)}, u32[]{:S(2)}, u32[]{:S(2)}) collective-permute-start(bf16[4,4,128,128]{3,2,1,0:T(8,128)(2,1)} %get-tuple-element.49), channel_id=1, source_target_pairs={{0,1},{1,0},{2,3},{3,2},{4,5},{5,4},{6,7},{7,6},{8,9},{9,8},{10,11... | collective-permute-start | bytes 1572872 | tf_op jit(solution)/shard_map/ppermute | solution.py:279
  5.9 2.8 %copy-start = (bf16[4,4,128,128]{3,2,1,0:T(8,128)(2,1)S(1)}, bf16[4,4,128,128]{3,2,1,0:T(8,128)(2,1)}, u32[]{:S(2)}) copy-start(bf16[4,4,128,128]{3,2,1,0:T(8,128)(2,1)} %get-tuple-element.48.mine_ref) | copy-start | bytes 1572868
  6.0 8.5 %collective-permute-start.1 = (bf16[2,4,128,128]{3,2,1,0:T(8,128)(2,1)S(1)}, bf16[2,4,128,128]{3,2,1,0:T(8,128)(2,1)S(1)}, u32[]{:S(2)}, u32[]{:S(2)}) collective-permute-start(bf16[2,4,128,128]{3,2,1,0:T(8,128)(2,1)S(1)} %get-tuple-element.42), channel_id=1, source_target_pairs={{0,6},{2,4},{4,2},{6,0},{8,14},{10,12},{12,10},{14,8},{16,22},{18,... | collective-permute-start | bytes 786440 | tf_op jit(solution)/shard_map/ppermute | solution.py:269
  8.2 13.2 %collective-permute-start.2 = (bf16[2,4,128,128]{3,2,1,0:T(8,128)(2,1)S(1)}, bf16[2,4,128,128]{3,2,1,0:T(8,128)(2,1)S(1)}, u32[]{:S(2)}, u32[]{:S(2)}) collective-permute-start(bf16[2,4,128,128]{3,2,1,0:T(8,128)(2,1)S(1)} %get-tuple-element.43), channel_id=1, source_target_pairs={{0,4},{2,6},{4,0},{6,2},{8,12},{10,14},{12,8},{14,10},{16,20},{18,... | collective-permute-start | bytes 786440 | tf_op jit(solution)/shard_map/ppermute | solution.py:269
  8.5 13.0 %collective-permute-start.3 = (bf16[2,4,128,128]{3,2,1,0:T(8,128)(2,1)S(1)}, bf16[2,4,128,128]{3,2,1,0:T(8,128)(2,1)S(1)}, u32[]{:S(2)}, u32[]{:S(2)}) collective-permute-start(bf16[2,4,128,128]{3,2,1,0:T(8,128)(2,1)S(1)} %get-tuple-element.44), channel_id=1, source_target_pairs={{0,2},{2,0},{4,6},{6,4},{8,10},{10,8},{12,14},{14,12},{16,18},{18,... | collective-permute-start | bytes 786440 | tf_op jit(solution)/shard_map/ppermute | solution.py:269
  8.8 22.0 %collective-permute-start.7 = (bf16[2,4,128,128]{3,2,1,0:T(8,128)(2,1)S(1)}, bf16[2,4,128,128]{3,2,1,0:T(8,128)(2,1)S(1)}, u32[]{:S(2)}, u32[]{:S(2)}) collective-permute-start(bf16[2,4,128,128]{3,2,1,0:T(8,128)(2,1)S(1)} %get-tuple-element.50), channel_id=1, source_target_pairs={{0,6},{2,4},{4,2},{6,0},{8,14},{10,12},{12,10},{14,8},{16,22},{18,... | collective-permute-start | bytes 786440 | tf_op jit(solution)/shard_map/ppermute | solution.py:269
  21.5 6.0 %copy-start.1 = (s32[4096]{0:T(1024)S(1)}, s32[4096]{0:T(1024)}, u32[]{:S(2)}) copy-start(s32[4096]{0:T(1024)} %param.9) | copy-start | bytes 49156
  21.6 9.2 %collective-permute-start.4 = (bf16[4,256,128]{2,1,0:T(8,128)(2,1)S(1)}, bf16[4,256,128]{2,1,0:T(8,128)(2,1)S(1)}, u32[]{:S(2)}, u32[]{:S(2)}) collective-permute-start(bf16[4,256,128]{2,1,0:T(8,128)(2,1)S(1)} %get-tuple-element.46), channel_id=1, source_target_pairs={{0,8},{8,0},{2,10},{10,2},{4,12},{12,4},{6,14},{14,6},{16,24},{24,... | collective-permute-start | bytes 786440 | tf_op jit(solution)/shard_map/ppermute | solution.py:294
  21.7 10.1 %collective-permute-start.5 = (bf16[4,256,128]{2,1,0:T(8,128)(2,1)S(1)}, bf16[4,256,128]{2,1,0:T(8,128)(2,1)S(1)}, u32[]{:S(2)}, u32[]{:S(2)}) collective-permute-start(bf16[4,256,128]{2,1,0:T(8,128)(2,1)S(1)} %get-tuple-element.47), channel_id=1, source_target_pairs={{8,16},{16,8},{10,18},{18,10},{12,20},{20,12},{14,22},{22,14},{9,1... | collective-permute-start | bytes 786440 | tf_op jit(solution)/shard_map/ppermute | solution.py:295
  26.2 8.5 %collective-permute-start.8 = (bf16[2,4,128,128]{3,2,1,0:T(8,128)(2,1)S(1)}, bf16[2,4,128,128]{3,2,1,0:T(8,128)(2,1)S(1)}, u32[]{:S(2)}, u32[]{:S(2)}) collective-permute-start(bf16[2,4,128,128]{3,2,1,0:T(8,128)(2,1)S(1)} %get-tuple-element.55), channel_id=1, source_target_pairs={{0,4},{2,6},{4,0},{6,2},{8,12},{10,14},{12,8},{14,10},{16,20},{18,... | collective-permute-start | bytes 786440 | tf_op jit(solution)/shard_map/ppermute | solution.py:269
  27.5 7.2 %collective-permute-start.9 = (bf16[2,4,128,128]{3,2,1,0:T(8,128)(2,1)S(1)}, bf16[2,4,128,128]{3,2,1,0:T(8,128)(2,1)S(1)}, u32[]{:S(2)}, u32[]{:S(2)}) collective-permute-start(bf16[2,4,128,128]{3,2,1,0:T(8,128)(2,1)S(1)} %get-tuple-element.56), channel_id=1, source_target_pairs={{0,2},{2,0},{4,6},{6,4},{8,10},{10,8},{12,14},{14,12},{16,18},{18,... | collective-permute-start | bytes 786440 | tf_op jit(solution)/shard_map/ppermute | solution.py:269
  33.1 9.3 %collective-permute-start.11 = (bf16[2,4,128,128]{3,2,1,0:T(8,128)(2,1)S(1)}, bf16[2,4,128,128]{3,2,1,0:T(8,128)(2,1)S(1)}, u32[]{:S(2)}, u32[]{:S(2)}) collective-permute-start(bf16[2,4,128,128]{3,2,1,0:T(8,128)(2,1)S(1)} %get-tuple-element.57), channel_id=1, source_target_pairs={{0,2},{2,0},{4,6},{6,4},{8,10},{10,8},{12,14},{14,12},{16,18},{18,... | collective-permute-start | bytes 786440 | tf_op jit(solution)/shard_map/ppermute | solution.py:269
  34.3 8.0 %collective-permute-start.10 = (bf16[2,4,128,128]{3,2,1,0:T(8,128)(2,1)S(1)}, bf16[2,4,128,128]{3,2,1,0:T(8,128)(2,1)S(1)}, u32[]{:S(2)}, u32[]{:S(2)}) collective-permute-start(bf16[2,4,128,128]{3,2,1,0:T(8,128)(2,1)S(1)} %get-tuple-element.58), channel_id=1, source_target_pairs={{0,4},{2,6},{4,0},{6,2},{8,12},{10,14},{12,8},{14,10},{16,20},{18,... | collective-permute-start | bytes 786440 | tf_op jit(solution)/shard_map/ppermute | solution.py:269
  34.7 7.6 %collective-permute-start.14 = (bf16[4,256,128]{2,1,0:T(8,128)(2,1)S(1)}, bf16[4,256,128]{2,1,0:T(8,128)(2,1)S(1)}, u32[]{:S(2)}, u32[]{:S(2)}) collective-permute-start(bf16[4,256,128]{2,1,0:T(8,128)(2,1)S(1)} %get-tuple-element.67), channel_id=1, source_target_pairs={{0,8},{8,0},{2,10},{10,2},{4,12},{12,4},{6,14},{14,6},{16,24},{24,... | collective-permute-start | bytes 786440 | tf_op jit(solution)/shard_map/ppermute | solution.py:294
  34.8 8.0 %collective-permute-start.15 = (bf16[4,256,128]{2,1,0:T(8,128)(2,1)S(1)}, bf16[4,256,128]{2,1,0:T(8,128)(2,1)S(1)}, u32[]{:S(2)}, u32[]{:S(2)}) collective-permute-start(bf16[4,256,128]{2,1,0:T(8,128)(2,1)S(1)} %get-tuple-element.68), channel_id=1, source_target_pairs={{8,16},{16,8},{10,18},{18,10},{12,20},{20,12},{14,22},{22,14},{9,1... | collective-permute-start | bytes 786440 | tf_op jit(solution)/shard_map/ppermute | solution.py:295
  37.9 8.9 %collective-permute-start.12 = (bf16[2,4,128,128]{3,2,1,0:T(8,128)(2,1)S(1)}, bf16[2,4,128,128]{3,2,1,0:T(8,128)(2,1)S(1)}, u32[]{:S(2)}, u32[]{:S(2)}) collective-permute-start(bf16[2,4,128,128]{3,2,1,0:T(8,128)(2,1)S(1)} %get-tuple-element.59), channel_id=1, source_target_pairs={{0,6},{2,4},{4,2},{6,0},{8,14},{10,12},{12,10},{14,8},{16,22},{18,... | collective-permute-start | bytes 786440 | tf_op jit(solution)/shard_map/ppermute | solution.py:269
  44.1 10.9 %collective-permute-start.16 = (bf16[2,4,128,128]{3,2,1,0:T(8,128)(2,1)S(1)}, bf16[2,4,128,128]{3,2,1,0:T(8,128)(2,1)S(1)}, u32[]{:S(2)}, u32[]{:S(2)}) collective-permute-start(bf16[2,4,128,128]{3,2,1,0:T(8,128)(2,1)S(1)} %get-tuple-element.71), channel_id=1, source_target_pairs={{0,4},{2,6},{4,0},{6,2},{8,12},{10,14},{12,8},{14,10},{16,20},{18,... | collective-permute-start | bytes 786440 | tf_op jit(solution)/shard_map/ppermute | solution.py:269
  45.2 9.8 %collective-permute-start.17 = (bf16[2,4,128,128]{3,2,1,0:T(8,128)(2,1)S(1)}, bf16[2,4,128,128]{3,2,1,0:T(8,128)(2,1)S(1)}, u32[]{:S(2)}, u32[]{:S(2)}) collective-permute-start(bf16[2,4,128,128]{3,2,1,0:T(8,128)(2,1)S(1)} %get-tuple-element.72), channel_id=1, source_target_pairs={{0,2},{2,0},{4,6},{6,4},{8,10},{10,8},{12,14},{14,12},{16,18},{18,... | collective-permute-start | bytes 786440 | tf_op jit(solution)/shard_map/ppermute | solution.py:269
  45.3 9.6 %collective-permute-start.18 = (bf16[2,4,128,128]{3,2,1,0:T(8,128)(2,1)S(1)}, bf16[2,4,128,128]{3,2,1,0:T(8,128)(2,1)S(1)}, u32[]{:S(2)}, u32[]{:S(2)}) collective-permute-start(bf16[2,4,128,128]{3,2,1,0:T(8,128)(2,1)S(1)} %get-tuple-element.73), channel_id=1, source_target_pairs={{0,6},{2,4},{4,2},{6,0},{8,14},{10,12},{12,10},{14,8},{16,22},{18,... | collective-permute-start | bytes 786440 | tf_op jit(solution)/shard_map/ppermute | solution.py:269
  46.8 13.2 %collective-permute-start.13 = (bf16[4,4,128,128]{3,2,1,0:T(8,128)(2,1)S(1)}, bf16[4,4,128,128]{3,2,1,0:T(8,128)(2,1)S(1)}, u32[]{:S(2)}, u32[]{:S(2)}) collective-permute-start(bf16[4,4,128,128]{3,2,1,0:T(8,128)(2,1)S(1)} %shard_map.92), channel_id=1, source_target_pairs={{0,1},{1,0},{2,3},{3,2},{4,5},{5,4},{6,7},{7,6},{8,9},{9,8},{10,11... | collective-permute-start | bytes 1572872 | tf_op jit(solution)/shard_map/ppermute | solution.py:319
  55.0 6.6 %collective-permute-start.19 = (bf16[4,4,128,128]{3,2,1,0:T(8,128)(2,1)S(1)}, bf16[4,4,128,128]{3,2,1,0:T(8,128)(2,1)S(1)}, u32[]{:S(2)}, u32[]{:S(2)}) collective-permute-start(bf16[4,4,128,128]{3,2,1,0:T(8,128)(2,1)S(1)} %shard_map.94), channel_id=1, source_target_pairs={{0,1},{1,0},{2,3},{3,2},{4,5},{5,4},{6,7},{7,6},{8,9},{9,8},{10,11... | collective-permute-start | bytes 1572872 | tf_op jit(solution)/shard_map/ppermute | solution.py:319

commit v8 on v7

--- a/solution.py
+++ b/solution.py
@@ -108,10 +108,9 @@
     rows = ext_ref.shape[1]
     position, core = lax.axis_index("blk"), lax.axis_index("head")
     place, parity = position % GROUP, (position // GROUP) % 2
-    result_ref[...] = res_ref[...]
-
     tiles = rows // edge
     base = (position // GROUP) * tiles
+    ends = []
 
     for side in range(2):
         from_even = parity == (1 - side)
@@ -129,8 +128,11 @@
                 tile_ids(table_ref, (base + tiles - 1) * 2),
                 tile_ids(table_ref, (base + tiles) * 2),
             )
+        ends.append((own, results, chosen))
+    result_ref[:, edge : rows - edge] = res_ref[:, edge : rows - edge]
+    for own, results, chosen in ends:
         for m, result in enumerate(results):
-            result = jnp.where(chosen, result, result_ref[m, own].astype(jnp.float32))
+            result = jnp.where(chosen, result, res_ref[m, own].astype(jnp.float32))
             result_ref[m, own] = result.astype(jnp.bfloat16)
     half = edge // 2
     for s in range(GROUP):
@@ -151,7 +153,6 @@
         out_specs=jax.tree.map(lambda _: WHOLE, out_shape),
         scratch_shapes=scratch,
         compiler_params=pltpu.CompilerParams(vmem_limit_bytes=VMEM),
-        cost_estimate=pl.CostEstimate(flops=1, bytes_accessed=1, transcendentals=0),
     )(*args)
 
 
@@ -222,11 +223,16 @@
             for which, block in enumerate((slot.at[0], received.at[s])):
                 base = (core ^ which) * (width // 2) + ((place ^ s) * chunks + j) * DH
                 blocks.append((pl.multiple_of(base, DH), block))
-    copies = [pltpu.make_async_copy(held.at[m], out, sems.at[m]) for m, out in enumerate(outs)]
-    for m, copy in enumerate(copies):
-        for first, block in blocks:
-            held[m, :, pl.ds(first, DH)] = block[m]
-        copy.start()
+    rows = held.shape[1]
+    parts = sems.shape[1]
+    copies = []
+    for m, out in enumerate(outs):
+        for i in range(parts):
+            at = slice(i * rows // parts, (i + 1) * rows // parts)
+            for first, block in blocks:
+                held[m, at, pl.ds(first, DH)] = block[m, at]
+            copies.append(pltpu.make_async_copy(held.at[m, at], out.at[at], sems.at[m, i]))
+            copies[-1].start()
     for copy in copies:
         copy.wait()
 
@@ -240,7 +246,7 @@
         out_specs=[pl.BlockSpec(memory_space=pl.ANY)] * 4,
         scratch_shapes=[
             pltpu.VMEM((4, rows, width), jnp.bfloat16),
-            pltpu.SemaphoreType.DMA((4,)),
+            pltpu.SemaphoreType.DMA((4, 2)),
         ],
         compiler_params=pltpu.CompilerParams(vmem_limit_bytes=VMEM),
     )(*blocks)

time: 63.5 us -> 63.5 us (level)
  no operation moved by 1% of the time
where the time goes in v8:
time: 63.5 us; the launch traced here: 63 us
  starting transfers between devices  31 us (49%)
  waiting for transfers between devices  17.4 us (27%)
  Pallas kernels  13.8 us (22%)
  between operations  0.79 us (1%)
    ppermute x12, waiting for transfers between devices, hop(): lax.ppermute(block, 'blk', [(i, i ^ s) for i in range(positions)])  12.7 us
    ppermute x12, starting transfers between devices, hop(): lax.ppermute(block, 'blk', [(i, i ^ s) for i in range(positions)])  11.8 us
    ppermute x2, starting transfers between devices, swap_back(): return back + [lax.ppermute(away, 'head', swap)]  10.9 us
    pallas_call x10, Pallas kernels, call(): pl.pallas_call(kernel, out_shape=out_shape, in_specs=[WHOLE] * len(args),...  9.45 us
    ppermute x2, starting transfers between devices, halo(): return (even, lax.ppermute(to_odd, 'blk', plane_pairs(1)))  7.52 us
    pallas_call x1, Pallas kernels, pack(): pl.pallas_call(functools.partial(pack_kernel, chunks), grid=(PACK_STEPS,)...  2.86 us
    ppermute x2, waiting for transfers between devices, body(): theirs = lax.ppermute(other, 'head', swap)  1.75 us
    ppermute x2, waiting for transfers between devices, swap_back(): return back + [lax.ppermute(away, 'head', swap)]  1.54 us
  transfers between devices with their start and end apart: 20, of which 7 were waited for; matrix products, arithmetic and copies ran while one was open for 0% of the time, Pallas kernels for 15%

profile of v8, /device:TPU:9, one launch (start us, length us, event | category | flops | bytes accessed | tf_op | source)
XLA Modules:
  0.0 63.0 jit_solution(1652693713607276440)
XLA Ops:
  0.6 2.9 %shard_map.84 = (bf16[4,4,128,128]{3,2,1,0:T(8,128)(2,1)S(1)}, bf16[4,4,128,128]{3,2,1,0:T(8,128)(2,1)}, bf16[4,4,128,128]{3,2,1,0:T(8,128)(2,1)}, bf16[4,4,128,128]{3,2,1,0:T(8,128)(2,1)}) custom-call(bf16[128,2048]{1,0:T(8,128)(2,1)} %refs_0_.1, bf16[128,2048]{1,0:T(8,128)(2,1)} %refs_1_.1, bf16[128,2048]{1,0:T(8,128)(2,1)} %refs_2_.1, ...), custom_call_target="tpu_custom_call" | custom-call | tf_op jit(solution)/shard_map/pallas_call | solution.py:176
  3.5 0.7 %collective-permute-start = (bf16[4,4,128,128]{3,2,1,0:T(8,128)(2,1)}, bf16[4,4,128,128]{3,2,1,0:T(8,128)(2,1)S(1)}, u32[]{:S(2)}, u32[]{:S(2)}) collective-permute-start(bf16[4,4,128,128]{3,2,1,0:T(8,128)(2,1)} %get-tuple-element.40), channel_id=1, source_target_pairs={{0,1},{1,0},{2,3},{3,2},{4,5},{5,4},{6,7},{7,6},{8,9},{9,8},{10,11... | collective-permute-start | bytes 1572872 | tf_op jit(solution)/shard_map/ppermute | solution.py:285
  4.2 1.7 %collective-permute-done.received_ref = bf16[4,4,128,128]{3,2,1,0:T(8,128)(2,1)S(1)} collective-permute-done((bf16[4,4,128,128]{3,2,1,0:T(8,128)(2,1)}, bf16[4,4,128,128]{3,2,1,0:T(8,128)(2,1)S(1)}, u32[]{:S(2)}, u32[]{:S(2)}) %collective-permute-start) | collective-permute-done | bytes 524320 | tf_op jit(solution)/shard_map/ppermute | solution.py:285
  6.0 2.2 %collective-permute-start.1 = (bf16[2,4,128,128]{3,2,1,0:T(8,128)(2,1)S(1)}, bf16[2,4,128,128]{3,2,1,0:T(8,128)(2,1)S(1)}, u32[]{:S(2)}, u32[]{:S(2)}) collective-permute-start(bf16[2,4,128,128]{3,2,1,0:T(8,128)(2,1)S(1)} %get-tuple-element.42), channel_id=1, source_target_pairs={{0,6},{2,4},{4,2},{6,0},{8,14},{10,12},{12,10},{14,8},{16,22},{18,... | collective-permute-start | bytes 786440 | tf_op jit(solution)/shard_map/ppermute | solution.py:275
  8.2 0.2 collective-permute-start.2
  8.5 0.3 collective-permute-start.3
  8.8 2.2 %collective-permute-start.7 = (bf16[2,4,128,128]{3,2,1,0:T(8,128)(2,1)S(1)}, bf16[2,4,128,128]{3,2,1,0:T(8,128)(2,1)S(1)}, u32[]{:S(2)}, u32[]{:S(2)}) collective-permute-start(bf16[2,4,128,128]{3,2,1,0:T(8,128)(2,1)S(1)} %get-tuple-element.50), channel_id=1, source_target_pairs={{0,6},{2,4},{4,2},{6,0},{8,14},{10,12},{12,10},{14,8},{16,22},{18,... | collective-permute-start | bytes 786440 | tf_op jit(solution)/shard_map/ppermute | solution.py:275
  11.0 3.5 %collective-permute-done.1.refs_1_ = bf16[2,4,128,128]{3,2,1,0:T(8,128)(2,1)S(1)} collective-permute-done((bf16[2,4,128,128]{3,2,1,0:T(8,128)(2,1)S(1)}, bf16[2,4,128,128]{3,2,1,0:T(8,128)(2,1)S(1)}, u32[]{:S(2)}, u32[]{:S(2)}) %collective-permute-start.1) | collective-permute-done | bytes 262176 | tf_op jit(solution)/shard_map/ppermute | solution.py:275
  14.5 6.9 %collective-permute-done.2.refs_2_ = bf16[2,4,128,128]{3,2,1,0:T(8,128)(2,1)S(1)} collective-permute-done((bf16[2,4,128,128]{3,2,1,0:T(8,128)(2,1)S(1)}, bf16[2,4,128,128]{3,2,1,0:T(8,128)(2,1)S(1)}, u32[]{:S(2)}, u32[]{:S(2)}) %collective-permute-start.2) | collective-permute-done | bytes 262176 | tf_op jit(solution)/shard_map/ppermute | solution.py:275
  21.5 0.1 shard_map.86
  21.6 0.1 collective-permute-start.4
  21.7 4.5 %collective-permute-start.5 = (bf16[4,256,128]{2,1,0:T(8,128)(2,1)S(1)}, bf16[4,256,128]{2,1,0:T(8,128)(2,1)S(1)}, u32[]{:S(2)}, u32[]{:S(2)}) collective-permute-start(bf16[4,256,128]{2,1,0:T(8,128)(2,1)S(1)} %get-tuple-element.47), channel_id=1, source_target_pairs={{8,16},{16,8},{10,18},{18,10},{12,20},{20,12},{14,22},{22,14},{9,1... | collective-permute-start | bytes 786440 | tf_op jit(solution)/shard_map/ppermute | solution.py:301
  26.2 1.3 %collective-permute-start.8 = (bf16[2,4,128,128]{3,2,1,0:T(8,128)(2,1)S(1)}, bf16[2,4,128,128]{3,2,1,0:T(8,128)(2,1)S(1)}, u32[]{:S(2)}, u32[]{:S(2)}) collective-permute-start(bf16[2,4,128,128]{3,2,1,0:T(8,128)(2,1)S(1)} %get-tuple-element.55), channel_id=1, source_target_pairs={{0,4},{2,6},{4,0},{6,2},{8,12},{10,14},{12,8},{14,10},{16,20},{18,... | collective-permute-start | bytes 786440 | tf_op jit(solution)/shard_map/ppermute | solution.py:275
  27.5 3.2 %shard_map.87.res_ref = bf16[4,1024,128]{2,1,0:T(8,128)(2,1)S(1)} custom-call(bf16[4,1024,128]{2,1,0:T(8,128)(2,1)S(1)} %get-tuple-element.45.ext_ref, s32[32,128]{1,0:T(8,128)S(1)} %bitcast.1), custom_call_target="tpu_custom_call" | custom-call | tf_op jit(solution)/shard_map/pallas_call | solution.py:149
  30.8 1.0 %collective-permute-done.5.odd_ref = bf16[4,256,128]{2,1,0:T(8,128)(2,1)S(1)} collective-permute-done((bf16[4,256,128]{2,1,0:T(8,128)(2,1)S(1)}, bf16[4,256,128]{2,1,0:T(8,128)(2,1)S(1)}, u32[]{:S(2)}, u32[]{:S(2)}) %collective-permute-start.5) | collective-permute-done | bytes 262176 | tf_op jit(solution)/shard_map/ppermute | solution.py:301
  31.8 1.3 %shard_map.89 = (bf16[2,4,128,128]{3,2,1,0:T(8,128)(2,1)S(1)}, bf16[2,4,128,128]{3,2,1,0:T(8,128)(2,1)S(1)}, bf16[2,4,128,128]{3,2,1,0:T(8,128)(2,1)S(1)}, bf16[2,4,128,128]{3,2,1,0:T(8,128)(2,1)S(1)}) custom-call(bf16[4,1024,128]{2,1,0:T(8,128)(2,1)S(1)} %get-tuple-element.45.ext_ref, bf16[4,256,128]{2,1,0:T(8,128)(2,1)S(1)} %collective-permute-done.4.even_ref, ...), custom_call_target="tpu_custom_call" | custom-call | tf_op jit(solution)/shard_map/pallas_call | solution.py:149
  33.1 1.3 %collective-permute-start.11 = (bf16[2,4,128,128]{3,2,1,0:T(8,128)(2,1)S(1)}, bf16[2,4,128,128]{3,2,1,0:T(8,128)(2,1)S(1)}, u32[]{:S(2)}, u32[]{:S(2)}) collective-permute-start(bf16[2,4,128,128]{3,2,1,0:T(8,128)(2,1)S(1)} %get-tuple-element.57), channel_id=1, source_target_pairs={{0,2},{2,0},{4,6},{6,4},{8,10},{10,8},{12,14},{14,12},{16,18},{18,... | collective-permute-start | bytes 786440 | tf_op jit(solution)/shard_map/ppermute | solution.py:275
  34.3 0.3 collective-permute-start.10
  34.6 0.1 shard_map.90
  34.8 3.0 %collective-permute-start.15 = (bf16[4,256,128]{2,1,0:T(8,128)(2,1)S(1)}, bf16[4,256,128]{2,1,0:T(8,128)(2,1)S(1)}, u32[]{:S(2)}, u32[]{:S(2)}) collective-permute-start(bf16[4,256,128]{2,1,0:T(8,128)(2,1)S(1)} %get-tuple-element.68), channel_id=1, source_target_pairs={{8,16},{16,8},{10,18},{18,10},{12,20},{20,12},{14,22},{22,14},{9,1... | collective-permute-start | bytes 786440 | tf_op jit(solution)/shard_map/ppermute | solution.py:301
  37.9 1.2 %collective-permute-start.12 = (bf16[2,4,128,128]{3,2,1,0:T(8,128)(2,1)S(1)}, bf16[2,4,128,128]{3,2,1,0:T(8,128)(2,1)S(1)}, u32[]{:S(2)}, u32[]{:S(2)}) collective-permute-start(bf16[2,4,128,128]{3,2,1,0:T(8,128)(2,1)S(1)} %get-tuple-element.59), channel_id=1, source_target_pairs={{0,6},{2,4},{4,2},{6,0},{8,14},{10,12},{12,10},{14,8},{16,22},{18,... | collective-permute-start | bytes 786440 | tf_op jit(solution)/shard_map/ppermute | solution.py:275
  39.1 3.2 %shard_map.91.res_ref = bf16[4,1024,128]{2,1,0:T(8,128)(2,1)S(1)} custom-call(bf16[4,1024,128]{2,1,0:T(8,128)(2,1)S(1)} %get-tuple-element.64.ext_ref, s32[32,128]{1,0:T(8,128)S(1)} %bitcast.3), custom_call_target="tpu_custom_call" | custom-call | tf_op jit(solution)/shard_map/pallas_call | solution.py:149
  42.4 0.4 collective-permute-done.15.odd_ref
  42.8 1.3 %shard_map.93 = (bf16[2,4,128,128]{3,2,1,0:T(8,128)(2,1)S(1)}, bf16[2,4,128,128]{3,2,1,0:T(8,128)(2,1)S(1)}, bf16[2,4,128,128]{3,2,1,0:T(8,128)(2,1)S(1)}, bf16[2,4,128,128]{3,2,1,0:T(8,128)(2,1)S(1)}) custom-call(bf16[4,1024,128]{2,1,0:T(8,128)(2,1)S(1)} %get-tuple-element.64.ext_ref, bf16[4,256,128]{2,1,0:T(8,128)(2,1)S(1)} %collective-permute-done.14.even_ref, ...), custom_call_target="tpu_custom_call" | custom-call | tf_op jit(solution)/shard_map/pallas_call | solution.py:149
  44.0 1.1 %collective-permute-start.16 = (bf16[2,4,128,128]{3,2,1,0:T(8,128)(2,1)S(1)}, bf16[2,4,128,128]{3,2,1,0:T(8,128)(2,1)S(1)}, u32[]{:S(2)}, u32[]{:S(2)}) collective-permute-start(bf16[2,4,128,128]{3,2,1,0:T(8,128)(2,1)S(1)} %get-tuple-element.71), channel_id=1, source_target_pairs={{0,4},{2,6},{4,0},{6,2},{8,12},{10,14},{12,8},{14,10},{16,20},{18,... | collective-permute-start | bytes 786440 | tf_op jit(solution)/shard_map/ppermute | solution.py:275
  45.1 0.1 collective-permute-start.17
  45.3 1.5 %collective-permute-start.18 = (bf16[2,4,128,128]{3,2,1,0:T(8,128)(2,1)S(1)}, bf16[2,4,128,128]{3,2,1,0:T(8,128)(2,1)S(1)}, u32[]{:S(2)}, u32[]{:S(2)}) collective-permute-start(bf16[2,4,128,128]{3,2,1,0:T(8,128)(2,1)S(1)} %get-tuple-element.73), channel_id=1, source_target_pairs={{0,6},{2,4},{4,2},{6,0},{8,14},{10,12},{12,10},{14,8},{16,22},{18,... | collective-permute-start | bytes 786440 | tf_op jit(solution)/shard_map/ppermute | solution.py:275
  46.8 5.9 %collective-permute-start.13 = (bf16[4,4,128,128]{3,2,1,0:T(8,128)(2,1)S(1)}, bf16[4,4,128,128]{3,2,1,0:T(8,128)(2,1)S(1)}, u32[]{:S(2)}, u32[]{:S(2)}) collective-permute-start(bf16[4,4,128,128]{3,2,1,0:T(8,128)(2,1)S(1)} %shard_map.92), channel_id=1, source_target_pairs={{0,1},{1,0},{2,3},{3,2},{4,5},{5,4},{6,7},{7,6},{8,9},{9,8},{10,11... | collective-permute-start | bytes 1572872 | tf_op jit(solution)/shard_map/ppermute | solution.py:325
  52.7 2.3 %collective-permute-done.16.refs_1_.refs_6_ = bf16[2,4,128,128]{3,2,1,0:T(8,128)(2,1)S(1)} collective-permute-done((bf16[2,4,128,128]{3,2,1,0:T(8,128)(2,1)S(1)}, bf16[2,4,128,128]{3,2,1,0:T(8,128)(2,1)S(1)}, u32[]{:S(2)}, u32[]{:S(2)}) %collective-permute-start.16) | collective-permute-done | bytes 262176 | tf_op jit(solution)/shard_map/ppermute | solution.py:275
  55.0 5.0 %collective-permute-start.19 = (bf16[4,4,128,128]{3,2,1,0:T(8,128)(2,1)S(1)}, bf16[4,4,128,128]{3,2,1,0:T(8,128)(2,1)S(1)}, u32[]{:S(2)}, u32[]{:S(2)}) collective-permute-start(bf16[4,4,128,128]{3,2,1,0:T(8,128)(2,1)S(1)} %shard_map.94), channel_id=1, source_target_pairs={{0,1},{1,0},{2,3},{3,2},{4,5},{5,4},{6,7},{7,6},{8,9},{9,8},{10,11... | collective-permute-start | bytes 1572872 | tf_op jit(solution)/shard_map/ppermute | solution.py:325
  60.0 1.5 %collective-permute-done.19.refs_9_ = bf16[4,4,128,128]{3,2,1,0:T(8,128)(2,1)S(1)} collective-permute-done((bf16[4,4,128,128]{3,2,1,0:T(8,128)(2,1)S(1)}, bf16[4,4,128,128]{3,2,1,0:T(8,128)(2,1)S(1)}, u32[]{:S(2)}, u32[]{:S(2)}) %collective-permute-start.19) | collective-permute-done | bytes 524320 | tf_op jit(solution)/shard_map/ppermute | solution.py:325
  61.5 1.4 %shard_map.95 = (bf16[128,2048]{1,0:T(8,128)(2,1)}, bf16[128,2048]{1,0:T(8,128)(2,1)}, bf16[128,2048]{1,0:T(8,128)(2,1)}, bf16[128,2048]{1,0:T(8,128)(2,1)}) custom-call(bf16[2,4,128,128]{3,2,1,0:T(8,128)(2,1)S(1)} %get-tuple-element.52.refs_0_, bf16[2,4,128,128]{3,2,1,0:T(8,128)(2,1)S(1)} %collective-permute-done.10.refs_1_, ...), custom_call_target="tpu_custom_call" | custom-call | tf_op jit(solution)/shard_map/pallas_call | solution.py:242
  (24 shorter events, 0.4 us)
Async XLA Ops:
  3.5 2.4 %collective-permute-start = (bf16[4,4,128,128]{3,2,1,0:T(8,128)(2,1)}, bf16[4,4,128,128]{3,2,1,0:T(8,128)(2,1)S(1)}, u32[]{:S(2)}, u32[]{:S(2)}) collective-permute-start(bf16[4,4,128,128]{3,2,1,0:T(8,128)(2,1)} %get-tuple-element.40), channel_id=1, source_target_pairs={{0,1},{1,0},{2,3},{3,2},{4,5},{5,4},{6,7},{7,6},{8,9},{9,8},{10,11... | collective-permute-start | bytes 1572872 | tf_op jit(solution)/shard_map/ppermute | solution.py:285
  4.2 4.5 %collective-permute-start.6 = (bf16[4,4,128,128]{3,2,1,0:T(8,128)(2,1)}, bf16[4,4,128,128]{3,2,1,0:T(8,128)(2,1)S(1)}, u32[]{:S(2)}, u32[]{:S(2)}) collective-permute-start(bf16[4,4,128,128]{3,2,1,0:T(8,128)(2,1)} %get-tuple-element.49), channel_id=1, source_target_pairs={{0,1},{1,0},{2,3},{3,2},{4,5},{5,4},{6,7},{7,6},{8,9},{9,8},{10,11... | collective-permute-start | bytes 1572872 | tf_op jit(solution)/shard_map/ppermute | solution.py:285
  5.9 2.8 %copy-start = (bf16[4,4,128,128]{3,2,1,0:T(8,128)(2,1)S(1)}, bf16[4,4,128,128]{3,2,1,0:T(8,128)(2,1)}, u32[]{:S(2)}) copy-start(bf16[4,4,128,128]{3,2,1,0:T(8,128)(2,1)} %get-tuple-element.48.mine_ref) | copy-start | bytes 1572868
  6.0 8.5 %collective-permute-start.1 = (bf16[2,4,128,128]{3,2,1,0:T(8,128)(2,1)S(1)}, bf16[2,4,128,128]{3,2,1,0:T(8,128)(2,1)S(1)}, u32[]{:S(2)}, u32[]{:S(2)}) collective-permute-start(bf16[2,4,128,128]{3,2,1,0:T(8,128)(2,1)S(1)} %get-tuple-element.42), channel_id=1, source_target_pairs={{0,6},{2,4},{4,2},{6,0},{8,14},{10,12},{12,10},{14,8},{16,22},{18,... | collective-permute-start | bytes 786440 | tf_op jit(solution)/shard_map/ppermute | solution.py:275
  8.2 13.2 %collective-permute-start.2 = (bf16[2,4,128,128]{3,2,1,0:T(8,128)(2,1)S(1)}, bf16[2,4,128,128]{3,2,1,0:T(8,128)(2,1)S(1)}, u32[]{:S(2)}, u32[]{:S(2)}) collective-permute-start(bf16[2,4,128,128]{3,2,1,0:T(8,128)(2,1)S(1)} %get-tuple-element.43), channel_id=1, source_target_pairs={{0,4},{2,6},{4,0},{6,2},{8,12},{10,14},{12,8},{14,10},{16,20},{18,... | collective-permute-start | bytes 786440 | tf_op jit(solution)/shard_map/ppermute | solution.py:275
  8.5 13.0 %collective-permute-start.3 = (bf16[2,4,128,128]{3,2,1,0:T(8,128)(2,1)S(1)}, bf16[2,4,128,128]{3,2,1,0:T(8,128)(2,1)S(1)}, u32[]{:S(2)}, u32[]{:S(2)}) collective-permute-start(bf16[2,4,128,128]{3,2,1,0:T(8,128)(2,1)S(1)} %get-tuple-element.44), channel_id=1, source_target_pairs={{0,2},{2,0},{4,6},{6,4},{8,10},{10,8},{12,14},{14,12},{16,18},{18,... | collective-permute-start | bytes 786440 | tf_op jit(solution)/shard_map/ppermute | solution.py:275
  8.8 22.0 %collective-permute-start.7 = (bf16[2,4,128,128]{3,2,1,0:T(8,128)(2,1)S(1)}, bf16[2,4,128,128]{3,2,1,0:T(8,128)(2,1)S(1)}, u32[]{:S(2)}, u32[]{:S(2)}) collective-permute-start(bf16[2,4,128,128]{3,2,1,0:T(8,128)(2,1)S(1)} %get-tuple-element.50), channel_id=1, source_target_pairs={{0,6},{2,4},{4,2},{6,0},{8,14},{10,12},{12,10},{14,8},{16,22},{18,... | collective-permute-start | bytes 786440 | tf_op jit(solution)/shard_map/ppermute | solution.py:275
  21.5 6.0 %copy-start.1 = (s32[4096]{0:T(1024)S(1)}, s32[4096]{0:T(1024)}, u32[]{:S(2)}) copy-start(s32[4096]{0:T(1024)} %param.9) | copy-start | bytes 49156
  21.6 9.2 %collective-permute-start.4 = (bf16[4,256,128]{2,1,0:T(8,128)(2,1)S(1)}, bf16[4,256,128]{2,1,0:T(8,128)(2,1)S(1)}, u32[]{:S(2)}, u32[]{:S(2)}) collective-permute-start(bf16[4,256,128]{2,1,0:T(8,128)(2,1)S(1)} %get-tuple-element.46), channel_id=1, source_target_pairs={{0,8},{8,0},{2,10},{10,2},{4,12},{12,4},{6,14},{14,6},{16,24},{24,... | collective-permute-start | bytes 786440 | tf_op jit(solution)/shard_map/ppermute | solution.py:300
  21.7 10.1 %collective-permute-start.5 = (bf16[4,256,128]{2,1,0:T(8,128)(2,1)S(1)}, bf16[4,256,128]{2,1,0:T(8,128)(2,1)S(1)}, u32[]{:S(2)}, u32[]{:S(2)}) collective-permute-start(bf16[4,256,128]{2,1,0:T(8,128)(2,1)S(1)} %get-tuple-element.47), channel_id=1, source_target_pairs={{8,16},{16,8},{10,18},{18,10},{12,20},{20,12},{14,22},{22,14},{9,1... | collective-permute-start | bytes 786440 | tf_op jit(solution)/shard_map/ppermute | solution.py:301
  26.2 8.4 %collective-permute-start.8 = (bf16[2,4,128,128]{3,2,1,0:T(8,128)(2,1)S(1)}, bf16[2,4,128,128]{3,2,1,0:T(8,128)(2,1)S(1)}, u32[]{:S(2)}, u32[]{:S(2)}) collective-permute-start(bf16[2,4,128,128]{3,2,1,0:T(8,128)(2,1)S(1)} %get-tuple-element.55), channel_id=1, source_target_pairs={{0,4},{2,6},{4,0},{6,2},{8,12},{10,14},{12,8},{14,10},{16,20},{18,... | collective-permute-start | bytes 786440 | tf_op jit(solution)/shard_map/ppermute | solution.py:275
  27.5 7.1 %collective-permute-start.9 = (bf16[2,4,128,128]{3,2,1,0:T(8,128)(2,1)S(1)}, bf16[2,4,128,128]{3,2,1,0:T(8,128)(2,1)S(1)}, u32[]{:S(2)}, u32[]{:S(2)}) collective-permute-start(bf16[2,4,128,128]{3,2,1,0:T(8,128)(2,1)S(1)} %get-tuple-element.56), channel_id=1, source_target_pairs={{0,2},{2,0},{4,6},{6,4},{8,10},{10,8},{12,14},{14,12},{16,18},{18,... | collective-permute-start | bytes 786440 | tf_op jit(solution)/shard_map/ppermute | solution.py:275
  33.1 9.3 %collective-permute-start.11 = (bf16[2,4,128,128]{3,2,1,0:T(8,128)(2,1)S(1)}, bf16[2,4,128,128]{3,2,1,0:T(8,128)(2,1)S(1)}, u32[]{:S(2)}, u32[]{:S(2)}) collective-permute-start(bf16[2,4,128,128]{3,2,1,0:T(8,128)(2,1)S(1)} %get-tuple-element.57), channel_id=1, source_target_pairs={{0,2},{2,0},{4,6},{6,4},{8,10},{10,8},{12,14},{14,12},{16,18},{18,... | collective-permute-start | bytes 786440 | tf_op jit(solution)/shard_map/ppermute | solution.py:275
  34.3 8.0 %collective-permute-start.10 = (bf16[2,4,128,128]{3,2,1,0:T(8,128)(2,1)S(1)}, bf16[2,4,128,128]{3,2,1,0:T(8,128)(2,1)S(1)}, u32[]{:S(2)}, u32[]{:S(2)}) collective-permute-start(bf16[2,4,128,128]{3,2,1,0:T(8,128)(2,1)S(1)} %get-tuple-element.58), channel_id=1, source_target_pairs={{0,4},{2,6},{4,0},{6,2},{8,12},{10,14},{12,8},{14,10},{16,20},{18,... | collective-permute-start | bytes 786440 | tf_op jit(solution)/shard_map/ppermute | solution.py:275
  34.7 7.6 %collective-permute-start.14 = (bf16[4,256,128]{2,1,0:T(8,128)(2,1)S(1)}, bf16[4,256,128]{2,1,0:T(8,128)(2,1)S(1)}, u32[]{:S(2)}, u32[]{:S(2)}) collective-permute-start(bf16[4,256,128]{2,1,0:T(8,128)(2,1)S(1)} %get-tuple-element.67), channel_id=1, source_target_pairs={{0,8},{8,0},{2,10},{10,2},{4,12},{12,4},{6,14},{14,6},{16,24},{24,... | collective-permute-start | bytes 786440 | tf_op jit(solution)/shard_map/ppermute | solution.py:300
  34.8 8.0 %collective-permute-start.15 = (bf16[4,256,128]{2,1,0:T(8,128)(2,1)S(1)}, bf16[4,256,128]{2,1,0:T(8,128)(2,1)S(1)}, u32[]{:S(2)}, u32[]{:S(2)}) collective-permute-start(bf16[4,256,128]{2,1,0:T(8,128)(2,1)S(1)} %get-tuple-element.68), channel_id=1, source_target_pairs={{8,16},{16,8},{10,18},{18,10},{12,20},{20,12},{14,22},{22,14},{9,1... | collective-permute-start | bytes 786440 | tf_op jit(solution)/shard_map/ppermute | solution.py:301
  37.9 8.9 %collective-permute-start.12 = (bf16[2,4,128,128]{3,2,1,0:T(8,128)(2,1)S(1)}, bf16[2,4,128,128]{3,2,1,0:T(8,128)(2,1)S(1)}, u32[]{:S(2)}, u32[]{:S(2)}) collective-permute-start(bf16[2,4,128,128]{3,2,1,0:T(8,128)(2,1)S(1)} %get-tuple-element.59), channel_id=1, source_target_pairs={{0,6},{2,4},{4,2},{6,0},{8,14},{10,12},{12,10},{14,8},{16,22},{18,... | collective-permute-start | bytes 786440 | tf_op jit(solution)/shard_map/ppermute | solution.py:275
  44.0 10.9 %collective-permute-start.16 = (bf16[2,4,128,128]{3,2,1,0:T(8,128)(2,1)S(1)}, bf16[2,4,128,128]{3,2,1,0:T(8,128)(2,1)S(1)}, u32[]{:S(2)}, u32[]{:S(2)}) collective-permute-start(bf16[2,4,128,128]{3,2,1,0:T(8,128)(2,1)S(1)} %get-tuple-element.71), channel_id=1, source_target_pairs={{0,4},{2,6},{4,0},{6,2},{8,12},{10,14},{12,8},{14,10},{16,20},{18,... | collective-permute-start | bytes 786440 | tf_op jit(solution)/shard_map/ppermute | solution.py:275
  45.1 9.8 %collective-permute-start.17 = (bf16[2,4,128,128]{3,2,1,0:T(8,128)(2,1)S(1)}, bf16[2,4,128,128]{3,2,1,0:T(8,128)(2,1)S(1)}, u32[]{:S(2)}, u32[]{:S(2)}) collective-permute-start(bf16[2,4,128,128]{3,2,1,0:T(8,128)(2,1)S(1)} %get-tuple-element.72), channel_id=1, source_target_pairs={{0,2},{2,0},{4,6},{6,4},{8,10},{10,8},{12,14},{14,12},{16,18},{18,... | collective-permute-start | bytes 786440 | tf_op jit(solution)/shard_map/ppermute | solution.py:275
  45.3 9.7 %collective-permute-start.18 = (bf16[2,4,128,128]{3,2,1,0:T(8,128)(2,1)S(1)}, bf16[2,4,128,128]{3,2,1,0:T(8,128)(2,1)S(1)}, u32[]{:S(2)}, u32[]{:S(2)}) collective-permute-start(bf16[2,4,128,128]{3,2,1,0:T(8,128)(2,1)S(1)} %get-tuple-element.73), channel_id=1, source_target_pairs={{0,6},{2,4},{4,2},{6,0},{8,14},{10,12},{12,10},{14,8},{16,22},{18,... | collective-permute-start | bytes 786440 | tf_op jit(solution)/shard_map/ppermute | solution.py:275
  46.8 13.2 %collective-permute-start.13 = (bf16[4,4,128,128]{3,2,1,0:T(8,128)(2,1)S(1)}, bf16[4,4,128,128]{3,2,1,0:T(8,128)(2,1)S(1)}, u32[]{:S(2)}, u32[]{:S(2)}) collective-permute-start(bf16[4,4,128,128]{3,2,1,0:T(8,128)(2,1)S(1)} %shard_map.92), channel_id=1, source_target_pairs={{0,1},{1,0},{2,3},{3,2},{4,5},{5,4},{6,7},{7,6},{8,9},{9,8},{10,11... | collective-permute-start | bytes 1572872 | tf_op jit(solution)/shard_map/ppermute | solution.py:325
  55.0 6.6 %collective-permute-start.19 = (bf16[4,4,128,128]{3,2,1,0:T(8,128)(2,1)S(1)}, bf16[4,4,128,128]{3,2,1,0:T(8,128)(2,1)S(1)}, u32[]{:S(2)}, u32[]{:S(2)}) collective-permute-start(bf16[4,4,128,128]{3,2,1,0:T(8,128)(2,1)S(1)} %shard_map.94), channel_id=1, source_target_pairs={{0,1},{1,0},{2,3},{3,2},{4,5},{5,4},{6,7},{7,6},{8,9},{9,8},{10,11... | collective-permute-start | bytes 1572872 | tf_op jit(solution)/shard_map/ppermute | solution.py:325

commit v9 on v8

--- a/solution.py
+++ b/solution.py
@@ -17,7 +17,7 @@
 SCALE = 1.0 / math.sqrt(DH)
 VMEM = 12 * 1024 * 1024
 PACK_VMEM = 53 * 1024 * 1024
-PACK_STEPS = 2
+PACK_STEPS = 1
 WHOLE = pl.BlockSpec(memory_space=pltpu.VMEM)
 
 
@@ -156,31 +156,32 @@
     )(*args)
 
 
-def pack_kernel(chunks, *refs):
+def pack_kernel(chunks, core_ref, *refs):
     ins, outs = refs[:4], refs[4:]
-    block, width = ins[0].shape
-    core, place = lax.axis_index("head"), lax.axis_index("blk") % GROUP
+    block = ins[0].shape[0]
+    place = lax.axis_index("blk") % GROUP
     at = pl.ds(pl.multiple_of(pl.program_id(0) * block, block), block)
     for j in range(chunks):
-        for which in range(2):
-            for s in range(GROUP):
-                base = (core ^ which) * (width // 2) + ((place ^ s) * chunks + j) * DH
-                first = pl.multiple_of(base, DH)
-                for m, ref in enumerate(ins):
-                    outs[2 * j + which][s, m, at] = ref[:, pl.ds(first, DH)]
-
-
-def pack(arrays, chunks):
+        for s in range(GROUP):
+            first = pl.multiple_of(((place ^ s) * chunks + j) * DH, DH)
+            for m, ref in enumerate(ins):
+                outs[j][s, m, at] = ref[:, pl.ds(first, DH)]
+
+
+def pack(arrays, chunks, core):
     rows, width = arrays[0].shape
     block = rows // PACK_STEPS
     return pl.pallas_call(
         functools.partial(pack_kernel, chunks),
-        grid=(PACK_STEPS,),
-        out_shape=[shape(GROUP, 4, rows, DH)] * (2 * chunks),
-        in_specs=[pl.BlockSpec((block, width), lambda i: (i, 0))] * 4,
-        out_specs=[WHOLE] * (2 * chunks),
+        grid_spec=pltpu.PrefetchScalarGridSpec(
+            num_scalar_prefetch=1,
+            grid=(PACK_STEPS,),
+            in_specs=[pl.BlockSpec((block, width // 2), lambda i, core: (i, core[0]))] * 4,
+            out_specs=[WHOLE] * chunks,
+        ),
+        out_shape=[shape(GROUP, 4, rows, DH)] * chunks,
         compiler_params=pltpu.CompilerParams(vmem_limit_bytes=PACK_VMEM),
-    )(*arrays)
+    )(core, *arrays)
 
 
 def join_kernel(mine_ref, received_ref, *outs):
@@ -278,10 +279,12 @@
     inputs = (query_rows, key_rows, value_rows, out_grad)
     unit = 2 * DH * edge * edge * 6
 
-    packed = pack(inputs, chunks)
+    core = lax.axis_index("head").reshape(1)
+    others = pack(inputs, chunks, 1 - core)
+    own = pack(inputs, chunks, core)
     arrived = []
     for j in range(chunks):
-        mine, other = packed[2 * j : 2 * j + 2]
+        mine, other = own[j], others[j]
         theirs = lax.ppermute(other, "head", swap)
         joined = call(join_kernel, [shape(2, 4, half, DH)] * GROUP, mine, theirs)
         arrived.append([hop(joined[s], s) for s in ORDER_IN])

time: 63.5 us -> 63.5 us (level)
  Pallas kernels: 13.8 us -> 15.4 us
  waiting for transfers between devices: 17.4 us -> 15.9 us
    ppermute x2, waiting for transfers between devices: 1.75 us -> 0.01 us  [body(): theirs = lax.ppermute(other, 'head', swap)]
    pallas_call x1 -> x2, Pallas kernels: 2.86 us -> 4.5 us  [pack(): pl.pallas_call(functools.partial(pack_kernel, chunks), grid_spec=pltpu.Pr...]
  transfers between devices with their start and end apart: 20 -> 20, of which waited for: 7 -> 6; matrix products, arithmetic and copies ran while one was open for 0% -> 0% of each run, Pallas kernels for 15% -> 19%
where the time goes in v9:
time: 63.5 us; the launch traced here: 63.1 us
  starting transfers between devices  31 us (49%)
  waiting for transfers between devices  15.9 us (25%)
  Pallas kernels  15.4 us (24%)
  between operations  0.79 us (1%)
    ppermute x12, waiting for transfers between devices, hop(): lax.ppermute(block, 'blk', [(i, i ^ s) for i in range(positions)])  12.9 us
    ppermute x12, starting transfers between devices, hop(): lax.ppermute(block, 'blk', [(i, i ^ s) for i in range(positions)])  11.8 us
    ppermute x2, starting transfers between devices, swap_back(): return back + [lax.ppermute(away, 'head', swap)]  10.9 us
    pallas_call x10, Pallas kernels, call(): pl.pallas_call(kernel, out_shape=out_shape, in_specs=[WHOLE] * len(args),...  9.46 us
    ppermute x2, starting transfers between devices, halo(): return (even, lax.ppermute(to_odd, 'blk', plane_pairs(1)))  7.52 us
    pallas_call x2, Pallas kernels, pack(): pl.pallas_call(functools.partial(pack_kernel, chunks), grid_spec=pltpu.Pr...  4.5 us
    ppermute x2, waiting for transfers between devices, swap_back(): return back + [lax.ppermute(away, 'head', swap)]  1.54 us
    pallas_call x1, Pallas kernels, unpack(): pl.pallas_call(functools.partial(unpack_kernel, len(chunks)), out_shape=[...  1.45 us
  transfers between devices with their start and end apart: 20, of which 6 were waited for; matrix products, arithmetic and copies ran while one was open for 0% of the time, Pallas kernels for 19%

profile of v9, /device:TPU:9, one launch (start us, length us, event | category | flops | bytes accessed | tf_op | source)
XLA Modules:
  0.0 63.1 jit_solution(4828598126744141480)
XLA Ops:
  0.6 2.3 %shard_map.85 = (bf16[4,4,128,128]{3,2,1,0:T(8,128)(2,1)S(1)}, bf16[4,4,128,128]{3,2,1,0:T(8,128)(2,1)}) custom-call(s32[1]{0:T(128)S(6)} %sub.3.core_ref, bf16[128,2048]{1,0:T(8,128)(2,1)} %refs_0_.3, bf16[128,2048]{1,0:T(8,128)(2,1)} %refs_1_.3, bf16[128,2048]{1,0:T(8,128)(2,1)} %refs_2_.3, bf16[128,2048]{1,0:T(8,128)(2,1)} %refs_3_.3), custom_call_target="tpu_custom_call" | custom-call | tf_op jit(solution)/shard_map/pallas_call | solution.py:174
  2.9 0.7 %collective-permute-start = (bf16[4,4,128,128]{3,2,1,0:T(8,128)(2,1)S(1)}, bf16[4,4,128,128]{3,2,1,0:T(8,128)(2,1)S(1)}, u32[]{:S(2)}, u32[]{:S(2)}) collective-permute-start(bf16[4,4,128,128]{3,2,1,0:T(8,128)(2,1)S(1)} %get-tuple-element.40), channel_id=1, source_target_pairs={{0,1},{1,0},{2,3},{3,2},{4,5},{5,4},{6,7},{7,6},{8,9},{9,8},{10,11... | collective-permute-start | bytes 1572872 | tf_op jit(solution)/shard_map/ppermute | solution.py:288
  3.6 2.2 %shard_map.84 = (bf16[4,4,128,128]{3,2,1,0:T(8,128)(2,1)S(1)}, bf16[4,4,128,128]{3,2,1,0:T(8,128)(2,1)}) custom-call(s32[1]{0:T(128)} %bitcast.core_ref, bf16[128,2048]{1,0:T(8,128)(2,1)} %refs_0_.3, bf16[128,2048]{1,0:T(8,128)(2,1)} %refs_1_.3, bf16[128,2048]{1,0:T(8,128)(2,1)} %refs_2_.3, bf16[128,2048]{1,0:T(8,128)(2,1)} %refs_3_.3), custom_call_target="tpu_custom_call" | custom-call | tf_op jit(solution)/shard_map/pallas_call | solution.py:174
  5.9 2.2 %collective-permute-start.1 = (bf16[2,4,128,128]{3,2,1,0:T(8,128)(2,1)S(1)}, bf16[2,4,128,128]{3,2,1,0:T(8,128)(2,1)S(1)}, u32[]{:S(2)}, u32[]{:S(2)}) collective-permute-start(bf16[2,4,128,128]{3,2,1,0:T(8,128)(2,1)S(1)} %get-tuple-element.42), channel_id=1, source_target_pairs={{0,6},{2,4},{4,2},{6,0},{8,14},{10,12},{12,10},{14,8},{16,22},{18,... | collective-permute-start | bytes 786440 | tf_op jit(solution)/shard_map/ppermute | solution.py:276
  8.1 0.2 collective-permute-start.2
  8.4 0.3 collective-permute-start.3
  8.7 2.2 %collective-permute-start.7 = (bf16[2,4,128,128]{3,2,1,0:T(8,128)(2,1)S(1)}, bf16[2,4,128,128]{3,2,1,0:T(8,128)(2,1)S(1)}, u32[]{:S(2)}, u32[]{:S(2)}) collective-permute-start(bf16[2,4,128,128]{3,2,1,0:T(8,128)(2,1)S(1)} %get-tuple-element.50), channel_id=1, source_target_pairs={{0,6},{2,4},{4,2},{6,0},{8,14},{10,12},{12,10},{14,8},{16,22},{18,... | collective-permute-start | bytes 786440 | tf_op jit(solution)/shard_map/ppermute | solution.py:276
  10.9 3.3 %collective-permute-done.1.refs_1_ = bf16[2,4,128,128]{3,2,1,0:T(8,128)(2,1)S(1)} collective-permute-done((bf16[2,4,128,128]{3,2,1,0:T(8,128)(2,1)S(1)}, bf16[2,4,128,128]{3,2,1,0:T(8,128)(2,1)S(1)}, u32[]{:S(2)}, u32[]{:S(2)}) %collective-permute-start.1) | collective-permute-done | bytes 262176 | tf_op jit(solution)/shard_map/ppermute | solution.py:276
  14.3 7.3 %collective-permute-done.2.refs_2_ = bf16[2,4,128,128]{3,2,1,0:T(8,128)(2,1)S(1)} collective-permute-done((bf16[2,4,128,128]{3,2,1,0:T(8,128)(2,1)S(1)}, bf16[2,4,128,128]{3,2,1,0:T(8,128)(2,1)S(1)}, u32[]{:S(2)}, u32[]{:S(2)}) %collective-permute-start.2) | collective-permute-done | bytes 262176 | tf_op jit(solution)/shard_map/ppermute | solution.py:276
  21.5 0.1 shard_map.87
  21.7 0.1 collective-permute-start.4
  21.7 4.5 %collective-permute-start.5 = (bf16[4,256,128]{2,1,0:T(8,128)(2,1)S(1)}, bf16[4,256,128]{2,1,0:T(8,128)(2,1)S(1)}, u32[]{:S(2)}, u32[]{:S(2)}) collective-permute-start(bf16[4,256,128]{2,1,0:T(8,128)(2,1)S(1)} %get-tuple-element.47), channel_id=1, source_target_pairs={{8,16},{16,8},{10,18},{18,10},{12,20},{20,12},{14,22},{22,14},{9,1... | collective-permute-start | bytes 786440 | tf_op jit(solution)/shard_map/ppermute | solution.py:304
  26.2 1.3 %collective-permute-start.8 = (bf16[2,4,128,128]{3,2,1,0:T(8,128)(2,1)S(1)}, bf16[2,4,128,128]{3,2,1,0:T(8,128)(2,1)S(1)}, u32[]{:S(2)}, u32[]{:S(2)}) collective-permute-start(bf16[2,4,128,128]{3,2,1,0:T(8,128)(2,1)S(1)} %get-tuple-element.55), channel_id=1, source_target_pairs={{0,4},{2,6},{4,0},{6,2},{8,12},{10,14},{12,8},{14,10},{16,20},{18,... | collective-permute-start | bytes 786440 | tf_op jit(solution)/shard_map/ppermute | solution.py:276
  27.6 3.2 %shard_map.88.res_ref = bf16[4,1024,128]{2,1,0:T(8,128)(2,1)S(1)} custom-call(bf16[4,1024,128]{2,1,0:T(8,128)(2,1)S(1)} %get-tuple-element.45.ext_ref, s32[32,128]{1,0:T(8,128)S(1)} %bitcast.2), custom_call_target="tpu_custom_call" | custom-call | tf_op jit(solution)/shard_map/pallas_call | solution.py:149
  30.9 1.0 %collective-permute-done.5.odd_ref = bf16[4,256,128]{2,1,0:T(8,128)(2,1)S(1)} collective-permute-done((bf16[4,256,128]{2,1,0:T(8,128)(2,1)S(1)}, bf16[4,256,128]{2,1,0:T(8,128)(2,1)S(1)}, u32[]{:S(2)}, u32[]{:S(2)}) %collective-permute-start.5) | collective-permute-done | bytes 262176 | tf_op jit(solution)/shard_map/ppermute | solution.py:304
  31.8 1.3 %shard_map.90 = (bf16[2,4,128,128]{3,2,1,0:T(8,128)(2,1)S(1)}, bf16[2,4,128,128]{3,2,1,0:T(8,128)(2,1)S(1)}, bf16[2,4,128,128]{3,2,1,0:T(8,128)(2,1)S(1)}, bf16[2,4,128,128]{3,2,1,0:T(8,128)(2,1)S(1)}) custom-call(bf16[4,1024,128]{2,1,0:T(8,128)(2,1)S(1)} %get-tuple-element.45.ext_ref, bf16[4,256,128]{2,1,0:T(8,128)(2,1)S(1)} %collective-permute-done.4.even_ref, ...), custom_call_target="tpu_custom_call" | custom-call | tf_op jit(solution)/shard_map/pallas_call | solution.py:149
  33.1 1.3 %collective-permute-start.11 = (bf16[2,4,128,128]{3,2,1,0:T(8,128)(2,1)S(1)}, bf16[2,4,128,128]{3,2,1,0:T(8,128)(2,1)S(1)}, u32[]{:S(2)}, u32[]{:S(2)}) collective-permute-start(bf16[2,4,128,128]{3,2,1,0:T(8,128)(2,1)S(1)} %get-tuple-element.57), channel_id=1, source_target_pairs={{0,2},{2,0},{4,6},{6,4},{8,10},{10,8},{12,14},{14,12},{16,18},{18,... | collective-permute-start | bytes 786440 | tf_op jit(solution)/shard_map/ppermute | solution.py:276
  34.4 0.3 collective-permute-start.10
  34.7 0.1 shard_map.91
  34.9 3.0 %collective-permute-start.15 = (bf16[4,256,128]{2,1,0:T(8,128)(2,1)S(1)}, bf16[4,256,128]{2,1,0:T(8,128)(2,1)S(1)}, u32[]{:S(2)}, u32[]{:S(2)}) collective-permute-start(bf16[4,256,128]{2,1,0:T(8,128)(2,1)S(1)} %get-tuple-element.68), channel_id=1, source_target_pairs={{8,16},{16,8},{10,18},{18,10},{12,20},{20,12},{14,22},{22,14},{9,1... | collective-permute-start | bytes 786440 | tf_op jit(solution)/shard_map/ppermute | solution.py:304
  37.9 1.2 %collective-permute-start.12 = (bf16[2,4,128,128]{3,2,1,0:T(8,128)(2,1)S(1)}, bf16[2,4,128,128]{3,2,1,0:T(8,128)(2,1)S(1)}, u32[]{:S(2)}, u32[]{:S(2)}) collective-permute-start(bf16[2,4,128,128]{3,2,1,0:T(8,128)(2,1)S(1)} %get-tuple-element.59), channel_id=1, source_target_pairs={{0,6},{2,4},{4,2},{6,0},{8,14},{10,12},{12,10},{14,8},{16,22},{18,... | collective-permute-start | bytes 786440 | tf_op jit(solution)/shard_map/ppermute | solution.py:276
  39.2 3.2 %shard_map.92.res_ref = bf16[4,1024,128]{2,1,0:T(8,128)(2,1)S(1)} custom-call(bf16[4,1024,128]{2,1,0:T(8,128)(2,1)S(1)} %get-tuple-element.64.ext_ref, s32[32,128]{1,0:T(8,128)S(1)} %bitcast.4), custom_call_target="tpu_custom_call" | custom-call | tf_op jit(solution)/shard_map/pallas_call | solution.py:149
  42.4 0.4 collective-permute-done.15.odd_ref
  42.8 1.3 %shard_map.94 = (bf16[2,4,128,128]{3,2,1,0:T(8,128)(2,1)S(1)}, bf16[2,4,128,128]{3,2,1,0:T(8,128)(2,1)S(1)}, bf16[2,4,128,128]{3,2,1,0:T(8,128)(2,1)S(1)}, bf16[2,4,128,128]{3,2,1,0:T(8,128)(2,1)S(1)}) custom-call(bf16[4,1024,128]{2,1,0:T(8,128)(2,1)S(1)} %get-tuple-element.64.ext_ref, bf16[4,256,128]{2,1,0:T(8,128)(2,1)S(1)} %collective-permute-done.14.even_ref, ...), custom_call_target="tpu_custom_call" | custom-call | tf_op jit(solution)/shard_map/pallas_call | solution.py:149
  44.1 1.1 %collective-permute-start.16 = (bf16[2,4,128,128]{3,2,1,0:T(8,128)(2,1)S(1)}, bf16[2,4,128,128]{3,2,1,0:T(8,128)(2,1)S(1)}, u32[]{:S(2)}, u32[]{:S(2)}) collective-permute-start(bf16[2,4,128,128]{3,2,1,0:T(8,128)(2,1)S(1)} %get-tuple-element.71), channel_id=1, source_target_pairs={{0,4},{2,6},{4,0},{6,2},{8,12},{10,14},{12,8},{14,10},{16,20},{18,... | collective-permute-start | bytes 786440 | tf_op jit(solution)/shard_map/ppermute | solution.py:276
  45.2 0.1 collective-permute-start.17
  45.4 1.5 %collective-permute-start.18 = (bf16[2,4,128,128]{3,2,1,0:T(8,128)(2,1)S(1)}, bf16[2,4,128,128]{3,2,1,0:T(8,128)(2,1)S(1)}, u32[]{:S(2)}, u32[]{:S(2)}) collective-permute-start(bf16[2,4,128,128]{3,2,1,0:T(8,128)(2,1)S(1)} %get-tuple-element.73), channel_id=1, source_target_pairs={{0,6},{2,4},{4,2},{6,0},{8,14},{10,12},{12,10},{14,8},{16,22},{18,... | collective-permute-start | bytes 786440 | tf_op jit(solution)/shard_map/ppermute | solution.py:276
  46.9 5.9 %collective-permute-start.13 = (bf16[4,4,128,128]{3,2,1,0:T(8,128)(2,1)S(1)}, bf16[4,4,128,128]{3,2,1,0:T(8,128)(2,1)S(1)}, u32[]{:S(2)}, u32[]{:S(2)}) collective-permute-start(bf16[4,4,128,128]{3,2,1,0:T(8,128)(2,1)S(1)} %shard_map.93), channel_id=1, source_target_pairs={{0,1},{1,0},{2,3},{3,2},{4,5},{5,4},{6,7},{7,6},{8,9},{9,8},{10,11... | collective-permute-start | bytes 1572872 | tf_op jit(solution)/shard_map/ppermute | solution.py:328
  52.7 2.3 %collective-permute-done.16.refs_1_.refs_6_ = bf16[2,4,128,128]{3,2,1,0:T(8,128)(2,1)S(1)} collective-permute-done((bf16[2,4,128,128]{3,2,1,0:T(8,128)(2,1)S(1)}, bf16[2,4,128,128]{3,2,1,0:T(8,128)(2,1)S(1)}, u32[]{:S(2)}, u32[]{:S(2)}) %collective-permute-start.16) | collective-permute-done | bytes 262176 | tf_op jit(solution)/shard_map/ppermute | solution.py:276
  55.1 5.0 %collective-permute-start.19 = (bf16[4,4,128,128]{3,2,1,0:T(8,128)(2,1)S(1)}, bf16[4,4,128,128]{3,2,1,0:T(8,128)(2,1)S(1)}, u32[]{:S(2)}, u32[]{:S(2)}) collective-permute-start(bf16[4,4,128,128]{3,2,1,0:T(8,128)(2,1)S(1)} %shard_map.95), channel_id=1, source_target_pairs={{0,1},{1,0},{2,3},{3,2},{4,5},{5,4},{6,7},{7,6},{8,9},{9,8},{10,11... | collective-permute-start | bytes 1572872 | tf_op jit(solution)/shard_map/ppermute | solution.py:328
  60.1 1.5 %collective-permute-done.19.refs_9_ = bf16[4,4,128,128]{3,2,1,0:T(8,128)(2,1)S(1)} collective-permute-done((bf16[4,4,128,128]{3,2,1,0:T(8,128)(2,1)S(1)}, bf16[4,4,128,128]{3,2,1,0:T(8,128)(2,1)S(1)}, u32[]{:S(2)}, u32[]{:S(2)}) %collective-permute-start.19) | collective-permute-done | bytes 524320 | tf_op jit(solution)/shard_map/ppermute | solution.py:328
  61.6 1.4 %shard_map.96 = (bf16[128,2048]{1,0:T(8,128)(2,1)}, bf16[128,2048]{1,0:T(8,128)(2,1)}, bf16[128,2048]{1,0:T(8,128)(2,1)}, bf16[128,2048]{1,0:T(8,128)(2,1)}) custom-call(bf16[2,4,128,128]{3,2,1,0:T(8,128)(2,1)S(1)} %get-tuple-element.52.refs_0_, bf16[2,4,128,128]{3,2,1,0:T(8,128)(2,1)S(1)} %collective-permute-done.10.refs_1_, ...), custom_call_target="tpu_custom_call" | custom-call | tf_op jit(solution)/shard_map/pallas_call | solution.py:243
  (25 shorter events, 0.4 us)
Async XLA Ops:
  2.9 2.9 %collective-permute-start = (bf16[4,4,128,128]{3,2,1,0:T(8,128)(2,1)S(1)}, bf16[4,4,128,128]{3,2,1,0:T(8,128)(2,1)S(1)}, u32[]{:S(2)}, u32[]{:S(2)}) collective-permute-start(bf16[4,4,128,128]{3,2,1,0:T(8,128)(2,1)S(1)} %get-tuple-element.40), channel_id=1, source_target_pairs={{0,1},{1,0},{2,3},{3,2},{4,5},{5,4},{6,7},{7,6},{8,9},{9,8},{10,11... | collective-permute-start | bytes 1572872 | tf_op jit(solution)/shard_map/ppermute | solution.py:288
  3.6 5.0 %collective-permute-start.6 = (bf16[4,4,128,128]{3,2,1,0:T(8,128)(2,1)}, bf16[4,4,128,128]{3,2,1,0:T(8,128)(2,1)S(1)}, u32[]{:S(2)}, u32[]{:S(2)}) collective-permute-start(bf16[4,4,128,128]{3,2,1,0:T(8,128)(2,1)} %get-tuple-element.49), channel_id=1, source_target_pairs={{0,1},{1,0},{2,3},{3,2},{4,5},{5,4},{6,7},{7,6},{8,9},{9,8},{10,11... | collective-permute-start | bytes 1572872 | tf_op jit(solution)/shard_map/ppermute | solution.py:288
  5.8 2.8 %copy-start = (bf16[4,4,128,128]{3,2,1,0:T(8,128)(2,1)S(1)}, bf16[4,4,128,128]{3,2,1,0:T(8,128)(2,1)}, u32[]{:S(2)}) copy-start(bf16[4,4,128,128]{3,2,1,0:T(8,128)(2,1)} %get-tuple-element.48.mine_ref) | copy-start | bytes 1572868
  5.9 8.4 %collective-permute-start.1 = (bf16[2,4,128,128]{3,2,1,0:T(8,128)(2,1)S(1)}, bf16[2,4,128,128]{3,2,1,0:T(8,128)(2,1)S(1)}, u32[]{:S(2)}, u32[]{:S(2)}) collective-permute-start(bf16[2,4,128,128]{3,2,1,0:T(8,128)(2,1)S(1)} %get-tuple-element.42), channel_id=1, source_target_pairs={{0,6},{2,4},{4,2},{6,0},{8,14},{10,12},{12,10},{14,8},{16,22},{18,... | collective-permute-start | bytes 786440 | tf_op jit(solution)/shard_map/ppermute | solution.py:276
  8.1 13.4 %collective-permute-start.2 = (bf16[2,4,128,128]{3,2,1,0:T(8,128)(2,1)S(1)}, bf16[2,4,128,128]{3,2,1,0:T(8,128)(2,1)S(1)}, u32[]{:S(2)}, u32[]{:S(2)}) collective-permute-start(bf16[2,4,128,128]{3,2,1,0:T(8,128)(2,1)S(1)} %get-tuple-element.43), channel_id=1, source_target_pairs={{0,4},{2,6},{4,0},{6,2},{8,12},{10,14},{12,8},{14,10},{16,20},{18,... | collective-permute-start | bytes 786440 | tf_op jit(solution)/shard_map/ppermute | solution.py:276
  8.4 13.2 %collective-permute-start.3 = (bf16[2,4,128,128]{3,2,1,0:T(8,128)(2,1)S(1)}, bf16[2,4,128,128]{3,2,1,0:T(8,128)(2,1)S(1)}, u32[]{:S(2)}, u32[]{:S(2)}) collective-permute-start(bf16[2,4,128,128]{3,2,1,0:T(8,128)(2,1)S(1)} %get-tuple-element.44), channel_id=1, source_target_pairs={{0,2},{2,0},{4,6},{6,4},{8,10},{10,8},{12,14},{14,12},{16,18},{18,... | collective-permute-start | bytes 786440 | tf_op jit(solution)/shard_map/ppermute | solution.py:276
  8.7 22.1 %collective-permute-start.7 = (bf16[2,4,128,128]{3,2,1,0:T(8,128)(2,1)S(1)}, bf16[2,4,128,128]{3,2,1,0:T(8,128)(2,1)S(1)}, u32[]{:S(2)}, u32[]{:S(2)}) collective-permute-start(bf16[2,4,128,128]{3,2,1,0:T(8,128)(2,1)S(1)} %get-tuple-element.50), channel_id=1, source_target_pairs={{0,6},{2,4},{4,2},{6,0},{8,14},{10,12},{12,10},{14,8},{16,22},{18,... | collective-permute-start | bytes 786440 | tf_op jit(solution)/shard_map/ppermute | solution.py:276
  21.5 6.0 %copy-start.1 = (s32[4096]{0:T(1024)S(1)}, s32[4096]{0:T(1024)}, u32[]{:S(2)}) copy-start(s32[4096]{0:T(1024)} %param.9) | copy-start | bytes 49156
  21.7 9.2 %collective-permute-start.4 = (bf16[4,256,128]{2,1,0:T(8,128)(2,1)S(1)}, bf16[4,256,128]{2,1,0:T(8,128)(2,1)S(1)}, u32[]{:S(2)}, u32[]{:S(2)}) collective-permute-start(bf16[4,256,128]{2,1,0:T(8,128)(2,1)S(1)} %get-tuple-element.46), channel_id=1, source_target_pairs={{0,8},{8,0},{2,10},{10,2},{4,12},{12,4},{6,14},{14,6},{16,24},{24,... | collective-permute-start | bytes 786440 | tf_op jit(solution)/shard_map/ppermute | solution.py:303
  21.7 10.1 %collective-permute-start.5 = (bf16[4,256,128]{2,1,0:T(8,128)(2,1)S(1)}, bf16[4,256,128]{2,1,0:T(8,128)(2,1)S(1)}, u32[]{:S(2)}, u32[]{:S(2)}) collective-permute-start(bf16[4,256,128]{2,1,0:T(8,128)(2,1)S(1)} %get-tuple-element.47), channel_id=1, source_target_pairs={{8,16},{16,8},{10,18},{18,10},{12,20},{20,12},{14,22},{22,14},{9,1... | collective-permute-start | bytes 786440 | tf_op jit(solution)/shard_map/ppermute | solution.py:304
  26.2 8.4 %collective-permute-start.8 = (bf16[2,4,128,128]{3,2,1,0:T(8,128)(2,1)S(1)}, bf16[2,4,128,128]{3,2,1,0:T(8,128)(2,1)S(1)}, u32[]{:S(2)}, u32[]{:S(2)}) collective-permute-start(bf16[2,4,128,128]{3,2,1,0:T(8,128)(2,1)S(1)} %get-tuple-element.55), channel_id=1, source_target_pairs={{0,4},{2,6},{4,0},{6,2},{8,12},{10,14},{12,8},{14,10},{16,20},{18,... | collective-permute-start | bytes 786440 | tf_op jit(solution)/shard_map/ppermute | solution.py:276
  27.5 7.1 %collective-permute-start.9 = (bf16[2,4,128,128]{3,2,1,0:T(8,128)(2,1)S(1)}, bf16[2,4,128,128]{3,2,1,0:T(8,128)(2,1)S(1)}, u32[]{:S(2)}, u32[]{:S(2)}) collective-permute-start(bf16[2,4,128,128]{3,2,1,0:T(8,128)(2,1)S(1)} %get-tuple-element.56), channel_id=1, source_target_pairs={{0,2},{2,0},{4,6},{6,4},{8,10},{10,8},{12,14},{14,12},{16,18},{18,... | collective-permute-start | bytes 786440 | tf_op jit(solution)/shard_map/ppermute | solution.py:276
  33.1 9.3 %collective-permute-start.11 = (bf16[2,4,128,128]{3,2,1,0:T(8,128)(2,1)S(1)}, bf16[2,4,128,128]{3,2,1,0:T(8,128)(2,1)S(1)}, u32[]{:S(2)}, u32[]{:S(2)}) collective-permute-start(bf16[2,4,128,128]{3,2,1,0:T(8,128)(2,1)S(1)} %get-tuple-element.57), channel_id=1, source_target_pairs={{0,2},{2,0},{4,6},{6,4},{8,10},{10,8},{12,14},{14,12},{16,18},{18,... | collective-permute-start | bytes 786440 | tf_op jit(solution)/shard_map/ppermute | solution.py:276
  34.4 8.0 %collective-permute-start.10 = (bf16[2,4,128,128]{3,2,1,0:T(8,128)(2,1)S(1)}, bf16[2,4,128,128]{3,2,1,0:T(8,128)(2,1)S(1)}, u32[]{:S(2)}, u32[]{:S(2)}) collective-permute-start(bf16[2,4,128,128]{3,2,1,0:T(8,128)(2,1)S(1)} %get-tuple-element.58), channel_id=1, source_target_pairs={{0,4},{2,6},{4,0},{6,2},{8,12},{10,14},{12,8},{14,10},{16,20},{18,... | collective-permute-start | bytes 786440 | tf_op jit(solution)/shard_map/ppermute | solution.py:276
  34.8 7.6 %collective-permute-start.14 = (bf16[4,256,128]{2,1,0:T(8,128)(2,1)S(1)}, bf16[4,256,128]{2,1,0:T(8,128)(2,1)S(1)}, u32[]{:S(2)}, u32[]{:S(2)}) collective-permute-start(bf16[4,256,128]{2,1,0:T(8,128)(2,1)S(1)} %get-tuple-element.67), channel_id=1, source_target_pairs={{0,8},{8,0},{2,10},{10,2},{4,12},{12,4},{6,14},{14,6},{16,24},{24,... | collective-permute-start | bytes 786440 | tf_op jit(solution)/shard_map/ppermute | solution.py:303
  34.9 8.0 %collective-permute-start.15 = (bf16[4,256,128]{2,1,0:T(8,128)(2,1)S(1)}, bf16[4,256,128]{2,1,0:T(8,128)(2,1)S(1)}, u32[]{:S(2)}, u32[]{:S(2)}) collective-permute-start(bf16[4,256,128]{2,1,0:T(8,128)(2,1)S(1)} %get-tuple-element.68), channel_id=1, source_target_pairs={{8,16},{16,8},{10,18},{18,10},{12,20},{20,12},{14,22},{22,14},{9,1... | collective-permute-start | bytes 786440 | tf_op jit(solution)/shard_map/ppermute | solution.py:304
  37.9 8.9 %collective-permute-start.12 = (bf16[2,4,128,128]{3,2,1,0:T(8,128)(2,1)S(1)}, bf16[2,4,128,128]{3,2,1,0:T(8,128)(2,1)S(1)}, u32[]{:S(2)}, u32[]{:S(2)}) collective-permute-start(bf16[2,4,128,128]{3,2,1,0:T(8,128)(2,1)S(1)} %get-tuple-element.59), channel_id=1, source_target_pairs={{0,6},{2,4},{4,2},{6,0},{8,14},{10,12},{12,10},{14,8},{16,22},{18,... | collective-permute-start | bytes 786440 | tf_op jit(solution)/shard_map/ppermute | solution.py:276
  44.1 10.9 %collective-permute-start.16 = (bf16[2,4,128,128]{3,2,1,0:T(8,128)(2,1)S(1)}, bf16[2,4,128,128]{3,2,1,0:T(8,128)(2,1)S(1)}, u32[]{:S(2)}, u32[]{:S(2)}) collective-permute-start(bf16[2,4,128,128]{3,2,1,0:T(8,128)(2,1)S(1)} %get-tuple-element.71), channel_id=1, source_target_pairs={{0,4},{2,6},{4,0},{6,2},{8,12},{10,14},{12,8},{14,10},{16,20},{18,... | collective-permute-start | bytes 786440 | tf_op jit(solution)/shard_map/ppermute | solution.py:276
  45.2 9.8 %collective-permute-start.17 = (bf16[2,4,128,128]{3,2,1,0:T(8,128)(2,1)S(1)}, bf16[2,4,128,128]{3,2,1,0:T(8,128)(2,1)S(1)}, u32[]{:S(2)}, u32[]{:S(2)}) collective-permute-start(bf16[2,4,128,128]{3,2,1,0:T(8,128)(2,1)S(1)} %get-tuple-element.72), channel_id=1, source_target_pairs={{0,2},{2,0},{4,6},{6,4},{8,10},{10,8},{12,14},{14,12},{16,18},{18,... | collective-permute-start | bytes 786440 | tf_op jit(solution)/shard_map/ppermute | solution.py:276
  45.4 9.7 %collective-permute-start.18 = (bf16[2,4,128,128]{3,2,1,0:T(8,128)(2,1)S(1)}, bf16[2,4,128,128]{3,2,1,0:T(8,128)(2,1)S(1)}, u32[]{:S(2)}, u32[]{:S(2)}) collective-permute-start(bf16[2,4,128,128]{3,2,1,0:T(8,128)(2,1)S(1)} %get-tuple-element.73), channel_id=1, source_target_pairs={{0,6},{2,4},{4,2},{6,0},{8,14},{10,12},{12,10},{14,8},{16,22},{18,... | collective-permute-start | bytes 786440 | tf_op jit(solution)/shard_map/ppermute | solution.py:276
  46.9 13.2 %collective-permute-start.13 = (bf16[4,4,128,128]{3,2,1,0:T(8,128)(2,1)S(1)}, bf16[4,4,128,128]{3,2,1,0:T(8,128)(2,1)S(1)}, u32[]{:S(2)}, u32[]{:S(2)}) collective-permute-start(bf16[4,4,128,128]{3,2,1,0:T(8,128)(2,1)S(1)} %shard_map.93), channel_id=1, source_target_pairs={{0,1},{1,0},{2,3},{3,2},{4,5},{5,4},{6,7},{7,6},{8,9},{9,8},{10,11... | collective-permute-start | bytes 1572872 | tf_op jit(solution)/shard_map/ppermute | solution.py:328
  55.1 6.5 %collective-permute-start.19 = (bf16[4,4,128,128]{3,2,1,0:T(8,128)(2,1)S(1)}, bf16[4,4,128,128]{3,2,1,0:T(8,128)(2,1)S(1)}, u32[]{:S(2)}, u32[]{:S(2)}) collective-permute-start(bf16[4,4,128,128]{3,2,1,0:T(8,128)(2,1)S(1)} %shard_map.95), channel_id=1, source_target_pairs={{0,1},{1,0},{2,3},{3,2},{4,5},{5,4},{6,7},{7,6},{8,9},{9,8},{10,11... | collective-permute-start | bytes 1572872 | tf_op jit(solution)/shard_map/ppermute | solution.py:328

commit v10 on v8

--- a/solution.py
+++ b/solution.py
@@ -15,7 +15,7 @@
 ORDER_IN = (0, 3, 2, 1)
 ORDER_OUT = (0, 2, 1, 3)
 SCALE = 1.0 / math.sqrt(DH)
-VMEM = 12 * 1024 * 1024
+VMEM = 20 * 1024 * 1024
 PACK_VMEM = 53 * 1024 * 1024
 PACK_STEPS = 2
 WHOLE = pl.BlockSpec(memory_space=pltpu.VMEM)

time: 63.5 us -> 63.5 us (level)
  no operation moved by 1% of the time
where the time goes in v10:
time: 63.5 us; the launch traced here: 63 us
  starting transfers between devices  31 us (49%)
  waiting for transfers between devices  17.4 us (27%)
  Pallas kernels  13.8 us (22%)
  between operations  0.79 us (1%)
    ppermute x12, waiting for transfers between devices, hop(): lax.ppermute(block, 'blk', [(i, i ^ s) for i in range(positions)])  12.7 us
    ppermute x12, starting transfers between devices, hop(): lax.ppermute(block, 'blk', [(i, i ^ s) for i in range(positions)])  11.8 us
    ppermute x2, starting transfers between devices, swap_back(): return back + [lax.ppermute(away, 'head', swap)]  10.9 us
    pallas_call x10, Pallas kernels, call(): pl.pallas_call(kernel, out_shape=out_shape, in_specs=[WHOLE] * len(args),...  9.45 us
    ppermute x2, starting transfers between devices, halo(): return (even, lax.ppermute(to_odd, 'blk', plane_pairs(1)))  7.52 us
    pallas_call x1, Pallas kernels, pack(): pl.pallas_call(functools.partial(pack_kernel, chunks), grid=(PACK_STEPS,)...  2.86 us
    ppermute x2, waiting for transfers between devices, body(): theirs = lax.ppermute(other, 'head', swap)  1.75 us
    ppermute x2, waiting for transfers between devices, swap_back(): return back + [lax.ppermute(away, 'head', swap)]  1.54 us
  transfers between devices with their start and end apart: 20, of which 7 were waited for; matrix products, arithmetic and copies ran while one was open for 0% of the time, Pallas kernels for 15%

profile of v10, /device:TPU:9, one launch (start us, length us, event | category | flops | bytes accessed | tf_op | source)
XLA Modules:
  0.0 63.0 jit_solution(4638701459094091792)
XLA Ops:
  0.6 2.9 %shard_map.84 = (bf16[4,4,128,128]{3,2,1,0:T(8,128)(2,1)S(1)}, bf16[4,4,128,128]{3,2,1,0:T(8,128)(2,1)}, bf16[4,4,128,128]{3,2,1,0:T(8,128)(2,1)}, bf16[4,4,128,128]{3,2,1,0:T(8,128)(2,1)}) custom-call(bf16[128,2048]{1,0:T(8,128)(2,1)} %refs_0_.1, bf16[128,2048]{1,0:T(8,128)(2,1)} %refs_1_.1, bf16[128,2048]{1,0:T(8,128)(2,1)} %refs_2_.1, ...), custom_call_target="tpu_custom_call" | custom-call | tf_op jit(solution)/shard_map/pallas_call | solution.py:176
  3.5 0.7 %collective-permute-start = (bf16[4,4,128,128]{3,2,1,0:T(8,128)(2,1)}, bf16[4,4,128,128]{3,2,1,0:T(8,128)(2,1)S(1)}, u32[]{:S(2)}, u32[]{:S(2)}) collective-permute-start(bf16[4,4,128,128]{3,2,1,0:T(8,128)(2,1)} %get-tuple-element.40), channel_id=1, source_target_pairs={{0,1},{1,0},{2,3},{3,2},{4,5},{5,4},{6,7},{7,6},{8,9},{9,8},{10,11... | collective-permute-start | bytes 1572872 | tf_op jit(solution)/shard_map/ppermute | solution.py:285
  4.2 1.7 %collective-permute-done.received_ref = bf16[4,4,128,128]{3,2,1,0:T(8,128)(2,1)S(1)} collective-permute-done((bf16[4,4,128,128]{3,2,1,0:T(8,128)(2,1)}, bf16[4,4,128,128]{3,2,1,0:T(8,128)(2,1)S(1)}, u32[]{:S(2)}, u32[]{:S(2)}) %collective-permute-start) | collective-permute-done | bytes 524320 | tf_op jit(solution)/shard_map/ppermute | solution.py:285
  6.0 2.2 %collective-permute-start.1 = (bf16[2,4,128,128]{3,2,1,0:T(8,128)(2,1)S(1)}, bf16[2,4,128,128]{3,2,1,0:T(8,128)(2,1)S(1)}, u32[]{:S(2)}, u32[]{:S(2)}) collective-permute-start(bf16[2,4,128,128]{3,2,1,0:T(8,128)(2,1)S(1)} %get-tuple-element.42), channel_id=1, source_target_pairs={{0,6},{2,4},{4,2},{6,0},{8,14},{10,12},{12,10},{14,8},{16,22},{18,... | collective-permute-start | bytes 786440 | tf_op jit(solution)/shard_map/ppermute | solution.py:275
  8.2 0.2 collective-permute-start.2
  8.5 0.3 collective-permute-start.3
  8.8 2.2 %collective-permute-start.7 = (bf16[2,4,128,128]{3,2,1,0:T(8,128)(2,1)S(1)}, bf16[2,4,128,128]{3,2,1,0:T(8,128)(2,1)S(1)}, u32[]{:S(2)}, u32[]{:S(2)}) collective-permute-start(bf16[2,4,128,128]{3,2,1,0:T(8,128)(2,1)S(1)} %get-tuple-element.50), channel_id=1, source_target_pairs={{0,6},{2,4},{4,2},{6,0},{8,14},{10,12},{12,10},{14,8},{16,22},{18,... | collective-permute-start | bytes 786440 | tf_op jit(solution)/shard_map/ppermute | solution.py:275
  11.0 3.5 %collective-permute-done.1.refs_1_ = bf16[2,4,128,128]{3,2,1,0:T(8,128)(2,1)S(1)} collective-permute-done((bf16[2,4,128,128]{3,2,1,0:T(8,128)(2,1)S(1)}, bf16[2,4,128,128]{3,2,1,0:T(8,128)(2,1)S(1)}, u32[]{:S(2)}, u32[]{:S(2)}) %collective-permute-start.1) | collective-permute-done | bytes 262176 | tf_op jit(solution)/shard_map/ppermute | solution.py:275
  14.5 6.9 %collective-permute-done.2.refs_2_ = bf16[2,4,128,128]{3,2,1,0:T(8,128)(2,1)S(1)} collective-permute-done((bf16[2,4,128,128]{3,2,1,0:T(8,128)(2,1)S(1)}, bf16[2,4,128,128]{3,2,1,0:T(8,128)(2,1)S(1)}, u32[]{:S(2)}, u32[]{:S(2)}) %collective-permute-start.2) | collective-permute-done | bytes 262176 | tf_op jit(solution)/shard_map/ppermute | solution.py:275
  21.5 0.1 shard_map.86
  21.6 0.1 collective-permute-start.4
  21.7 4.5 %collective-permute-start.5 = (bf16[4,256,128]{2,1,0:T(8,128)(2,1)S(1)}, bf16[4,256,128]{2,1,0:T(8,128)(2,1)S(1)}, u32[]{:S(2)}, u32[]{:S(2)}) collective-permute-start(bf16[4,256,128]{2,1,0:T(8,128)(2,1)S(1)} %get-tuple-element.47), channel_id=1, source_target_pairs={{8,16},{16,8},{10,18},{18,10},{12,20},{20,12},{14,22},{22,14},{9,1... | collective-permute-start | bytes 786440 | tf_op jit(solution)/shard_map/ppermute | solution.py:301
  26.2 1.3 %collective-permute-start.8 = (bf16[2,4,128,128]{3,2,1,0:T(8,128)(2,1)S(1)}, bf16[2,4,128,128]{3,2,1,0:T(8,128)(2,1)S(1)}, u32[]{:S(2)}, u32[]{:S(2)}) collective-permute-start(bf16[2,4,128,128]{3,2,1,0:T(8,128)(2,1)S(1)} %get-tuple-element.55), channel_id=1, source_target_pairs={{0,4},{2,6},{4,0},{6,2},{8,12},{10,14},{12,8},{14,10},{16,20},{18,... | collective-permute-start | bytes 786440 | tf_op jit(solution)/shard_map/ppermute | solution.py:275
  27.5 3.2 %shard_map.87.res_ref = bf16[4,1024,128]{2,1,0:T(8,128)(2,1)S(1)} custom-call(bf16[4,1024,128]{2,1,0:T(8,128)(2,1)S(1)} %get-tuple-element.45.ext_ref, s32[32,128]{1,0:T(8,128)S(1)} %bitcast.1), custom_call_target="tpu_custom_call" | custom-call | tf_op jit(solution)/shard_map/pallas_call | solution.py:149
  30.8 1.0 %collective-permute-done.5.odd_ref = bf16[4,256,128]{2,1,0:T(8,128)(2,1)S(1)} collective-permute-done((bf16[4,256,128]{2,1,0:T(8,128)(2,1)S(1)}, bf16[4,256,128]{2,1,0:T(8,128)(2,1)S(1)}, u32[]{:S(2)}, u32[]{:S(2)}) %collective-permute-start.5) | collective-permute-done | bytes 262176 | tf_op jit(solution)/shard_map/ppermute | solution.py:301
  31.8 1.3 %shard_map.89 = (bf16[2,4,128,128]{3,2,1,0:T(8,128)(2,1)S(1)}, bf16[2,4,128,128]{3,2,1,0:T(8,128)(2,1)S(1)}, bf16[2,4,128,128]{3,2,1,0:T(8,128)(2,1)S(1)}, bf16[2,4,128,128]{3,2,1,0:T(8,128)(2,1)S(1)}) custom-call(bf16[4,1024,128]{2,1,0:T(8,128)(2,1)S(1)} %get-tuple-element.45.ext_ref, bf16[4,256,128]{2,1,0:T(8,128)(2,1)S(1)} %collective-permute-done.4.even_ref, ...), custom_call_target="tpu_custom_call" | custom-call | tf_op jit(solution)/shard_map/pallas_call | solution.py:149
  33.1 1.3 %collective-permute-start.11 = (bf16[2,4,128,128]{3,2,1,0:T(8,128)(2,1)S(1)}, bf16[2,4,128,128]{3,2,1,0:T(8,128)(2,1)S(1)}, u32[]{:S(2)}, u32[]{:S(2)}) collective-permute-start(bf16[2,4,128,128]{3,2,1,0:T(8,128)(2,1)S(1)} %get-tuple-element.57), channel_id=1, source_target_pairs={{0,2},{2,0},{4,6},{6,4},{8,10},{10,8},{12,14},{14,12},{16,18},{18,... | collective-permute-start | bytes 786440 | tf_op jit(solution)/shard_map/ppermute | solution.py:275
  34.3 0.3 collective-permute-start.10
  34.6 0.1 shard_map.90
  34.8 3.0 %collective-permute-start.15 = (bf16[4,256,128]{2,1,0:T(8,128)(2,1)S(1)}, bf16[4,256,128]{2,1,0:T(8,128)(2,1)S(1)}, u32[]{:S(2)}, u32[]{:S(2)}) collective-permute-start(bf16[4,256,128]{2,1,0:T(8,128)(2,1)S(1)} %get-tuple-element.68), channel_id=1, source_target_pairs={{8,16},{16,8},{10,18},{18,10},{12,20},{20,12},{14,22},{22,14},{9,1... | collective-permute-start | bytes 786440 | tf_op jit(solution)/shard_map/ppermute | solution.py:301
  37.9 1.2 %collective-permute-start.12 = (bf16[2,4,128,128]{3,2,1,0:T(8,128)(2,1)S(1)}, bf16[2,4,128,128]{3,2,1,0:T(8,128)(2,1)S(1)}, u32[]{:S(2)}, u32[]{:S(2)}) collective-permute-start(bf16[2,4,128,128]{3,2,1,0:T(8,128)(2,1)S(1)} %get-tuple-element.59), channel_id=1, source_target_pairs={{0,6},{2,4},{4,2},{6,0},{8,14},{10,12},{12,10},{14,8},{16,22},{18,... | collective-permute-start | bytes 786440 | tf_op jit(solution)/shard_map/ppermute | solution.py:275
  39.1 3.2 %shard_map.91.res_ref = bf16[4,1024,128]{2,1,0:T(8,128)(2,1)S(1)} custom-call(bf16[4,1024,128]{2,1,0:T(8,128)(2,1)S(1)} %get-tuple-element.64.ext_ref, s32[32,128]{1,0:T(8,128)S(1)} %bitcast.3), custom_call_target="tpu_custom_call" | custom-call | tf_op jit(solution)/shard_map/pallas_call | solution.py:149
  42.4 0.4 collective-permute-done.15.odd_ref
  42.8 1.3 %shard_map.93 = (bf16[2,4,128,128]{3,2,1,0:T(8,128)(2,1)S(1)}, bf16[2,4,128,128]{3,2,1,0:T(8,128)(2,1)S(1)}, bf16[2,4,128,128]{3,2,1,0:T(8,128)(2,1)S(1)}, bf16[2,4,128,128]{3,2,1,0:T(8,128)(2,1)S(1)}) custom-call(bf16[4,1024,128]{2,1,0:T(8,128)(2,1)S(1)} %get-tuple-element.64.ext_ref, bf16[4,256,128]{2,1,0:T(8,128)(2,1)S(1)} %collective-permute-done.14.even_ref, ...), custom_call_target="tpu_custom_call" | custom-call | tf_op jit(solution)/shard_map/pallas_call | solution.py:149
  44.0 1.1 %collective-permute-start.16 = (bf16[2,4,128,128]{3,2,1,0:T(8,128)(2,1)S(1)}, bf16[2,4,128,128]{3,2,1,0:T(8,128)(2,1)S(1)}, u32[]{:S(2)}, u32[]{:S(2)}) collective-permute-start(bf16[2,4,128,128]{3,2,1,0:T(8,128)(2,1)S(1)} %get-tuple-element.71), channel_id=1, source_target_pairs={{0,4},{2,6},{4,0},{6,2},{8,12},{10,14},{12,8},{14,10},{16,20},{18,... | collective-permute-start | bytes 786440 | tf_op jit(solution)/shard_map/ppermute | solution.py:275
  45.1 0.1 collective-permute-start.17
  45.3 1.5 %collective-permute-start.18 = (bf16[2,4,128,128]{3,2,1,0:T(8,128)(2,1)S(1)}, bf16[2,4,128,128]{3,2,1,0:T(8,128)(2,1)S(1)}, u32[]{:S(2)}, u32[]{:S(2)}) collective-permute-start(bf16[2,4,128,128]{3,2,1,0:T(8,128)(2,1)S(1)} %get-tuple-element.73), channel_id=1, source_target_pairs={{0,6},{2,4},{4,2},{6,0},{8,14},{10,12},{12,10},{14,8},{16,22},{18,... | collective-permute-start | bytes 786440 | tf_op jit(solution)/shard_map/ppermute | solution.py:275
  46.8 5.9 %collective-permute-start.13 = (bf16[4,4,128,128]{3,2,1,0:T(8,128)(2,1)S(1)}, bf16[4,4,128,128]{3,2,1,0:T(8,128)(2,1)S(1)}, u32[]{:S(2)}, u32[]{:S(2)}) collective-permute-start(bf16[4,4,128,128]{3,2,1,0:T(8,128)(2,1)S(1)} %shard_map.92), channel_id=1, source_target_pairs={{0,1},{1,0},{2,3},{3,2},{4,5},{5,4},{6,7},{7,6},{8,9},{9,8},{10,11... | collective-permute-start | bytes 1572872 | tf_op jit(solution)/shard_map/ppermute | solution.py:325
  52.7 2.3 %collective-permute-done.16.refs_1_.refs_6_ = bf16[2,4,128,128]{3,2,1,0:T(8,128)(2,1)S(1)} collective-permute-done((bf16[2,4,128,128]{3,2,1,0:T(8,128)(2,1)S(1)}, bf16[2,4,128,128]{3,2,1,0:T(8,128)(2,1)S(1)}, u32[]{:S(2)}, u32[]{:S(2)}) %collective-permute-start.16) | collective-permute-done | bytes 262176 | tf_op jit(solution)/shard_map/ppermute | solution.py:275
  55.0 5.0 %collective-permute-start.19 = (bf16[4,4,128,128]{3,2,1,0:T(8,128)(2,1)S(1)}, bf16[4,4,128,128]{3,2,1,0:T(8,128)(2,1)S(1)}, u32[]{:S(2)}, u32[]{:S(2)}) collective-permute-start(bf16[4,4,128,128]{3,2,1,0:T(8,128)(2,1)S(1)} %shard_map.94), channel_id=1, source_target_pairs={{0,1},{1,0},{2,3},{3,2},{4,5},{5,4},{6,7},{7,6},{8,9},{9,8},{10,11... | collective-permute-start | bytes 1572872 | tf_op jit(solution)/shard_map/ppermute | solution.py:325
  60.0 1.5 %collective-permute-done.19.refs_9_ = bf16[4,4,128,128]{3,2,1,0:T(8,128)(2,1)S(1)} collective-permute-done((bf16[4,4,128,128]{3,2,1,0:T(8,128)(2,1)S(1)}, bf16[4,4,128,128]{3,2,1,0:T(8,128)(2,1)S(1)}, u32[]{:S(2)}, u32[]{:S(2)}) %collective-permute-start.19) | collective-permute-done | bytes 524320 | tf_op jit(solution)/shard_map/ppermute | solution.py:325
  61.5 1.4 %shard_map.95 = (bf16[128,2048]{1,0:T(8,128)(2,1)}, bf16[128,2048]{1,0:T(8,128)(2,1)}, bf16[128,2048]{1,0:T(8,128)(2,1)}, bf16[128,2048]{1,0:T(8,128)(2,1)}) custom-call(bf16[2,4,128,128]{3,2,1,0:T(8,128)(2,1)S(1)} %get-tuple-element.52.refs_0_, bf16[2,4,128,128]{3,2,1,0:T(8,128)(2,1)S(1)} %collective-permute-done.10.refs_1_, ...), custom_call_target="tpu_custom_call" | custom-call | tf_op jit(solution)/shard_map/pallas_call | solution.py:242
  (24 shorter events, 0.4 us)
Async XLA Ops:
  3.5 2.4 %collective-permute-start = (bf16[4,4,128,128]{3,2,1,0:T(8,128)(2,1)}, bf16[4,4,128,128]{3,2,1,0:T(8,128)(2,1)S(1)}, u32[]{:S(2)}, u32[]{:S(2)}) collective-permute-start(bf16[4,4,128,128]{3,2,1,0:T(8,128)(2,1)} %get-tuple-element.40), channel_id=1, source_target_pairs={{0,1},{1,0},{2,3},{3,2},{4,5},{5,4},{6,7},{7,6},{8,9},{9,8},{10,11... | collective-permute-start | bytes 1572872 | tf_op jit(solution)/shard_map/ppermute | solution.py:285
  4.2 4.5 %collective-permute-start.6 = (bf16[4,4,128,128]{3,2,1,0:T(8,128)(2,1)}, bf16[4,4,128,128]{3,2,1,0:T(8,128)(2,1)S(1)}, u32[]{:S(2)}, u32[]{:S(2)}) collective-permute-start(bf16[4,4,128,128]{3,2,1,0:T(8,128)(2,1)} %get-tuple-element.49), channel_id=1, source_target_pairs={{0,1},{1,0},{2,3},{3,2},{4,5},{5,4},{6,7},{7,6},{8,9},{9,8},{10,11... | collective-permute-start | bytes 1572872 | tf_op jit(solution)/shard_map/ppermute | solution.py:285
  5.9 2.8 %copy-start = (bf16[4,4,128,128]{3,2,1,0:T(8,128)(2,1)S(1)}, bf16[4,4,128,128]{3,2,1,0:T(8,128)(2,1)}, u32[]{:S(2)}) copy-start(bf16[4,4,128,128]{3,2,1,0:T(8,128)(2,1)} %get-tuple-element.48.mine_ref) | copy-start | bytes 1572868
  6.0 8.5 %collective-permute-start.1 = (bf16[2,4,128,128]{3,2,1,0:T(8,128)(2,1)S(1)}, bf16[2,4,128,128]{3,2,1,0:T(8,128)(2,1)S(1)}, u32[]{:S(2)}, u32[]{:S(2)}) collective-permute-start(bf16[2,4,128,128]{3,2,1,0:T(8,128)(2,1)S(1)} %get-tuple-element.42), channel_id=1, source_target_pairs={{0,6},{2,4},{4,2},{6,0},{8,14},{10,12},{12,10},{14,8},{16,22},{18,... | collective-permute-start | bytes 786440 | tf_op jit(solution)/shard_map/ppermute | solution.py:275
  8.2 13.2 %collective-permute-start.2 = (bf16[2,4,128,128]{3,2,1,0:T(8,128)(2,1)S(1)}, bf16[2,4,128,128]{3,2,1,0:T(8,128)(2,1)S(1)}, u32[]{:S(2)}, u32[]{:S(2)}) collective-permute-start(bf16[2,4,128,128]{3,2,1,0:T(8,128)(2,1)S(1)} %get-tuple-element.43), channel_id=1, source_target_pairs={{0,4},{2,6},{4,0},{6,2},{8,12},{10,14},{12,8},{14,10},{16,20},{18,... | collective-permute-start | bytes 786440 | tf_op jit(solution)/shard_map/ppermute | solution.py:275
  8.5 13.0 %collective-permute-start.3 = (bf16[2,4,128,128]{3,2,1,0:T(8,128)(2,1)S(1)}, bf16[2,4,128,128]{3,2,1,0:T(8,128)(2,1)S(1)}, u32[]{:S(2)}, u32[]{:S(2)}) collective-permute-start(bf16[2,4,128,128]{3,2,1,0:T(8,128)(2,1)S(1)} %get-tuple-element.44), channel_id=1, source_target_pairs={{0,2},{2,0},{4,6},{6,4},{8,10},{10,8},{12,14},{14,12},{16,18},{18,... | collective-permute-start | bytes 786440 | tf_op jit(solution)/shard_map/ppermute | solution.py:275
  8.8 22.0 %collective-permute-start.7 = (bf16[2,4,128,128]{3,2,1,0:T(8,128)(2,1)S(1)}, bf16[2,4,128,128]{3,2,1,0:T(8,128)(2,1)S(1)}, u32[]{:S(2)}, u32[]{:S(2)}) collective-permute-start(bf16[2,4,128,128]{3,2,1,0:T(8,128)(2,1)S(1)} %get-tuple-element.50), channel_id=1, source_target_pairs={{0,6},{2,4},{4,2},{6,0},{8,14},{10,12},{12,10},{14,8},{16,22},{18,... | collective-permute-start | bytes 786440 | tf_op jit(solution)/shard_map/ppermute | solution.py:275
  21.5 6.0 %copy-start.1 = (s32[4096]{0:T(1024)S(1)}, s32[4096]{0:T(1024)}, u32[]{:S(2)}) copy-start(s32[4096]{0:T(1024)} %param.9) | copy-start | bytes 49156
  21.6 9.2 %collective-permute-start.4 = (bf16[4,256,128]{2,1,0:T(8,128)(2,1)S(1)}, bf16[4,256,128]{2,1,0:T(8,128)(2,1)S(1)}, u32[]{:S(2)}, u32[]{:S(2)}) collective-permute-start(bf16[4,256,128]{2,1,0:T(8,128)(2,1)S(1)} %get-tuple-element.46), channel_id=1, source_target_pairs={{0,8},{8,0},{2,10},{10,2},{4,12},{12,4},{6,14},{14,6},{16,24},{24,... | collective-permute-start | bytes 786440 | tf_op jit(solution)/shard_map/ppermute | solution.py:300
  21.7 10.1 %collective-permute-start.5 = (bf16[4,256,128]{2,1,0:T(8,128)(2,1)S(1)}, bf16[4,256,128]{2,1,0:T(8,128)(2,1)S(1)}, u32[]{:S(2)}, u32[]{:S(2)}) collective-permute-start(bf16[4,256,128]{2,1,0:T(8,128)(2,1)S(1)} %get-tuple-element.47), channel_id=1, source_target_pairs={{8,16},{16,8},{10,18},{18,10},{12,20},{20,12},{14,22},{22,14},{9,1... | collective-permute-start | bytes 786440 | tf_op jit(solution)/shard_map/ppermute | solution.py:301
  26.2 8.4 %collective-permute-start.8 = (bf16[2,4,128,128]{3,2,1,0:T(8,128)(2,1)S(1)}, bf16[2,4,128,128]{3,2,1,0:T(8,128)(2,1)S(1)}, u32[]{:S(2)}, u32[]{:S(2)}) collective-permute-start(bf16[2,4,128,128]{3,2,1,0:T(8,128)(2,1)S(1)} %get-tuple-element.55), channel_id=1, source_target_pairs={{0,4},{2,6},{4,0},{6,2},{8,12},{10,14},{12,8},{14,10},{16,20},{18,... | collective-permute-start | bytes 786440 | tf_op jit(solution)/shard_map/ppermute | solution.py:275
  27.5 7.1 %collective-permute-start.9 = (bf16[2,4,128,128]{3,2,1,0:T(8,128)(2,1)S(1)}, bf16[2,4,128,128]{3,2,1,0:T(8,128)(2,1)S(1)}, u32[]{:S(2)}, u32[]{:S(2)}) collective-permute-start(bf16[2,4,128,128]{3,2,1,0:T(8,128)(2,1)S(1)} %get-tuple-element.56), channel_id=1, source_target_pairs={{0,2},{2,0},{4,6},{6,4},{8,10},{10,8},{12,14},{14,12},{16,18},{18,... | collective-permute-start | bytes 786440 | tf_op jit(solution)/shard_map/ppermute | solution.py:275
  33.1 9.3 %collective-permute-start.11 = (bf16[2,4,128,128]{3,2,1,0:T(8,128)(2,1)S(1)}, bf16[2,4,128,128]{3,2,1,0:T(8,128)(2,1)S(1)}, u32[]{:S(2)}, u32[]{:S(2)}) collective-permute-start(bf16[2,4,128,128]{3,2,1,0:T(8,128)(2,1)S(1)} %get-tuple-element.57), channel_id=1, source_target_pairs={{0,2},{2,0},{4,6},{6,4},{8,10},{10,8},{12,14},{14,12},{16,18},{18,... | collective-permute-start | bytes 786440 | tf_op jit(solution)/shard_map/ppermute | solution.py:275
  34.3 8.0 %collective-permute-start.10 = (bf16[2,4,128,128]{3,2,1,0:T(8,128)(2,1)S(1)}, bf16[2,4,128,128]{3,2,1,0:T(8,128)(2,1)S(1)}, u32[]{:S(2)}, u32[]{:S(2)}) collective-permute-start(bf16[2,4,128,128]{3,2,1,0:T(8,128)(2,1)S(1)} %get-tuple-element.58), channel_id=1, source_target_pairs={{0,4},{2,6},{4,0},{6,2},{8,12},{10,14},{12,8},{14,10},{16,20},{18,... | collective-permute-start | bytes 786440 | tf_op jit(solution)/shard_map/ppermute | solution.py:275
  34.7 7.6 %collective-permute-start.14 = (bf16[4,256,128]{2,1,0:T(8,128)(2,1)S(1)}, bf16[4,256,128]{2,1,0:T(8,128)(2,1)S(1)}, u32[]{:S(2)}, u32[]{:S(2)}) collective-permute-start(bf16[4,256,128]{2,1,0:T(8,128)(2,1)S(1)} %get-tuple-element.67), channel_id=1, source_target_pairs={{0,8},{8,0},{2,10},{10,2},{4,12},{12,4},{6,14},{14,6},{16,24},{24,... | collective-permute-start | bytes 786440 | tf_op jit(solution)/shard_map/ppermute | solution.py:300
  34.8 8.0 %collective-permute-start.15 = (bf16[4,256,128]{2,1,0:T(8,128)(2,1)S(1)}, bf16[4,256,128]{2,1,0:T(8,128)(2,1)S(1)}, u32[]{:S(2)}, u32[]{:S(2)}) collective-permute-start(bf16[4,256,128]{2,1,0:T(8,128)(2,1)S(1)} %get-tuple-element.68), channel_id=1, source_target_pairs={{8,16},{16,8},{10,18},{18,10},{12,20},{20,12},{14,22},{22,14},{9,1... | collective-permute-start | bytes 786440 | tf_op jit(solution)/shard_map/ppermute | solution.py:301
  37.9 8.9 %collective-permute-start.12 = (bf16[2,4,128,128]{3,2,1,0:T(8,128)(2,1)S(1)}, bf16[2,4,128,128]{3,2,1,0:T(8,128)(2,1)S(1)}, u32[]{:S(2)}, u32[]{:S(2)}) collective-permute-start(bf16[2,4,128,128]{3,2,1,0:T(8,128)(2,1)S(1)} %get-tuple-element.59), channel_id=1, source_target_pairs={{0,6},{2,4},{4,2},{6,0},{8,14},{10,12},{12,10},{14,8},{16,22},{18,... | collective-permute-start | bytes 786440 | tf_op jit(solution)/shard_map/ppermute | solution.py:275
  44.0 10.9 %collective-permute-start.16 = (bf16[2,4,128,128]{3,2,1,0:T(8,128)(2,1)S(1)}, bf16[2,4,128,128]{3,2,1,0:T(8,128)(2,1)S(1)}, u32[]{:S(2)}, u32[]{:S(2)}) collective-permute-start(bf16[2,4,128,128]{3,2,1,0:T(8,128)(2,1)S(1)} %get-tuple-element.71), channel_id=1, source_target_pairs={{0,4},{2,6},{4,0},{6,2},{8,12},{10,14},{12,8},{14,10},{16,20},{18,... | collective-permute-start | bytes 786440 | tf_op jit(solution)/shard_map/ppermute | solution.py:275
  45.1 9.8 %collective-permute-start.17 = (bf16[2,4,128,128]{3,2,1,0:T(8,128)(2,1)S(1)}, bf16[2,4,128,128]{3,2,1,0:T(8,128)(2,1)S(1)}, u32[]{:S(2)}, u32[]{:S(2)}) collective-permute-start(bf16[2,4,128,128]{3,2,1,0:T(8,128)(2,1)S(1)} %get-tuple-element.72), channel_id=1, source_target_pairs={{0,2},{2,0},{4,6},{6,4},{8,10},{10,8},{12,14},{14,12},{16,18},{18,... | collective-permute-start | bytes 786440 | tf_op jit(solution)/shard_map/ppermute | solution.py:275
  45.3 9.7 %collective-permute-start.18 = (bf16[2,4,128,128]{3,2,1,0:T(8,128)(2,1)S(1)}, bf16[2,4,128,128]{3,2,1,0:T(8,128)(2,1)S(1)}, u32[]{:S(2)}, u32[]{:S(2)}) collective-permute-start(bf16[2,4,128,128]{3,2,1,0:T(8,128)(2,1)S(1)} %get-tuple-element.73), channel_id=1, source_target_pairs={{0,6},{2,4},{4,2},{6,0},{8,14},{10,12},{12,10},{14,8},{16,22},{18,... | collective-permute-start | bytes 786440 | tf_op jit(solution)/shard_map/ppermute | solution.py:275
  46.8 13.2 %collective-permute-start.13 = (bf16[4,4,128,128]{3,2,1,0:T(8,128)(2,1)S(1)}, bf16[4,4,128,128]{3,2,1,0:T(8,128)(2,1)S(1)}, u32[]{:S(2)}, u32[]{:S(2)}) collective-permute-start(bf16[4,4,128,128]{3,2,1,0:T(8,128)(2,1)S(1)} %shard_map.92), channel_id=1, source_target_pairs={{0,1},{1,0},{2,3},{3,2},{4,5},{5,4},{6,7},{7,6},{8,9},{9,8},{10,11... | collective-permute-start | bytes 1572872 | tf_op jit(solution)/shard_map/ppermute | solution.py:325
  55.0 6.6 %collective-permute-start.19 = (bf16[4,4,128,128]{3,2,1,0:T(8,128)(2,1)S(1)}, bf16[4,4,128,128]{3,2,1,0:T(8,128)(2,1)S(1)}, u32[]{:S(2)}, u32[]{:S(2)}) collective-permute-start(bf16[4,4,128,128]{3,2,1,0:T(8,128)(2,1)S(1)} %shard_map.94), channel_id=1, source_target_pairs={{0,1},{1,0},{2,3},{3,2},{4,5},{5,4},{6,7},{7,6},{8,9},{9,8},{10,11... | collective-permute-start | bytes 1572872 | tf_op jit(solution)/shard_map/ppermute | solution.py:325
